TPU v7x, 32 devices: a whole 2x2x4 slice. The times are simulated.
32 devices in a mesh: ctx: 4 (over y, x), ch: 8 (over z, core).
Axes of the slice: x: 2, y: 2, z: 4, core: 2. Of those that a mesh axis runs over, the one named last changes fastest.
Arguments:
- hidden_in: bfloat16 [4096, 1024], P(('ctx', 'ch')), may hold values from -6 to 6
- norm_gain: float32 [1024], replicated, may hold values from 0.1 to 1.9
- in_weight: bfloat16 [1024, 4096], P('ch'), may hold values from -0.1875 to 0.1875
- conv_weight: float32 [2048, 4], replicated, may hold values from -2 to 2
- conv_bias: float32 [2048], replicated, may hold values from -2 to 2
- x_weight: bfloat16 [2048, 96], replicated, may hold values from -0.25 to 0.25
- dt_weight: bfloat16 [64, 2048], P(None, 'ch'), may hold values from -0.75 to 0.75
- dt_bias: float32 [2048], P('ch'), may hold values from -8.5 to -2.5
- a_log: float32 [2048, 16], P('ch'), may hold values from 0 to 2.77
- skip: float32 [2048], P('ch'), may hold values from 0.5 to 1.5
- out_weight: bfloat16 [2048, 1024], P('ch'), may hold values from -0.25 to 0.25
- lengths: int32 [4, 4], P('ctx'), may hold values from 1 to 1021, as said below
- resets: int32 [4096], P('ctx'), may hold values from 0 to 1, as said below
- out_grad: bfloat16 [4096, 1024], P(('ctx', 'ch')), may hold values from -6 to 6
Outputs:
- output: bfloat16 [4096, 1024], P(('ctx', 'ch'))
- d_hidden: bfloat16 [4096, 1024], P(('ctx', 'ch'))
- d_norm_gain: float32 [1024], P('ch')
- d_in_weight: float32 [1024, 4096], P('ch')
- d_conv_weight: float32 [2048, 4], P('ch')
- d_conv_bias: float32 [2048], P('ch')
- d_x_weight: float32 [2048, 96], P('ch')
- d_dt_weight: float32 [64, 2048], P(None, 'ch')
- d_dt_bias: float32 [2048], P('ch')
- d_a_log: float32 [2048, 16], P('ch')
- d_skip: float32 [2048], P('ch')
- d_out_weight: float32 [2048, 1024], P('ch')
Inputs may be any that keep to these rules, and one draw needn't show every extreme that they name: Each row lists the context lengths of one group in order and sums to 1024; the second context of a group is its longest. `resets`: 1 marks a token where the scan state is zeroed.
All inputs are finite; a program needn't handle non-finite values.
Results may differ from a plain program's by a relative error of at most 0.012.
The roundings to bfloat16 on the way count: a program that leaves them out, or rounds other values in their place, can miss the bound.
Values may be sent and summed in bfloat16 or wider, within the bound.
No kernel may reach another device: no remote copies, remote signals or barrier semaphores. Data moves between devices by JAX's collectives and lax.ppermute only.
A program may use at most 256 MiB of HBM per device.

v0:
```python
import math

import jax
import jax.numpy as jnp
from jax import lax
from jax.sharding import PartitionSpec as P

HIGH = lax.Precision.HIGHEST
eps = 1e-05


def passed_along(value, axis, steps):
    count = lax.axis_size(axis)
    first, last = (max(0, -steps), min(count, count - steps))
    return lax.ppermute(value, axis, [(source, source + steps) for source in range(first, last)])


def in_blocks(array, dim, peers):
    dims = array.shape
    tiles = array.reshape(*dims[:dim], peers, dims[dim] // peers, *dims[dim + 1 :])
    return jnp.moveaxis(tiles, dim, 0)


def sum_at_owner(array, axis, dim):
    tiles = in_blocks(array, dim, lax.axis_size(axis))
    arrived = lax.all_to_all(tiles, axis, split_axis=0, concat_axis=0, tiled=True)
    return arrived.astype(jnp.float32).sum(axis=0)


def silu(v):
    return v * jax.nn.sigmoid(v)


def silu_slope(v):
    sig = jax.nn.sigmoid(v)
    return sig * (1.0 + v * (1.0 - sig))


def context_place(offsets, places):
    begins = jnp.max(jnp.where(offsets[:, None] <= places[None, :], offsets[:, None], 0), axis=0)
    return places - begins


def chain(first, second):
    return (first[0] * second[0], second[0] * first[1] + second[1])


def block_inputs(arrays, keep, start, size):
    pieces = tuple((lax.dynamic_slice_in_dim(a, start, size, 1) for a in arrays))
    return (pieces, lax.dynamic_slice_in_dim(keep, start, size, 0))


def split_sub(array, sub):
    lead = array.shape[:-1]
    blocks = array.shape[-1] // sub
    return jnp.moveaxis(array.reshape(lead + (blocks, sub)), -1, 0)


def merge_sub(array):
    moved = jnp.moveaxis(array, 0, -1)
    return moved.reshape(moved.shape[:-2] + (moved.shape[-2] * moved.shape[-1],))


def step_decay(delta_row, keep_row, rates):
    return jnp.exp(delta_row[:, None, :] * rates[:, :, None]) * keep_row[None, None, :]


def local_sweep(delta_sub, values_sub, b_sub, keep_sub, rates, state):
    rises = []
    products = []
    running = None
    product = None
    for j in range(delta_sub.shape[0]):
        factor = step_decay(delta_sub[j], keep_sub[j], rates)
        push = (delta_sub[j] * values_sub[j])[:, None, :] * b_sub[j][None, :, :]
        if j == 0:
            running = push
            product = factor
        else:
            running = factor * running + push
            product = factor * product
        rises.append(running)
        products.append(product)
    factors, adds = lax.associative_scan(chain, (products[-1], rises[-1]), axis=2)
    ends = factors * state[:, :, None] + adds
    carry_in = jnp.concatenate([state[:, :, None], ends[:, :, :-1]], axis=2)
    tracks = [rises[j] + products[j] * carry_in for j in range(len(rises))]
    return (tracks, carry_in, ends[:, :, -1])


def scan_forward(delta, values, b_in, c_out, keep, rates, size):
    chans, total = delta.shape
    states_n = rates.shape[1]
    count = total // size
    sub = math.gcd(size, 16)

    def step(index, carry):
        state, result, starts = carry
        start = index * size
        (blk_delta, blk_values, blk_b, blk_c), blk_keep = block_inputs(
            (delta, values, b_in, c_out), keep, start, size
        )
        c_sub = split_sub(blk_c, sub)
        tracks, carry_in, final = local_sweep(
            split_sub(blk_delta, sub),
            split_sub(blk_values, sub),
            split_sub(blk_b, sub),
            split_sub(blk_keep, sub),
            rates,
            state,
        )
        outs = jnp.stack(
            [jnp.sum(tracks[j] * c_sub[j][None, :, :], axis=1) for j in range(sub)], axis=0
        )
        starts = lax.dynamic_update_index_in_dim(starts, state, index, 0)
        result = lax.dynamic_update_slice_in_dim(result, merge_sub(outs), start, 1)
        return (final, result, starts)

    init = (
        jnp.zeros((chans, states_n), jnp.float32),
        jnp.zeros((chans, total), jnp.float32),
        jnp.zeros((count, chans, states_n), jnp.float32),
    )
    _, result, starts = lax.fori_loop(0, count, step, init)
    return (result, starts)


def scan_backward(delta, values, b_in, c_out, keep, rates, starts, d_scan, size):
    chans, total = delta.shape
    states_n = rates.shape[1]
    count = total // size
    sub = math.gcd(size, 16)

    def step(turn, carry):
        incoming, d_delta, d_values, d_b, d_c, d_rates = carry
        index = count - 1 - turn
        start = index * size
        (blk_delta, blk_values, blk_b, blk_c, blk_dy), blk_keep = block_inputs(
            (delta, values, b_in, c_out, d_scan), keep, start, size
        )
        delta_sub = split_sub(blk_delta, sub)
        values_sub = split_sub(blk_values, sub)
        b_sub = split_sub(blk_b, sub)
        c_sub = split_sub(blk_c, sub)
        dy_sub = split_sub(blk_dy, sub)
        keep_sub = split_sub(blk_keep, sub)
        state = lax.dynamic_index_in_dim(starts, index, 0, keepdims=False)
        tracks, carry_in, _ = local_sweep(delta_sub, values_sub, b_sub, keep_sub, rates, state)
        decays = [step_decay(delta_sub[j], keep_sub[j], rates) for j in range(sub)]
        backs = [None] * sub
        spans = [None] * sub
        for j in range(sub - 1, -1, -1):
            direct = dy_sub[j][:, None, :] * c_sub[j][None, :, :]
            if j == sub - 1:
                backs[j] = direct
                spans[j] = jnp.ones_like(direct)
            else:
                backs[j] = direct + decays[j + 1] * backs[j + 1]
                spans[j] = decays[j + 1] * spans[j + 1]
        lead_gain = decays[0] * spans[0]
        lead_add = decays[0] * backs[0]
        factors, adds = lax.associative_scan(
            chain, (jnp.flip(lead_gain, 2), jnp.flip(lead_add, 2)), axis=2
        )
        flipped = jnp.concatenate(
            [incoming[:, :, None], factors[:, :, :-1] * incoming[:, :, None] + adds[:, :, :-1]],
            axis=2,
        )
        carry_out = jnp.flip(flipped, 2)
        onward = lead_gain[:, :, 0] * carry_out[:, :, 0] + lead_add[:, :, 0]
        parts_delta = []
        parts_values = []
        parts_b = []
        parts_c = []
        for j in range(sub):
            adjoint = backs[j] + spans[j] * carry_out
            before = carry_in if j == 0 else tracks[j - 1]
            through = adjoint * before * decays[j]
            parts_delta.append(
                jnp.sum(
                    through * rates[:, :, None]
                    + adjoint * b_sub[j][None, :, :] * values_sub[j][:, None, :],
                    axis=1,
                )
            )
            parts_values.append(jnp.sum(adjoint * b_sub[j][None, :, :], axis=1) * delta_sub[j])
            parts_b.append(jnp.sum(adjoint * (delta_sub[j] * values_sub[j])[:, None, :], axis=0))
            parts_c.append(jnp.sum(dy_sub[j][:, None, :] * tracks[j], axis=0))
            d_rates = d_rates + jnp.sum(through * delta_sub[j][:, None, :], axis=2)
        d_delta = lax.dynamic_update_slice_in_dim(
            d_delta, merge_sub(jnp.stack(parts_delta, 0)), start, 1
        )
        d_values = lax.dynamic_update_slice_in_dim(
            d_values, merge_sub(jnp.stack(parts_values, 0)), start, 1
        )
        d_b = lax.dynamic_update_slice_in_dim(d_b, merge_sub(jnp.stack(parts_b, 0)), start, 1)
        d_c = lax.dynamic_update_slice_in_dim(d_c, merge_sub(jnp.stack(parts_c, 0)), start, 1)
        return (onward, d_delta, d_values, d_b, d_c, d_rates)

    init = (
        jnp.zeros((chans, states_n), jnp.float32),
        jnp.zeros((chans, total), jnp.float32),
        jnp.zeros((chans, total), jnp.float32),
        jnp.zeros((states_n, total), jnp.float32),
        jnp.zeros((states_n, total), jnp.float32),
        jnp.zeros((chans, states_n), jnp.float32),
    )
    _, d_delta, d_values, d_b, d_c, d_rates = lax.fori_loop(0, count, step, init)
    return (d_delta, d_values, d_b, d_c, d_rates)


def on_device(
    hidden_in,
    norm_gain,
    in_weight,
    conv_weight,
    conv_bias,
    x_weight,
    dt_weight,
    dt_bias,
    a_log,
    skip,
    out_weight,
    lengths,
    resets,
    out_grad,
):
    f32 = jnp.float32
    bf16 = jnp.bfloat16
    full_in, full_out = (
        lax.all_gather(in_weight, "ch", axis=0, tiled=True),
        lax.all_gather(out_weight, "ch", axis=0, tiled=True),
    )
    inner = full_out.shape[0]
    tok_rows = hidden_in.shape[0]
    taps = conv_weight.shape[1]
    hidden = hidden_in.astype(f32)
    scale = lax.rsqrt(jnp.mean(hidden * hidden, axis=1, keepdims=True) + eps)
    unit = hidden * scale
    normed = (unit * norm_gain[None, :]).astype(bf16)
    mixed = lax.dot_general(full_in, normed, (((0,), (1,)), ((), ())), preferred_element_type=f32)
    x_tokens = mixed[:inner].astype(bf16)
    gate_tokens = mixed[inner:].astype(bf16)
    left_rim = passed_along(x_tokens[:, tok_rows - (taps - 1) :], "ch", 1)
    x_extended = jnp.concatenate([left_rim, x_tokens], axis=1).astype(f32)
    sizes = lengths[0]
    offsets = jnp.cumsum(sizes) - sizes
    first_place = lax.axis_index("ch") * tok_rows
    local_in = context_place(offsets, first_place + jnp.arange(tok_rows, dtype=jnp.int32))
    masks = [(local_in >= taps - 1 - k).astype(f32) for k in range(taps)]
    pre = conv_bias[:, None] + sum(
        [
            conv_weight[:, k : k + 1] * x_extended[:, k : k + tok_rows] * masks[k][None, :]
            for k in range(taps)
        ]
    )
    values_tok = silu(pre).astype(bf16)
    proj_tok = lax.dot_general(
        x_weight, values_tok, (((0,), (0,)), ((), ())), preferred_element_type=f32
    ).astype(bf16)
    value_cols, z_cols = (
        lax.all_to_all(values_tok, "ch", split_axis=0, concat_axis=1, tiled=True),
        lax.all_to_all(gate_tokens, "ch", split_axis=0, concat_axis=1, tiled=True),
    )
    proj = lax.all_gather(proj_tok, "ch", axis=1, tiled=True)
    chans, total = value_cols.shape
    value_f = value_cols.astype(f32)
    z_vals = z_cols.astype(f32)
    where_in = context_place(offsets, jnp.arange(total, dtype=jnp.int32))
    rank = dt_weight.shape[0]
    states_n = a_log.shape[1]
    dt_low = proj[:rank]
    b_in = proj[rank : rank + states_n].astype(f32)
    c_out = proj[rank + states_n :].astype(f32)
    dt_pre = (
        lax.dot_general(dt_weight, dt_low, (((0,), (0,)), ((), ())), preferred_element_type=f32)
        + dt_bias[:, None]
    )
    delta = jax.nn.softplus(dt_pre)
    rates = -jnp.exp(a_log)
    keep = jnp.where((where_in == 0) | (resets == 1), 0.0, 1.0).astype(f32)
    size = math.gcd(total, 2048)
    scanned, starts = scan_forward(delta, value_f, b_in, c_out, keep, rates, size)
    full_scan = scanned + skip[:, None] * value_f
    gate_act = silu(z_vals)
    gated = (full_scan * gate_act).astype(bf16)
    gated_rows = lax.all_to_all(gated, "ch", split_axis=1, concat_axis=0, tiled=True)
    branch = lax.dot_general(
        gated_rows, full_out, (((0,), (0,)), ((), ())), preferred_element_type=f32
    )
    output = (hidden + branch).astype(bf16)
    d_gated_rows = lax.dot_general(
        full_out, out_grad, (((1,), (1,)), ((), ())), preferred_element_type=f32
    ).astype(bf16)
    d_out_weight = lax.dot_general(
        gated_rows, out_grad, (((1,), (0,)), ((), ())), preferred_element_type=f32
    )
    d_gated = lax.all_to_all(d_gated_rows, "ch", split_axis=0, concat_axis=1, tiled=True).astype(
        f32
    )
    d_scan = d_gated * gate_act
    d_gate = (d_gated * full_scan * silu_slope(z_vals)).astype(bf16)
    d_skip = jnp.sum(d_scan * value_f, axis=1)
    d_delta, d_state_values, d_b, d_c, d_rates = scan_backward(
        delta, value_f, b_in, c_out, keep, rates, starts, d_scan, size
    )
    d_dt_pre = d_delta * jax.nn.sigmoid(dt_pre)
    d_dt_bias = jnp.sum(d_dt_pre, axis=1)
    d_dt_weight = lax.dot_general(
        dt_low.astype(f32), d_dt_pre, (((1,), (1,)), ((), ())), precision=HIGH
    )
    d_low = lax.dot_general(
        dt_weight.astype(f32), d_dt_pre, (((1,), (0,)), ((), ())), precision=HIGH
    )
    d_a_log = d_rates * rates
    partial_grad = jnp.concatenate([d_low, d_b, d_c], axis=0)
    own_grad = sum_at_owner(partial_grad.astype(jnp.bfloat16), "ch", 1).astype(bf16)
    value_part = d_state_values + d_scan * skip[:, None]
    d_value_tok, d_gate_tok = (
        lax.all_to_all(
            value_part.astype(jnp.bfloat16), "ch", split_axis=1, concat_axis=0, tiled=True
        ).astype(value_part.dtype),
        lax.all_to_all(
            d_gate.astype(f32).astype(jnp.bfloat16), "ch", split_axis=1, concat_axis=0, tiled=True
        ).astype(jnp.float32),
    )
    d_values = d_value_tok + lax.dot_general(
        x_weight, own_grad, (((1,), (0,)), ((), ())), preferred_element_type=f32
    )
    d_x_weight = lax.dot_general(
        values_tok, own_grad, (((1,), (1,)), ((), ())), preferred_element_type=f32
    )
    d_pre = d_values * silu_slope(pre)
    d_conv_bias = jnp.sum(d_pre, axis=1)
    masked = [d_pre * masks[k][None, :] for k in range(taps)]
    d_conv_weight = jnp.stack(
        [jnp.sum(masked[k] * x_extended[:, k : k + tok_rows], axis=1) for k in range(taps)], axis=1
    )
    spread_back = sum(
        [
            conv_weight[:, k : k + 1] * jnp.pad(masked[k], ((0, 0), (k, taps - 1 - k)))
            for k in range(taps)
        ]
    )
    from_next = passed_along(spread_back[:, : taps - 1], "ch", -1)
    d_x_tok = spread_back[:, taps - 1 :] + jnp.pad(from_next, ((0, 0), (tok_rows - (taps - 1), 0)))
    d_mixed = jnp.concatenate([d_x_tok.astype(bf16), d_gate_tok.astype(bf16)], axis=0)
    d_normed = lax.dot_general(
        d_mixed, full_in, (((0,), (1,)), ((), ())), preferred_element_type=f32
    )
    d_in_weight = lax.dot_general(
        normed, d_mixed, (((0,), (1,)), ((), ())), preferred_element_type=f32
    )
    d_gain = jnp.sum(d_normed * unit, axis=0)
    d_unit = d_normed * norm_gain[None, :]
    d_hidden = (
        out_grad.astype(f32)
        + scale * (d_unit - unit * jnp.mean(d_unit * unit, axis=1, keepdims=True))
    ).astype(bf16)
    in_part, out_part, gain_part, xw_part, cw_part, cb_part = (
        lax.psum_scatter(d_in_weight, "ch", scatter_dimension=0, tiled=True),
        lax.psum_scatter(d_out_weight, "ch", scatter_dimension=0, tiled=True),
        lax.psum_scatter(d_gain, "ch", scatter_dimension=0, tiled=True),
        lax.psum_scatter(d_x_weight, "ch", scatter_dimension=0, tiled=True),
        lax.psum_scatter(d_conv_weight, "ch", scatter_dimension=0, tiled=True),
        lax.psum_scatter(d_conv_bias, "ch", scatter_dimension=0, tiled=True),
    )
    (
        in_sum,
        out_sum,
        gain_sum,
        x_w_sum,
        conv_w_sum,
        conv_b_sum,
        dt_w_sum,
        dt_b_sum,
        a_log_sum,
        skip_sum,
    ) = (
        lax.psum(in_part.astype(jnp.bfloat16), "ctx").astype(jnp.float32),
        lax.psum(out_part.astype(jnp.bfloat16), "ctx").astype(jnp.float32),
        lax.psum(gain_part.astype(jnp.bfloat16), "ctx").astype(jnp.float32),
        lax.psum(xw_part.astype(jnp.bfloat16), "ctx").astype(jnp.float32),
        lax.psum(cw_part.astype(jnp.bfloat16), "ctx").astype(jnp.float32),
        lax.psum(cb_part.astype(jnp.bfloat16), "ctx").astype(jnp.float32),
        lax.psum(d_dt_weight.astype(jnp.bfloat16), "ctx").astype(jnp.float32),
        lax.psum(d_dt_bias.astype(jnp.bfloat16), "ctx").astype(jnp.float32),
        lax.psum(d_a_log.astype(jnp.bfloat16), "ctx").astype(jnp.float32),
        lax.psum(d_skip.astype(jnp.bfloat16), "ctx").astype(jnp.float32),
    )
    return (
        output,
        d_hidden,
        gain_sum,
        in_sum,
        conv_w_sum,
        conv_b_sum,
        x_w_sum,
        dt_w_sum,
        dt_b_sum,
        a_log_sum,
        skip_sum,
        out_sum,
    )


def solution(mesh):
    return jax.shard_map(
        on_device,
        mesh=mesh,
        in_specs=(
            P(("ctx", "ch"), None),
            P(),
            P("ch", None),
            P(),
            P(),
            P(),
            P(None, "ch"),
            P("ch"),
            P("ch", None),
            P("ch"),
            P("ch", None),
            P("ctx", None),
            P("ctx"),
            P(("ctx", "ch"), None),
        ),
        out_specs=(
            P(("ctx", "ch"), None),
            P(("ctx", "ch"), None),
            P("ch"),
            P("ch", None),
            P("ch", None),
            P("ch"),
            P("ch", None),
            P(None, "ch"),
            P("ch"),
            P("ch", None),
            P("ch"),
            P("ch", None),
        ),
        check_vma=False,
    )
```

profile of v0, /device:TPU:0, one launch (start us, length us, event | category | flops | bytes accessed | tf_op | source)
XLA Modules:
  0.0 1272.3 jit_solution(3958788113611448013)
XLA Ops:
  12.2 47.3 %all-gather.5.cloned.1.call-done = bf16[2048,1024]{1,0:T(8,128)(2,1)} async-done(((bf16[256,1024]{1,0:T(8,128)(2,1)}), bf16[2048,1024]{1,0:T(8,128)(2,1)}) %all-gather.5.cloned.1.call-update) | async-done | bytes 4194320 | tf_op jit(solution)/shard_map/all_gather | solution.py:232
  68.8 27.9 %all-to-all-done.3 = bf16[8,256,128]{1,2,0:T(8,128)(2,1)S(1)} async-done(((bf16[8,256,128]{1,2,0:T(8,128)(2,1)}), bf16[8,256,128]{1,2,0:T(8,128)(2,1)S(1)}, u32[]{:S(2)}, u32[]{:S(2)}) %all-to-all-start.3) | async-done | bytes 524320 | tf_op jit(solution)/shard_map/all_to_all | solution.py:298
  97.9 54.4 %all-gather.3.cloned.1.call-done = bf16[1024,4096]{1,0:T(8,128)(2,1)} async-done(((bf16[128,4096]{1,0:T(8,128)(2,1)}), bf16[1024,4096]{1,0:T(8,128)(2,1)}) %all-gather.3.cloned.1.call-update) | async-done | bytes 8388624 | tf_op jit(solution)/shard_map/all_gather | solution.py:231
  166.8 19.1 %all_gather.10 = bf16[96,1024]{1,0:T(8,128)(2,1)S(1)} all-gather(bf16[96,128]{1,0:T(8,128)(2,1)S(1)} %fusion.6), channel_id=1, replica_groups=mesh['ctx'=4,'ch'=8] {'ch'}, dimensions={1}, use_global_device_ids=true | all-gather | bytes 221184 | tf_op jit(solution)/shard_map/all_gather | solution.py:265
  195.0 5.3 fusion.116
  235.0 5.3 fusion.115
  264.7 12.7 copy.701
  296.4 7.3 fusion.49
  367.2 8.7 pad.313
  375.9 8.7 pad.314
  386.7 15.6 %pad.491 = f32[256,16,64]{0,1,2:T(8,128)} pad(f32[256,16,32]{0,1,2:T(8,128)} %add.1079, f32[]{:T(128)} %constant.27.clone.1), padding=0_0_0x0_0_0x1_0_1 | pad | bytes 1572868
  402.3 8.7 pad.301
  411.0 8.7 pad.302
  421.7 15.6 %pad.492 = f32[256,16,64]{0,1,2:T(8,128)} pad(f32[256,16,32]{0,1,2:T(8,128)} %add.1063, f32[]{:T(128)} %constant.27.clone.1), padding=0_0_0x0_0_0x1_0_1 | pad | bytes 1572868
  441.2 15.7 %pad.381 = f32[256,16,63]{0,1,2:T(8,128)} pad(f32[256,16,32]{0,1,2:T(8,128)} %pad_maximum_fusion.5, f32[]{:T(128)} %constant.27.clone.1), padding=0_0_0x0_0_0x0_0_1 | pad | bytes 1556484 | tf_op jit(solution)/shard_map/while/body/eval_jaxpr/slice | solution.py:166
  458.7 15.6 %pad.383 = f32[256,16,63]{0,1,2:T(8,128)} pad(f32[256,16,32]{0,1,2:T(8,128)} %pad_maximum_fusion.6, f32[]{:T(128)} %constant.27.clone.1), padding=0_0_0x0_0_0x0_0_1 | pad | bytes 1556484 | tf_op jit(solution)/shard_map/while/body/eval_jaxpr/slice | solution.py:166
  481.0 6.5 multiply_add_fusion.47
  530.7 4.8 pad.287
  553.1 5.8 pad.289
  558.9 8.7 pad.290
  569.2 8.7 pad.277
  577.9 9.1 pad.278
  600.0 15.6 %pad.489 = f32[256,16,64]{0,1,2:T(8,128)} pad(f32[256,16,32]{0,1,2:T(8,128)} %add.1020, f32[]{:T(128)} %constant.27.clone.1), padding=0_0_0x0_0_0x1_0_1 | pad | bytes 1572868
  615.6 10.6 pad.490
  627.3 10.6 pad.377
  638.9 10.7 pad.379
  654.7 8.5 multiply_reduce_fusion.15
  663.5 9.0 multiply_reduce_fusion.1
  674.5 6.6 multiply_reduce_fusion.3
  681.5 10.0 multiply_reduce_fusion.5
  692.4 10.0 multiply_reduce_fusion.7
  703.8 10.1 multiply_reduce_fusion.9
  715.3 10.1 multiply_reduce_fusion.11
  726.7 6.1 multiply_reduce_fusion.14
  732.9 6.8 multiply_reduce_fusion.13
  759.3 5.0 all-to-all-start.5
  793.7 5.1 all-to-all-start.4
  799.7 14.6 %all-to-all-done.4 = bf16[256,8,128]{0,2,1:T(8,128)(2,1)} async-done(((bf16[256,8,128]{0,2,1:T(8,128)(2,1)}), bf16[256,8,128]{0,2,1:T(8,128)(2,1)}, u32[]{:S(2)}, u32[]{:S(2)}) %all-to-all-start.4) | async-done | bytes 524320 | tf_op jit(solution)/shard_map/all_to_all | solution.py:320
  815.5 5.1 multiply_reduce_fusion.19
  823.3 23.7 %all_to_all.86 = bf16[256,8,128]{0,2,1:T(8,128)(2,1)S(1)} all-to-all(bf16[256,8,128]{0,2,1:T(8,128)(2,1)S(1)} %get-tuple-element.278), channel_id=1, replica_groups=mesh['ctx'=4,'ch'=8] {'ch'}, dimensions={1} | all-to-all | bytes 1048576 | tf_op jit(solution)/shard_map/all_to_all | solution.py:287
  859.6 13.3 %all-to-all-done.6 = bf16[256,8,128]{0,2,1:T(8,128)(2,1)S(1)} async-done(((bf16[256,8,128]{0,2,1:T(8,128)(2,1)}), bf16[256,8,128]{0,2,1:T(8,128)(2,1)S(1)}, u32[]{:S(2)}, u32[]{:S(2)}) %all-to-all-start.6) | async-done | bytes 524320 | tf_op jit(solution)/shard_map/all_to_all | solution.py:323
  873.1 8.3 fusion.55
  886.6 6.4 fusion.63
  893.0 27.1 %all-reduce.57 = (bf16[1024]{0:T(1024)(128)(2,1)S(1)}, bf16[2048]{0:T(1024)(128)(2,1)S(1)}) all-reduce(f32[1024]{0:T(1024)S(1)} %get-tuple-element.196, f32[2048]{0:T(1024)S(1)} %copy-done.353), channel_id=2, replica_groups=mesh['ctx'=4,'ch'=8] {'ch'}, use_global_device_ids=true, to_apply=%region_87.88.clone | all-reduce | flops 3072 | bytes 18432
  924.4 55.6 %reduce-scatter.11.cloned.1.call-done = f32[256,1024]{1,0:T(8,128)} async-done(((f32[2048,1024]{1,0:T(8,128)}), f32[256,1024]{1,0:T(8,128)}) %reduce-scatter.11.cloned.1.call-update) | async-done | bytes 1048592 | tf_op jit(solution)/shard_map/reduce_scatter | solution.py:362
  982.1 166.7 %reduce-scatter.7.cloned.1.call-done = f32[128,4096]{1,0:T(8,128)} async-done(((f32[1024,4096]{1,0:T(8,128)}), f32[128,4096]{1,0:T(8,128)}) %reduce-scatter.7.cloned.1.call-update) | async-done | bytes 2097168 | tf_op jit(solution)/shard_map/reduce_scatter | solution.py:361
  1156.2 39.8 %all-reduce.63.cloned.1.call-done = (bf16[128]{0:T(256)(128)(2,1)}, bf16[256,4]{0,1:T(4,128)(2,1)}, bf16[256]{0:T(256)(128)(2,1)}, bf16[256,96]{0,1:T(8,128)(2,1...) async-done(((bf16[128]{0:T(256)(128)(2,1)}, bf16[256,4]{0,1:T(4,128)(2,1)}, bf16[256]{0:T(256)(128)(2,1)}, ...) | async-done | bytes 93968 | tf_op jit(solution)/shard_map/psum | solution.py:382
  1206.1 55.2 %all-reduce.65.cloned.1.call-done = (bf16[128,4096]{1,0:T(8,128)(2,1)}, bf16[256,1024]{1,0:T(8,128)(2,1)}) async-done(((bf16[128,4096]{1,0:T(8,128)(2,1)}, bf16[256,1024]{1,0:T(8,128)(2,1)}), (bf16[128,4096]{1,0:T(8,128)(2,1)}, bf16[256,1024]{1,0:T(8,128)(2,1)})) %all-reduce.65.cloned.1.call-update) | async-done | bytes 1572880 | tf_op jit(solution)/shard_map/psum | solution.py:380
  (1208 shorter events, 380.0 us)
Async XLA Ops:
  7.2 159.4 %copy-start = (bf16[2048,96]{0,1:T(8,128)(2,1)S(1)}, bf16[2048,96]{0,1:T(8,128)(2,1)}, u32[]{:S(2)}) copy-start(bf16[2048,96]{0,1:T(8,128)(2,1)} %param.19) | copy-start | bytes 1179652
  7.2 52.3 %all-gather.5.cloned.1.call-start = ((), (), s32[]{:S(2)}) async-start(), calls=%async_computation.12 | async-start | bytes 4718592 | tf_op jit(solution)/shard_map/all_gather | solution.py:232
  7.9 144.3 %all-gather.3.cloned.1.call-start = ((), (), s32[]{:S(2)}) async-start(), calls=%async_computation.11 | async-start | bytes 9437184 | tf_op jit(solution)/shard_map/all_gather | solution.py:231
  12.2 152.2 %copy-start.381 = (f32[128]{0:T(128)}, f32[128]{0:T(128)S(1)}, u32[]{:S(2)}) copy-start(f32[128]{0:T(128)S(1)} %get-tuple-element.275) | copy-start | bytes 1540
  63.0 89.3 %copy-start.6 = (bf16[128,1024]{1,0:T(8,128)(2,1)S(1)}, bf16[128,1024]{1,0:T(8,128)(2,1)}, u32[]{:S(2)}) copy-start(bf16[128,1024]{1,0:T(8,128)(2,1)} %param.14) | copy-start | bytes 786436
  63.0 89.3 %copy-start.81 = (f32[1024]{0:T(1024)S(1)}, f32[1024]{0:T(1024)}, u32[]{:S(2)}) copy-start(f32[1024]{0:T(1024)} %param.15) | copy-start | bytes 12292
  64.0 32.7 %all-to-all-start.3 = ((bf16[8,256,128]{1,2,0:T(8,128)(2,1)}), bf16[8,256,128]{1,2,0:T(8,128)(2,1)S(1)}, u32[]{:S(2)}, u32[]{:S(2)}) async-start(bf16[8,256,128]{1,2,0:T(8,128)(2,1)} %copy.650), calls=%async_computation.3 | async-start | bytes 1048576 | tf_op jit(solution)/shard_map/all_to_all | solution.py:298
  68.6 120.7 %copy-start.354 = (f32[64]{0:T(128)}, f32[64]{0:T(128)S(1)}, u32[]{:S(2)}) copy-start(f32[64]{0:T(128)S(1)} %get-tuple-element.200) | copy-start | bytes 772
  68.6 120.7 %copy-start.358 = (f32[64]{0:T(128)}, f32[64]{0:T(128)S(1)}, u32[]{:S(2)}) copy-start(f32[64]{0:T(128)S(1)} %get-tuple-element.201) | copy-start | bytes 772
  68.6 120.7 %copy-start.362 = (f32[64]{0:T(128)}, f32[64]{0:T(128)S(1)}, u32[]{:S(2)}) copy-start(f32[64]{0:T(128)S(1)} %get-tuple-element.211) | copy-start | bytes 772
  68.6 120.7 %copy-start.366 = (f32[64]{0:T(128)}, f32[64]{0:T(128)S(1)}, u32[]{:S(2)}) copy-start(f32[64]{0:T(128)S(1)} %get-tuple-element.212) | copy-start | bytes 772
  68.6 120.8 %copy-start.370 = (f32[64]{0:T(128)}, f32[64]{0:T(128)S(1)}, u32[]{:S(2)}) copy-start(f32[64]{0:T(128)S(1)} %get-tuple-element.213) | copy-start | bytes 772
  68.6 120.8 %copy-start.374 = (f32[64]{0:T(128)}, f32[64]{0:T(128)S(1)}, u32[]{:S(2)}) copy-start(f32[64]{0:T(128)S(1)} %get-tuple-element.198) | copy-start | bytes 772
  68.6 120.8 %copy-start.377 = (f32[64]{0:T(128)}, f32[64]{0:T(128)S(1)}, u32[]{:S(2)}) copy-start(f32[64]{0:T(128)S(1)} %get-tuple-element.199) | copy-start | bytes 772
  68.6 120.8 %copy-start.385 = (f32[64]{0:T(128)}, f32[64]{0:T(128)S(1)}, u32[]{:S(2)}) copy-start(f32[64]{0:T(128)S(1)} %get-tuple-element.202) | copy-start | bytes 772
  68.6 95.8 %copy-start.382 = (f32[128]{0:T(128)}, f32[128]{0:T(128)S(1)}, u32[]{:S(2)}) copy-start(f32[128]{0:T(128)S(1)} %get-tuple-element.448) | copy-start | bytes 1540
  68.6 95.8 %copy-start.383 = (f32[128]{0:T(128)}, f32[128]{0:T(128)S(1)}, u32[]{:S(2)}) copy-start(f32[128]{0:T(128)S(1)} %get-tuple-element.449) | copy-start | bytes 1540
  68.7 95.8 %copy-start.384 = (f32[128]{0:T(128)}, f32[128]{0:T(128)S(1)}, u32[]{:S(2)}) copy-start(f32[128]{0:T(128)S(1)} %get-tuple-element.450) | copy-start | bytes 1540
  68.7 120.7 %copy-start.126 = (f32[256,16]{0,1:T(8,128)}, f32[256,16]{0,1:T(8,128)S(1)}, u32[]{:S(2)}) copy-start(f32[256,16]{0,1:T(8,128)S(1)} %exponential_negate_fusion) | copy-start | bytes 49156
  68.7 95.8 %copy-start.147 = (f32[2048,1]{0,1:T(1,128)}, f32[2048,1]{0,1:T(1,128)S(1)}, u32[]{:S(2)}) copy-start(f32[2048,1]{0,1:T(1,128)S(1)} %get-tuple-element.445) | copy-start | bytes 24580
  68.7 95.8 %copy-start.149 = (f32[2048,1]{0,1:T(1,128)}, f32[2048,1]{0,1:T(1,128)S(1)}, u32[]{:S(2)}) copy-start(f32[2048,1]{0,1:T(1,128)S(1)} %get-tuple-element.446) | copy-start | bytes 24580
  68.8 95.8 %copy-start.151 = (f32[2048,1]{0,1:T(1,128)}, f32[2048,1]{0,1:T(1,128)S(1)}, u32[]{:S(2)}) copy-start(f32[2048,1]{0,1:T(1,128)S(1)} %get-tuple-element.447) | copy-start | bytes 24580
  96.7 60.3 %copy-start.7 = (bf16[8,256,128]{1,2,0:T(8,128)(2,1)}, bf16[8,256,128]{1,2,0:T(8,128)(2,1)S(1)}, u32[]{:S(2)}) copy-start(bf16[8,256,128]{1,2,0:T(8,128)(2,1)S(1)} %all-to-all-done.3) | copy-start | bytes 1572868
  157.0 7.3 collective-permute-start
  160.1 128.7 %all-to-all-start.1 = ((bf16[8,256,128]{1,2,0:T(8,128)(2,1)}), bf16[8,256,128]{1,2,0:T(8,128)(2,1)}, u32[]{:S(2)}, u32[]{:S(2)}) async-start(bf16[8,256,128]{1,2,0:T(8,128)(2,1)} %bitcast.532), calls=%async_computation.1 | async-start | bytes 1048576 | tf_op jit(solution)/shard_map/all_to_all | solution.py:263
  164.5 22.1 %copy-start.273 = (bf16[64,256]{1,0:T(8,128)(2,1)S(1)}, bf16[64,256]{1,0:T(8,128)(2,1)}, u32[]{:S(2)}) copy-start(bf16[64,256]{1,0:T(8,128)(2,1)} %param.20) | copy-start | bytes 98308
  164.5 22.1 %copy-start.407 = (f32[256]{0:T(256)S(1)}, f32[256]{0:T(256)}, u32[]{:S(2)}) copy-start(f32[256]{0:T(256)} %param.21) | copy-start | bytes 3076
  166.5 22.5 %copy-start.3 = (bf16[2048,128]{0,1:T(8,128)(2,1)}, bf16[2048,128]{0,1:T(8,128)(2,1)S(1)}, u32[]{:S(2)}) copy-start(bf16[2048,128]{0,1:T(8,128)(2,1)S(1)} %get-tuple-element.273) | copy-start | bytes 1572868
  189.3 106.4 %copy-start.90 = (f32[256,64]{0,1:T(8,128)}, f32[256,64]{0,1:T(8,128)S(1)}, u32[]{:S(2)}) copy-start(f32[256,64]{0,1:T(8,128)S(1)} %get-tuple-element.345) | copy-start | bytes 196612
  189.3 106.4 %copy-start.93 = (f32[256,64]{0,1:T(8,128)}, f32[256,64]{0,1:T(8,128)S(1)}, u32[]{:S(2)}) copy-start(f32[256,64]{0,1:T(8,128)S(1)} %get-tuple-element.346) | copy-start | bytes 196612
  189.3 106.4 %copy-start.96 = (f32[256,64]{0,1:T(8,128)}, f32[256,64]{0,1:T(8,128)S(1)}, u32[]{:S(2)}) copy-start(f32[256,64]{0,1:T(8,128)S(1)} %get-tuple-element.355) | copy-start | bytes 196612
  254.1 27.5 %copy-start.35 = (f32[1,16,64]{0,2,1:T(8,128)S(1)}, f32[1,16,64]{0,2,1:T(8,128)}, u32[]{:S(2)}) copy-start(f32[1,16,64]{0,2,1:T(8,128)} %get-tuple-element.366) | copy-start | bytes 12292
  288.8 189.2 %all-to-all-start = ((bf16[8,256,128]{1,2,0:T(8,128)(2,1)}), bf16[8,256,128]{1,2,0:T(8,128)(2,1)S(1)}, u32[]{:S(2)}, u32[]{:S(2)}) async-start(bf16[8,256,128]{1,2,0:T(8,128)(2,1)} %bitcast.567), calls=%async_computation | async-start | bytes 1048576 | tf_op jit(solution)/shard_map/all_to_all | solution.py:262
  549.4 18.2 %copy-start.202 = (f32[256,16,1]{0,1,2:T(8,128)S(1)}, f32[256,16,1]{0,1,2:T(8,128)}, u32[]{:S(2)}) copy-start(f32[256,16,1]{0,1,2:T(8,128)} %slice.1679) | copy-start | bytes 49156
  593.9 21.7 %copy-start.34 = (f32[256,16,32]{0,1,2:T(8,128)S(1)}, f32[256,16,32]{0,1,2:T(8,128)}, u32[]{:S(2)}) copy-start(f32[256,16,32]{0,1,2:T(8,128)} %add.989) | copy-start | bytes 1572868
  597.3 28.9 %slice-start.1 = ((f32[256,16,64]{0,1,2:T(8,128)}), f32[256,16,1]{0,1,2:T(8,128)S(1)}, s32[]{:S(2)}) async-start(f32[256,16,64]{0,1,2:T(8,128)} %copy-done.23), calls=%async_computation.20 | async-start | bytes 32768 | tf_op jit(solution)/shard_map/while/body/eval_jaxpr/slice | solution.py:84
  758.6 19.0 %copy-start.199 = (f32[256,64]{0,1:T(8,128)S(1)}, f32[256,64]{0,1:T(8,128)}, u32[]{:S(2)}) copy-start(f32[256,64]{0,1:T(8,128)} %get-tuple-element.133) | copy-start | bytes 196612
  759.3 34.4 %all-to-all-start.5 = ((bf16[8,96,128]{2,1,0:T(8,128)(2,1)}), bf16[8,96,128]{2,1,0:T(8,128)(2,1)S(1)}, u32[]{:S(2)}, u32[]{:S(2)}) async-start(bf16[8,96,128]{2,1,0:T(8,128)(2,1)} %maximum_bitcast_fusion), calls=%async_computation.5 | async-start | bytes 393216 | tf_op jit(solution)/shard_map/all_to_all | solution.py:26
  793.7 20.6 %all-to-all-start.4 = ((bf16[256,8,128]{0,2,1:T(8,128)(2,1)}), bf16[256,8,128]{0,2,1:T(8,128)(2,1)}, u32[]{:S(2)}, u32[]{:S(2)}) async-start(bf16[256,8,128]{0,2,1:T(8,128)(2,1)} %get-tuple-element.285), calls=%async_computation.4 | async-start | bytes 1048576 | tf_op jit(solution)/shard_map/all_to_all | solution.py:320
  798.8 122.5 %reduce-scatter.13.cloned.1.call-start = ((), (), s32[]{:S(2)}) async-start(), calls=%async_computation.16 | async-start | bytes 1179648
  822.0 25.3 %copy-start.44 = (bf16[128,1024]{1,0:T(8,128)(2,1)S(1)}, bf16[128,1024]{1,0:T(8,128)(2,1)}, u32[]{:S(2)}) copy-start(bf16[128,1024]{1,0:T(8,128)(2,1)} %param.27) | copy-start | bytes 786436
  822.1 100.8 %reduce-scatter.9.cloned.1.call-start = ((), (), s32[]{:S(2)}) async-start(), calls=%async_computation.14 | async-start | bytes 884736 | tf_op jit(solution)/shard_map/reduce_scatter | solution.py:364
  823.3 156.8 %reduce-scatter.11.cloned.1.call-start = ((), (), s32[]{:S(2)}) async-start(), calls=%async_computation.15 | async-start | bytes 9437184 | tf_op jit(solution)/shard_map/reduce_scatter | solution.py:362
  851.9 21.0 %all-to-all-start.6 = ((bf16[256,8,128]{0,2,1:T(8,128)(2,1)}), bf16[256,8,128]{0,2,1:T(8,128)(2,1)S(1)}, u32[]{:S(2)}, u32[]{:S(2)}) async-start(bf16[256,8,128]{0,2,1:T(8,128)(2,1)} %get-tuple-element.277), calls=%async_computation.6 | async-start | bytes 1048576 | tf_op jit(solution)/shard_map/all_to_all | solution.py:323
  855.5 293.3 %reduce-scatter.7.cloned.1.call-start = ((), (), s32[]{:S(2)}) async-start(), calls=%async_computation.13 | async-start | bytes 18874368 | tf_op jit(solution)/shard_map/reduce_scatter | solution.py:361
  858.3 14.6 %collective-permute-start.1 = (f32[2048,3]{0,1:T(4,128)S(1)}, f32[2048,3]{0,1:T(4,128)S(1)}, u32[]{:S(2)}, u32[]{:S(2)}) collective-permute-start(f32[2048,3]{0,1:T(4,128)S(1)} %slice.1815), channel_id=1, source_target_pairs={{1,0},{2,1},{3,2},{4,3},{5,4},{6,5},{7,6},{9,8},{10,9},{11,10},{12... | collective-permute-start | bytes 73736 | tf_op jit(solution)/shard_map/ppermute | solution.py:15
  881.5 314.5 %all-reduce.63.cloned.1.call-start = ((), (), s32[]{:S(2)}) async-start(), calls=%async_computation.17 | async-start | bytes 188416 | tf_op jit(solution)/shard_map/psum | solution.py:382
  924.4 336.9 %all-reduce.65.cloned.1.call-start = ((), (), s32[]{:S(2)}) async-start(), calls=%async_computation.18 | async-start | bytes 3145728 | tf_op jit(solution)/shard_map/psum | solution.py:380
  (381 other events, 1865.5 us)
Sparse Core Ops, SparseCore 0:
  9.6 49.8 all-gather.4
  61.1 91.1 all-gather.2
  822.2 33.4 reduce-scatter.12
  857.8 31.4 reduce-scatter.8
  891.5 88.4 reduce-scatter.10
  982.4 166.3 reduce-scatter.6
  1154.0 41.9 all-reduce.62
  1200.2 61.0 all-reduce.64
where the time goes:
time: 1300 us; the launch traced here: 1270 us
  waiting for transfers between devices  476 us (37%)
  local copies, waits for them, and re-layouts  406 us (31%)
  other arithmetic  228 us (18%)
  blocking collectives  69.9 us (5%)
  matrix products  41.2 us (3%)
  starting transfers between devices  28.9 us (2%)
  between operations  21.5 us (2%)
    reduce_scatter x1, waiting for transfers between devices, on_device(): lax.psum_scatter(d_in_weight, 'ch', scatter_dimension=0, tiled=True)  167 us
    reduce_sum x9, other arithmetic, step(): d_rates = d_rates + jnp.sum(through * delta_sub[j][:, None, :], axis=2)  77.1 us
    unnamed x869, local copies, waits for them, and re-layouts  73.2 us
    pad x16, local copies, waits for them, and re-layouts, local_sweep(): lax.associative_scan(chain, (products[-1], rises[-1]), axis=2)  67.4 us
    pad x16, local copies, waits for them, and re-layouts, step(): lax.associative_scan(chain, (jnp.flip(lead_gain, 2), jnp.flip(lead_add, 2...  67.2 us
    reduce_scatter x1, waiting for transfers between devices, on_device(): lax.psum_scatter(d_out_weight, 'ch', scatter_dimension=0, tiled=True)  55.6 us
    psum x1, waiting for transfers between devices, on_device(): lax.psum(in_part.astype(jnp.bfloat16), 'ctx').astype(jnp.float32)  55.2 us
    all_gather x1, waiting for transfers between devices, on_device(): lax.all_gather(in_weight, 'ch', axis=0, tiled=True)  54.4 us
  transfers between devices with their start and end apart: 16, of which 9 were waited for; matrix products, arithmetic and copies ran while one was open for 30% of the time, Pallas kernels for 0%

commit v1 on v0

v1 whole, which is shorter than its diff:
```python
import functools
import math

import jax
import jax.numpy as jnp
from jax import lax
from jax.experimental import pallas as pl
from jax.experimental.pallas import tpu as pltpu
from jax.sharding import PartitionSpec as P

HIGH = lax.Precision.HIGHEST
f32 = jnp.float32
bf16 = jnp.bfloat16
eps = 1e-05
LOG2E = 1.4426950408889634
CUT = 1e30
SEGS = 8
MIB = 1 << 20


def silu(v):
    return v * jax.nn.sigmoid(v)


def silu_slope(v):
    sig = jax.nn.sigmoid(v)
    return sig * (1.0 + v * (1.0 - sig))


def context_place(offsets, places):
    begins = jnp.max(jnp.where(offsets[:, None] <= places[None, :], offsets[:, None], 0), axis=0)
    return places - begins


def dot(a, b, dims, precision=None):
    return lax.dot_general(a, b, ((dims[:1], dims[1:]), ((), ())), precision=precision, preferred_element_type=f32)


def lane_groups(chans):
    width = 128 if chans % 128 == 0 else chans
    return chans // width, width


def softplus(v):
    small = jnp.exp(-jnp.abs(v))
    series = small * (1.0 - small * (0.5 - small * (1.0 / 3.0)))
    return jnp.maximum(v, 0.0) + jnp.where(small < 0.01, series, jnp.log(1.0 + small))


def by_rows(total, body):
    size = math.gcd(total, 256)

    def step(k, carry):
        body(pl.ds(pl.multiple_of(k * size, size), size))
        return carry

    lax.fori_loop(0, total // size, step, 0)


def step_params(proj_ref, dtw_ref, dtb_ref, rank, rows):
    return dot(proj_ref[rows, :rank], dtw_ref[...], (1, 0)) + dtb_ref[...]


def put(ref, rows, value, groups, width):
    for g in range(groups):
        ref[g, rows, :] = value[:, g * width : (g + 1) * width]


def take(ref, rows, groups):
    return jnp.concatenate([ref[g, rows, :] for g in range(groups)], axis=1) if groups > 1 else ref[0, rows, :]


def rows_at(ref, g, i, steps):
    return ref[g, pl.ds(i, SEGS, stride=steps), :]


def forward_kernel(
    rank, states, span, proj_ref, val_ref, gate_ref, dg_ref, dtw_ref, dtb_ref, alog_ref, skip_ref,
    gated_ref, dgate_ref, hist_ref, dc_ref, dskip_ref,
    s_cut, s_dx, s_dy, s_bc, s_rate, s_state,
):
    total, chans = val_ref.shape
    steps = total // SEGS
    groups, width = lane_groups(chans)
    pairs = [(n, g) for n in range(states) for g in range(groups)]
    b_at, c_at = rank, rank + states
    turn = pl.program_id(0)

    def rate(n, g):
        return s_rate[n : n + 1, g * width : (g + 1) * width]

    @pl.when(turn == 0)
    def _():
        s_rate[...] = -jnp.exp(alog_ref[...]) * LOG2E

        def fill(rows):
            delta = softplus(step_params(proj_ref, dtw_ref, dtb_ref, rank, rows))
            wide = proj_ref[rows, :].astype(f32)
            s_bc[0, rows, :] = wide
            cut = wide[:, rank + 2 * states : rank + 2 * states + 1] * CUT
            put(s_cut, rows, delta + cut, groups, width)
            put(s_dx, rows, delta * val_ref[rows, :].astype(f32), groups, width)
            d_scan = dg_ref[rows, :].astype(f32) * silu(gate_ref[rows, :].astype(f32))
            put(s_dy, rows, d_scan, groups, width)

        by_rows(total, fill)

        def sweep(i, carry):
            held, span_sum = carry
            cuts = [rows_at(s_cut, g, i, steps) for g in range(groups)]
            dxs = [rows_at(s_dx, g, i, steps) for g in range(groups)]
            bc = rows_at(s_bc, 0, i, steps)
            out = []
            for n, g in pairs:
                push = dxs[g] * bc[:, b_at + n : b_at + n + 1]
                out.append(jnp.exp2(cuts[g] * rate(n, g)) * held[n * groups + g] + push)
            return tuple(out), tuple(span_sum[g] + cuts[g] for g in range(groups))

        zero = jnp.zeros((SEGS, width), f32)
        ends, sums = lax.fori_loop(0, steps, sweep, ((zero,) * len(pairs), (zero,) * groups))
        first = lax.broadcasted_iota(jnp.int32, (SEGS, width), 0) == 0
        for n, g in pairs:
            gain = jnp.exp2(sums[g] * rate(n, g))
            end = ends[n * groups + g]
            start = zero
            for _ in range(SEGS - 1):
                start = jnp.where(first, 0.0, pltpu.roll(gain * start + end, 1, 0))
            s_state[n * groups + g] = start

    lane = lax.broadcasted_iota(jnp.int32, (SEGS, dc_ref.shape[1]), 1)

    def sweep(k, held):
        i = turn * span + k
        cuts = [rows_at(s_cut, g, i, steps) for g in range(groups)]
        dxs = [rows_at(s_dx, g, i, steps) for g in range(groups)]
        dys = [rows_at(s_dy, g, i, steps) for g in range(groups)]
        bc = rows_at(s_bc, 0, i, steps)
        ys = [jnp.zeros((SEGS, width), f32) for _ in range(groups)]
        dc_row = jnp.zeros(lane.shape, f32)
        out = []
        for n in range(states):
            b_n = bc[:, b_at + n : b_at + n + 1]
            c_n = bc[:, c_at + n : c_at + n + 1]
            mix = None
            for g in range(groups):
                old = held[n * groups + g]
                hist_ref[k, n * groups + g] = old
                new = jnp.exp2(cuts[g] * rate(n, g)) * old + dxs[g] * b_n
                out.append(new)
                ys[g] = ys[g] + new * c_n
                term = dys[g] * new
                mix = term if mix is None else mix + term
            dc_row = jnp.where(lane == c_at + n, jnp.sum(mix, axis=1, keepdims=True), dc_row)
        for g in range(groups):
            s_dx[g, pl.ds(i, SEGS, stride=steps), :] = ys[g]
        dc_ref[pl.ds(i, SEGS, stride=steps), :] = dc_row
        return tuple(out)

    held = lax.fori_loop(0, span, sweep, tuple(s_state[j] for j in range(len(pairs))))
    for j in range(len(pairs)):
        s_state[j] = held[j]

    @pl.when(turn == pl.num_programs(0) - 1)
    def _():
        dskip_ref[...] = jnp.zeros_like(dskip_ref)

        def finish(rows):
            vals = val_ref[rows, :].astype(f32)
            gate = gate_ref[rows, :].astype(f32)
            scanned = take(s_dx, rows, groups) + skip_ref[...] * vals
            gated_ref[rows, :] = (scanned * silu(gate)).astype(bf16)
            dgate_ref[rows, :] = (dg_ref[rows, :].astype(f32) * scanned * silu_slope(gate)).astype(bf16)
            dskip_ref[...] += jnp.sum(take(s_dy, rows, groups) * vals, axis=0, keepdims=True)

        by_rows(total, finish)


def backward_kernel(
    rank, states, span, proj_ref, val_ref, gate_ref, dg_ref, dtw_ref, dtwt_ref, dtb_ref, alog_ref, skip_ref, hist_ref,
    dc_ref, part_ref, dval_ref, ddtw_ref, ddtb_ref, dalog_ref,
    s_cut, s_delta, s_val, s_dy, s_bc, s_rate, s_state, s_drate,
):
    total, chans = val_ref.shape
    steps = total // SEGS
    groups, width = lane_groups(chans)
    pairs = [(n, g) for n in range(states) for g in range(groups)]
    b_at, c_at = rank, rank + states
    turn = pl.program_id(0)
    turns = pl.num_programs(0)

    def rate(n, g):
        return s_rate[n : n + 1, g * width : (g + 1) * width]

    @pl.when(turn == 0)
    def _():
        s_rate[...] = -jnp.exp(alog_ref[...]) * LOG2E
        s_drate[...] = jnp.zeros_like(s_drate)

        def fill(rows):
            delta = softplus(step_params(proj_ref, dtw_ref, dtb_ref, rank, rows))
            wide = proj_ref[rows, :].astype(f32)
            s_bc[0, rows, :] = wide
            cut = wide[:, rank + 2 * states : rank + 2 * states + 1] * CUT
            put(s_cut, rows, delta + cut, groups, width)
            put(s_delta, rows, delta, groups, width)
            put(s_val, rows, val_ref[rows, :].astype(f32), groups, width)
            d_scan = dg_ref[rows, :].astype(f32) * silu(gate_ref[rows, :].astype(f32))
            put(s_dy, rows, d_scan, groups, width)

        by_rows(total, fill)

        def sweep(k, carry):
            i = steps - 1 - k
            held, span_sum = carry
            cuts = [rows_at(s_cut, g, i, steps) for g in range(groups)]
            dys = [rows_at(s_dy, g, i, steps) for g in range(groups)]
            bc = rows_at(s_bc, 0, i, steps)
            out = []
            for n, g in pairs:
                lam = dys[g] * bc[:, c_at + n : c_at + n + 1] + held[n * groups + g]
                out.append(jnp.exp2(cuts[g] * rate(n, g)) * lam)
            return tuple(out), tuple(span_sum[g] + cuts[g] for g in range(groups))

        zero = jnp.zeros((SEGS, width), f32)
        ends, sums = lax.fori_loop(0, steps, sweep, ((zero,) * len(pairs), (zero,) * groups))
        last = lax.broadcasted_iota(jnp.int32, (SEGS, width), 0) == SEGS - 1
        for n, g in pairs:
            gain = jnp.exp2(sums[g] * rate(n, g))
            end = ends[n * groups + g]
            start = zero
            for _ in range(SEGS - 1):
                start = jnp.where(last, 0.0, pltpu.roll(gain * start + end, SEGS - 1, 0))
            s_state[n * groups + g] = start

    lane = lax.broadcasted_iota(jnp.int32, (SEGS, part_ref.shape[1]), 1)

    def sweep(back, held):
        k = span - 1 - back
        i = (turns - 1 - turn) * span + k
        cuts = [rows_at(s_cut, g, i, steps) for g in range(groups)]
        deltas = [rows_at(s_delta, g, i, steps) for g in range(groups)]
        vals = [rows_at(s_val, g, i, steps) for g in range(groups)]
        dys = [rows_at(s_dy, g, i, steps) for g in range(groups)]
        dxs = [deltas[g] * vals[g] for g in range(groups)]
        bc = rows_at(s_bc, 0, i, steps)
        zero = jnp.zeros((SEGS, width), f32)
        by_rate = [zero] * groups
        by_b = [zero] * groups
        db_row = jnp.zeros(lane.shape, f32)
        out = []
        for n in range(states):
            b_n = bc[:, b_at + n : b_at + n + 1]
            c_n = bc[:, c_at + n : c_at + n + 1]
            mix = None
            for g in range(groups):
                j = n * groups + g
                lam = dys[g] * c_n + held[j]
                onward = jnp.exp2(cuts[g] * rate(n, g)) * lam
                out.append(onward)
                through = onward * hist_ref[k, j]
                by_rate[g] = by_rate[g] + through * rate(n, g)
                by_b[g] = by_b[g] + lam * b_n
                s_drate[j] = s_drate[j] + through * deltas[g]
                term = lam * dxs[g]
                mix = term if mix is None else mix + term
            db_row = jnp.where(lane == b_at + n, jnp.sum(mix, axis=1, keepdims=True), db_row)
        for g in range(groups):
            skip = skip_ref[:, g * width : (g + 1) * width]
            here = pl.ds(i, SEGS, stride=steps)
            s_delta[g, here, :] = by_rate[g] * (1.0 / LOG2E) + by_b[g] * vals[g]
            dval_ref[g, here, :] = by_b[g] * deltas[g] + dys[g] * skip
        part_ref[pl.ds(i, SEGS, stride=steps), :] = db_row
        return tuple(out)

    held = lax.fori_loop(0, span, sweep, tuple(s_state[j] for j in range(len(pairs))))
    for j in range(len(pairs)):
        s_state[j] = held[j]

    @pl.when(turn == turns - 1)
    def _():
        ddtb_ref[...] = jnp.zeros_like(ddtb_ref)
        ddtw_ref[...] = jnp.zeros_like(ddtw_ref)

        def finish(rows):
            pre = step_params(proj_ref, dtw_ref, dtb_ref, rank, rows)
            d_pre = take(s_delta, rows, groups) * jax.nn.sigmoid(pre)
            ddtb_ref[...] += jnp.sum(d_pre, axis=0, keepdims=True)
            ddtw_ref[...] += dot(proj_ref[rows, :rank].astype(f32), d_pre, (0, 0), HIGH)
            part_ref[rows, :] += dot(d_pre, dtwt_ref[...].astype(f32), (1, 0), HIGH) + dc_ref[rows, :]

        by_rows(total, finish)
        sums = [jnp.sum(s_drate[j], axis=0, keepdims=True) for j in range(len(pairs))]
        rows = [jnp.concatenate(sums[n * groups : (n + 1) * groups], axis=1) for n in range(states)]
        dalog_ref[...] = jnp.concatenate(rows, axis=0) * s_rate[...] * (1.0 / LOG2E)


def padded(rows, lanes, size):
    return -(-rows // 16) * 16 * (-(-lanes // 128) * 128) * size


def scan_span(steps):
    return math.gcd(steps, 32)


def run_forward(proj, values, gate, d_gated, dt_weight, dt_bias, a_log_t, skip, states):
    total, chans = values.shape
    rank = dt_weight.shape[0]
    steps = total // SEGS
    span = scan_span(steps)
    groups, width = lane_groups(chans)
    count = states * groups
    whole = lambda *shape: pl.BlockSpec(shape, lambda t: (0,) * len(shape))
    lanes = proj.shape[1]
    need = 5 * padded(total, chans, 2) + 3 * padded(total, chans, 4) + 3 * padded(total, lanes, 4)
    need += 2 * span * count * 32 * 128 + 8 * MIB
    return pl.pallas_call(
        functools.partial(forward_kernel, rank, states, span),
        grid=(steps // span,),
        in_specs=[
            whole(total, lanes), whole(total, chans), whole(total, chans), whole(total, chans),
            whole(rank, chans), whole(1, chans), whole(states, chans), whole(1, chans),
        ],
        out_specs=[
            whole(total, chans), whole(total, chans),
            pl.BlockSpec((span, count, SEGS, width), lambda t: (t, 0, 0, 0)),
            whole(total, lanes), whole(1, chans),
        ],
        out_shape=[
            jax.ShapeDtypeStruct((total, chans), bf16), jax.ShapeDtypeStruct((total, chans), bf16),
            jax.ShapeDtypeStruct((steps, count, SEGS, width), f32),
            jax.ShapeDtypeStruct((total, lanes), f32), jax.ShapeDtypeStruct((1, chans), f32),
        ],
        scratch_shapes=[
            pltpu.VMEM((groups, total, width), f32), pltpu.VMEM((groups, total, width), f32),
            pltpu.VMEM((groups, total, width), f32), pltpu.VMEM((1, total, lanes), f32),
            pltpu.VMEM((states, chans), f32), pltpu.VMEM((count, SEGS, width), f32),
        ],
        compiler_params=pltpu.CompilerParams(vmem_limit_bytes=need),
        name="scan_forward",
    )(proj, values, gate, d_gated, dt_weight, dt_bias, a_log_t, skip)


def run_backward(proj, values, gate, d_gated, dt_weight, dt_weight_t, dt_bias, a_log_t, skip, hist, dc, states):
    total, chans = values.shape
    rank = dt_weight.shape[0]
    steps = total // SEGS
    span = scan_span(steps)
    groups, width = lane_groups(chans)
    count = states * groups
    whole = lambda *shape: pl.BlockSpec(shape, lambda t: (0,) * len(shape))
    lanes = proj.shape[1]
    turns = steps // span
    need = 3 * padded(total, chans, 2) + 5 * padded(total, chans, 4) + 4 * padded(total, lanes, 4)
    need += 2 * span * count * 32 * 128 + 8 * MIB
    return pl.pallas_call(
        functools.partial(backward_kernel, rank, states, span),
        grid=(turns,),
        in_specs=[
            whole(total, lanes), whole(total, chans), whole(total, chans), whole(total, chans),
            whole(rank, chans), whole(chans, lanes), whole(1, chans), whole(states, chans), whole(1, chans),
            pl.BlockSpec((span, count, SEGS, width), lambda t: (turns - 1 - t, 0, 0, 0)),
            whole(total, lanes),
        ],
        out_specs=[
            whole(total, lanes), whole(groups, total, width), whole(rank, chans), whole(1, chans), whole(states, chans),
        ],
        out_shape=[
            jax.ShapeDtypeStruct((total, lanes), f32), jax.ShapeDtypeStruct((groups, total, width), f32),
            jax.ShapeDtypeStruct((rank, chans), f32), jax.ShapeDtypeStruct((1, chans), f32),
            jax.ShapeDtypeStruct((states, chans), f32),
        ],
        scratch_shapes=[
            pltpu.VMEM((groups, total, width), f32), pltpu.VMEM((groups, total, width), f32),
            pltpu.VMEM((groups, total, width), f32), pltpu.VMEM((groups, total, width), f32),
            pltpu.VMEM((1, total, lanes), f32), pltpu.VMEM((states, chans), f32),
            pltpu.VMEM((count, SEGS, width), f32), pltpu.VMEM((count, SEGS, width), f32),
        ],
        compiler_params=pltpu.CompilerParams(vmem_limit_bytes=need),
        name="scan_backward",
    )(proj, values, gate, d_gated, dt_weight, dt_weight_t, dt_bias, a_log_t, skip, hist, dc)


def shifted(array, steps):
    if steps == 0:
        return array
    zeros = jnp.zeros((abs(steps), array.shape[1]), array.dtype)
    if steps > 0:
        return jnp.concatenate([zeros, array[:-steps]], axis=0)
    return jnp.concatenate([array[-steps:], zeros], axis=0)


def sum_parts(array, axes, lead):
    got = lax.all_to_all(array, axes, split_axis=0, concat_axis=0, tiled=True)
    got = got.reshape((lead, got.shape[0] // lead) + got.shape[1:])
    return got.astype(f32).sum(axis=0)


def on_device(
    hidden_in, norm_gain, in_weight, conv_weight, conv_bias, x_weight, dt_weight, dt_bias, a_log, skip, out_weight,
    lengths, resets, out_grad,
):
    peers = lax.axis_size("ch")
    packs = lax.axis_size("ctx")
    me = lax.axis_index("ch")
    rows, width = hidden_in.shape
    chans = out_weight.shape[0]
    inner = chans * peers
    taps = conv_weight.shape[1]
    rank, states = dt_weight.shape[0], a_log.shape[1]
    total = rows * peers

    hidden_all = lax.all_gather(hidden_in, "ch", axis=0, tiled=True)
    in_rows = in_weight.shape[0]
    pieces = jnp.moveaxis(in_weight.reshape(in_rows, 2, peers, chans), 2, 0)
    my_cols = lax.all_to_all(pieces, "ch", split_axis=0, concat_axis=0, tiled=True).reshape(width, 2 * chans)
    grad_all = lax.all_gather(out_grad, "ch", axis=0, tiled=True)

    wide = hidden_all.astype(f32)
    scale_all = lax.rsqrt(jnp.mean(wide * wide, axis=1, keepdims=True) + eps)
    unit_all = wide * scale_all
    normed = (unit_all * norm_gain[None, :]).astype(bf16)
    mixed = dot(normed, my_cols, (1, 0)).astype(bf16)
    x_in, gate = mixed[:, :chans], mixed[:, chans:]

    sizes = lengths[0]
    offsets = jnp.cumsum(sizes) - sizes
    where_in = context_place(offsets, jnp.arange(total, dtype=jnp.int32))
    masks = [(where_in >= taps - 1 - k).astype(f32)[:, None] for k in range(taps)]
    cut = ((where_in == 0) | (resets == 1)).astype(bf16)[:, None]
    conv_w = lax.dynamic_slice_in_dim(conv_weight, me * chans, chans, 0)
    conv_b = lax.dynamic_slice_in_dim(conv_bias, me * chans, chans, 0)
    x_w = lax.dynamic_slice_in_dim(x_weight, me * chans, chans, 0)
    x_f = x_in.astype(f32)
    delayed = [shifted(x_f, taps - 1 - k) * masks[k] for k in range(taps)]
    pre = conv_b[None, :] + sum(conv_w[:, k][None, :] * delayed[k] for k in range(taps))
    values = silu(pre).astype(bf16)

    proj_part = dot(values, x_w, (1, 0)).astype(bf16)
    proj_own = sum_parts(proj_part, "ch", peers).astype(bf16)
    proj = lax.all_gather(proj_own, "ch", axis=0, tiled=True)
    low_cols = rank + 2 * states
    lanes = -(-(low_cols + 1) // 128) * 128
    proj_ext = jnp.concatenate([proj, cut, jnp.zeros((total, lanes - low_cols - 1), bf16)], axis=1)

    d_gated = dot(grad_all, out_weight, (1, 1)).astype(bf16)
    a_log_t = a_log.T
    dt_b, skip_row = dt_bias[None, :], skip[None, :]
    gated, d_gate, hist, dc, d_skip = run_forward(
        proj_ext, values, gate, d_gated, dt_weight, dt_b, a_log_t, skip_row, states
    )
    branch_part = dot(gated, out_weight, (1, 0)).astype(bf16)
    branch = lax.psum_scatter(branch_part, "ch", scatter_dimension=0, tiled=True)
    output = (hidden_in.astype(f32) + branch.astype(f32)).astype(bf16)
    d_out_weight = dot(gated, grad_all, (0, 0))

    dt_w_t = jnp.pad(dt_weight.T, ((0, 0), (0, lanes - rank)))
    d_part, value_part, d_dt_weight, d_dt_bias, d_a_log_t = run_backward(
        proj_ext, values, gate, d_gated, dt_weight, dt_w_t, dt_b, a_log_t, skip_row, hist, dc, states
    )
    d_proj_own = sum_parts(d_part[:, :low_cols].astype(bf16), "ch", peers).astype(bf16)
    d_proj = lax.all_gather(d_proj_own, "ch", axis=0, tiled=True)

    value_part = jnp.moveaxis(value_part, 0, 1).reshape(total, chans)
    d_values = value_part + dot(d_proj, x_w, (1, 1))
    d_x_weight = dot(values, d_proj, (0, 0))
    d_pre = d_values * silu_slope(pre)
    d_conv_bias = jnp.sum(d_pre, axis=0)
    d_conv_weight = jnp.stack([jnp.sum(d_pre * delayed[k], axis=0) for k in range(taps)], axis=1)
    d_x = sum(conv_w[:, k][None, :] * shifted(d_pre * masks[k], k + 1 - taps) for k in range(taps))
    d_mixed = jnp.concatenate([d_x.astype(bf16), d_gate], axis=1)

    d_normed_part = dot(d_mixed, my_cols, (1, 1))
    d_normed = lax.psum_scatter(d_normed_part.astype(bf16), "ch", scatter_dimension=0, tiled=True).astype(f32)
    d_gain = jnp.sum(d_normed_part * unit_all, axis=0)
    d_in = dot(normed, d_mixed, (0, 0)).astype(bf16)

    hidden = hidden_in.astype(f32)
    scale = lax.rsqrt(jnp.mean(hidden * hidden, axis=1, keepdims=True) + eps)
    unit = hidden * scale
    d_unit = d_normed * norm_gain[None, :]
    d_hidden = (
        out_grad.astype(f32) + scale * (d_unit - unit * jnp.mean(d_unit * unit, axis=1, keepdims=True))
    ).astype(bf16)

    in_parts = jnp.moveaxis(d_in.reshape(peers, packs, in_rows // packs, 2 * chans), 1, 0)
    in_parts = in_parts.reshape(packs * peers, in_rows // packs, 2 * chans)
    in_own = sum_parts(in_parts, ("ctx", "ch"), packs).astype(bf16)
    in_own = jnp.transpose(in_own.reshape(peers, in_rows // packs, 2, chans), (1, 2, 0, 3))
    in_own = in_own.reshape(in_rows // packs, 2 * inner)
    in_sum = lax.all_gather(in_own, "ctx", axis=0, tiled=True).astype(f32)

    out_own = sum_parts(d_out_weight.astype(bf16), "ctx", packs).astype(bf16)
    out_sum = lax.all_gather(out_own, "ctx", axis=0, tiled=True).astype(f32)

    gain_own = sum_parts(d_gain.astype(bf16), "ch", peers)
    small = [
        gain_own, d_conv_weight, d_conv_bias, d_x_weight, d_dt_weight, d_dt_bias[0], d_a_log_t.T, d_skip[0],
    ]
    flat = jnp.concatenate([a.reshape(-1) for a in small]).astype(bf16)
    every = lax.all_gather(flat, "ctx", axis=0, tiled=False).astype(f32).sum(axis=0)
    sums = []
    at = 0
    for a in small:
        sums.append(every[at : at + a.size].reshape(a.shape))
        at += a.size
    gain_sum, conv_w_sum, conv_b_sum, x_w_sum, dt_w_sum, dt_b_sum, a_log_sum, skip_sum = sums
    return (
        output, d_hidden, gain_sum, in_sum, conv_w_sum, conv_b_sum, x_w_sum, dt_w_sum, dt_b_sum, a_log_sum,
        skip_sum, out_sum,
    )


def solution(mesh):
    return jax.shard_map(
        on_device,
        mesh=mesh,
        in_specs=(
            P(("ctx", "ch"), None), P(), P("ch", None), P(), P(), P(), P(None, "ch"), P("ch"), P("ch", None),
            P("ch"), P("ch", None), P("ctx", None), P("ctx"), P(("ctx", "ch"), None),
        ),
        out_specs=(
            P(("ctx", "ch"), None), P(("ctx", "ch"), None), P("ch"), P("ch", None), P("ch", None), P("ch"),
            P("ch", None), P(None, "ch"), P("ch"), P("ch", None), P("ch"), P("ch", None),
        ),
        check_vma=False,
    )
```

time: 1300 us -> 459 us (0.35); the launches traced: 1270 us -> 458 us
  local copies, waits for them, and re-layouts: 406 us -> 17.5 us
  waiting for transfers between devices: 476 us -> 115 us
  other arithmetic: 228 us -> 16.9 us
  Pallas kernels: 0 us -> 173 us
  matrix products: 41.2 us -> 18.5 us
  blocking collectives: 69.9 us -> 83.1 us
    reduce_scatter x3 -> x2, waiting for transfers between devices: 222 us -> 38.1 us  [the longest x1 35.4 us: on_device(): lax.psum_scatter(branch_part, 'ch', scatter_dimension=0, tiled=True)]
    pallas_call x0 -> x2, Pallas kernels: none -> 173 us  [the longest x1 90.1 us: run_backward(): pl.pallas_call(functools.partial(backward_kernel, rank, states, span), gr...]
    pad x32 -> x1, local copies, waits for them, and re-layouts: 135 us -> 0.02 us  [on_device(): dt_w_t = jnp.pad(dt_weight.T, ((0, 0), (0, lanes - rank)))]
    psum x2 -> x0, waiting for transfers between devices: 95 us -> none  [the longest x1 55.2 us: on_device(): lax.psum(in_part.astype(jnp.bfloat16), 'ctx').astype(jnp.float32)]
    all_gather x2 -> x3, waiting for transfers between devices: 102 us -> 21 us  [the longest x1 21 us: on_device(): grad_all = lax.all_gather(out_grad, 'ch', axis=0, tiled=True)]
    slice x35 -> x11, local copies, waits for them, and re-layouts: 80 us -> 2.26 us  [the longest x6 1.11 us: on_device(): sums.append(every[at:at + a.size].reshape(a.shape))]
    mul x33 -> x0, local copies, waits for them, and re-layouts: 75.1 us -> none  [the longest x16 42.3 us: local_sweep(): push = (delta_sub[j] * values_sub[j])[:, None, :] * b_sub[j][None, :, :]]
    reduce_sum x11 -> x9, other arithmetic: 80.2 us -> 7.35 us  [the longest x1 2.46 us: on_device(): scale_all = lax.rsqrt(jnp.mean(wide * wide, axis=1, keepdims=True) + eps)]
  transfers between devices with their start and end apart: 16 -> 10, of which waited for: 9 -> 6; matrix products, arithmetic and copies ran while one was open for 30% -> 8% of each run, Pallas kernels for 0% -> 0%
where the time goes in v1:
time: 459 us; the launch traced here: 458 us
  Pallas kernels  173 us (38%)
  waiting for transfers between devices  115 us (25%)
  blocking collectives  83.1 us (18%)
  starting transfers between devices  20.1 us (4%)
  matrix products  18.5 us (4%)
  local copies, waits for them, and re-layouts  17.5 us (4%)
  other arithmetic  16.9 us (4%)
  between operations  14.4 us (3%)
    pallas_call x1, Pallas kernels, run_backward(): pl.pallas_call(functools.partial(backward_kernel, rank, states, span), gr...  90.1 us
    pallas_call x1, Pallas kernels, run_forward(): pl.pallas_call(functools.partial(forward_kernel, rank, states, span), gri...  83 us
    all_to_all x1, waiting for transfers between devices, on_device(): lax.all_to_all(pieces, 'ch', split_axis=0, concat_axis=0, tiled=True)  41.5 us
    reduce_scatter x1, waiting for transfers between devices, on_device(): lax.psum_scatter(branch_part, 'ch', scatter_dimension=0, tiled=True)  35.4 us
    all_to_all x1, blocking collectives, sum_parts(): got = lax.all_to_all(array, axes, split_axis=0, concat_axis=0, tiled=True)  30.4 us
    all_gather x1, waiting for transfers between devices, on_device(): grad_all = lax.all_gather(out_grad, 'ch', axis=0, tiled=True)  21 us
    dot_general x9, matrix products, dot(): lax.dot_general(a, b, ((dims[:1], dims[1:]), ((), ())), precision=precisi...  18.5 us
    all_gather x1, blocking collectives, on_device(): lax.all_gather(flat, 'ctx', axis=0, tiled=False).astype(f32).sum(axis=0)  15.2 us
  transfers between devices with their start and end apart: 10, of which 6 were waited for; matrix products, arithmetic and copies ran while one was open for 8% of the time, Pallas kernels for 0%

profile of v1, /device:TPU:0, one launch (start us, length us, event | category | flops | bytes accessed | tf_op | source)
XLA Modules:
  0.0 458.4 jit_solution(6431199555583555651)
XLA Ops:
  7.2 0.7 all-gather.5.cloned.1.call-update
  8.0 0.7 all-gather.7.cloned.1.call-update
  8.7 1.6 copy.106
  10.3 1.0 copy.107
  11.4 6.3 %all-to-all-start = ((bf16[8,128,2,256]{1,3,2,0:T(8,128)(2,1)}), bf16[8,128,2,256]{1,3,2,0:T(8,128)(2,1)S(1)}, u32[]{:S(2)}, u32[]{:S(2)}) async-start(bf16[8,128,2,256]{1,3,2,0:T(8,128)(2,1)} %copy.107), calls=%async_computation | async-start | bytes 2097152 | tf_op jit(solution)/shard_map/all_to_all | solution.py:415
  17.9 0.8 dynamic_slice.9
  18.6 0.9 constant_dynamic-slice_fusion
  19.7 41.5 %all-to-all-done = bf16[8,128,2,256]{1,3,2,0:T(8,128)(2,1)S(1)} async-done(((bf16[8,128,2,256]{1,3,2,0:T(8,128)(2,1)}), bf16[8,128,2,256]{1,3,2,0:T(8,128)(2,1)S(1)}, u32[]{:S(2)}, u32[]{:S(2)}) %all-to-all-start) | async-done | bytes 1048608 | tf_op jit(solution)/shard_map/all_to_all | solution.py:415
  61.1 0.7 copy.108
  61.9 2.5 fusion.4
  64.4 1.3 convolution_convert_fusion.2
  65.9 2.2 multiply_convert_fusion
  68.1 1.1 fusion.6
  69.2 0.7 copy.143
  69.9 3.4 all-to-all-start.1
  73.8 21.0 %all-gather.7.cloned.1.call-done = bf16[1024,1024]{1,0:T(8,128)(2,1)} async-done(((bf16[128,1024]{1,0:T(8,128)(2,1)}), bf16[1024,1024]{1,0:T(8,128)(2,1)}) %all-gather.7.cloned.1.call-update) | async-done | bytes 2097168 | tf_op jit(solution)/shard_map/all_gather | solution.py:416
  94.7 2.3 convolution_convert_fusion.4.dg_ref
  97.2 14.2 %all_gather.23 = bf16[1024,96]{1,0:T(8,128)(2,1)S(1)} all-gather(bf16[128,96]{1,0:T(8,128)(2,1)S(1)} %copy.111), channel_id=1, replica_groups=mesh['ctx'=4,'ch'=8] {'ch'}, dimensions={0}, use_global_device_ids=true | all-gather | bytes 221184 | tf_op jit(solution)/shard_map/all_gather | solution.py:440
  111.7 83.0 %scan_forward.1 = (bf16[1024,256]{1,0:T(8,128)(2,1)S(1)}, bf16[1024,256]{1,0:T(8,128)(2,1)S(1)}, f32[128,32,8,128]{3,2,1,0:T(8,128)S(1)}, f32[1024,128]{1,0:T(8,128)S(1)}, f32[1,256]{1,0:T(1,128)S(1)}) custom-call(bf16[1024,128]{1,0:T(8,128)(2,1)S(1)} %maximum_maximum_fusion.proj_ref, bf16[1024,256]{1,0:T(8,128)(2,1)S(1)} %get-tuple-element.109.val_ref, ...), custom_call_target="tpu_custom_call" | custom-call | tf_op jit(solution)/shard_map/scan_forward/pallas_call | solution.py:316
  194.7 90.1 %scan_backward.1 = (f32[1024,128]{1,0:T(8,128)S(1)}, f32[2,1024,128]{2,1,0:T(8,128)S(1)}, f32[64,256]{1,0:T(8,128)S(1)}, f32[1,256]{1,0:T(1,128)S(1)}, f32[16,256]{1,0:T(8,128)S(1)}) custom-call(bf16[1024,128]{1,0:T(8,128)(2,1)S(1)} %maximum_maximum_fusion.proj_ref, bf16[1024,256]{1,0:T(8,128)(2,1)S(1)} %get-tuple-element.109.val_ref, ...), custom_call_target="tpu_custom_call" | custom-call | tf_op jit(solution)/shard_map/scan_backward/pallas_call | solution.py:355
  284.8 1.0 copy-done.5
  285.8 0.8 copy.115
  286.7 3.4 all-to-all-start.2
  290.3 8.0 %all-to-all-done.2 = bf16[8,128,96]{1,2,0:T(8,128)(2,1)S(1)} async-done(((bf16[8,128,96]{1,2,0:T(8,128)(2,1)}), bf16[8,128,96]{1,2,0:T(8,128)(2,1)S(1)}, u32[]{:S(2)}, u32[]{:S(2)}) %all-to-all-start.2) | async-done | bytes 196640 | tf_op jit(solution)/shard_map/all_to_all | solution.py:393
  298.3 13.1 %all_gather.25 = bf16[1024,96]{0,1:T(8,128)(2,1)S(1)} all-gather(bf16[128,96]{0,1:T(8,128)(2,1)S(1)} %reduce_sum.150), channel_id=1, replica_groups=mesh['ctx'=4,'ch'=8] {'ch'}, dimensions={0}, use_global_device_ids=true | all-gather | bytes 221184 | tf_op jit(solution)/shard_map/all_gather | solution.py:461
  311.5 2.1 fusion.5
  314.3 0.8 copy-done.7
  315.4 2.1 fusion.29
  317.5 1.5 convolution_convert_fusion.1
  319.1 30.4 %all_to_all.43 = bf16[32,32,512]{2,1,0:T(8,128)(2,1)S(1)} all-to-all(bf16[32,32,512]{2,1,0:T(8,128)(2,1)S(1)} %bitcast.86), channel_id=1, replica_groups=mesh['ctx'=4,'ch'=8] {'ctx','ch'}, dimensions={0} | all-to-all | bytes 2097152 | tf_op jit(solution)/shard_map/all_to_all | solution.py:393
  350.0 0.8 copy.130
  350.9 4.7 %fusion.3 = (bf16[1024]{0:T(1024)(128)(2,1)S(1)}, bf16[1024,1024]{1,0:T(8,128)(2,1)}) fusion(bf16[1024,1024]{1,0:T(8,128)(2,1)} %all-gather.5.cloned.1.call-done, f32[1024]{0:T(1024)S(1)} %add_rsqrt_fusion, bf16[64,8,8,128]{3,2,1,0:T(8,128)(2,1)} %bitcast.91, bf16[1024,256]{1,0:T(8,128)(2,1)S(1)} %get-tuple-element.27, bf16[1024,256]{1,0:T(8,128)(2,1)} %copy-done.17), kind=kOutput, calls=%fused_computation.5 | convolution fusion | flops 1081080832 | bytes 6297600 | tf_op jit(solution)/shard_map/dot_general | solution.py:36
  355.7 0.9 copy-done.10
  357.0 2.0 convolution_convert_fusion
  359.1 3.2 convolution_convert_fusion.3
  363.2 3.3 all-to-all-start.3
  367.0 4.8 %all-to-all-done.3 = bf16[8,128,1]{1,2,0:T(2,128)(2,1)S(1)} async-done(((bf16[8,128,1]{1,2,0:T(2,128)(2,1)}), bf16[8,128,1]{1,2,0:T(2,128)(2,1)S(1)}, u32[]{:S(2)}, u32[]{:S(2)}) %all-to-all-start.3) | async-done | bytes 2080 | tf_op jit(solution)/shard_map/all_to_all | solution.py:393
  371.9 3.5 all-to-all-start.5
  375.7 15.2 %all-gather = bf16[4,1,46976]{2,1,0:T(2,128)(2,1)S(1)} all-gather(bf16[1,1,46976]{2,1,0:T(2,128)(2,1)S(1)} %bitcast.98), channel_id=1, replica_groups=mesh['ctx'=4,'ch'=8] {'ctx'}, dimensions={0}, use_global_device_ids=true | all-gather | bytes 469760 | tf_op jit(solution)/shard_map/all_gather | solution.py:500
  390.9 1.2 convert_reduce_fusion
  393.5 0.7 copy.123
  396.5 10.1 %all_gather.28 = bf16[256,1024]{1,0:T(8,128)(2,1)S(1)} all-gather(bf16[64,1024]{1,0:T(8,128)(2,1)S(1)} %reduce_sum.161), channel_id=1, replica_groups=mesh['ctx'=4,'ch'=8] {'ctx'}, dimensions={0}, use_global_device_ids=true | all-gather | bytes 655360 | tf_op jit(solution)/shard_map/all_gather | solution.py:493
  406.6 1.1 convert_element_type.156
  407.6 2.8 convert_element_type.154
  410.5 2.7 reduce-scatter.5.cloned.1.call-done
  413.2 1.2 fusion.16
  414.3 35.4 %reduce-scatter.3.cloned.1.call-done = bf16[128,1024]{1,0:T(8,128)(2,1)} async-done(((bf16[1024,1024]{1,0:T(8,128)(2,1)}), bf16[128,1024]{1,0:T(8,128)(2,1)}) %reduce-scatter.3.cloned.1.call-update) | async-done | bytes 262160 | tf_op jit(solution)/shard_map/reduce_scatter | solution.py:452
  449.8 2.1 fusion.20
  (120 shorter events, 9.0 us)
Async XLA Ops:
  7.2 87.5 %copy-start = (bf16[256,1024]{1,0:T(8,128)(2,1)S(1)}, bf16[256,1024]{1,0:T(8,128)(2,1)}, u32[]{:S(2)}) copy-start(bf16[256,1024]{1,0:T(8,128)(2,1)} %param.24) | copy-start | bytes 1572868
  7.2 54.7 %all-gather.5.cloned.1.call-start = ((), (), s32[]{:S(2)}) async-start(), calls=%async_computation.8 | async-start | bytes 2359296 | tf_op jit(solution)/shard_map/all_gather | solution.py:412
  7.9 86.8 %all-gather.7.cloned.1.call-start = ((), (), s32[]{:S(2)}) async-start(), calls=%async_computation.9 | async-start | bytes 2359296 | tf_op jit(solution)/shard_map/all_gather | solution.py:416
  10.3 7.4 %copy-start.21 = (s32[1,4]{1,0:T(1,128)S(1)}, s32[1,4]{1,0:T(1,128)}, u32[]{:S(2)}) copy-start(s32[1,4]{1,0:T(1,128)} %param.25) | copy-start | bytes 52
  10.3 9.3 %copy-start.19 = (s32[1024]{0:T(1024)S(1)}, s32[1024]{0:T(1024)}, u32[]{:S(2)}) copy-start(s32[1024]{0:T(1024)} %param.26) | copy-start | bytes 12292
  11.4 49.8 %all-to-all-start = ((bf16[8,128,2,256]{1,3,2,0:T(8,128)(2,1)}), bf16[8,128,2,256]{1,3,2,0:T(8,128)(2,1)S(1)}, u32[]{:S(2)}, u32[]{:S(2)}) async-start(bf16[8,128,2,256]{1,3,2,0:T(8,128)(2,1)} %copy.107), calls=%async_computation | async-start | bytes 2097152 | tf_op jit(solution)/shard_map/all_to_all | solution.py:415
  19.7 44.7 %copy-start.18 = (f32[1024]{0:T(1024)S(1)}, f32[1024]{0:T(1024)}, u32[]{:S(2)}) copy-start(f32[1024]{0:T(1024)} %param.15) | copy-start | bytes 12292
  61.8 2.5 copy-start.13
  61.9 2.6 copy-start.11
  65.8 2.3 copy-start.8
  65.9 2.2 copy-start.6
  65.9 7.4 %copy-start.1 = (bf16[64,256]{1,0:T(8,128)(2,1)S(1)}, bf16[64,256]{1,0:T(8,128)(2,1)}, u32[]{:S(2)}) copy-start(bf16[64,256]{1,0:T(8,128)(2,1)} %dtw_ref.3) | copy-start | bytes 98308
  69.9 27.2 %all-to-all-start.1 = ((bf16[8,128,96]{1,2,0:T(8,128)(2,1)}), bf16[8,128,96]{1,2,0:T(8,128)(2,1)S(1)}, u32[]{:S(2)}, u32[]{:S(2)}) async-start(bf16[8,128,96]{1,2,0:T(8,128)(2,1)} %bitcast.70), calls=%async_computation.1 | async-start | bytes 393216 | tf_op jit(solution)/shard_map/all_to_all | solution.py:393
  73.8 37.9 %copy-start.2 = (f32[256,16]{0,1:T(8,128)S(1)}, f32[256,16]{0,1:T(8,128)}, u32[]{:S(2)}) copy-start(f32[256,16]{0,1:T(8,128)} %param.22) | copy-start | bytes 49156
  73.8 37.9 %copy-start.3 = (f32[256]{0:T(256)S(1)}, f32[256]{0:T(256)}, u32[]{:S(2)}) copy-start(f32[256]{0:T(256)} %param.21) | copy-start | bytes 3076
  73.8 37.9 %copy-start.4 = (f32[256]{0:T(256)S(1)}, f32[256]{0:T(256)}, u32[]{:S(2)}) copy-start(f32[256]{0:T(256)} %param.23) | copy-start | bytes 3076
  284.8 1.0 copy-start.5
  286.7 11.7 %all-to-all-start.2 = ((bf16[8,128,96]{1,2,0:T(8,128)(2,1)}), bf16[8,128,96]{1,2,0:T(8,128)(2,1)S(1)}, u32[]{:S(2)}, u32[]{:S(2)}) async-start(bf16[8,128,96]{1,2,0:T(8,128)(2,1)} %copy.115), calls=%async_computation.3 | async-start | bytes 393216 | tf_op jit(solution)/shard_map/all_to_all | solution.py:393
  290.1 117.6 %all-gather.9.cloned.1.call-start = ((), (), s32[]{:S(2)}) async-start(), calls=%async_computation.12 | async-start | bytes 1310720 | tf_op jit(solution)/shard_map/all_gather | solution.py:490
  311.5 2.1 copy-start.15
  313.9 1.2 copy-start.7
  313.9 1.5 copy-start.9
  315.4 2.1 copy-start.12
  317.5 1.5 copy-start.17
  350.9 62.3 %reduce-scatter.5.cloned.1.call-start = ((), (), s32[]{:S(2)}) async-start(), calls=%async_computation.11 | async-start | bytes 2359296 | tf_op jit(solution)/shard_map/reduce_scatter | solution.py:473
  355.6 1.0 copy-start.10
  355.7 94.1 %reduce-scatter.3.cloned.1.call-start = ((), (), s32[]{:S(2)}) async-start(), calls=%async_computation.10 | async-start | bytes 2359296 | tf_op jit(solution)/shard_map/reduce_scatter | solution.py:452
  359.1 3.2 copy-start.16
  359.1 3.4 copy-start.20
  363.2 8.7 %all-to-all-start.3 = ((bf16[8,128,1]{1,2,0:T(2,128)(2,1)}), bf16[8,128,1]{1,2,0:T(2,128)(2,1)S(1)}, u32[]{:S(2)}, u32[]{:S(2)}) async-start(bf16[8,128,1]{1,2,0:T(2,128)(2,1)} %copy.116), calls=%async_computation.5 | async-start | bytes 8192 | tf_op jit(solution)/shard_map/all_to_all | solution.py:393
  371.9 24.5 %all-to-all-start.5 = ((bf16[4,64,1024]{2,1,0:T(8,128)(2,1)}), bf16[4,64,1024]{2,1,0:T(8,128)(2,1)S(1)}, u32[]{:S(2)}, u32[]{:S(2)}) async-start(bf16[4,64,1024]{2,1,0:T(8,128)(2,1)} %bitcast.24), calls=%async_computation.7 | async-start | bytes 1048576 | tf_op jit(solution)/shard_map/all_to_all | solution.py:393
  407.6 42.1 %copy-start.14 = (bf16[128,1024]{1,0:T(8,128)(2,1)S(1)}, bf16[128,1024]{1,0:T(8,128)(2,1)}, u32[]{:S(2)}) copy-start(bf16[128,1024]{1,0:T(8,128)(2,1)} %param.27) | copy-start | bytes 786436
Sparse Core Ops, SparseCore 0:
  9.6 51.3 all-gather.4
  62.6 32.0 all-gather.6
  351.0 24.2 all-gather.8
  377.4 35.7 reduce-scatter.4
  415.3 34.4 reduce-scatter.2

commit v2 on v1

v2 whole, which is shorter than its diff:
```python
import functools
import math

import jax
import jax.numpy as jnp
from jax import lax
from jax.experimental import pallas as pl
from jax.experimental.pallas import tpu as pltpu
from jax.sharding import PartitionSpec as P

f32 = jnp.float32
bf16 = jnp.bfloat16
eps = 1e-05
LOG2E = 1.4426950408889634
CUT = 1e30
SEGS = 8
UNROLL_FIRST = 4
UNROLL_SECOND = 4
MIB = 1 << 20
ROOM = 56 * MIB


def silu(v):
    return v * jax.nn.sigmoid(v)


def silu_slope(v):
    sig = jax.nn.sigmoid(v)
    return sig * (1.0 + v * (1.0 - sig))


def context_place(offsets, places):
    begins = jnp.max(jnp.where(offsets[:, None] <= places[None, :], offsets[:, None], 0), axis=0)
    return places - begins


def dot(a, b, dims, precision=None):
    return lax.dot_general(a, b, ((dims[:1], dims[1:]), ((), ())), precision=precision, preferred_element_type=f32)


def lane_groups(chans):
    width = 128 if chans % 128 == 0 else chans
    return chans // width, width


def softplus(v):
    small = jnp.exp(-jnp.abs(v))
    series = small * (1.0 - small * (0.5 - small * (1.0 / 3.0)))
    return jnp.maximum(v, 0.0) + jnp.where(small < 0.01, series, jnp.log(1.0 + small))


def mixing(span, back):
    size = span * SEGS
    row = lax.broadcasted_iota(jnp.int32, (size, size), 0)
    column = lax.broadcasted_iota(jnp.int32, (size, size), 1)
    if back:
        hit = (row % span) * SEGS + row // span == column
    else:
        hit = (row % SEGS) * span + row // SEGS == column
    return hit.astype(f32).astype(bf16)


def context_positions(starts_ref, first_row, rows, steps, chans):
    groups, width = lane_groups(chans)
    row = lax.broadcasted_iota(jnp.int32, (rows, width), 0) + first_row
    token = jnp.bitwise_and(row, SEGS - 1) * steps + jnp.right_shift(row, SEGS.bit_length() - 1)
    begin = jnp.zeros((rows, width), jnp.int32)
    for c in range(starts_ref.shape[1]):
        begin = jnp.where(starts_ref[0, c] <= token, starts_ref[0, c], begin)
    place = token - begin
    return jnp.concatenate([place] * groups, axis=1) if groups > 1 else place


def split_dot(wide, narrow, dims, swapped=False):
    high = wide.astype(bf16)
    low = (wide - high.astype(f32)).astype(bf16)
    if swapped:
        return dot(narrow, high, dims) + dot(narrow, low, dims)
    return dot(high, narrow, dims) + dot(low, narrow, dims)


def put(ref, rows, value, groups, width):
    for g in range(groups):
        ref[g, rows, :] = value[:, g * width : (g + 1) * width]


def take(ref, rows, groups):
    return jnp.concatenate([ref[g, rows, :] for g in range(groups)], axis=1) if groups > 1 else ref[0, rows, :]


def block_rows(t, size):
    return pl.ds(pl.multiple_of(t * size, size), size)


def entry_kernel(
    span, taps, rank_cols, starts_ref, hid_ref, w_ref, gain_ref, cw_ref, cb_ref, xw_ref,
    normed_ref, scale_ref, x_ref, gate_ref, val_ref, pre_ref, proj_ref, s_x, s_mixing,
):
    turn = pl.program_id(0)
    turns = pl.num_programs(0)
    chans = x_ref.shape[1]
    size = span * SEGS
    steps = span * turns
    halo = (taps - 1) * SEGS

    @pl.when(turn == 0)
    def _():
        s_mixing[...] = mixing(span, False)

    wide = hid_ref[...].astype(f32).reshape(size, hid_ref.shape[2])
    scale = lax.rsqrt(jnp.mean(wide * wide, axis=1, keepdims=True) + eps)
    normed = (wide * scale * gain_ref[...]).astype(bf16)
    normed_ref[...] = normed.reshape(normed_ref.shape)
    scale_ref[...] = scale.reshape(scale_ref.shape)
    mixed = dot(normed, w_ref[...], (1, 0)).astype(bf16)
    mixed = dot(s_mixing[...], mixed, (1, 0))
    rows = block_rows(turn, size)
    x_ref[rows, :] = mixed[:, :chans].astype(bf16)
    gate_ref[rows, :] = mixed[:, chans:].astype(bf16)
    s_x[pl.ds(pl.multiple_of(turn * size + halo, SEGS), size), :] = mixed[:, :chans]

    @pl.when(turn == turns - 1)
    def _():
        first = lax.broadcasted_iota(jnp.int32, (SEGS, chans), 0) == 0
        for j in range(taps - 1):
            last = s_x[steps * SEGS + j * SEGS : steps * SEGS + (j + 1) * SEGS, :]
            s_x[j * SEGS : (j + 1) * SEGS, :] = jnp.where(first, 0.0, pltpu.roll(last, 1, 0))

        def step(t, carry):
            place = context_positions(starts_ref, t * size, size, steps, chans)
            pre = cb_ref[...] + jnp.zeros((size, chans), f32)
            for k in range(taps):
                lag = taps - 1 - k
                at = pl.ds(pl.multiple_of(t * size + halo - lag * SEGS, SEGS), size)
                pre = pre + cw_ref[k : k + 1, :] * jnp.where(place >= lag, s_x[at, :], 0.0)
            rows = block_rows(t, size)
            pre_ref[rows, :] = pre
            values = silu(pre).astype(bf16)
            val_ref[rows, :] = values
            proj_ref[rows, :] = dot(values, xw_ref[...], (1, 0)).astype(bf16)
            return carry

        lax.fori_loop(0, turns, step, 0)


def gate_kernel(
    span, grad_ref, w_ref, gate_ref, val_ref, y_ref, skip_ref,
    branch_ref, gated_ref, dy_ref, dgate_ref, dskip_ref, s_in, s_out,
):
    turn = pl.program_id(0)
    size = span * SEGS

    @pl.when(turn == 0)
    def _():
        s_in[...] = mixing(span, False)
        s_out[...] = mixing(span, True)
        dskip_ref[...] = jnp.zeros_like(dskip_ref)

    vals = val_ref[...].astype(f32)
    gate = gate_ref[...].astype(f32)
    sig = jax.nn.sigmoid(gate)
    act = gate * sig
    scanned = y_ref[...] + skip_ref[...] * vals
    gated = dot(s_out[...], (scanned * act).astype(bf16), (1, 0)).astype(bf16)
    gated_ref[...] = gated.reshape(gated_ref.shape)
    branch_ref[...] = dot(gated, w_ref[...], (1, 0)).astype(bf16).reshape(branch_ref.shape)
    grad = grad_ref[...].reshape(size, grad_ref.shape[2])
    d_gated = dot(s_in[...], dot(grad, w_ref[...], (1, 1)).astype(bf16), (1, 0))
    dy = d_gated * act
    dy_ref[...] = dy
    d_gate = (d_gated * scanned * (sig * (1.0 + gate * (1.0 - sig)))).astype(bf16)
    d_gate = dot(s_out[...], d_gate, (1, 0)).astype(bf16)
    dgate_ref[...] = d_gate.reshape(dgate_ref.shape)
    dskip_ref[...] += jnp.sum(dy * vals, axis=0, keepdims=True)


def exit_kernel(
    span, taps, low_cols, starts_ref, dproj_ref, part_ref, pre_ref, x_ref, val_ref, cw_ref, xw_ref, dgate_ref, w_ref,
    hid_ref, scale_ref, gain_ref, ddtw_ref, dalog_ref, ddtb_ref, dskip_ref,
    dn_ref, din_ref, small_ref, dgain_ref, s_pre, s_dx, s_din,
):
    total, chans = x_ref.shape
    size = span * SEGS
    steps = total // SEGS
    turns = steps // span
    halo = (taps - 1) * SEGS
    turn = pl.program_id(0)

    @pl.when(turn == 0)
    def _():

        def first(t, carry):
            rows = block_rows(t, size)
            d_proj = dproj_ref[rows, :]
            d_values = part_ref[rows, :] + dot(d_proj, xw_ref[...], (1, 1))
            d_pre = d_values * silu_slope(pre_ref[rows, :])
            s_pre[rows, :] = d_pre
            d_bias, d_xw = carry
            return d_bias + jnp.sum(d_pre, axis=0, keepdims=True), d_xw + dot(d_proj, val_ref[rows, :], (0, 0))

        begin = (jnp.zeros((1, chans), f32), jnp.zeros((dproj_ref.shape[1], chans), f32))
        d_bias, d_xw = lax.fori_loop(0, turns, first, begin)
        last = lax.broadcasted_iota(jnp.int32, (SEGS, chans), 0) == SEGS - 1
        for j in range(taps - 1):
            head = s_pre[j * SEGS : (j + 1) * SEGS, :]
            s_pre[total + j * SEGS : total + (j + 1) * SEGS, :] = jnp.where(last, 0.0, pltpu.roll(head, SEGS - 1, 0))
        back = mixing(span, True)

        def second(t, sums):
            rows = block_rows(t, size)
            x = x_ref[rows, :].astype(f32)
            d_x = jnp.zeros((size, chans), f32)
            out = []
            for k in range(taps):
                lag = taps - 1 - k
                place = context_positions(starts_ref, t * size + lag * SEGS, size, steps, chans)
                later = s_pre[pl.ds(pl.multiple_of(t * size + lag * SEGS, SEGS), size), :]
                later = jnp.where(place >= lag, later, 0.0)
                d_x = d_x + cw_ref[k : k + 1, :] * later
                out.append(sums[k] + jnp.sum(later * x, axis=0, keepdims=True))
            natural = dot(back, d_x.astype(bf16), (1, 0)).astype(bf16).reshape(SEGS, span, chans)
            s_dx[:, block_rows(t, span), :] = natural
            return tuple(out)

        sums = lax.fori_loop(0, turns, second, (jnp.zeros((1, chans), f32),) * taps)
        s_din[...] = jnp.zeros_like(s_din)
        dgain_ref[...] = jnp.zeros_like(dgain_ref)
        rest = [*sums, d_bias, ddtb_ref[...], dskip_ref[...]]
        pad = small_ref.shape[0] - low_cols - ddtw_ref.shape[0] - dalog_ref.shape[0] - len(rest)
        small = [d_xw[:low_cols], ddtw_ref[...], dalog_ref[...], *rest, jnp.zeros((pad, chans), f32)]
        small_ref[...] = jnp.concatenate(small, axis=0).astype(bf16)

    @pl.when(turn > 0)
    def _():
        rows = hid_ref.shape[0]
        per_segment = steps // rows if rows <= steps else 1
        if rows <= steps:
            here = pl.ds(pl.multiple_of((turn - 1) % per_segment * rows, rows), rows)
            d_x = s_dx[(turn - 1) // per_segment, here, :]
        else:
            d_x = s_dx[pl.ds((turn - 1) * (rows // steps), rows // steps)].reshape(rows, chans)
        both = jnp.concatenate([d_x, dgate_ref[...]], axis=1)
        d_normed = dot(both, w_ref[...], (1, 1)).astype(bf16)
        dn_ref[...] = d_normed
        unit = hid_ref[...].astype(f32) * scale_ref[...]
        dgain_ref[...] += jnp.sum(d_normed.astype(f32) * unit, axis=0, keepdims=True)
        s_din[...] += dot(d_x, (unit * gain_ref[...]).astype(bf16), (0, 0))

    @pl.when(turn == pl.num_programs(0) - 1)
    def _():
        din_ref[...] = s_din[...].T.astype(bf16)


def prepare_spread(hot_ref, rank, states):
    row = lax.broadcasted_iota(jnp.int32, (hot_ref.shape[0], 128), 0)
    for n in range(2 * states):
        hot_ref[:, n * 128 : (n + 1) * 128] = (row == rank + n).astype(f32).astype(bf16)


def spread_columns(out_ref, slot, hot_ref, proj_ref, rows, states):
    block = proj_ref[rows, :]
    for n in range(0, 2 * states, 2):
        both = dot(block, hot_ref[:, n * 128 : (n + 2) * 128], (1, 0))
        out_ref[slot, n] = both[:, :128]
        out_ref[slot, n + 1] = both[:, 128:]


def prepare_sums(pick_ref, rank):
    column = lax.broadcasted_iota(jnp.int32, (128, pick_ref.shape[1]), 1)
    for n in range(pick_ref.shape[0] // 128):
        pick_ref[n * 128 : (n + 1) * 128, :] = (column == rank + n).astype(f32).astype(bf16)


def sum_lanes(mix_ref, pick_ref):
    total = None
    for first in range(0, mix_ref.shape[1], 512):
        part = dot(mix_ref[:, first : first + 512].astype(bf16), pick_ref[first : first + 512, :], (1, 0))
        total = part if total is None else total + part
    return total


def forward_kernel(
    rank, states, span, proj_ref, val_ref, cut_ref, dtw_ref, dtb_ref, alog_ref,
    y_ref, hist_ref, delta_ref, s_cut, s_dx, s_rate, s_state, s_wide, s_hot,
):
    total, chans = val_ref.shape
    steps = total // SEGS
    size = span * SEGS
    groups, width = lane_groups(chans)
    pairs = [(n, g) for n in range(states) for g in range(groups)]
    turn = pl.program_id(0)
    turns = steps // span
    slots = s_wide.shape[0]

    def rate(n, g):
        return s_rate[n : n + 1, g * width : (g + 1) * width]

    @pl.when(turn == 0)
    def _():
        s_rate[...] = -jnp.exp(alog_ref[...]) * LOG2E
        prepare_spread(s_hot, rank, states)

        def block(t, carry):
            rows = block_rows(t, size)
            slot = t if slots > 1 else 0
            spread_columns(s_wide, slot, s_hot, proj_ref, rows, states)
            delta = softplus(dot(proj_ref[rows, :rank], dtw_ref[...], (1, 0)) + dtb_ref[...])
            put(delta_ref, rows, delta, groups, width)
            put(s_cut, rows, delta + cut_ref[rows, :] * CUT, groups, width)
            put(s_dx, rows, delta * val_ref[rows, :].astype(f32), groups, width)

            def sweep(k, carry):
                held, span_sum = carry
                at = block_rows(t * span + k, SEGS)
                here = block_rows(k, SEGS)
                cuts = [s_cut[g, at, :] for g in range(groups)]
                dxs = [s_dx[g, at, :] for g in range(groups)]
                out = []
                for n, g in pairs:
                    push = dxs[g] * s_wide[slot, n, here, :width]
                    out.append(jnp.exp2(cuts[g] * rate(n, g)) * held[n * groups + g] + push)
                return tuple(out), tuple(span_sum[g] + cuts[g] for g in range(groups))

            return lax.fori_loop(0, span, sweep, carry, unroll=UNROLL_FIRST)

        zero = jnp.zeros((SEGS, width), f32)
        ends, sums = lax.fori_loop(0, turns, block, ((zero,) * len(pairs), (zero,) * groups))
        first = lax.broadcasted_iota(jnp.int32, (SEGS, width), 0) == 0
        for n, g in pairs:
            gain = jnp.exp2(sums[g] * rate(n, g))
            end = ends[n * groups + g]
            start = zero
            for _ in range(SEGS - 1):
                start = jnp.where(first, 0.0, pltpu.roll(gain * start + end, 1, 0))
            s_state[n * groups + g] = start

    slot = turn if slots > 1 else 0
    if slots == 1:
        spread_columns(s_wide, slot, s_hot, proj_ref, block_rows(turn, size), states)

    def sweep(k, held):
        at = block_rows(turn * span + k, SEGS)
        here = block_rows(k, SEGS)
        cuts = [s_cut[g, at, :] for g in range(groups)]
        dxs = [s_dx[g, at, :] for g in range(groups)]
        ys = [jnp.zeros((SEGS, width), f32) for _ in range(groups)]
        out = []
        for n in range(states):
            b_n = s_wide[slot, n, here, :width]
            c_n = s_wide[slot, states + n, here, :width]
            for g in range(groups):
                old = held[n * groups + g]
                hist_ref[0, k, n * groups + g] = old
                new = jnp.exp2(cuts[g] * rate(n, g)) * old + dxs[g] * b_n
                out.append(new)
                ys[g] = ys[g] + new * c_n
        for g in range(groups):
            y_ref[at, g * width : (g + 1) * width] = ys[g]
        return tuple(out)

    held = lax.fori_loop(0, span, sweep, tuple(s_state[j] for j in range(len(pairs))), unroll=UNROLL_SECOND)
    for j in range(len(pairs)):
        s_state[j] = held[j]
        hist_ref[0, span, j] = held[j]


def backward_kernel(
    rank, states, span, proj_ref, val_ref, cut_ref, dy_ref, delta_ref, dtw_ref, dtwt_ref, dtb_ref, alog_ref, skip_ref,
    hist_ref, part_ref, dval_ref, ddtw_ref, ddtb_ref, dalog_ref,
    s_cut, s_val, s_dy, s_dd, s_rate, s_state, s_drate, s_wide, s_mix, s_hot, s_pick,
):
    total, chans = val_ref.shape
    steps = total // SEGS
    size = span * SEGS
    groups, width = lane_groups(chans)
    pairs = [(n, g) for n in range(states) for g in range(groups)]
    turns = steps // span
    turn = pl.program_id(0)
    place = turns - 1 - turn
    slots = s_wide.shape[0]

    def rate(n, g):
        return s_rate[n : n + 1, g * width : (g + 1) * width]

    @pl.when(turn == 0)
    def _():
        s_rate[...] = -jnp.exp(alog_ref[...]) * LOG2E
        prepare_spread(s_hot, rank, states)
        prepare_sums(s_pick, rank)
        s_drate[...] = jnp.zeros_like(s_drate)
        s_mix[...] = jnp.zeros_like(s_mix)

        def block(turned, carry):
            t = turns - 1 - turned
            rows = block_rows(t, size)
            slot = t if slots > 1 else 0
            spread_columns(s_wide, slot, s_hot, proj_ref, rows, states)
            delta = take(delta_ref, rows, groups)
            put(s_cut, rows, delta + cut_ref[rows, :] * CUT, groups, width)
            put(s_val, rows, val_ref[rows, :].astype(f32), groups, width)
            put(s_dy, rows, dy_ref[rows, :], groups, width)

            def sweep(turned, carry):
                k = span - 1 - turned
                held, span_sum = carry
                at = block_rows(t * span + k, SEGS)
                here = block_rows(k, SEGS)
                cuts = [s_cut[g, at, :] for g in range(groups)]
                dys = [s_dy[g, at, :] for g in range(groups)]
                out = []
                for n, g in pairs:
                    lam = dys[g] * s_wide[slot, states + n, here, :width] + held[n * groups + g]
                    out.append(jnp.exp2(cuts[g] * rate(n, g)) * lam)
                return tuple(out), tuple(span_sum[g] + cuts[g] for g in range(groups))

            return lax.fori_loop(0, span, sweep, carry, unroll=UNROLL_FIRST)

        zero = jnp.zeros((SEGS, width), f32)
        ends, sums = lax.fori_loop(0, turns, block, ((zero,) * len(pairs), (zero,) * groups))
        last = lax.broadcasted_iota(jnp.int32, (SEGS, width), 0) == SEGS - 1
        for n, g in pairs:
            gain = jnp.exp2(sums[g] * rate(n, g))
            end = ends[n * groups + g]
            start = zero
            for _ in range(SEGS - 1):
                start = jnp.where(last, 0.0, pltpu.roll(gain * start + end, SEGS - 1, 0))
            s_state[n * groups + g] = start

    slot = place if slots > 1 else 0
    if slots == 1:
        spread_columns(s_wide, slot, s_hot, proj_ref, block_rows(place, size), states)

    def sweep(turned, held):
        k = span - 1 - turned
        at = block_rows(place * span + k, SEGS)
        here = block_rows(k, SEGS)
        cuts = [s_cut[g, at, :] for g in range(groups)]
        deltas = [delta_ref[g, at, :] for g in range(groups)]
        vals = [s_val[g, at, :] for g in range(groups)]
        dys = [s_dy[g, at, :] for g in range(groups)]
        dxs = [deltas[g] * vals[g] for g in range(groups)]
        zero = jnp.zeros((SEGS, width), f32)
        by_rate = [zero] * groups
        by_b = [zero] * groups
        out = []
        for n in range(states):
            b_n = s_wide[slot, n, here, :width]
            c_n = s_wide[slot, states + n, here, :width]
            mix = None
            mix_c = None
            for g in range(groups):
                j = n * groups + g
                lam = dys[g] * c_n + held[j]
                onward = jnp.exp2(cuts[g] * rate(n, g)) * lam
                out.append(onward)
                through = onward * hist_ref[0, k, j]
                by_rate[g] = by_rate[g] + through * rate(n, g)
                by_b[g] = by_b[g] + lam * b_n
                s_drate[j] = s_drate[j] + through * deltas[g]
                term = lam * dxs[g]
                mix = term if mix is None else mix + term
                term = dys[g] * hist_ref[0, k + 1, j]
                mix_c = term if mix_c is None else mix_c + term
            s_mix[here, n * 128 : n * 128 + width] = mix
            s_mix[here, (states + n) * 128 : (states + n) * 128 + width] = mix_c
        for g in range(groups):
            skip = skip_ref[:, g * width : (g + 1) * width]
            s_dd[g, at, :] = by_rate[g] * (1.0 / LOG2E) + by_b[g] * vals[g]
            dval_ref[at, g * width : (g + 1) * width] = by_b[g] * deltas[g] + dys[g] * skip
        return tuple(out)

    held = lax.fori_loop(0, span, sweep, tuple(s_state[j] for j in range(len(pairs))), unroll=UNROLL_SECOND)
    for j in range(len(pairs)):
        s_state[j] = held[j]
    rows = block_rows(place, size)
    pre = dot(proj_ref[rows, :rank], dtw_ref[...], (1, 0)) + dtb_ref[...]
    d_pre = take(s_dd, rows, groups) * jax.nn.sigmoid(pre)
    d_bias = jnp.sum(d_pre, axis=0, keepdims=True)
    d_dtw = split_dot(d_pre, proj_ref[rows, :rank], (0, 0), swapped=True)
    part = split_dot(d_pre, dtwt_ref[...], (1, 0))
    part_ref[rows, :] = (part + sum_lanes(s_mix, s_pick)).astype(bf16)

    @pl.when(turn == 0)
    def _():
        ddtb_ref[...] = d_bias
        ddtw_ref[...] = d_dtw

    @pl.when(turn > 0)
    def _():
        ddtb_ref[...] += d_bias
        ddtw_ref[...] += d_dtw

    @pl.when(turn == turns - 1)
    def _():
        sums = [jnp.sum(s_drate[j], axis=0, keepdims=True) for j in range(len(pairs))]
        rows = [jnp.concatenate(sums[n * groups : (n + 1) * groups], axis=1) for n in range(states)]
        dalog_ref[...] = jnp.concatenate(rows, axis=0) * s_rate[...] * (1.0 / LOG2E)


def scan_span(steps):
    return math.gcd(steps, 32)


def wide_slots(steps, span, states):
    turns = steps // span
    return turns if turns * 2 * states * span * SEGS * 128 * 4 <= 16 * MIB else 1


def whole(*shape):
    return pl.BlockSpec(shape, lambda *t: (0,) * len(shape))


def like(*shape, dtype=f32):
    return jax.ShapeDtypeStruct(shape, dtype)


def about(micros):
    return pl.CostEstimate(flops=int(micros * 1.1e9), bytes_accessed=1 << 20, transcendentals=0)


SCALARS = pl.BlockSpec(memory_space=pltpu.SMEM)


def run_entry(starts, hidden_all, weight, gain, conv_w, conv_b, x_w, span):
    total, width = hidden_all.shape
    taps, chans = conv_w.shape
    lanes = x_w.shape[1]
    steps = total // SEGS
    segments = pl.BlockSpec((SEGS, span, width), lambda t: (0, t, 0))
    normed, scale, *rest = pl.pallas_call(
        functools.partial(entry_kernel, span, taps, lanes),
        grid=(steps // span,),
        in_specs=[
            SCALARS, segments, whole(width, 2 * chans), whole(1, width), whole(taps, chans), whole(1, chans),
            whole(chans, lanes),
        ],
        out_specs=[segments, pl.BlockSpec((SEGS, span, 1), lambda t: (0, t, 0))]
        + [whole(total, chans)] * 4 + [whole(total, lanes)],
        out_shape=[like(SEGS, steps, width, dtype=bf16), like(SEGS, steps, 1)] + [like(total, chans, dtype=bf16)] * 3
        + [like(total, chans), like(total, lanes, dtype=bf16)],
        scratch_shapes=[
            pltpu.VMEM((total + (taps - 1) * SEGS, chans), f32), pltpu.VMEM((span * SEGS, span * SEGS), bf16),
        ],
        compiler_params=pltpu.CompilerParams(vmem_limit_bytes=ROOM),
        cost_estimate=about(6 * total * chans / 262144),
        name="entry",
    )(starts, hidden_all.reshape(SEGS, steps, width), weight, gain, conv_w, conv_b, x_w)
    return (normed, scale.reshape(total, 1), *rest)


def run_gate(grad_all, out_w, gate, values, y, skip, span):
    total, width = grad_all.shape
    chans = gate.shape[1]
    steps = total // SEGS
    rows = pl.BlockSpec((span * SEGS, chans), lambda t: (t, 0))
    part = pl.BlockSpec((SEGS, span, chans), lambda t: (0, t, 0))
    full = pl.BlockSpec((SEGS, span, width), lambda t: (0, t, 0))
    natural = like(SEGS, steps, chans, dtype=bf16)
    branch, gated, dy, d_gate, d_skip = pl.pallas_call(
        functools.partial(gate_kernel, span),
        grid=(steps // span,),
        in_specs=[full, whole(chans, width), rows, rows, rows, whole(1, chans)],
        out_specs=[full, part, rows, part, whole(1, chans)],
        out_shape=[like(SEGS, steps, width, dtype=bf16), natural, like(total, chans), natural, like(1, chans)],
        scratch_shapes=[pltpu.VMEM((span * SEGS, span * SEGS), bf16)] * 2,
        compiler_params=pltpu.CompilerParams(vmem_limit_bytes=ROOM),
        cost_estimate=about(6 * total * chans / 262144),
        name="gate",
    )(grad_all.reshape(SEGS, steps, width), out_w, gate, values, y, skip)
    return branch.reshape(total, width), gated.reshape(total, chans), dy, d_gate.reshape(total, chans), d_skip


def run_exit(
    starts, d_proj, value_part, pre, x_in, values, conv_w, x_w, d_gate, weight, hidden_all, scale, gain,
    d_dtw, d_alog_t, d_dtb, d_skip, low_cols, small_rows, span,
):
    total, chans = x_in.shape
    taps = conv_w.shape[0]
    lanes = x_w.shape[1]
    width = hidden_all.shape[1]
    steps = total // SEGS
    size = math.gcd(total, 256)

    def rows(lanes):
        return pl.BlockSpec((size, lanes), lambda t: (jnp.maximum(t - 1, 0), 0))

    return pl.pallas_call(
        functools.partial(exit_kernel, span, taps, low_cols),
        grid=(1 + total // size,),
        in_specs=[SCALARS, whole(total, lanes)] + [whole(total, chans)] * 4 + [
            whole(taps, chans), whole(chans, lanes), rows(chans), whole(width, 2 * chans), rows(width), rows(1),
            whole(1, width), whole(*d_dtw.shape), whole(*d_alog_t.shape), whole(1, chans), whole(1, chans),
        ],
        out_specs=[rows(width), whole(width, chans), whole(small_rows, chans), whole(1, width)],
        out_shape=[
            like(total, width, dtype=bf16), like(width, chans, dtype=bf16), like(small_rows, chans, dtype=bf16),
            like(1, width),
        ],
        scratch_shapes=[
            pltpu.VMEM((total + (taps - 1) * SEGS, chans), f32), pltpu.VMEM((SEGS, steps, chans), bf16),
            pltpu.VMEM((chans, width), f32),
        ],
        compiler_params=pltpu.CompilerParams(vmem_limit_bytes=ROOM),
        cost_estimate=about(10 * total * chans / 262144),
        name="exit",
    )(
        starts, d_proj, value_part, pre, x_in, values, conv_w, x_w, d_gate, weight, hidden_all, scale, gain,
        d_dtw, d_alog_t, d_dtb, d_skip,
    )


def run_forward(proj, values, cut, dt_weight, dt_bias, a_log_t, states, span):
    total, chans = values.shape
    rank = dt_weight.shape[0]
    steps = total // SEGS
    groups, width = lane_groups(chans)
    count = states * groups
    lanes = proj.shape[1]
    slots = wide_slots(steps, span, states)
    by_group = pltpu.VMEM((groups, total, width), f32)
    return pl.pallas_call(
        functools.partial(forward_kernel, rank, states, span),
        grid=(steps // span,),
        in_specs=[
            whole(total, lanes), whole(total, chans), whole(total, 1), whole(rank, chans), whole(1, chans),
            whole(states, chans),
        ],
        out_specs=[
            whole(total, chans), pl.BlockSpec((1, span + 1, count, SEGS, width), lambda t: (t, 0, 0, 0, 0)),
            whole(groups, total, width),
        ],
        out_shape=[
            like(total, chans), like(steps // span, span + 1, count, SEGS, width), like(groups, total, width),
        ],
        scratch_shapes=[
            by_group, by_group, pltpu.VMEM((states, chans), f32), pltpu.VMEM((count, SEGS, width), f32),
            pltpu.VMEM((slots, 2 * states, span * SEGS, 128), f32), pltpu.VMEM((lanes, 2 * states * 128), bf16),
        ],
        compiler_params=pltpu.CompilerParams(vmem_limit_bytes=ROOM),
        cost_estimate=about(18 * total * chans / 262144),
        name="scan_forward",
    )(proj, values, cut, dt_weight, dt_bias, a_log_t)


def run_backward(proj, values, cut, dy, delta, dt_weight, dt_weight_t, dt_bias, a_log_t, skip, hist, states, span):
    total, chans = values.shape
    rank = dt_weight.shape[0]
    steps = total // SEGS
    groups, width = lane_groups(chans)
    count = states * groups
    lanes = proj.shape[1]
    turns = steps // span
    slots = wide_slots(steps, span, states)
    by_group = pltpu.VMEM((groups, total, width), f32)
    return pl.pallas_call(
        functools.partial(backward_kernel, rank, states, span),
        grid=(turns,),
        in_specs=[
            whole(total, lanes), whole(total, chans), whole(total, 1), whole(total, chans), whole(groups, total, width),
            whole(rank, chans), whole(chans, lanes), whole(1, chans), whole(states, chans), whole(1, chans),
            pl.BlockSpec((1, span + 1, count, SEGS, width), lambda t: (turns - 1 - t, 0, 0, 0, 0)),
        ],
        out_specs=[
            whole(total, lanes), whole(total, chans), whole(rank, chans), whole(1, chans), whole(states, chans),
        ],
        out_shape=[
            like(total, lanes, dtype=bf16), like(total, chans), like(rank, chans), like(1, chans), like(states, chans),
        ],
        scratch_shapes=[
            by_group, by_group, by_group, by_group, pltpu.VMEM((states, chans), f32),
            pltpu.VMEM((count, SEGS, width), f32), pltpu.VMEM((count, SEGS, width), f32),
            pltpu.VMEM((slots, 2 * states, span * SEGS, 128), f32), pltpu.VMEM((span * SEGS, 2 * states * 128), f32),
            pltpu.VMEM((lanes, 2 * states * 128), bf16), pltpu.VMEM((2 * states * 128, lanes), bf16),
        ],
        compiler_params=pltpu.CompilerParams(vmem_limit_bytes=ROOM),
        cost_estimate=about(22 * total * chans / 262144),
        name="scan_backward",
    )(proj, values, cut, dy, delta, dt_weight, dt_weight_t, dt_bias, a_log_t, skip, hist)


def tree_sum(parts):
    parts = [p.astype(f32) for p in parts]
    while len(parts) > 1:
        parts = [parts[i] + parts[i + 1] for i in range(0, len(parts), 2)]
    return parts[0]


def swap(value, axis, mask):
    return lax.ppermute(value, axis, [(i, i ^ mask) for i in range(lax.axis_size(axis))])


def pick(blocks, index, dim=0):
    return lax.dynamic_index_in_dim(blocks, index, dim, keepdims=False)


def collected(pieces, me):
    out = jnp.zeros((len(pieces),) + pieces[0].shape, pieces[0].dtype)
    for d, piece in enumerate(pieces):
        out = lax.dynamic_update_index_in_dim(out, piece, me ^ d, 0)
    return out


def owned_parts(blocks, axis):
    me = lax.axis_index(axis)
    size = lax.axis_size(axis)
    return [pick(blocks, me)] + [swap(pick(blocks, me ^ d), axis, d) for d in range(1, size)]


def collect(value, axis):
    me = lax.axis_index(axis)
    return collected([value] + [swap(value, axis, d) for d in range(1, lax.axis_size(axis))], me)


def sum_over_peers(part):
    peers = lax.axis_size("ch")
    rows, lanes = part.shape
    if peers != 8:
        got = lax.all_to_all(part.reshape(peers, rows // peers, lanes), "ch", split_axis=0, concat_axis=0, tiled=True)
        return lax.all_gather(got.astype(f32).sum(axis=0).astype(bf16), "ch", axis=0, tiled=True)
    core, chip = lax.axis_index("ch") % 2, lax.axis_index("ch") // 2
    chips = peers // 2
    halves = part.reshape(2, chips, rows // peers, lanes)
    got = swap(pick(halves, 1 - core), "ch", 1)
    half = tree_sum([pick(halves, core), got]).astype(bf16)
    pieces = [pick(half, chip)] + [swap(pick(half, chip ^ d), "ch", 2 * d) for d in range(1, chips)]
    own = tree_sum(pieces).astype(bf16)
    half = collected([own] + [swap(own, "ch", 2 * d) for d in range(1, chips)], chip)
    return collected([half, swap(half, "ch", 1)], core).reshape(rows, lanes)


def to_peers(blocks):
    return lax.all_to_all(blocks, "ch", split_axis=0, concat_axis=0, tiled=True)


def finish_kernel(
    parts, me_ref, *refs,
):
    n = parts
    late, outs, (cross_ref, branch_ref, dn_ref, hid_ref, grad_ref, gain_ref) = refs[:n], refs[n : 2 * n], refs[2 * n : 2 * n + 6]
    (out_ref, dh_ref, dgain_ref, din_ref, dcw_ref, dcb_ref, dxw_ref, ddtw_ref, ddtb_ref, dalog_ref, dskip_ref,
     dout_ref, s_small) = refs[2 * n + 6 :]
    chans = dcb_ref.shape[1]
    inner = din_ref.shape[1] // 2
    share = din_ref.shape[0] // n
    peers = inner // chans
    low_cols, rank, states, taps = dxw_ref.shape[0], ddtw_ref.shape[0], dalog_ref.shape[0], dcw_ref.shape[0]
    for d in range(n):
        who = jnp.bitwise_xor(me_ref[0], d)
        rows = block_rows(who, share)
        for p in range(peers):
            block = late[d][p * 2 * share : (p + 1) * 2 * share, :].astype(f32)
            din_ref[rows, p * chans : (p + 1) * chans] = block[:share]
            din_ref[rows, inner + p * chans : inner + (p + 1) * chans] = block[share:]
        small = late[d][2 * share * peers :, :].astype(f32)
        s_small[block_rows(who, small.shape[0]), :] = small
        dout_ref[block_rows(who, outs[d].shape[0]), :] = outs[d][...].astype(f32)
    gain = jnp.sum(cross_ref[:, 2 * share :, :].astype(f32), axis=0)
    dgain_ref[...] = gain[:1, : dgain_ref.shape[1]]
    at = low_cols + rank
    ddtw_ref[...] = s_small[low_cols:at, :]
    dxw_ref[...] = s_small[:low_cols, :]
    tail = s_small[at:, :]
    dalog_ref[...] = tail[:states]
    dcw_ref[...] = tail[states : states + taps]
    at = states + taps
    dcb_ref[...] = tail[at : at + 1]
    ddtb_ref[...] = tail[at + 1 : at + 2]
    dskip_ref[...] = tail[at + 2 : at + 3]
    hidden = hid_ref[...].astype(f32)
    out_ref[...] = (hidden + branch_ref[...].astype(f32)).astype(bf16)
    scale = lax.rsqrt(jnp.mean(hidden * hidden, axis=1, keepdims=True) + eps)
    unit = hidden * scale
    d_unit = dn_ref[...].astype(f32) * gain_ref[...]
    mean = jnp.mean(d_unit * unit, axis=1, keepdims=True)
    dh_ref[...] = (grad_ref[...].astype(f32) + scale * (d_unit - unit * mean)).astype(bf16)


def run_finish(late, outs, cross, branch, d_normed, hidden, grad, gain, sizes, me):
    rows, width = hidden.shape
    low_cols, rank, states, taps, small_rows = sizes
    packs = len(late)
    chans = late[0].shape[1]
    in_rows = width // cross.shape[0]
    inner = chans * cross.shape[0]
    wide = [*late, *outs, cross, branch, d_normed, hidden, grad, gain]
    shapes = [
        like(rows, width, dtype=bf16), like(rows, width, dtype=bf16), like(1, in_rows), like(in_rows, 2 * inner),
        like(taps, chans), like(1, chans), like(low_cols, chans), like(rank, chans), like(1, chans),
        like(states, chans), like(1, chans), like(chans, width),
    ]
    return pl.pallas_call(
        functools.partial(finish_kernel, packs),
        grid=(1,),
        in_specs=[SCALARS] + [whole(*a.shape) for a in wide],
        out_specs=[whole(*a.shape) for a in shapes],
        out_shape=shapes,
        scratch_shapes=[pltpu.VMEM((small_rows, chans), f32)],
        compiler_params=pltpu.CompilerParams(vmem_limit_bytes=ROOM),
        cost_estimate=about(4),
        name="finish",
    )(me[None], *wide)


def finish_plain(late, outs, cross, branch, d_normed, hidden, grad, gain, sizes, me):
    low_cols, rank, states, taps, small_rows = sizes
    packs, peers, chans = len(late), cross.shape[0], late[0].shape[1]
    share = hidden.shape[1] // (peers * packs)
    late = collected(late, me).astype(f32)
    halves = late[:, : 2 * share * peers].reshape(packs, peers, 2, share, chans)
    d_in = jnp.transpose(halves, (0, 3, 2, 1, 4)).reshape(packs * share, 2 * peers * chans)
    small = late[:, 2 * share * peers :].reshape(small_rows, chans)
    parts = []
    at = 0
    for count in (low_cols, rank, states, taps, 1, 1, 1):
        parts.append(small[at : at + count])
        at += count
    d_xw, d_dtw, d_alog, d_cw, d_cb, d_dtb, d_skip = parts
    d_gain = cross[:, 2 * share :].astype(f32).sum(axis=0).reshape(1, -1)[:, : share * packs]
    hidden = hidden.astype(f32)
    output = (hidden + branch.astype(f32)).astype(bf16)
    scale = lax.rsqrt(jnp.mean(hidden * hidden, axis=1, keepdims=True) + eps)
    unit = hidden * scale
    d_unit = d_normed.astype(f32) * gain
    mean = jnp.mean(d_unit * unit, axis=1, keepdims=True)
    d_hidden = (grad.astype(f32) + scale * (d_unit - unit * mean)).astype(bf16)
    d_out = collected(outs, me).astype(f32).reshape(chans, -1)
    return output, d_hidden, d_gain, d_in, d_cw, d_cb, d_xw, d_dtw, d_dtb, d_alog, d_skip, d_out


def on_device(
    hidden_in, norm_gain, in_weight, conv_weight, conv_bias, x_weight, dt_weight, dt_bias, a_log, skip, out_weight,
    lengths, resets, out_grad,
):
    peers = lax.axis_size("ch")
    packs = lax.axis_size("ctx")
    me = lax.axis_index("ch")
    rows, width = hidden_in.shape
    chans = out_weight.shape[0]
    taps = conv_weight.shape[1]
    rank, states = dt_weight.shape[0], a_log.shape[1]
    total = rows * peers

    hidden_all = lax.all_gather(hidden_in, "ch", axis=0, tiled=True)
    in_rows = in_weight.shape[0]
    share = in_rows // packs
    my_share = lax.dynamic_slice_in_dim(in_weight, lax.axis_index("ctx") * share, share, 0)
    got = to_peers(jnp.moveaxis(my_share.reshape(share, 2, peers, chans), 2, 0))
    shares = collect(got.reshape(peers, share, 2 * chans), "ctx")
    my_cols = jnp.moveaxis(shares, 0, 1).reshape(width, 2 * chans)
    grad_all = lax.all_gather(out_grad, "ch", axis=0, tiled=True)

    steps = total // SEGS
    span = scan_span(steps)
    low_cols = rank + 2 * states
    lanes = -(-low_cols // 128) * 128
    sizes = lengths[0]
    offsets = jnp.cumsum(sizes) - sizes
    where_in = context_place(offsets, jnp.arange(total, dtype=jnp.int32))
    cut = ((where_in == 0) | (resets == 1)).astype(f32).reshape(SEGS, steps).T.reshape(total, 1)
    starts = offsets[None, :]
    conv_w = lax.dynamic_slice_in_dim(conv_weight, me * chans, chans, 0).T
    conv_b = lax.dynamic_slice_in_dim(conv_bias, me * chans, chans, 0)[None, :]
    x_w = lax.dynamic_slice_in_dim(x_weight, me * chans, chans, 0)
    x_w = jnp.pad(x_w, ((0, 0), (0, lanes - low_cols)))

    normed, scale_all, x_in, gate, values, pre, proj_part = run_entry(
        starts, hidden_all, my_cols, norm_gain[None, :], conv_w, conv_b, x_w, span
    )
    proj = sum_over_peers(proj_part)

    a_log_t = a_log.T
    dt_b, skip_row = dt_bias[None, :], skip[None, :]
    y, hist, delta = run_forward(proj, values, cut, dt_weight, dt_b, a_log_t, states, span)
    branch_part, gated, dy, d_gate, d_skip = run_gate(grad_all, out_weight, gate, values, y, skip_row, span)
    branch = lax.psum_scatter(branch_part, "ch", scatter_dimension=0, tiled=True)
    sides = width // chans
    out_share = chans // packs
    d_out = dot(gated, grad_all, (0, 0)).astype(bf16).reshape(packs, out_share, sides, chans)
    d_out = jnp.moveaxis(d_out, 2, 1).reshape(packs, out_share * sides, chans)
    d_in_gate = dot(normed.reshape(total, width), d_gate, (0, 0)).astype(bf16)

    def by_pack(d_in):
        return jnp.moveaxis(d_in.reshape(peers, packs, share, chans), 1, 0).reshape(packs, peers * share, chans)

    early = owned_parts(jnp.concatenate([d_out, by_pack(d_in_gate)], axis=1), "ctx")

    dt_w_t = jnp.pad(dt_weight.T, ((0, 0), (0, lanes - rank)))
    d_part, value_part, d_dt_weight, d_dt_bias, d_a_log_t = run_backward(
        proj, values, cut, dy, delta, dt_weight, dt_w_t, dt_b, a_log_t, skip_row, hist, states, span
    )
    early, d_part = lax.optimization_barrier((early, d_part))
    d_proj = sum_over_peers(d_part)
    early = tree_sum(early).astype(bf16)
    branch, early, d_proj = lax.optimization_barrier((branch, early, d_proj))
    d_out = jnp.moveaxis(early[: out_share * sides].reshape(sides, out_share, chans), 0, 1).reshape(out_share, width)
    counts = (low_cols, rank, states, taps)
    small_rows = -(-(sum(counts) + 3) // (16 * packs)) * 16 * packs
    d_normed_part, d_in_x, small, d_gain = run_exit(
        starts, d_proj, value_part, pre, x_in, values, conv_w, x_w, d_gate, my_cols, hidden_all, scale_all,
        norm_gain[None, :], d_dt_weight, d_a_log_t, d_dt_bias, d_skip, low_cols, small_rows, span,
    )
    d_normed = lax.psum_scatter(d_normed_part, "ch", scatter_dimension=0, tiled=True)

    gain_rows = d_gain.astype(bf16).reshape(sides, chans)
    gain_rows = jnp.pad(gain_rows, ((0, -sides % 16), (0, 0)))
    late = [by_pack(d_in_x), small.reshape(packs, small_rows // packs, chans)]
    late.append(jnp.broadcast_to(gain_rows, (packs,) + gain_rows.shape))
    late = tree_sum(owned_parts(jnp.concatenate(late, axis=1), "ctx")).astype(bf16)
    own_rows = peers * share
    gain_rows = late[own_rows + small_rows // packs :][:sides].reshape(peers, in_rows)
    pad_rows = -(-in_rows // chans)
    gain_rows = jnp.pad(gain_rows, ((0, 0), (0, pad_rows * chans - in_rows))).reshape(peers, pad_rows, chans)
    gain_rows = jnp.pad(gain_rows, ((0, 0), (0, -pad_rows % 16), (0, 0)))
    cross = [late[:own_rows].reshape(peers, share, chans), early[out_share * sides :].reshape(peers, share, chans)]
    cross, d_out = lax.optimization_barrier((jnp.concatenate([*cross, gain_rows], axis=1), d_out))
    cross = to_peers(cross)
    outs = [d_out] + [swap(d_out, "ctx", d) for d in range(1, packs)]
    outs, cross = lax.optimization_barrier((outs, cross))
    own = [cross[:, : 2 * share].reshape(2 * own_rows, chans), late[own_rows : own_rows + small_rows // packs]]
    own = jnp.concatenate(own, axis=0)
    late = [own] + [swap(own, "ctx", d) for d in range(1, packs)]
    finish = run_finish if share % 16 == 0 and chans % 128 == 0 else finish_plain
    (
        output, d_hidden, gain_sum, in_sum, conv_w_sum, conv_b_sum, x_w_sum, dt_w_sum, dt_b_sum, a_log_sum, skip_sum,
        out_sum,
    ) = finish(
        late, outs, cross, branch, d_normed, hidden_in, out_grad, norm_gain[None, :], (*counts, small_rows),
        lax.axis_index("ctx"),
    )
    return (
        output, d_hidden, gain_sum[0], in_sum, conv_w_sum.T, conv_b_sum[0], x_w_sum.T, dt_w_sum, dt_b_sum[0],
        a_log_sum.T, skip_sum[0], out_sum,
    )


def solution(mesh):
    return jax.shard_map(
        on_device,
        mesh=mesh,
        in_specs=(
            P(("ctx", "ch"), None), P(), P("ch", None), P(), P(), P(), P(None, "ch"), P("ch"), P("ch", None),
            P("ch"), P("ch", None), P("ctx", None), P("ctx"), P(("ctx", "ch"), None),
        ),
        out_specs=(
            P(("ctx", "ch"), None), P(("ctx", "ch"), None), P("ch"), P("ch", None), P("ch", None), P("ch"),
            P("ch", None), P(None, "ch"), P("ch"), P("ch", None), P("ch"), P("ch", None),
        ),
        check_vma=False,
    )
```

time: 459 us -> 233 us (0.51)
  Pallas kernels: 173 us -> 73.7 us
  blocking collectives: 83.1 us -> 0 us
  waiting for transfers between devices: 115 us -> 74.7 us
  starting transfers between devices: 20.1 us -> 47.4 us
  matrix products: 18.5 us -> 2.68 us
  other arithmetic: 16.9 us -> 3.9 us
    pallas_call x1, Pallas kernels: 83 us -> 16.6 us  [run_forward(): pl.pallas_call(functools.partial(forward_kernel, rank, states, span), gri...]
    pallas_call x1, Pallas kernels: 90.1 us -> 25.9 us  [run_backward(): pl.pallas_call(functools.partial(backward_kernel, rank, states, span), gr...]
    ppermute x0 -> x31, waiting for transfers between devices: none -> 57.3 us  [swap(): lax.ppermute(value, axis, [(i, i ^ mask) for i in range(lax.axis_size(axi...]
    all_gather x4 -> x0, blocking collectives: 52.7 us -> none  [the longest x1 15.2 us: on_device(): lax.all_gather(flat, 'ctx', axis=0, tiled=False).astype(f32).sum(axis=0)]
    all_to_all x5 -> x2, waiting for transfers between devices: 54.3 us -> 15.9 us  [to_peers(): return lax.all_to_all(blocks, 'ch', split_axis=0, concat_axis=0, tiled=True)]
    ppermute x0 -> x31, starting transfers between devices: none -> 37.3 us  [swap(): lax.ppermute(value, axis, [(i, i ^ mask) for i in range(lax.axis_size(axi...]
    reduce_scatter x1, waiting for transfers between devices: 35.4 us -> 0.02 us  [on_device(): lax.psum_scatter(branch_part, 'ch', scatter_dimension=0, tiled=True)]
    pallas_call x0 -> x4, Pallas kernels: none -> 31.3 us  [the longest x1 11.2 us: run_exit(): pl.pallas_call(functools.partial(exit_kernel, span, taps, low_cols), grid...]
  transfers between devices with their start and end apart: 10 -> 37, of which waited for: 6 -> 25; matrix products, arithmetic and copies ran while one was open for 8% -> 6% of each run, Pallas kernels for 0% -> 22%
where the time goes in v2:
time: 233 us; the launch traced here: 232 us
  waiting for transfers between devices  74.7 us (32%)
  Pallas kernels  73.7 us (32%)
  starting transfers between devices  47.4 us (20%)
  local copies, waits for them, and re-layouts  15.6 us (7%)
  between operations  14.4 us (6%)
  other arithmetic  3.9 us (2%)
  matrix products  2.68 us (1%)
    ppermute x31, waiting for transfers between devices, swap(): lax.ppermute(value, axis, [(i, i ^ mask) for i in range(lax.axis_size(axi...  57.3 us
    ppermute x31, starting transfers between devices, swap(): lax.ppermute(value, axis, [(i, i ^ mask) for i in range(lax.axis_size(axi...  37.3 us
    pallas_call x1, Pallas kernels, run_backward(): pl.pallas_call(functools.partial(backward_kernel, rank, states, span), gr...  25.9 us
    pallas_call x1, Pallas kernels, run_forward(): pl.pallas_call(functools.partial(forward_kernel, rank, states, span), gri...  16.6 us
    all_to_all x2, waiting for transfers between devices, to_peers(): return lax.all_to_all(blocks, 'ch', split_axis=0, concat_axis=0, tiled=True)  15.9 us
    pallas_call x1, Pallas kernels, run_exit(): pl.pallas_call(functools.partial(exit_kernel, span, taps, low_cols), grid...  11.2 us
    all_to_all x2, starting transfers between devices, to_peers(): return lax.all_to_all(blocks, 'ch', split_axis=0, concat_axis=0, tiled=True)  9.76 us
    pallas_call x1, Pallas kernels, run_entry(): pl.pallas_call(functools.partial(entry_kernel, span, taps, lanes), grid=(...  8.4 us
  transfers between devices with their start and end apart: 37, of which 25 were waited for; matrix products, arithmetic and copies ran while one was open for 6% of the time, Pallas kernels for 22%

profile of v2, /device:TPU:0, one launch (start us, length us, event | category | flops | bytes accessed | tf_op | source)
XLA Modules:
  0.0 232.5 jit_solution(3872444952393526916)
XLA Ops:
  9.4 6.3 %all-to-all-start = ((bf16[8,32,2,256]{3,2,1,0:T(2,128)(2,1)}), bf16[8,32,2,256]{3,2,1,0:T(2,128)(2,1)S(1)}, u32[]{:S(2)}, u32[]{:S(2)}) async-start(bf16[8,32,2,256]{3,2,1,0:T(2,128)(2,1)} %copy.79), calls=%async_computation | async-start | bytes 524288 | tf_op jit(solution)/shard_map/all_to_all | solution.py:732
  18.0 9.6 %all-to-all-done = bf16[8,32,2,256]{3,2,1,0:T(2,128)(2,1)S(1)} async-done(((bf16[8,32,2,256]{3,2,1,0:T(2,128)(2,1)}), bf16[8,32,2,256]{3,2,1,0:T(2,128)(2,1)S(1)}, u32[]{:S(2)}, u32[]{:S(2)}) %all-to-all-start) | async-done | bytes 262176 | tf_op jit(solution)/shard_map/all_to_all | solution.py:732
  28.5 1.5 collective-permute-start
  30.0 1.3 fusion.19.cw_ref
  31.4 1.3 dynamic_slice.78
  33.4 1.5 collective-permute-start.1
  35.7 9.4 %collective-permute-done.1 = bf16[8,32,512]{2,1,0:T(8,128)(2,1)S(1)} collective-permute-done((bf16[8,32,512]{2,1,0:T(8,128)(2,1)}, bf16[8,32,512]{2,1,0:T(8,128)(2,1)S(1)}, u32[]{:S(2)}, u32[]{:S(2)}) %collective-permute-start.1) | collective-permute-done | bytes 262176 | tf_op jit(solution)/shard_map/ppermute | solution.py:689
  46.2 8.4 %entry.1 = (bf16[8,128,1024]{2,1,0:T(8,128)(2,1)}, f32[8,128,1]{2,1,0:T(8,128)}, bf16[1024,256]{1,0:T(8,128)(2,1)}, bf16[1024,256]{1,0:T(8,128)(2,1)}, bf16[1024...) custom-call(s32[1,4]{1,0:T(1,128)} %bitcast_subtract_fusion.1.starts_ref, ...), custom_call_target="tpu_custom_call" | custom-call | flops 6600000000 | bytes 1048576 | tf_op jit(solution)/shard_map/entry/pallas_call | solution.py:530
  55.6 1.3 collective-permute-done.3
  57.9 1.3 collective-permute-start.4
  59.2 4.6 %collective-permute-start.5 = (bf16[128,128]{1,0:T(8,128)(2,1)S(1)}, bf16[128,128]{1,0:T(8,128)(2,1)S(1)}, u32[]{:S(2)}, u32[]{:S(2)}) collective-permute-start(bf16[128,128]{1,0:T(8,128)(2,1)S(1)} %get-tuple-element.132), channel_id=1, source_target_pairs={{0,4},{1,5},{2,6},{3,7},{4,0},{5,1},{6,2},{7,3},{8,12},{9,13},{10,... | collective-permute-start | bytes 98312 | tf_op jit(solution)/shard_map/ppermute | solution.py:689
  63.9 5.1 %collective-permute-done.5 = bf16[128,128]{1,0:T(8,128)(2,1)S(1)} collective-permute-done((bf16[128,128]{1,0:T(8,128)(2,1)S(1)}, bf16[128,128]{1,0:T(8,128)(2,1)S(1)}, u32[]{:S(2)}, u32[]{:S(2)}) %collective-permute-start.5) | collective-permute-done | bytes 32800 | tf_op jit(solution)/shard_map/ppermute | solution.py:689
  70.2 2.2 collective-permute-start.7
  75.2 1.5 collective-permute-start.9
  76.7 2.6 %collective-permute-done.8 = bf16[128,128]{1,0:T(8,128)(2,1)S(1)} collective-permute-done((bf16[128,128]{1,0:T(8,128)(2,1)S(1)}, bf16[128,128]{1,0:T(8,128)(2,1)S(1)}, u32[]{:S(2)}, u32[]{:S(2)}) %collective-permute-start.8) | collective-permute-done | bytes 32800 | tf_op jit(solution)/shard_map/ppermute | solution.py:689
  79.3 1.6 collective-permute-done.9
  81.0 1.3 collective-permute-done.10
  83.0 16.6 %scan_forward.1 = (f32[1024,256]{1,0:T(8,128)}, f32[4,33,32,8,128]{4,3,2,1,0:T(8,128)}, f32[2,1024,128]{2,1,0:T(8,128)}) custom-call(bf16[1024,128]{1,0:T(8,128)(2,1)} %bitcast.181, bf16[1024,256]{1,0:T(8,128)(2,1)} %get-tuple-element.64.val_ref, f32[1024,1]{1,0:T(8,128)} %reshape.194.cut_ref, bf16[64,256]{1,0:T(8,128)(2,1)} %dtw_ref.3, f32[1,256]{1,0:T(1,128)} %bitcast.196, ...), custom_call_target="tpu_custom_call" | custom-call | flops 19800000512 | bytes 1048576 | tf_op jit(solution)/shard_map/scan_forward/pallas_call | solution.py:621
  99.5 7.7 %gate.1 = (bf16[8,128,1024]{2,1,0:T(8,128)(2,1)}, bf16[8,128,256]{2,1,0:T(8,128)(2,1)}, f32[1024,256]{1,0:T(8,128)}, bf16[8,128,256]{2,1,0:T(8,128)(2,1)}, f32[1,256]{1,0:T(1,128)}) custom-call(bf16[8,128,1024]{2,1,0:T(8,128)(2,1)} %bitcast.161, bf16[256,1024]{1,0:T(8,128)(2,1)} %w_ref.1, bf16[1024,256]{1,0:T(8,128)(2,1)} %get-tuple-element.63.gate_ref, ...), custom_call_target="tpu_custom_call" | custom-call | flops 6600000000 | bytes 1048576 | tf_op jit(solution)/shard_map/gate/pallas_call | solution.py:559
  107.3 2.0 fusion
  111.4 1.5 collective-permute-start.12
  112.9 1.2 collective-permute-start.13
  114.4 25.9 %scan_backward.1 = (bf16[1024,128]{1,0:T(8,128)(2,1)}, f32[1024,256]{1,0:T(8,128)}, f32[64,256]{1,0:T(8,128)}, f32[1,256]{1,0:T(1,128)}, f32[16,256]{1,0:T(8,128)}) custom-call(bf16[1024,128]{1,0:T(8,128)(2,1)} %bitcast.182, bf16[1024,256]{1,0:T(8,128)(2,1)} %get-tuple-element.64.val_ref, f32[1024,1]{1,0:T(8,128)} %reshape.194.cut_ref, ...), custom_call_target="tpu_custom_call" | custom-call | flops 24199999488 | bytes 1048576 | tf_op jit(solution)/shard_map/scan_backward/pallas_call | solution.py:655
  141.3 1.4 collective-permute-done.14
  143.9 1.9 collective-permute-start.16
  145.8 2.3 collective-permute-start.17
  149.1 2.5 %collective-permute-done.17 = bf16[128,128]{1,0:T(8,128)(2,1)S(1)} collective-permute-done((bf16[128,128]{1,0:T(8,128)(2,1)S(1)}, bf16[128,128]{1,0:T(8,128)(2,1)S(1)}, u32[]{:S(2)}, u32[]{:S(2)}) %collective-permute-start.17) | collective-permute-done | bytes 32800 | tf_op jit(solution)/shard_map/ppermute | solution.py:689
  151.8 2.9 %collective-permute-start.19 = (bf16[128,128]{1,0:T(8,128)(2,1)S(1)}, bf16[128,128]{1,0:T(8,128)(2,1)S(1)}, u32[]{:S(2)}, u32[]{:S(2)}) collective-permute-start(bf16[128,128]{1,0:T(8,128)(2,1)S(1)} %get-tuple-element.115), channel_id=1, source_target_pairs={{0,4},{1,5},{2,6},{3,7},{4,0},{5,1},{6,2},{7,3},{8,12},{9,13},{10,... | collective-permute-start | bytes 98312 | tf_op jit(solution)/shard_map/ppermute | solution.py:689
  154.7 1.5 collective-permute-start.20
  156.7 3.7 %collective-permute-done.20 = bf16[128,128]{1,0:T(8,128)(2,1)S(1)} collective-permute-done((bf16[128,128]{1,0:T(8,128)(2,1)S(1)}, bf16[128,128]{1,0:T(8,128)(2,1)S(1)}, u32[]{:S(2)}, u32[]{:S(2)}) %collective-permute-start.20) | collective-permute-done | bytes 32800 | tf_op jit(solution)/shard_map/ppermute | solution.py:689
  160.5 1.3 collective-permute-done.21
  162.5 11.2 %exit.1 = (bf16[1024,1024]{1,0:T(8,128)(2,1)}, bf16[1024,256]{1,0:T(8,128)(2,1)}, bf16[192,256]{1,0:T(8,128)(2,1)}, f32[1,1024]{1,0:T(1,128)}) custom-call(s32[1,4]{1,0:T(1,128)} %bitcast_subtract_fusion.1.starts_ref, bf16[1024,128]{1,0:T(8,128)(2,1)} %bitcast.180, f32[1024,256]{1,0:T(8,128)} %get-tuple-element.81.part_ref, ...), custom_call_target="tpu_custom_call" | custom-call | flops 11000000512 | bytes 1048576 | tf_op jit(solution)/shard_map/exit/pallas_call | solution.py:587
  175.7 1.5 collective-permute-start.23
  177.2 1.3 collective-permute-start.24
  178.7 3.4 %collective-permute-done.22 = bf16[320,256]{1,0:T(8,128)(2,1)S(1)} collective-permute-done((bf16[320,256]{1,0:T(8,128)(2,1)S(1)}, bf16[320,256]{1,0:T(8,128)(2,1)S(1)}, u32[]{:S(2)}, u32[]{:S(2)}) %collective-permute-start.22) | collective-permute-done | bytes 163872 | tf_op jit(solution)/shard_map/ppermute | solution.py:689
  182.1 2.2 collective-permute-done.23
  184.3 1.5 collective-permute-done.24
  186.7 3.4 %all-to-all-start.1 = ((bf16[8,80,256]{2,1,0:T(8,128)(2,1)}), bf16[8,80,256]{2,1,0:T(8,128)(2,1)S(1)}, u32[]{:S(2)}, u32[]{:S(2)}) async-start(bf16[8,80,256]{2,1,0:T(8,128)(2,1)} %fusion.2), calls=%async_computation.2 | async-start | bytes 655360 | tf_op jit(solution)/shard_map/all_to_all | solution.py:732
  191.0 1.6 collective-permute-start.26
  192.5 1.2 collective-permute-start.27
  193.7 2.8 %collective-permute-done.25.refs_5_ = bf16[64,1024]{1,0:T(8,128)(2,1)S(1)} collective-permute-done((bf16[64,1024]{1,0:T(8,128)(2,1)S(1)}, bf16[64,1024]{1,0:T(8,128)(2,1)S(1)}, u32[]{:S(2)}, u32[]{:S(2)}) %collective-permute-start.25) | collective-permute-done | bytes 131104 | tf_op jit(solution)/shard_map/ppermute | solution.py:689
  196.5 1.8 collective-permute-done.26.refs_6_
  199.2 6.3 %all-to-all-done.1.refs_8_ = bf16[8,80,256]{2,1,0:T(8,128)(2,1)S(1)} async-done(((bf16[8,80,256]{2,1,0:T(8,128)(2,1)}), bf16[8,80,256]{2,1,0:T(8,128)(2,1)S(1)}, u32[]{:S(2)}, u32[]{:S(2)}) %all-to-all-start.1) | async-done | bytes 327712 | tf_op jit(solution)/shard_map/all_to_all | solution.py:732
  205.6 1.2 collective-permute-start.28
  206.8 1.5 collective-permute-start.29
  209.2 6.2 %collective-permute-done.28.refs_1_ = bf16[560,256]{1,0:T(8,128)(2,1)S(1)} collective-permute-done((bf16[560,256]{1,0:T(8,128)(2,1)S(1)}, bf16[560,256]{1,0:T(8,128)(2,1)S(1)}, u32[]{:S(2)}, u32[]{:S(2)}) %collective-permute-start.28) | collective-permute-done | bytes 286752 | tf_op jit(solution)/shard_map/ppermute | solution.py:689
  215.4 4.7 %collective-permute-done.29.refs_2_ = bf16[560,256]{1,0:T(8,128)(2,1)S(1)} collective-permute-done((bf16[560,256]{1,0:T(8,128)(2,1)S(1)}, bf16[560,256]{1,0:T(8,128)(2,1)S(1)}, u32[]{:S(2)}, u32[]{:S(2)}) %collective-permute-start.29) | collective-permute-done | bytes 286752 | tf_op jit(solution)/shard_map/ppermute | solution.py:689
  222.0 4.0 %finish.1 = (bf16[128,1024]{1,0:T(8,128)(2,1)}, bf16[128,1024]{1,0:T(8,128)(2,1)}, f32[1,128]{1,0:T(1,128)}, f32[128,4096]{1,0:T(8,128)}, f32[4,256]{1,0:T(4,128...) custom-call(s32[1]{0:T(128)} %bitcast.me_ref, ...), custom_call_target="tpu_custom_call" | custom-call | flops 4400000000 | bytes 1048576 | tf_op jit(solution)/shard_map/finish/pallas_call | solution.py:791
  (153 shorter events, 29.0 us)
Async XLA Ops:
  7.2 9.3 %copy-start.20 = (s32[1,4]{1,0:T(1,128)S(1)}, s32[1,4]{1,0:T(1,128)}, u32[]{:S(2)}) copy-start(s32[1,4]{1,0:T(1,128)} %param.25) | copy-start | bytes 52
  7.2 38.0 %all-gather.5.cloned.1.call-start = ((), (), s32[]{:S(2)}) async-start(), calls=%async_computation.5 | async-start | bytes 2359296 | tf_op jit(solution)/shard_map/all_gather | solution.py:843
  9.4 18.2 %all-to-all-start = ((bf16[8,32,2,256]{3,2,1,0:T(2,128)(2,1)}), bf16[8,32,2,256]{3,2,1,0:T(2,128)(2,1)S(1)}, u32[]{:S(2)}, u32[]{:S(2)}) async-start(bf16[8,32,2,256]{3,2,1,0:T(2,128)(2,1)} %copy.79), calls=%async_computation | async-start | bytes 524288 | tf_op jit(solution)/shard_map/all_to_all | solution.py:732
  15.7 83.8 %all-gather.3.cloned.1.call-start = ((), (), s32[]{:S(2)}) async-start(), calls=%async_computation.4 | async-start | bytes 2359296 | tf_op jit(solution)/shard_map/all_gather | solution.py:850
  16.5 145.4 %reduce-scatter.3.cloned.1.call-start = ((), (), s32[]{:S(2)}) async-start(), calls=%async_computation.6 | async-start | bytes 2359296 | tf_op jit(solution)/shard_map/reduce_scatter | solution.py:875
  28.5 7.2 %collective-permute-start = (bf16[8,32,512]{2,1,0:T(8,128)(2,1)}, bf16[8,32,512]{2,1,0:T(8,128)(2,1)S(1)}, u32[]{:S(2)}, u32[]{:S(2)}) collective-permute-start(bf16[8,32,512]{2,1,0:T(8,128)(2,1)} %reshape.153), channel_id=1, source_target_pairs={{0,8},{8,0},{16,24},{24,16},{1,9},{9,1},{17,25},{25,17},{2,10},{10... | collective-permute-start | bytes 786440 | tf_op jit(solution)/shard_map/ppermute | solution.py:689
  33.4 11.8 %collective-permute-start.1 = (bf16[8,32,512]{2,1,0:T(8,128)(2,1)}, bf16[8,32,512]{2,1,0:T(8,128)(2,1)S(1)}, u32[]{:S(2)}, u32[]{:S(2)}) collective-permute-start(bf16[8,32,512]{2,1,0:T(8,128)(2,1)} %reshape.153), channel_id=1, source_target_pairs={{0,16},{8,24},{16,0},{24,8},{1,17},{9,25},{17,1},{25,9},{2,18},{10... | collective-permute-start | bytes 786440 | tf_op jit(solution)/shard_map/ppermute | solution.py:689
  34.9 10.3 %collective-permute-start.2 = (bf16[8,32,512]{2,1,0:T(8,128)(2,1)}, bf16[8,32,512]{2,1,0:T(8,128)(2,1)S(1)}, u32[]{:S(2)}, u32[]{:S(2)}) collective-permute-start(bf16[8,32,512]{2,1,0:T(8,128)(2,1)} %reshape.153), channel_id=1, source_target_pairs={{0,24},{8,16},{16,8},{24,0},{1,25},{9,17},{17,9},{25,1},{2,26},{10... | collective-permute-start | bytes 786440 | tf_op jit(solution)/shard_map/ppermute | solution.py:689
  46.2 26.3 %copy-start.12 = (s32[1024]{0:T(1024)S(1)}, s32[1024]{0:T(1024)}, u32[]{:S(2)}) copy-start(s32[1024]{0:T(1024)} %param.26) | copy-start | bytes 12292
  46.2 27.4 %copy-start.11 = (bf16[64,256]{1,0:T(8,128)(2,1)S(1)}, bf16[64,256]{1,0:T(8,128)(2,1)}, u32[]{:S(2)}) copy-start(bf16[64,256]{1,0:T(8,128)(2,1)} %dtw_ref.3) | copy-start | bytes 98308
  55.5 1.4 collective-permute-start.3
  57.9 6.0 %collective-permute-start.4 = (bf16[128,128]{1,0:T(8,128)(2,1)S(1)}, bf16[128,128]{1,0:T(8,128)(2,1)S(1)}, u32[]{:S(2)}, u32[]{:S(2)}) collective-permute-start(bf16[128,128]{1,0:T(8,128)(2,1)S(1)} %get-tuple-element.130), channel_id=1, source_target_pairs={{0,2},{1,3},{2,0},{3,1},{4,6},{5,7},{6,4},{7,5},{8,10},{9,11},{10,... | collective-permute-start | bytes 98312 | tf_op jit(solution)/shard_map/ppermute | solution.py:689
  59.2 9.8 %collective-permute-start.5 = (bf16[128,128]{1,0:T(8,128)(2,1)S(1)}, bf16[128,128]{1,0:T(8,128)(2,1)S(1)}, u32[]{:S(2)}, u32[]{:S(2)}) collective-permute-start(bf16[128,128]{1,0:T(8,128)(2,1)S(1)} %get-tuple-element.132), channel_id=1, source_target_pairs={{0,4},{1,5},{2,6},{3,7},{4,0},{5,1},{6,2},{7,3},{8,12},{9,13},{10,... | collective-permute-start | bytes 98312 | tf_op jit(solution)/shard_map/ppermute | solution.py:689
  63.8 6.4 %collective-permute-start.6 = (bf16[128,128]{1,0:T(8,128)(2,1)S(1)}, bf16[128,128]{1,0:T(8,128)(2,1)S(1)}, u32[]{:S(2)}, u32[]{:S(2)}) collective-permute-start(bf16[128,128]{1,0:T(8,128)(2,1)S(1)} %get-tuple-element.131), channel_id=1, source_target_pairs={{0,6},{1,7},{2,4},{3,5},{4,2},{5,3},{6,0},{7,1},{8,14},{9,15},{10,... | collective-permute-start | bytes 98312 | tf_op jit(solution)/shard_map/ppermute | solution.py:689
  70.2 6.4 %collective-permute-start.7 = (bf16[128,128]{1,0:T(8,128)(2,1)S(1)}, bf16[128,128]{1,0:T(8,128)(2,1)S(1)}, u32[]{:S(2)}, u32[]{:S(2)}) collective-permute-start(bf16[128,128]{1,0:T(8,128)(2,1)S(1)} %get-tuple-element.117), channel_id=1, source_target_pairs={{0,2},{1,3},{2,0},{3,1},{4,6},{5,7},{6,4},{7,5},{8,10},{9,11},{10,... | collective-permute-start | bytes 98312 | tf_op jit(solution)/shard_map/ppermute | solution.py:689
  74.3 5.0 %collective-permute-start.8 = (bf16[128,128]{1,0:T(8,128)(2,1)S(1)}, bf16[128,128]{1,0:T(8,128)(2,1)S(1)}, u32[]{:S(2)}, u32[]{:S(2)}) collective-permute-start(bf16[128,128]{1,0:T(8,128)(2,1)S(1)} %get-tuple-element.117), channel_id=1, source_target_pairs={{0,4},{1,5},{2,6},{3,7},{4,0},{5,1},{6,2},{7,3},{8,12},{9,13},{10,... | collective-permute-start | bytes 98312 | tf_op jit(solution)/shard_map/ppermute | solution.py:689
  75.2 5.7 %collective-permute-start.9 = (bf16[128,128]{1,0:T(8,128)(2,1)S(1)}, bf16[128,128]{1,0:T(8,128)(2,1)S(1)}, u32[]{:S(2)}, u32[]{:S(2)}) collective-permute-start(bf16[128,128]{1,0:T(8,128)(2,1)S(1)} %get-tuple-element.117), channel_id=1, source_target_pairs={{0,6},{1,7},{2,4},{3,5},{4,2},{5,3},{6,0},{7,1},{8,14},{9,15},{10,... | collective-permute-start | bytes 98312 | tf_op jit(solution)/shard_map/ppermute | solution.py:689
  80.9 1.3 collective-permute-start.10
  99.5 7.7 %copy-start.21 = (bf16[8,128,1024]{2,1,0:T(8,128)(2,1)S(1)}, bf16[8,128,1024]{2,1,0:T(8,128)(2,1)}, u32[]{:S(2)}) copy-start(bf16[8,128,1024]{2,1,0:T(8,128)(2,1)} %get-tuple-element.69) | copy-start | bytes 6291460
  110.6 29.7 %collective-permute-start.11 = (bf16[512,256]{1,0:T(8,128)(2,1)S(1)}, bf16[512,256]{1,0:T(8,128)(2,1)S(1)}, u32[]{:S(2)}, u32[]{:S(2)}) collective-permute-start(bf16[512,256]{1,0:T(8,128)(2,1)S(1)} %get-tuple-element.120), channel_id=1, source_target_pairs={{0,8},{8,0},{16,24},{24,16},{1,9},{9,1},{17,25},{25,17},{2,10},{10... | collective-permute-start | bytes 786440 | tf_op jit(solution)/shard_map/ppermute | solution.py:689
  111.4 28.9 %collective-permute-start.12 = (bf16[512,256]{1,0:T(8,128)(2,1)S(1)}, bf16[512,256]{1,0:T(8,128)(2,1)S(1)}, u32[]{:S(2)}, u32[]{:S(2)}) collective-permute-start(bf16[512,256]{1,0:T(8,128)(2,1)S(1)} %get-tuple-element.121), channel_id=1, source_target_pairs={{0,16},{8,24},{16,0},{24,8},{1,17},{9,25},{17,1},{25,9},{2,18},{10... | collective-permute-start | bytes 786440 | tf_op jit(solution)/shard_map/ppermute | solution.py:689
  112.9 27.4 %collective-permute-start.13 = (bf16[512,256]{1,0:T(8,128)(2,1)S(1)}, bf16[512,256]{1,0:T(8,128)(2,1)S(1)}, u32[]{:S(2)}, u32[]{:S(2)}) collective-permute-start(bf16[512,256]{1,0:T(8,128)(2,1)S(1)} %get-tuple-element.118), channel_id=1, source_target_pairs={{0,24},{8,16},{16,8},{24,0},{1,25},{9,17},{17,9},{25,1},{2,26},{10... | collective-permute-start | bytes 786440 | tf_op jit(solution)/shard_map/ppermute | solution.py:689
  114.2 107.1 %reduce-scatter.5.cloned.1.call-start = ((), (), s32[]{:S(2)}) async-start(), calls=%async_computation.7 | async-start | bytes 2359296 | tf_op jit(solution)/shard_map/reduce_scatter | solution.py:902
  141.3 1.4 collective-permute-start.14
  143.7 4.6 %collective-permute-start.15 = (bf16[128,128]{1,0:T(8,128)(2,1)S(1)}, bf16[128,128]{1,0:T(8,128)(2,1)S(1)}, u32[]{:S(2)}, u32[]{:S(2)}) collective-permute-start(bf16[128,128]{1,0:T(8,128)(2,1)S(1)} %get-tuple-element.127), channel_id=1, source_target_pairs={{0,2},{1,3},{2,0},{3,1},{4,6},{5,7},{6,4},{7,5},{8,10},{9,11},{10,... | collective-permute-start | bytes 98312 | tf_op jit(solution)/shard_map/ppermute | solution.py:689
  143.9 5.2 %collective-permute-start.16 = (bf16[128,128]{1,0:T(8,128)(2,1)S(1)}, bf16[128,128]{1,0:T(8,128)(2,1)S(1)}, u32[]{:S(2)}, u32[]{:S(2)}) collective-permute-start(bf16[128,128]{1,0:T(8,128)(2,1)S(1)} %get-tuple-element.129), channel_id=1, source_target_pairs={{0,4},{1,5},{2,6},{3,7},{4,0},{5,1},{6,2},{7,3},{8,12},{9,13},{10,... | collective-permute-start | bytes 98312 | tf_op jit(solution)/shard_map/ppermute | solution.py:689
  145.8 5.7 %collective-permute-start.17 = (bf16[128,128]{1,0:T(8,128)(2,1)S(1)}, bf16[128,128]{1,0:T(8,128)(2,1)S(1)}, u32[]{:S(2)}, u32[]{:S(2)}) collective-permute-start(bf16[128,128]{1,0:T(8,128)(2,1)S(1)} %get-tuple-element.128), channel_id=1, source_target_pairs={{0,6},{1,7},{2,4},{3,5},{4,2},{5,3},{6,0},{7,1},{8,14},{9,15},{10,... | collective-permute-start | bytes 98312 | tf_op jit(solution)/shard_map/ppermute | solution.py:689
  151.6 4.7 %collective-permute-start.18 = (bf16[128,128]{1,0:T(8,128)(2,1)S(1)}, bf16[128,128]{1,0:T(8,128)(2,1)S(1)}, u32[]{:S(2)}, u32[]{:S(2)}) collective-permute-start(bf16[128,128]{1,0:T(8,128)(2,1)S(1)} %get-tuple-element.115), channel_id=1, source_target_pairs={{0,2},{1,3},{2,0},{3,1},{4,6},{5,7},{6,4},{7,5},{8,10},{9,11},{10,... | collective-permute-start | bytes 98312 | tf_op jit(solution)/shard_map/ppermute | solution.py:689
  151.8 4.9 %collective-permute-start.19 = (bf16[128,128]{1,0:T(8,128)(2,1)S(1)}, bf16[128,128]{1,0:T(8,128)(2,1)S(1)}, u32[]{:S(2)}, u32[]{:S(2)}) collective-permute-start(bf16[128,128]{1,0:T(8,128)(2,1)S(1)} %get-tuple-element.115), channel_id=1, source_target_pairs={{0,4},{1,5},{2,6},{3,7},{4,0},{5,1},{6,2},{7,3},{8,12},{9,13},{10,... | collective-permute-start | bytes 98312 | tf_op jit(solution)/shard_map/ppermute | solution.py:689
  154.7 5.7 %collective-permute-start.20 = (bf16[128,128]{1,0:T(8,128)(2,1)S(1)}, bf16[128,128]{1,0:T(8,128)(2,1)S(1)}, u32[]{:S(2)}, u32[]{:S(2)}) collective-permute-start(bf16[128,128]{1,0:T(8,128)(2,1)S(1)} %get-tuple-element.115), channel_id=1, source_target_pairs={{0,6},{1,7},{2,4},{3,5},{4,2},{5,3},{6,0},{7,1},{8,14},{9,15},{10,... | collective-permute-start | bytes 98312 | tf_op jit(solution)/shard_map/ppermute | solution.py:689
  160.5 1.3 collective-permute-start.21
  175.0 7.1 %collective-permute-start.22 = (bf16[320,256]{1,0:T(8,128)(2,1)S(1)}, bf16[320,256]{1,0:T(8,128)(2,1)S(1)}, u32[]{:S(2)}, u32[]{:S(2)}) collective-permute-start(bf16[320,256]{1,0:T(8,128)(2,1)S(1)} %get-tuple-element.122), channel_id=1, source_target_pairs={{0,8},{8,0},{16,24},{24,16},{1,9},{9,1},{17,25},{25,17},{2,10},{10... | collective-permute-start | bytes 491528 | tf_op jit(solution)/shard_map/ppermute | solution.py:689
  175.7 8.6 %collective-permute-start.23 = (bf16[320,256]{1,0:T(8,128)(2,1)S(1)}, bf16[320,256]{1,0:T(8,128)(2,1)S(1)}, u32[]{:S(2)}, u32[]{:S(2)}) collective-permute-start(bf16[320,256]{1,0:T(8,128)(2,1)S(1)} %get-tuple-element.124), channel_id=1, source_target_pairs={{0,16},{8,24},{16,0},{24,8},{1,17},{9,25},{17,1},{25,9},{2,18},{10... | collective-permute-start | bytes 491528 | tf_op jit(solution)/shard_map/ppermute | solution.py:689
  177.2 8.6 %collective-permute-start.24 = (bf16[320,256]{1,0:T(8,128)(2,1)S(1)}, bf16[320,256]{1,0:T(8,128)(2,1)S(1)}, u32[]{:S(2)}, u32[]{:S(2)}) collective-permute-start(bf16[320,256]{1,0:T(8,128)(2,1)S(1)} %get-tuple-element.123), channel_id=1, source_target_pairs={{0,24},{8,16},{16,8},{24,0},{1,25},{9,17},{17,9},{25,1},{2,26},{10... | collective-permute-start | bytes 491528 | tf_op jit(solution)/shard_map/ppermute | solution.py:689
  178.7 42.6 %copy-start.9 = (bf16[8,8,4,256]{3,1,2,0:T(8,128)(2,1)}, bf16[8,8,4,256]{3,1,2,0:T(8,128)(2,1)S(1)}, u32[]{:S(2)}) copy-start(bf16[8,8,4,256]{3,1,2,0:T(8,128)(2,1)S(1)} %copy.98) | copy-start | bytes 393220
  186.7 18.9 %all-to-all-start.1 = ((bf16[8,80,256]{2,1,0:T(8,128)(2,1)}), bf16[8,80,256]{2,1,0:T(8,128)(2,1)S(1)}, u32[]{:S(2)}, u32[]{:S(2)}) async-start(bf16[8,80,256]{2,1,0:T(8,128)(2,1)} %fusion.2), calls=%async_computation.2 | async-start | bytes 655360 | tf_op jit(solution)/shard_map/all_to_all | solution.py:732
  190.2 6.4 %collective-permute-start.25 = (bf16[64,1024]{1,0:T(8,128)(2,1)S(1)}, bf16[64,1024]{1,0:T(8,128)(2,1)S(1)}, u32[]{:S(2)}, u32[]{:S(2)}) collective-permute-start(bf16[64,1024]{1,0:T(8,128)(2,1)S(1)} %bitcast.184), channel_id=1, source_target_pairs={{0,8},{8,0},{16,24},{24,16},{1,9},{9,1},{17,25},{25,17},{2,10},{10... | collective-permute-start | bytes 393224 | tf_op jit(solution)/shard_map/ppermute | solution.py:689
  191.0 7.4 %collective-permute-start.26 = (bf16[64,1024]{1,0:T(8,128)(2,1)S(1)}, bf16[64,1024]{1,0:T(8,128)(2,1)S(1)}, u32[]{:S(2)}, u32[]{:S(2)}) collective-permute-start(bf16[64,1024]{1,0:T(8,128)(2,1)S(1)} %bitcast.185), channel_id=1, source_target_pairs={{0,16},{8,24},{16,0},{24,8},{1,17},{9,25},{17,1},{25,9},{2,18},{10... | collective-permute-start | bytes 393224 | tf_op jit(solution)/shard_map/ppermute | solution.py:689
  192.5 6.7 %collective-permute-start.27 = (bf16[64,1024]{1,0:T(8,128)(2,1)S(1)}, bf16[64,1024]{1,0:T(8,128)(2,1)S(1)}, u32[]{:S(2)}, u32[]{:S(2)}) collective-permute-start(bf16[64,1024]{1,0:T(8,128)(2,1)S(1)} %bitcast.186), channel_id=1, source_target_pairs={{0,24},{8,16},{16,8},{24,0},{1,25},{9,17},{17,9},{25,1},{2,26},{10... | collective-permute-start | bytes 393224 | tf_op jit(solution)/shard_map/ppermute | solution.py:689
  196.5 24.7 %copy-start.17 = (bf16[64,1024]{1,0:T(8,128)(2,1)}, bf16[64,1024]{1,0:T(8,128)(2,1)S(1)}, u32[]{:S(2)}) copy-start(bf16[64,1024]{1,0:T(8,128)(2,1)S(1)} %collective-permute-done.25.refs_5_) | copy-start | bytes 393220
  198.4 22.9 %copy-start.18 = (bf16[64,1024]{1,0:T(8,128)(2,1)}, bf16[64,1024]{1,0:T(8,128)(2,1)S(1)}, u32[]{:S(2)}) copy-start(bf16[64,1024]{1,0:T(8,128)(2,1)S(1)} %collective-permute-done.26.refs_6_) | copy-start | bytes 393220
  199.2 22.0 %copy-start.19 = (bf16[64,1024]{1,0:T(8,128)(2,1)}, bf16[64,1024]{1,0:T(8,128)(2,1)S(1)}, u32[]{:S(2)}) copy-start(bf16[64,1024]{1,0:T(8,128)(2,1)S(1)} %collective-permute-done.27.refs_7_) | copy-start | bytes 393220
  205.6 15.7 %copy-start.2 = (bf16[8,80,256]{2,1,0:T(8,128)(2,1)}, bf16[8,80,256]{2,1,0:T(8,128)(2,1)S(1)}, u32[]{:S(2)}) copy-start(bf16[8,80,256]{2,1,0:T(8,128)(2,1)S(1)} %all-to-all-done.1.refs_8_) | copy-start | bytes 983044
  205.6 15.7 %copy-start.6 = (bf16[560,256]{1,0:T(8,128)(2,1)}, bf16[560,256]{1,0:T(8,128)(2,1)S(1)}, u32[]{:S(2)}) copy-start(bf16[560,256]{1,0:T(8,128)(2,1)S(1)} %pad_maximum_fusion.1.refs_0_) | copy-start | bytes 860164
  205.6 9.8 %collective-permute-start.28 = (bf16[560,256]{1,0:T(8,128)(2,1)S(1)}, bf16[560,256]{1,0:T(8,128)(2,1)S(1)}, u32[]{:S(2)}, u32[]{:S(2)}) collective-permute-start(bf16[560,256]{1,0:T(8,128)(2,1)S(1)} %pad_maximum_fusion.1.refs_0_), channel_id=1, source_target_pairs={{0,8},{8,0},{16,24},{24,16},{1,9},{9,1},{17,25},{25,17},{2,10},{10... | collective-permute-start | bytes 860168 | tf_op jit(solution)/shard_map/ppermute | solution.py:689
  206.8 13.3 %collective-permute-start.29 = (bf16[560,256]{1,0:T(8,128)(2,1)S(1)}, bf16[560,256]{1,0:T(8,128)(2,1)S(1)}, u32[]{:S(2)}, u32[]{:S(2)}) collective-permute-start(bf16[560,256]{1,0:T(8,128)(2,1)S(1)} %pad_maximum_fusion.1.refs_0_), channel_id=1, source_target_pairs={{0,16},{8,24},{16,0},{24,8},{1,17},{9,25},{17,1},{25,9},{2,18},{10... | collective-permute-start | bytes 860168 | tf_op jit(solution)/shard_map/ppermute | solution.py:689
  208.3 13.0 %collective-permute-start.30 = (bf16[560,256]{1,0:T(8,128)(2,1)S(1)}, bf16[560,256]{1,0:T(8,128)(2,1)S(1)}, u32[]{:S(2)}, u32[]{:S(2)}) collective-permute-start(bf16[560,256]{1,0:T(8,128)(2,1)S(1)} %pad_maximum_fusion.1.refs_0_), channel_id=1, source_target_pairs={{0,24},{8,16},{16,8},{24,0},{1,25},{9,17},{17,9},{25,1},{2,26},{10... | collective-permute-start | bytes 860168 | tf_op jit(solution)/shard_map/ppermute | solution.py:689
  215.4 5.9 %copy-start.14 = (bf16[560,256]{1,0:T(8,128)(2,1)}, bf16[560,256]{1,0:T(8,128)(2,1)S(1)}, u32[]{:S(2)}) copy-start(bf16[560,256]{1,0:T(8,128)(2,1)S(1)} %collective-permute-done.28.refs_1_) | copy-start | bytes 860164
  (11 other events, 12.8 us)
Sparse Core Ops, SparseCore 0:
  9.6 34.1 all-gather.4
  45.5 31.4 all-gather.2
  114.3 34.4 reduce-scatter.2
  173.9 36.9 reduce-scatter.4

commit v3 on v2

--- a/solution.py
+++ b/solution.py
@@ -14,8 +14,8 @@
 LOG2E = 1.4426950408889634
 CUT = 1e30
 SEGS = 8
-UNROLL_FIRST = 4
-UNROLL_SECOND = 4
+BATCH = 4
+TOGETHER = 4
 MIB = 1 << 20
 ROOM = 56 * MIB
 
@@ -60,15 +60,13 @@
     return hit.astype(f32).astype(bf16)
 
 
-def context_positions(starts_ref, first_row, rows, steps, chans):
-    groups, width = lane_groups(chans)
-    row = lax.broadcasted_iota(jnp.int32, (rows, width), 0) + first_row
+def context_positions(starts_ref, first_row, rows, steps, lanes):
+    row = lax.broadcasted_iota(jnp.int32, (rows, lanes), 0) + first_row
     token = jnp.bitwise_and(row, SEGS - 1) * steps + jnp.right_shift(row, SEGS.bit_length() - 1)
-    begin = jnp.zeros((rows, width), jnp.int32)
+    begin = jnp.zeros((rows, lanes), jnp.int32)
     for c in range(starts_ref.shape[1]):
         begin = jnp.where(starts_ref[0, c] <= token, starts_ref[0, c], begin)
-    place = token - begin
-    return jnp.concatenate([place] * groups, axis=1) if groups > 1 else place
+    return token - begin
 
 
 def split_dot(wide, narrow, dims, swapped=False):
@@ -111,7 +109,7 @@
     scale = lax.rsqrt(jnp.mean(wide * wide, axis=1, keepdims=True) + eps)
     normed = (wide * scale * gain_ref[...]).astype(bf16)
     normed_ref[...] = normed.reshape(normed_ref.shape)
-    scale_ref[...] = scale.reshape(scale_ref.shape)
+    scale_ref[...] = jnp.broadcast_to(scale, (size, 128)).reshape(scale_ref.shape)
     mixed = dot(normed, w_ref[...], (1, 0)).astype(bf16)
     mixed = dot(s_mixing[...], mixed, (1, 0))
     rows = block_rows(turn, size)
@@ -127,7 +125,8 @@
             s_x[j * SEGS : (j + 1) * SEGS, :] = jnp.where(first, 0.0, pltpu.roll(last, 1, 0))
 
         def step(t, carry):
-            place = context_positions(starts_ref, t * size, size, steps, chans)
+            groups, width = lane_groups(chans)
+            place = jnp.concatenate([context_positions(starts_ref, t * size, size, steps, width)] * groups, axis=1)
             pre = cb_ref[...] + jnp.zeros((size, chans), f32)
             for k in range(taps):
                 lag = taps - 1 - k
@@ -177,13 +176,14 @@
 def exit_kernel(
     span, taps, low_cols, starts_ref, dproj_ref, part_ref, pre_ref, x_ref, val_ref, cw_ref, xw_ref, dgate_ref, w_ref,
     hid_ref, scale_ref, gain_ref, ddtw_ref, dalog_ref, ddtb_ref, dskip_ref,
-    dn_ref, din_ref, small_ref, dgain_ref, s_pre, s_dx, s_din,
+    dn_ref, din_ref, small_ref, dgain_ref, s_pre, s_dx, s_din, s_place,
 ):
     total, chans = x_ref.shape
     size = span * SEGS
     steps = total // SEGS
     turns = steps // span
     halo = (taps - 1) * SEGS
+    groups, width = lane_groups(chans)
     turn = pl.program_id(0)
 
     @pl.when(turn == 0)
@@ -195,11 +195,13 @@
             d_values = part_ref[rows, :] + dot(d_proj, xw_ref[...], (1, 1))
             d_pre = d_values * silu_slope(pre_ref[rows, :])
             s_pre[rows, :] = d_pre
+            s_place[rows, :] = context_positions(starts_ref, t * size, size, steps, width)
             d_bias, d_xw = carry
             return d_bias + jnp.sum(d_pre, axis=0, keepdims=True), d_xw + dot(d_proj, val_ref[rows, :], (0, 0))
 
         begin = (jnp.zeros((1, chans), f32), jnp.zeros((dproj_ref.shape[1], chans), f32))
         d_bias, d_xw = lax.fori_loop(0, turns, first, begin)
+        s_place[total : total + halo, :] = context_positions(starts_ref, total, halo, steps, width)
         last = lax.broadcasted_iota(jnp.int32, (SEGS, chans), 0) == SEGS - 1
         for j in range(taps - 1):
             head = s_pre[j * SEGS : (j + 1) * SEGS, :]
@@ -213,9 +215,9 @@
             out = []
             for k in range(taps):
                 lag = taps - 1 - k
-                place = context_positions(starts_ref, t * size + lag * SEGS, size, steps, chans)
-                later = s_pre[pl.ds(pl.multiple_of(t * size + lag * SEGS, SEGS), size), :]
-                later = jnp.where(place >= lag, later, 0.0)
+                at = pl.ds(pl.multiple_of(t * size + lag * SEGS, SEGS), size)
+                valid = jnp.concatenate([s_place[at, :]] * groups, axis=1) >= lag
+                later = jnp.where(valid, s_pre[at, :], 0.0)
                 d_x = d_x + cw_ref[k : k + 1, :] * later
                 out.append(sums[k] + jnp.sum(later * x, axis=0, keepdims=True))
             natural = dot(back, d_x.astype(bf16), (1, 0)).astype(bf16).reshape(SEGS, span, chans)
@@ -242,7 +244,7 @@
         both = jnp.concatenate([d_x, dgate_ref[...]], axis=1)
         d_normed = dot(both, w_ref[...], (1, 1)).astype(bf16)
         dn_ref[...] = d_normed
-        unit = hid_ref[...].astype(f32) * scale_ref[...]
+        unit = hid_ref[...].astype(f32) * jnp.concatenate([scale_ref[...]] * (hid_ref.shape[1] // 128), axis=1)
         dgain_ref[...] += jnp.sum(d_normed.astype(f32) * unit, axis=0, keepdims=True)
         s_din[...] += dot(d_x, (unit * gain_ref[...]).astype(bf16), (0, 0))
 
@@ -252,247 +254,461 @@
 
 
 def prepare_spread(hot_ref, rank, states):
-    row = lax.broadcasted_iota(jnp.int32, (hot_ref.shape[0], 128), 0)
+    hot_ref[...] = jnp.zeros_like(hot_ref)
+    row = lax.broadcasted_iota(jnp.int32, (16, 128), 0)
     for n in range(2 * states):
-        hot_ref[:, n * 128 : (n + 1) * 128] = (row == rank + n).astype(f32).astype(bf16)
-
-
-def spread_columns(out_ref, slot, hot_ref, proj_ref, rows, states):
-    block = proj_ref[rows, :]
-    for n in range(0, 2 * states, 2):
-        both = dot(block, hot_ref[:, n * 128 : (n + 2) * 128], (1, 0))
-        out_ref[slot, n] = both[:, :128]
-        out_ref[slot, n + 1] = both[:, 128:]
-
-
-def prepare_sums(pick_ref, rank):
-    column = lax.broadcasted_iota(jnp.int32, (128, pick_ref.shape[1]), 1)
-    for n in range(pick_ref.shape[0] // 128):
-        pick_ref[n * 128 : (n + 1) * 128, :] = (column == rank + n).astype(f32).astype(bf16)
-
-
-def sum_lanes(mix_ref, pick_ref):
-    total = None
-    for first in range(0, mix_ref.shape[1], 512):
-        part = dot(mix_ref[:, first : first + 512].astype(bf16), pick_ref[first : first + 512, :], (1, 0))
-        total = part if total is None else total + part
-    return total
+        first = (rank + n) // 16 * 16
+        hot_ref[first : first + 16, n * 128 : (n + 1) * 128] = (row + first == rank + n).astype(f32).astype(bf16)
+
+
+def spread_pair(out_ref, slot, hot_ref, proj_ref, rows, first, pair):
+    at = first * 128 + pair * 256
+    both = dot(proj_ref[rows, :], hot_ref[:, pl.ds(at if isinstance(at, int) else pl.multiple_of(at, 256), 256)], (1, 0))
+    out_ref[slot, 2 * pair] = both[:, :128]
+    out_ref[slot, 2 * pair + 1] = both[:, 128:]
+
+
+def sum_lanes(mix_ref, hot_ref):
+    return dot(hot_ref[...], mix_ref[...], (1, 1)).T
 
 
 def forward_kernel(
     rank, states, span, proj_ref, val_ref, cut_ref, dtw_ref, dtb_ref, alog_ref,
-    y_ref, hist_ref, delta_ref, s_cut, s_dx, s_rate, s_state, s_wide, s_hot,
+    y_ref, hist_ref, delta_ref, s_cut, s_dx, s_rate, s_state, s_sum, s_b, s_c, s_hot,
+):
+    total, chans = val_ref.shape
+    steps = total // SEGS
+    size = span * SEGS
+    groups, width = lane_groups(chans)
+    turn = pl.program_id(0)
+    turns = steps // span
+    slots = s_b.shape[0]
+    half = states // 2
+    count = span // BATCH
+
+    def rate(n, g):
+        return s_rate[n : n + 1, g * width : (g + 1) * width]
+
+    @pl.when(turn == 0)
+    def _():
+        s_rate[...] = -jnp.exp(alog_ref[...]) * LOG2E
+        prepare_spread(s_hot, rank, states)
+        s_state[...] = jnp.zeros_like(s_state)
+        s_sum[...] = jnp.zeros_like(s_sum)
+        def block(t, carry):
+            rows = block_rows(t, size)
+            slot = t if slots > 1 else 0
+            for pair in range(half):
+                spread_pair(s_b, slot, s_hot, proj_ref, rows, 0, pair)
+                spread_pair(s_c, slot, s_hot, proj_ref, rows, states, pair)
+            delta = softplus(dot(proj_ref[rows, :rank], dtw_ref[...], (1, 0)) + dtb_ref[...])
+            put(delta_ref, rows, delta, groups, width)
+            cut = cut_ref[rows, :].astype(f32) * CUT
+            put(s_cut, rows, delta + jnp.concatenate([cut] * groups, axis=1), groups, width)
+            put(s_dx, rows, delta * val_ref[rows, :].astype(f32), groups, width)
+
+            def sweep(q, carry):
+                at = [block_rows(t * span + q * BATCH + j, SEGS) for j in range(BATCH)]
+                here = [block_rows(q * BATCH + j, SEGS) for j in range(BATCH)]
+                for g in range(groups):
+                    cuts = [s_cut[g, at[j], :] for j in range(BATCH)]
+                    dxs = [s_dx[g, at[j], :] for j in range(BATCH)]
+                    s_sum[g] = s_sum[g] + sum(cuts)
+                    for n in range(states):
+                        held = s_state[n * groups + g]
+                        for j in range(BATCH):
+                            push = dxs[j] * s_b[slot, n, here[j], :width]
+                            held = jnp.exp2(cuts[j] * rate(n, g)) * held + push
+                        s_state[n * groups + g] = held
+                return carry
+
+            return lax.fori_loop(0, count, sweep, carry)
+
+        lax.fori_loop(0, turns, block, 0)
+        first = lax.broadcasted_iota(jnp.int32, (SEGS, width), 0) == 0
+        for n in range(states):
+            for g in range(groups):
+                gain = jnp.exp2(s_sum[g] * rate(n, g))
+                end = s_state[n * groups + g]
+                start = jnp.zeros((SEGS, width), f32)
+                for _ in range(SEGS - 1):
+                    start = jnp.where(first, 0.0, pltpu.roll(gain * start + end, 1, 0))
+                s_state[n * groups + g] = start
+
+    slot = turn if slots > 1 else 0
+    if slots == 1:
+        for pair in range(half):
+            spread_pair(s_b, 0, s_hot, proj_ref, block_rows(turn, size), 0, pair)
+            spread_pair(s_c, 0, s_hot, proj_ref, block_rows(turn, size), states, pair)
+
+    def sweep(q, carry):
+        at = [block_rows(turn * span + q * BATCH + j, SEGS) for j in range(BATCH)]
+        here = [block_rows(q * BATCH + j, SEGS) for j in range(BATCH)]
+        for g in range(groups):
+            cuts = [s_cut[g, at[j], :] for j in range(BATCH)]
+            dxs = [s_dx[g, at[j], :] for j in range(BATCH)]
+            ys = [None] * BATCH
+            for n in range(states):
+                i = n * groups + g
+                held = s_state[i]
+                for j in range(BATCH):
+                    hist_ref[0, q * BATCH + j, i] = held
+                    push = dxs[j] * s_b[slot, n, here[j], :width]
+                    held = jnp.exp2(cuts[j] * rate(n, g)) * held + push
+                    term = held * s_c[slot, n, here[j], :width]
+                    ys[j] = term if n == 0 else ys[j] + term
+                s_state[i] = held
+            for j in range(BATCH):
+                y_ref[at[j], g * width : (g + 1) * width] = ys[j]
+        return carry
+
+    lax.fori_loop(0, count, sweep, 0)
+    hist_ref[0, span] = s_state[...]
+
+
+def backward_kernel(
+    rank, states, span, proj_ref, val_ref, cut_ref, dy_ref, delta_ref, dtw_ref, dtwt_ref, dtb_ref, alog_ref, skip_ref,
+    hist_ref, part_ref, dval_ref, ddtw_ref, ddtb_ref, dalog_ref,
+    s_cut, s_val, s_dd, s_rate, s_state, s_sum, s_drate, s_b, s_c, s_mix, s_hot, s_bc,
+):
+    total, chans = val_ref.shape
+    steps = total // SEGS
+    size = span * SEGS
+    groups, width = lane_groups(chans)
+    turns = steps // span
+    turn = pl.program_id(0)
+    place = turns - 1 - turn
+    slots = s_b.shape[0]
+    half = states // 2
+    count = span // BATCH
+    lane = [slice(g * width, (g + 1) * width) for g in range(groups)]
+
+    def rate(n, g):
+        return s_rate[n : n + 1, lane[g]]
+
+    @pl.when(turn == 0)
+    def _():
+        s_rate[...] = -jnp.exp(alog_ref[...]) * LOG2E
+        s_drate[...] = jnp.zeros_like(s_drate)
+        s_state[...] = jnp.zeros_like(s_state)
+        s_sum[...] = jnp.zeros_like(s_sum)
+        if width < 128:
+            s_mix[...] = jnp.zeros_like(s_mix)
+        prepare_spread(s_hot, rank, states)
+        def block(turned, carry):
+            t = turns - 1 - turned
+            rows = block_rows(t, size)
+            slot = t if slots > 1 else 0
+            for pair in range(half):
+                spread_pair(s_b, slot, s_hot, proj_ref, rows, 0, pair)
+                spread_pair(s_c, slot, s_hot, proj_ref, rows, states, pair)
+            cut = cut_ref[rows, :].astype(f32) * CUT
+            delta = take(delta_ref, rows, groups)
+            put(s_cut, rows, delta + jnp.concatenate([cut] * groups, axis=1), groups, width)
+            put(s_val, rows, val_ref[rows, :].astype(f32), groups, width)
+
+            def sweep(q, carry):
+                k = span - BATCH - q * BATCH
+                at = [block_rows(t * span + k + j, SEGS) for j in range(BATCH)]
+                here = [block_rows(k + j, SEGS) for j in range(BATCH)]
+                for g in range(groups):
+                    cuts = [s_cut[g, at[j], :] for j in range(BATCH)]
+                    dys = [dy_ref[at[j], lane[g]] for j in range(BATCH)]
+                    s_sum[g] = s_sum[g] + sum(cuts)
+                    for n in range(states):
+                        held = s_state[n * groups + g]
+                        for j in reversed(range(BATCH)):
+                            held = dys[j] * s_c[slot, n, here[j], :width] + held
+                            held = jnp.exp2(cuts[j] * rate(n, g)) * held
+                        s_state[n * groups + g] = held
+                return carry
+
+            return lax.fori_loop(0, count, sweep, carry)
+
+        lax.fori_loop(0, turns, block, 0)
+        last = lax.broadcasted_iota(jnp.int32, (SEGS, width), 0) == SEGS - 1
+        for n in range(states):
+            for g in range(groups):
+                gain = jnp.exp2(s_sum[g] * rate(n, g))
+                end = s_state[n * groups + g]
+                start = jnp.zeros((SEGS, width), f32)
+                for _ in range(SEGS - 1):
+                    start = jnp.where(last, 0.0, pltpu.roll(gain * start + end, SEGS - 1, 0))
+                s_state[n * groups + g] = start
+
+    slot = place if slots > 1 else 0
+    if slots == 1:
+        for pair in range(half):
+            spread_pair(s_b, 0, s_hot, proj_ref, block_rows(place, size), 0, pair)
+            spread_pair(s_c, 0, s_hot, proj_ref, block_rows(place, size), states, pair)
+
+    def sweep(q, carry):
+        k = span - BATCH - q * BATCH
+        at = [block_rows(place * span + k + j, SEGS) for j in range(BATCH)]
+        here = [block_rows(k + j, SEGS) for j in range(BATCH)]
+        each = [(j, g) for j in range(BATCH) for g in range(groups)]
+        cuts = {(j, g): s_cut[g, at[j], :] for j, g in each}
+        deltas = {(j, g): delta_ref[g, at[j], :] for j, g in each}
+        vals = {(j, g): s_val[g, at[j], :] for j, g in each}
+        dys = {(j, g): dy_ref[at[j], lane[g]] for j, g in each}
+        dxs = {e: deltas[e] * vals[e] for e in each}
+        by_rate, by_b = {}, {}
+        for first in range(0, states, TOGETHER):
+            some = [(n, g) for n in range(first, first + TOGETHER) for g in range(groups)]
+            held = {(n, g): s_state[n * groups + g] for n, g in some}
+            d_rate = {(n, g): s_drate[n * groups + g] for n, g in some}
+            after = {(n, g): hist_ref[0, k + BATCH, n * groups + g] for n, g in some}
+            mix = {}
+            for j in reversed(range(BATCH)):
+                for n, g in some:
+                    e, i = (j, g), (n, g)
+                    b_n = s_b[slot, n, here[j], :width]
+                    c_n = s_c[slot, n, here[j], :width]
+                    before = hist_ref[0, k + j, n * groups + g]
+                    lam = dys[e] * c_n + held[i]
+                    held[i] = jnp.exp2(cuts[e] * rate(n, g)) * lam
+                    through = held[i] * before
+                    d_rate[i] = d_rate[i] + through * deltas[e]
+                    terms = (through * rate(n, g), lam * b_n, lam * dxs[e], dys[e] * after[i])
+                    by_rate[e] = by_rate[e] + terms[0] if e in by_rate else terms[0]
+                    by_b[e] = by_b[e] + terms[1] if e in by_b else terms[1]
+                    for m, term in ((n, terms[2]), (states + n, terms[3])):
+                        mix[j, m] = mix[j, m] + term if (j, m) in mix else term
+                    after[i] = before
+                if j % 2 == 0:
+                    two = pl.ds(pl.multiple_of((k + j) * SEGS, 2 * SEGS), 2 * SEGS)
+                    for n in range(first, first + TOGETHER):
+                        for m in (n, states + n):
+                            value = jnp.concatenate([mix[j, m], mix[j + 1, m]], axis=0).astype(bf16)
+                            s_mix[two, m * 128 : m * 128 + width] = value
+            for n, g in some:
+                s_state[n * groups + g] = held[n, g]
+                s_drate[n * groups + g] = d_rate[n, g]
+        for j, g in each:
+            e = (j, g)
+            s_dd[g, at[j], :] = by_rate[e] * (1.0 / LOG2E) + by_b[e] * vals[e]
+            dval_ref[at[j], lane[g]] = by_b[e] * deltas[e] + dys[e] * skip_ref[:, lane[g]]
+        return carry
+
+    lax.fori_loop(0, count, sweep, 0)
+    rows = block_rows(place, size)
+    s_bc[...] = sum_lanes(s_mix, s_hot)
+    pre = dot(proj_ref[rows, :rank], dtw_ref[...], (1, 0)) + dtb_ref[...]
+    d_pre = take(s_dd, rows, groups) * jax.nn.sigmoid(pre)
+    d_bias = jnp.sum(d_pre, axis=0, keepdims=True)
+    d_dtw = split_dot(d_pre, proj_ref[rows, :rank], (0, 0), swapped=True)
+    part = split_dot(d_pre, dtwt_ref[...], (1, 0))
+    part_ref[rows, :] = (part + s_bc[...]).astype(bf16)
+
+    @pl.when(turn == 0)
+    def _():
+        ddtb_ref[...] = d_bias
+        ddtw_ref[...] = d_dtw
+
+    @pl.when(turn > 0)
+    def _():
+        ddtb_ref[...] += d_bias
+        ddtw_ref[...] += d_dtw
+
+    @pl.when(turn == turns - 1)
+    def _():
+        sums = [jnp.sum(s_drate[i], axis=0, keepdims=True) for i in range(states * groups)]
+        rows = [jnp.concatenate(sums[n * groups : (n + 1) * groups], axis=1) for n in range(states)]
+        dalog_ref[...] = jnp.concatenate(rows, axis=0) * s_rate[...] * (1.0 / LOG2E)
+
+
+def scan_kernel(
+    rank, states, span, proj_ref, val_ref, gate_ref, cut_ref, grad_ref, w_ref, dtw_ref, dtwt_ref, dtb_ref, alog_ref,
+    skip_ref, branch_ref, gated_ref, dgate_ref, part_ref, dval_ref, ddtw_ref, ddtb_ref, dalog_ref, dskip_ref,
+    s_cut, s_delta, s_val, s_dy, s_hist, s_b, s_c, s_y, s_rate, s_state, s_drate, s_mix, s_hot, s_in, s_out,
 ):
     total, chans = val_ref.shape
     steps = total // SEGS
     size = span * SEGS
     groups, width = lane_groups(chans)
     pairs = [(n, g) for n in range(states) for g in range(groups)]
+    every = range(groups)
+    lane = [slice(g * width, (g + 1) * width) for g in every]
+    turns = steps // span
     turn = pl.program_id(0)
-    turns = steps // span
-    slots = s_wide.shape[0]
-
-    def rate(n, g):
-        return s_rate[n : n + 1, g * width : (g + 1) * width]
-
-    @pl.when(turn == 0)
-    def _():
-        s_rate[...] = -jnp.exp(alog_ref[...]) * LOG2E
-        prepare_spread(s_hot, rank, states)
-
-        def block(t, carry):
-            rows = block_rows(t, size)
-            slot = t if slots > 1 else 0
-            spread_columns(s_wide, slot, s_hot, proj_ref, rows, states)
-            delta = softplus(dot(proj_ref[rows, :rank], dtw_ref[...], (1, 0)) + dtb_ref[...])
-            put(delta_ref, rows, delta, groups, width)
-            put(s_cut, rows, delta + cut_ref[rows, :] * CUT, groups, width)
-            put(s_dx, rows, delta * val_ref[rows, :].astype(f32), groups, width)
-
-            def sweep(k, carry):
-                held, span_sum = carry
-                at = block_rows(t * span + k, SEGS)
-                here = block_rows(k, SEGS)
-                cuts = [s_cut[g, at, :] for g in range(groups)]
-                dxs = [s_dx[g, at, :] for g in range(groups)]
-                out = []
-                for n, g in pairs:
-                    push = dxs[g] * s_wide[slot, n, here, :width]
-                    out.append(jnp.exp2(cuts[g] * rate(n, g)) * held[n * groups + g] + push)
-                return tuple(out), tuple(span_sum[g] + cuts[g] for g in range(groups))
-
-            return lax.fori_loop(0, span, sweep, carry, unroll=UNROLL_FIRST)
-
-        zero = jnp.zeros((SEGS, width), f32)
-        ends, sums = lax.fori_loop(0, turns, block, ((zero,) * len(pairs), (zero,) * groups))
-        first = lax.broadcasted_iota(jnp.int32, (SEGS, width), 0) == 0
+    zero = jnp.zeros((SEGS, width), f32)
+    sublane = lax.broadcasted_iota(jnp.int32, (SEGS, width), 0)
+
+    def decay(cut, n, g):
+        return jnp.exp2(cut * s_rate[n : n + 1, lane[g]])
+
+    def chained(ends, sums, edge, shift):
         for n, g in pairs:
-            gain = jnp.exp2(sums[g] * rate(n, g))
+            gain = decay(sums[g], n, g)
             end = ends[n * groups + g]
             start = zero
             for _ in range(SEGS - 1):
-                start = jnp.where(first, 0.0, pltpu.roll(gain * start + end, 1, 0))
+                start = jnp.where(sublane == edge, 0.0, pltpu.roll(gain * start + end, shift, 0))
             s_state[n * groups + g] = start
 
-    slot = turn if slots > 1 else 0
-    if slots == 1:
-        spread_columns(s_wide, slot, s_hot, proj_ref, block_rows(turn, size), states)
-
-    def sweep(k, held):
-        at = block_rows(turn * span + k, SEGS)
-        here = block_rows(k, SEGS)
-        cuts = [s_cut[g, at, :] for g in range(groups)]
-        dxs = [s_dx[g, at, :] for g in range(groups)]
-        ys = [jnp.zeros((SEGS, width), f32) for _ in range(groups)]
-        out = []
-        for n in range(states):
-            b_n = s_wide[slot, n, here, :width]
-            c_n = s_wide[slot, states + n, here, :width]
-            for g in range(groups):
-                old = held[n * groups + g]
-                hist_ref[0, k, n * groups + g] = old
-                new = jnp.exp2(cuts[g] * rate(n, g)) * old + dxs[g] * b_n
-                out.append(new)
-                ys[g] = ys[g] + new * c_n
-        for g in range(groups):
-            y_ref[at, g * width : (g + 1) * width] = ys[g]
-        return tuple(out)
-
-    held = lax.fori_loop(0, span, sweep, tuple(s_state[j] for j in range(len(pairs))), unroll=UNROLL_SECOND)
-    for j in range(len(pairs)):
-        s_state[j] = held[j]
-        hist_ref[0, span, j] = held[j]
-
-
-def backward_kernel(
-    rank, states, span, proj_ref, val_ref, cut_ref, dy_ref, delta_ref, dtw_ref, dtwt_ref, dtb_ref, alog_ref, skip_ref,
-    hist_ref, part_ref, dval_ref, ddtw_ref, ddtb_ref, dalog_ref,
-    s_cut, s_val, s_dy, s_dd, s_rate, s_state, s_drate, s_wide, s_mix, s_hot, s_pick,
-):
-    total, chans = val_ref.shape
-    steps = total // SEGS
-    size = span * SEGS
-    groups, width = lane_groups(chans)
-    pairs = [(n, g) for n in range(states) for g in range(groups)]
-    turns = steps // span
-    turn = pl.program_id(0)
-    place = turns - 1 - turn
-    slots = s_wide.shape[0]
-
-    def rate(n, g):
-        return s_rate[n : n + 1, g * width : (g + 1) * width]
-
     @pl.when(turn == 0)
     def _():
         s_rate[...] = -jnp.exp(alog_ref[...]) * LOG2E
+        s_drate[...] = jnp.zeros_like(s_drate)
+        dskip_ref[...] = jnp.zeros_like(dskip_ref)
+        s_in[...] = mixing(span, False)
+        s_out[...] = mixing(span, True)
         prepare_spread(s_hot, rank, states)
-        prepare_sums(s_pick, rank)
-        s_drate[...] = jnp.zeros_like(s_drate)
-        s_mix[...] = jnp.zeros_like(s_mix)
-
-        def block(turned, carry):
-            t = turns - 1 - turned
+
+        def fill(t, carry):
             rows = block_rows(t, size)
-            slot = t if slots > 1 else 0
-            spread_columns(s_wide, slot, s_hot, proj_ref, rows, states)
-            delta = take(delta_ref, rows, groups)
-            put(s_cut, rows, delta + cut_ref[rows, :] * CUT, groups, width)
+            for n in range(0, states, 2):
+                for ref, first in ((s_b, n), (s_c, states + n)):
+                    both = dot(proj_ref[rows, :], s_hot[:, first * 128 : (first + 2) * 128], (1, 0))
+                    ref[n, rows, :] = both[:, :128]
+                    ref[n + 1, rows, :] = both[:, 128:]
+            delta = softplus(dot(proj_ref[rows, :rank], dtw_ref[...], (1, 0)) + dtb_ref[...])
+            cut = cut_ref[rows, :].astype(f32) * CUT
+            put(s_delta, rows, delta, groups, width)
+            put(s_cut, rows, delta + jnp.concatenate([cut] * groups, axis=1), groups, width)
             put(s_val, rows, val_ref[rows, :].astype(f32), groups, width)
-            put(s_dy, rows, dy_ref[rows, :], groups, width)
-
-            def sweep(turned, carry):
-                k = span - 1 - turned
-                held, span_sum = carry
-                at = block_rows(t * span + k, SEGS)
-                here = block_rows(k, SEGS)
-                cuts = [s_cut[g, at, :] for g in range(groups)]
-                dys = [s_dy[g, at, :] for g in range(groups)]
-                out = []
-                for n, g in pairs:
-                    lam = dys[g] * s_wide[slot, states + n, here, :width] + held[n * groups + g]
-                    out.append(jnp.exp2(cuts[g] * rate(n, g)) * lam)
-                return tuple(out), tuple(span_sum[g] + cuts[g] for g in range(groups))
-
-            return lax.fori_loop(0, span, sweep, carry, unroll=UNROLL_FIRST)
-
-        zero = jnp.zeros((SEGS, width), f32)
-        ends, sums = lax.fori_loop(0, turns, block, ((zero,) * len(pairs), (zero,) * groups))
-        last = lax.broadcasted_iota(jnp.int32, (SEGS, width), 0) == SEGS - 1
-        for n, g in pairs:
-            gain = jnp.exp2(sums[g] * rate(n, g))
-            end = ends[n * groups + g]
-            start = zero
-            for _ in range(SEGS - 1):
-                start = jnp.where(last, 0.0, pltpu.roll(gain * start + end, SEGS - 1, 0))
-            s_state[n * groups + g] = start
-
-    slot = place if slots > 1 else 0
-    if slots == 1:
-        spread_columns(s_wide, slot, s_hot, proj_ref, block_rows(place, size), states)
-
-    def sweep(turned, held):
-        k = span - 1 - turned
-        at = block_rows(place * span + k, SEGS)
-        here = block_rows(k, SEGS)
-        cuts = [s_cut[g, at, :] for g in range(groups)]
-        deltas = [delta_ref[g, at, :] for g in range(groups)]
-        vals = [s_val[g, at, :] for g in range(groups)]
-        dys = [s_dy[g, at, :] for g in range(groups)]
-        dxs = [deltas[g] * vals[g] for g in range(groups)]
-        zero = jnp.zeros((SEGS, width), f32)
-        by_rate = [zero] * groups
-        by_b = [zero] * groups
-        out = []
-        for n in range(states):
-            b_n = s_wide[slot, n, here, :width]
-            c_n = s_wide[slot, states + n, here, :width]
-            mix = None
-            mix_c = None
-            for g in range(groups):
-                j = n * groups + g
-                lam = dys[g] * c_n + held[j]
-                onward = jnp.exp2(cuts[g] * rate(n, g)) * lam
-                out.append(onward)
-                through = onward * hist_ref[0, k, j]
-                by_rate[g] = by_rate[g] + through * rate(n, g)
-                by_b[g] = by_b[g] + lam * b_n
-                s_drate[j] = s_drate[j] + through * deltas[g]
-                term = lam * dxs[g]
-                mix = term if mix is None else mix + term
-                term = dys[g] * hist_ref[0, k + 1, j]
-                mix_c = term if mix_c is None else mix_c + term
-            s_mix[here, n * 128 : n * 128 + width] = mix
-            s_mix[here, (states + n) * 128 : (states + n) * 128 + width] = mix_c
-        for g in range(groups):
-            skip = skip_ref[:, g * width : (g + 1) * width]
-            s_dd[g, at, :] = by_rate[g] * (1.0 / LOG2E) + by_b[g] * vals[g]
-            dval_ref[at, g * width : (g + 1) * width] = by_b[g] * deltas[g] + dys[g] * skip
-        return tuple(out)
-
-    held = lax.fori_loop(0, span, sweep, tuple(s_state[j] for j in range(len(pairs))), unroll=UNROLL_SECOND)
-    for j in range(len(pairs)):
-        s_state[j] = held[j]
-    rows = block_rows(place, size)
-    pre = dot(proj_ref[rows, :rank], dtw_ref[...], (1, 0)) + dtb_ref[...]
-    d_pre = take(s_dd, rows, groups) * jax.nn.sigmoid(pre)
-    d_bias = jnp.sum(d_pre, axis=0, keepdims=True)
-    d_dtw = split_dot(d_pre, proj_ref[rows, :rank], (0, 0), swapped=True)
-    part = split_dot(d_pre, dtwt_ref[...], (1, 0))
-    part_ref[rows, :] = (part + sum_lanes(s_mix, s_pick)).astype(bf16)
-
-    @pl.when(turn == 0)
-    def _():
-        ddtb_ref[...] = d_bias
-        ddtw_ref[...] = d_dtw
-
-    @pl.when(turn > 0)
-    def _():
-        ddtb_ref[...] += d_bias
-        ddtw_ref[...] += d_dtw
-
-    @pl.when(turn == turns - 1)
-    def _():
-        sums = [jnp.sum(s_drate[j], axis=0, keepdims=True) for j in range(len(pairs))]
+            return carry
+
+        lax.fori_loop(0, turns, fill, 0)
+
+        def sweep(i, carry):
+            held, sums = carry
+            at = block_rows(i, SEGS)
+            cuts = [s_cut[g, at, :] for g in every]
+            dxs = [s_delta[g, at, :] * s_val[g, at, :] for g in every]
+            out = [decay(cuts[g], n, g) * held[n * groups + g] + dxs[g] * s_b[n, at, :width] for n, g in pairs]
+            return tuple(out), tuple(sums[g] + cuts[g] for g in every)
+
+        begin = ((zero,) * len(pairs), (zero,) * groups)
+        chained(*lax.fori_loop(0, steps, sweep, begin, unroll=4), 0, 1)
+
+    @pl.when(turn < turns)
+    def _():
+
+        def sweep(k, held):
+            i = turn * span + k
+            at = block_rows(i, SEGS)
+            cuts = [s_cut[g, at, :] for g in every]
+            dxs = [s_delta[g, at, :] * s_val[g, at, :] for g in every]
+            ys = [zero] * groups
+            out = []
+            for n in range(states):
+                b_n = s_b[n, at, :width]
+                c_n = s_c[n, at, :width]
+                for g in every:
+                    old = held[n * groups + g]
+                    s_hist[i, n * groups + g] = old
+                    new = decay(cuts[g], n, g) * old + dxs[g] * b_n
+                    out.append(new)
+                    ys[g] = ys[g] + new * c_n
+            for g in every:
+                s_y[block_rows(k, SEGS), lane[g]] = ys[g]
+            return tuple(out)
+
+        held = lax.fori_loop(0, span, sweep, tuple(s_state[j] for j in range(len(pairs))), unroll=4)
+        for j in range(len(pairs)):
+            s_state[j] = held[j]
+
+        @pl.when(turn == turns - 1)
+        def _():
+            s_hist[steps] = s_state[...]
+
+        rows = block_rows(turn, size)
+        vals = val_ref[rows, :].astype(f32)
+        gate = gate_ref[rows, :].astype(f32)
+        sig = jax.nn.sigmoid(gate)
+        act = gate * sig
+        scanned = s_y[...] + skip_ref[...] * vals
+        gated = dot(s_out[...], (scanned * act).astype(bf16), (1, 0)).astype(bf16)
+        gated_ref[...] = gated.reshape(gated_ref.shape)
+        branch_ref[...] = dot(gated, w_ref[...], (1, 0)).astype(bf16).reshape(branch_ref.shape)
+        grad = grad_ref[...].reshape(size, grad_ref.shape[2])
+        d_gated = dot(s_in[...], dot(grad, w_ref[...], (1, 1)).astype(bf16), (1, 0))
+        dy = d_gated * act
+        put(s_dy, rows, dy, groups, width)
+        d_gate = (d_gated * scanned * (sig * (1.0 + gate * (1.0 - sig)))).astype(bf16)
+        dgate_ref[...] = dot(s_out[...], d_gate, (1, 0)).astype(bf16).reshape(dgate_ref.shape)
+        dskip_ref[...] += jnp.sum(dy * vals, axis=0, keepdims=True)
+
+    @pl.when(turn == turns)
+    def _():
+        ddtb_ref[...] = jnp.zeros_like(ddtb_ref)
+        ddtw_ref[...] = jnp.zeros_like(ddtw_ref)
+
+        def sweep(back, carry):
+            held, sums = carry
+            at = block_rows(steps - 1 - back, SEGS)
+            cuts = [s_cut[g, at, :] for g in every]
+            dys = [s_dy[g, at, :] for g in every]
+            out = []
+            for n, g in pairs:
+                lam = dys[g] * s_c[n, at, :width] + held[n * groups + g]
+                out.append(decay(cuts[g], n, g) * lam)
+            return tuple(out), tuple(sums[g] + cuts[g] for g in every)
+
+        begin = ((zero,) * len(pairs), (zero,) * groups)
+        chained(*lax.fori_loop(0, steps, sweep, begin, unroll=4), SEGS - 1, SEGS - 1)
+
+    @pl.when(turn >= turns)
+    def _():
+        place = 2 * turns - 1 - turn
+
+        def sweep(back, held):
+            k = span - 1 - back
+            i = place * span + k
+            at = block_rows(i, SEGS)
+            cuts = [s_cut[g, at, :] for g in every]
+            deltas = [s_delta[g, at, :] for g in every]
+            vals = [s_val[g, at, :] for g in every]
+            dys = [s_dy[g, at, :] for g in every]
+            dxs = [deltas[g] * vals[g] for g in every]
+            by_rate = [zero] * groups
+            by_b = [zero] * groups
+            out = []
+            mixes = {}
+            for n in range(states):
+                b_n = s_b[n, at, :width]
+                c_n = s_c[n, at, :width]
+                mix = mix_c = None
+                for g in every:
+                    j = n * groups + g
+                    lam = dys[g] * c_n + held[j]
+                    onward = decay(cuts[g], n, g) * lam
+                    out.append(onward)
+                    through = onward * s_hist[i, j]
+                    by_rate[g] = by_rate[g] + through * s_rate[n : n + 1, lane[g]]
+                    by_b[g] = by_b[g] + lam * b_n
+                    s_drate[j] = s_drate[j] + through * deltas[g]
+                    term, term_c = lam * dxs[g], dys[g] * s_hist[i + 1, j]
+                    mix = term if mix is None else mix + term
+                    mix_c = term_c if mix_c is None else mix_c + term_c
+                mixes[n], mixes[states + n] = mix, mix_c
+                if n % 2:
+                    for first in (n - 1, states + n - 1):
+                        two = jnp.concatenate([mixes[first], mixes[first + 1]], axis=0).astype(bf16)
+                        s_mix[block_rows(k, 2 * SEGS), first * 64 : first * 64 + width] = two
+            for g in every:
+                s_cut[g, at, :] = by_rate[g] * (1.0 / LOG2E) + by_b[g] * vals[g]
+                dval_ref[at, lane[g]] = by_b[g] * deltas[g] + dys[g] * skip_ref[:, lane[g]]
+            return tuple(out)
+
+        held = lax.fori_loop(0, span, sweep, tuple(s_state[j] for j in range(len(pairs))), unroll=4)
+        for j in range(len(pairs)):
+            s_state[j] = held[j]
+        rows = block_rows(place, size)
+        pre = dot(proj_ref[rows, :rank], dtw_ref[...], (1, 0)) + dtb_ref[...]
+        d_pre = take(s_cut, rows, groups) * jax.nn.sigmoid(pre)
+        ddtb_ref[...] += jnp.sum(d_pre, axis=0, keepdims=True)
+        ddtw_ref[...] += split_dot(d_pre, proj_ref[rows, :rank], (0, 0), swapped=True)
+        part = split_dot(d_pre, dtwt_ref[...], (1, 0))
+        even = jnp.concatenate([s_hot[:, n * 128 : (n + 1) * 128] for n in range(0, 2 * states, 2)], axis=1)
+        found = dot(s_mix[...], even, (1, 1)).reshape(span, 2, SEGS, part_ref.shape[1])
+        odd = pltpu.roll(found[:, 1].reshape(size, part_ref.shape[1]), 1, 1)
+        part_ref[rows, :] = (part + found[:, 0].reshape(size, part_ref.shape[1]) + odd).astype(bf16)
+
+    @pl.when(turn == 2 * turns - 1)
+    def _():
+        sums = [jnp.sum(s_drate[i], axis=0, keepdims=True) for i in range(states * groups)]
         rows = [jnp.concatenate(sums[n * groups : (n + 1) * groups], axis=1) for n in range(states)]
         dalog_ref[...] = jnp.concatenate(rows, axis=0) * s_rate[...] * (1.0 / LOG2E)
 
@@ -534,9 +750,9 @@
             SCALARS, segments, whole(width, 2 * chans), whole(1, width), whole(taps, chans), whole(1, chans),
             whole(chans, lanes),
         ],
-        out_specs=[segments, pl.BlockSpec((SEGS, span, 1), lambda t: (0, t, 0))]
+        out_specs=[segments, pl.BlockSpec((SEGS, span, 128), lambda t: (0, t, 0))]
         + [whole(total, chans)] * 4 + [whole(total, lanes)],
-        out_shape=[like(SEGS, steps, width, dtype=bf16), like(SEGS, steps, 1)] + [like(total, chans, dtype=bf16)] * 3
+        out_shape=[like(SEGS, steps, width, dtype=bf16), like(SEGS, steps, 128)] + [like(total, chans, dtype=bf16)] * 3
         + [like(total, chans), like(total, lanes, dtype=bf16)],
         scratch_shapes=[
             pltpu.VMEM((total + (taps - 1) * SEGS, chans), f32), pltpu.VMEM((span * SEGS, span * SEGS), bf16),
@@ -545,7 +761,7 @@
         cost_estimate=about(6 * total * chans / 262144),
         name="entry",
     )(starts, hidden_all.reshape(SEGS, steps, width), weight, gain, conv_w, conv_b, x_w)
-    return (normed, scale.reshape(total, 1), *rest)
+    return (normed, scale.reshape(total, 128), *rest)
 
 
 def run_gate(grad_all, out_w, gate, values, y, skip, span):
@@ -570,6 +786,51 @@
     return branch.reshape(total, width), gated.reshape(total, chans), dy, d_gate.reshape(total, chans), d_skip
 
 
+def run_scan(proj, values, gate, cut, grad_all, out_w, dt_weight, dt_weight_t, dt_bias, a_log_t, skip, states, span):
+    total, chans = values.shape
+    width_all = grad_all.shape[1]
+    rank = dt_weight.shape[0]
+    steps = total // SEGS
+    groups, width = lane_groups(chans)
+    count = states * groups
+    lanes = proj.shape[1]
+    turns = steps // span
+    size = span * SEGS
+    by_group = pltpu.VMEM((groups, total, width), f32)
+    spread = pltpu.VMEM((states, total, 128), f32)
+    held = pltpu.VMEM((count, SEGS, width), f32)
+    order = pltpu.VMEM((size, size), bf16)
+    part = pl.BlockSpec((SEGS, span, chans), lambda t: (0, jnp.minimum(t, turns - 1), 0))
+    full = pl.BlockSpec((SEGS, span, width_all), lambda t: (0, jnp.minimum(t, turns - 1), 0))
+    natural = like(SEGS, steps, chans, dtype=bf16)
+    branch, gated, d_gate, *rest = pl.pallas_call(
+        functools.partial(scan_kernel, rank, states, span),
+        grid=(2 * turns,),
+        in_specs=[
+            whole(total, lanes), whole(total, chans), whole(total, chans), whole(total, width), full,
+            whole(chans, width_all), whole(rank, chans), whole(chans, lanes), whole(1, chans), whole(states, chans),
+            whole(1, chans),
+        ],
+        out_specs=[
+            full, part, part, whole(total, lanes), whole(total, chans), whole(rank, chans), whole(1, chans),
+            whole(states, chans), whole(1, chans),
+        ],
+        out_shape=[
+            like(SEGS, steps, width_all, dtype=bf16), natural, natural, like(total, lanes, dtype=bf16),
+            like(total, chans), like(rank, chans), like(1, chans), like(states, chans), like(1, chans),
+        ],
+        scratch_shapes=[
+            by_group, by_group, by_group, by_group, pltpu.VMEM((steps + 1, count, SEGS, width), f32), spread, spread,
+            pltpu.VMEM((size, chans), f32), pltpu.VMEM((states, chans), f32), held, held,
+            pltpu.VMEM((2 * size, states * 128), bf16), pltpu.VMEM((lanes, 2 * states * 128), bf16), order, order,
+        ],
+        compiler_params=pltpu.CompilerParams(vmem_limit_bytes=ROOM),
+        cost_estimate=about(38),
+        name="scan",
+    )(proj, values, gate, cut, grad_all.reshape(SEGS, steps, width_all), out_w, dt_weight, dt_weight_t, dt_bias, a_log_t, skip)
+    return (branch.reshape(total, width_all), gated.reshape(total, chans), d_gate.reshape(total, chans), *rest)
+
+
 def run_exit(
     starts, d_proj, value_part, pre, x_in, values, conv_w, x_w, d_gate, weight, hidden_all, scale, gain,
     d_dtw, d_alog_t, d_dtb, d_skip, low_cols, small_rows, span,
@@ -588,7 +849,7 @@
         functools.partial(exit_kernel, span, taps, low_cols),
         grid=(1 + total // size,),
         in_specs=[SCALARS, whole(total, lanes)] + [whole(total, chans)] * 4 + [
-            whole(taps, chans), whole(chans, lanes), rows(chans), whole(width, 2 * chans), rows(width), rows(1),
+            whole(taps, chans), whole(chans, lanes), rows(chans), whole(width, 2 * chans), rows(width), rows(128),
             whole(1, width), whole(*d_dtw.shape), whole(*d_alog_t.shape), whole(1, chans), whole(1, chans),
         ],
         out_specs=[rows(width), whole(width, chans), whole(small_rows, chans), whole(1, width)],
@@ -598,7 +859,7 @@
         ],
         scratch_shapes=[
             pltpu.VMEM((total + (taps - 1) * SEGS, chans), f32), pltpu.VMEM((SEGS, steps, chans), bf16),
-            pltpu.VMEM((chans, width), f32),
+            pltpu.VMEM((chans, width), f32), pltpu.VMEM((total + (taps - 1) * SEGS, lane_groups(chans)[1]), jnp.int32),
         ],
         compiler_params=pltpu.CompilerParams(vmem_limit_bytes=ROOM),
         cost_estimate=about(10 * total * chans / 262144),
@@ -622,7 +883,7 @@
         functools.partial(forward_kernel, rank, states, span),
         grid=(steps // span,),
         in_specs=[
-            whole(total, lanes), whole(total, chans), whole(total, 1), whole(rank, chans), whole(1, chans),
+            whole(total, lanes), whole(total, chans), whole(total, width), whole(rank, chans), whole(1, chans),
             whole(states, chans),
         ],
         out_specs=[
@@ -634,7 +895,9 @@
         ],
         scratch_shapes=[
             by_group, by_group, pltpu.VMEM((states, chans), f32), pltpu.VMEM((count, SEGS, width), f32),
-            pltpu.VMEM((slots, 2 * states, span * SEGS, 128), f32), pltpu.VMEM((lanes, 2 * states * 128), bf16),
+            pltpu.VMEM((groups, SEGS, width), f32),
+            pltpu.VMEM((slots, states, span * SEGS, 128), f32),
+            pltpu.VMEM((slots, states, span * SEGS, 128), f32), pltpu.VMEM((lanes, 2 * states * 128), bf16),
         ],
         compiler_params=pltpu.CompilerParams(vmem_limit_bytes=ROOM),
         cost_estimate=about(18 * total * chans / 262144),
@@ -656,7 +919,7 @@
         functools.partial(backward_kernel, rank, states, span),
         grid=(turns,),
         in_specs=[
-            whole(total, lanes), whole(total, chans), whole(total, 1), whole(total, chans), whole(groups, total, width),
+            whole(total, lanes), whole(total, chans), whole(total, width), whole(total, chans), whole(groups, total, width),
             whole(rank, chans), whole(chans, lanes), whole(1, chans), whole(states, chans), whole(1, chans),
             pl.BlockSpec((1, span + 1, count, SEGS, width), lambda t: (turns - 1 - t, 0, 0, 0, 0)),
         ],
@@ -667,10 +930,12 @@
             like(total, lanes, dtype=bf16), like(total, chans), like(rank, chans), like(1, chans), like(states, chans),
         ],
         scratch_shapes=[
-            by_group, by_group, by_group, by_group, pltpu.VMEM((states, chans), f32),
-            pltpu.VMEM((count, SEGS, width), f32), pltpu.VMEM((count, SEGS, width), f32),
-            pltpu.VMEM((slots, 2 * states, span * SEGS, 128), f32), pltpu.VMEM((span * SEGS, 2 * states * 128), f32),
-            pltpu.VMEM((lanes, 2 * states * 128), bf16), pltpu.VMEM((2 * states * 128, lanes), bf16),
+            by_group, by_group, by_group, pltpu.VMEM((states, chans), f32),
+            pltpu.VMEM((count, SEGS, width), f32), pltpu.VMEM((groups, SEGS, width), f32),
+            pltpu.VMEM((count, SEGS, width), f32),
+            pltpu.VMEM((slots, states, span * SEGS, 128), f32),
+            pltpu.VMEM((slots, states, span * SEGS, 128), f32), pltpu.VMEM((span * SEGS, 2 * states * 128), bf16),
+            pltpu.VMEM((lanes, 2 * states * 128), bf16), pltpu.VMEM((span * SEGS, lanes), f32),
         ],
         compiler_params=pltpu.CompilerParams(vmem_limit_bytes=ROOM),
         cost_estimate=about(22 * total * chans / 262144),
@@ -856,7 +1121,8 @@
     sizes = lengths[0]
     offsets = jnp.cumsum(sizes) - sizes
     where_in = context_place(offsets, jnp.arange(total, dtype=jnp.int32))
-    cut = ((where_in == 0) | (resets == 1)).astype(f32).reshape(SEGS, steps).T.reshape(total, 1)
+    cut = ((where_in == 0) | (resets == 1)).astype(bf16).reshape(SEGS, steps).T.reshape(total, 1)
+    cut = jnp.broadcast_to(cut, (total, lane_groups(chans)[1]))
     starts = offsets[None, :]
     conv_w = lax.dynamic_slice_in_dim(conv_weight, me * chans, chans, 0).T
     conv_b = lax.dynamic_slice_in_dim(conv_bias, me * chans, chans, 0)[None, :]
@@ -870,8 +1136,19 @@
 
     a_log_t = a_log.T
     dt_b, skip_row = dt_bias[None, :], skip[None, :]
-    y, hist, delta = run_forward(proj, values, cut, dt_weight, dt_b, a_log_t, states, span)
-    branch_part, gated, dy, d_gate, d_skip = run_gate(grad_all, out_weight, gate, values, y, skip_row, span)
+    dt_w_t = jnp.pad(dt_weight.T, ((0, 0), (0, lanes - rank)))
+    if total * chans * states <= 1 << 22 and chans % 128 == 0:
+        (
+            branch_part, gated, d_gate, d_part, value_part, d_dt_weight, d_dt_bias, d_a_log_t, d_skip,
+        ) = run_scan(
+            proj, values, gate, cut, grad_all, out_weight, dt_weight, dt_w_t, dt_b, a_log_t, skip_row, states, span
+        )
+    else:
+        y, hist, delta = run_forward(proj, values, cut, dt_weight, dt_b, a_log_t, states, span)
+        branch_part, gated, dy, d_gate, d_skip = run_gate(grad_all, out_weight, gate, values, y, skip_row, span)
+        d_part, value_part, d_dt_weight, d_dt_bias, d_a_log_t = run_backward(
+            proj, values, cut, dy, delta, dt_weight, dt_w_t, dt_b, a_log_t, skip_row, hist, states, span
+        )
     branch = lax.psum_scatter(branch_part, "ch", scatter_dimension=0, tiled=True)
     sides = width // chans
     out_share = chans // packs
@@ -884,14 +1161,9 @@
 
     early = owned_parts(jnp.concatenate([d_out, by_pack(d_in_gate)], axis=1), "ctx")
 
-    dt_w_t = jnp.pad(dt_weight.T, ((0, 0), (0, lanes - rank)))
-    d_part, value_part, d_dt_weight, d_dt_bias, d_a_log_t = run_backward(
-        proj, values, cut, dy, delta, dt_weight, dt_w_t, dt_b, a_log_t, skip_row, hist, states, span
-    )
-    early, d_part = lax.optimization_barrier((early, d_part))
     d_proj = sum_over_peers(d_part)
+    early, d_proj = lax.optimization_barrier((early, d_proj))
     early = tree_sum(early).astype(bf16)
-    branch, early, d_proj = lax.optimization_barrier((branch, early, d_proj))
     d_out = jnp.moveaxis(early[: out_share * sides].reshape(sides, out_share, chans), 0, 1).reshape(out_share, width)
     counts = (low_cols, rank, states, taps)
     small_rows = -(-(sum(counts) + 3) // (16 * packs)) * 16 * packs

time: 233 us -> 218 us (0.936)
  Pallas kernels: 73.7 us -> 60.6 us
    pallas_call x3 -> x1, Pallas kernels: 50.2 us -> 38 us  [run_scan(): pl.pallas_call(functools.partial(scan_kernel, rank, states, span), grid=(...]
    unnamed x48 -> x50, local copies, waits for them, and re-layouts: 4.76 us -> 4.11 us
  transfers between devices with their start and end apart: 37 -> 37, of which waited for: 25 -> 22; matrix products, arithmetic and copies ran while one was open for 6% -> 7% of each run, Pallas kernels for 22% -> 9%
where the time goes in v3:
time: 218 us; the launch traced here: 217 us
  waiting for transfers between devices  74.3 us (34%)
  Pallas kernels  60.6 us (28%)
  starting transfers between devices  47.5 us (22%)
  between operations  14.5 us (7%)
  local copies, waits for them, and re-layouts  14.1 us (6%)
  matrix products  3.23 us (1%)
  other arithmetic  2.98 us (1%)
    ppermute x31, waiting for transfers between devices, swap(): lax.ppermute(value, axis, [(i, i ^ mask) for i in range(lax.axis_size(axi...  56.4 us
    pallas_call x1, Pallas kernels, run_scan(): pl.pallas_call(functools.partial(scan_kernel, rank, states, span), grid=(...  38 us
    ppermute x31, starting transfers between devices, swap(): lax.ppermute(value, axis, [(i, i ^ mask) for i in range(lax.axis_size(axi...  37.4 us
    all_to_all x2, waiting for transfers between devices, to_peers(): return lax.all_to_all(blocks, 'ch', split_axis=0, concat_axis=0, tiled=True)  16.4 us
    pallas_call x1, Pallas kernels, run_exit(): pl.pallas_call(functools.partial(exit_kernel, span, taps, low_cols), grid...  10.3 us
    all_to_all x2, starting transfers between devices, to_peers(): return lax.all_to_all(blocks, 'ch', split_axis=0, concat_axis=0, tiled=True)  9.76 us
    pallas_call x1, Pallas kernels, run_entry(): pl.pallas_call(functools.partial(entry_kernel, span, taps, lanes), grid=(...  8.37 us
  transfers between devices with their start and end apart: 37, of which 22 were waited for; matrix products, arithmetic and copies ran while one was open for 7% of the time, Pallas kernels for 9%

profile of v3, /device:TPU:0, one launch (start us, length us, event | category | flops | bytes accessed | tf_op | source)
XLA Modules:
  0.0 217.1 jit_solution(10792933216854194212)
XLA Ops:
  9.4 6.3 %all-to-all-start = ((bf16[8,32,2,256]{3,2,1,0:T(2,128)(2,1)}), bf16[8,32,2,256]{3,2,1,0:T(2,128)(2,1)S(1)}, u32[]{:S(2)}, u32[]{:S(2)}) async-start(bf16[8,32,2,256]{3,2,1,0:T(2,128)(2,1)} %copy.72), calls=%async_computation | async-start | bytes 524288 | tf_op jit(solution)/shard_map/all_to_all | solution.py:997
  18.0 9.6 %all-to-all-done = bf16[8,32,2,256]{3,2,1,0:T(2,128)(2,1)S(1)} async-done(((bf16[8,32,2,256]{3,2,1,0:T(2,128)(2,1)}), bf16[8,32,2,256]{3,2,1,0:T(2,128)(2,1)S(1)}, u32[]{:S(2)}, u32[]{:S(2)}) %all-to-all-start) | async-done | bytes 262176 | tf_op jit(solution)/shard_map/all_to_all | solution.py:997
  28.5 1.5 collective-permute-start
  30.0 1.3 fusion.19.cw_ref
  31.4 1.3 dynamic_slice.78
  33.4 1.5 collective-permute-start.1
  35.7 9.4 %collective-permute-done.1 = bf16[8,32,512]{2,1,0:T(8,128)(2,1)S(1)} collective-permute-done((bf16[8,32,512]{2,1,0:T(8,128)(2,1)}, bf16[8,32,512]{2,1,0:T(8,128)(2,1)S(1)}, u32[]{:S(2)}, u32[]{:S(2)}) %collective-permute-start.1) | collective-permute-done | bytes 262176 | tf_op jit(solution)/shard_map/ppermute | solution.py:954
  46.2 8.4 %entry.1 = (bf16[8,128,1024]{2,1,0:T(8,128)(2,1)}, f32[8,128,128]{2,1,0:T(8,128)}, bf16[1024,256]{1,0:T(8,128)(2,1)}, bf16[1024,256]{1,0:T(8,128)(2,1)}, bf16[10...) custom-call(s32[1,4]{1,0:T(1,128)} %bitcast_subtract_fusion.1.starts_ref, ...), custom_call_target="tpu_custom_call" | custom-call | flops 6600000000 | bytes 1048576 | tf_op jit(solution)/shard_map/entry/pallas_call | solution.py:746
  55.6 1.3 collective-permute-done.3
  57.9 1.3 collective-permute-start.4
  59.2 4.6 %collective-permute-start.5 = (bf16[128,128]{1,0:T(8,128)(2,1)S(1)}, bf16[128,128]{1,0:T(8,128)(2,1)S(1)}, u32[]{:S(2)}, u32[]{:S(2)}) collective-permute-start(bf16[128,128]{1,0:T(8,128)(2,1)S(1)} %get-tuple-element.118), channel_id=1, source_target_pairs={{0,4},{1,5},{2,6},{3,7},{4,0},{5,1},{6,2},{7,3},{8,12},{9,13},{10,... | collective-permute-start | bytes 98312 | tf_op jit(solution)/shard_map/ppermute | solution.py:954
  63.9 5.1 %collective-permute-done.5 = bf16[128,128]{1,0:T(8,128)(2,1)S(1)} collective-permute-done((bf16[128,128]{1,0:T(8,128)(2,1)S(1)}, bf16[128,128]{1,0:T(8,128)(2,1)S(1)}, u32[]{:S(2)}, u32[]{:S(2)}) %collective-permute-start.5) | collective-permute-done | bytes 32800 | tf_op jit(solution)/shard_map/ppermute | solution.py:954
  69.0 1.1 collective-permute-done.6
  70.2 2.2 %collective-permute-start.7 = (bf16[128,128]{1,0:T(8,128)(2,1)S(1)}, bf16[128,128]{1,0:T(8,128)(2,1)S(1)}, u32[]{:S(2)}, u32[]{:S(2)}) collective-permute-start(bf16[128,128]{1,0:T(8,128)(2,1)S(1)} %get-tuple-element.103), channel_id=1, source_target_pairs={{0,2},{1,3},{2,0},{3,1},{4,6},{5,7},{6,4},{7,5},{8,10},{9,11},{10,... | collective-permute-start | bytes 98312 | tf_op jit(solution)/shard_map/ppermute | solution.py:954
  74.3 1.5 collective-permute-start.9
  75.9 2.6 %collective-permute-done.8 = bf16[128,128]{1,0:T(8,128)(2,1)S(1)} collective-permute-done((bf16[128,128]{1,0:T(8,128)(2,1)S(1)}, bf16[128,128]{1,0:T(8,128)(2,1)S(1)}, u32[]{:S(2)}, u32[]{:S(2)}) %collective-permute-start.8) | collective-permute-done | bytes 32800 | tf_op jit(solution)/shard_map/ppermute | solution.py:954
  78.4 1.6 collective-permute-done.9
  80.1 1.3 collective-permute-done.10
  82.4 38.0 %scan.1 = (bf16[8,128,1024]{2,1,0:T(8,128)(2,1)}, bf16[8,128,256]{2,1,0:T(8,128)(2,1)}, bf16[8,128,256]{2,1,0:T(8,128)(2,1)}, bf16[1024,128]{1,0:T(8,128)(2,1)},...) custom-call(bf16[1024,128]{1,0:T(8,128)(2,1)} %bitcast.181, ...), custom_call_target="tpu_custom_call" | custom-call | flops 41799999488 | bytes 1048576 | tf_op jit(solution)/shard_map/scan/pallas_call | solution.py:806
  121.5 2.5 %fusion = bf16[1024,256]{1,0:T(8,128)(2,1)S(1)} fusion(bf16[8,128,1024]{2,1,0:T(8,128)(2,1)} %get-tuple-element.60, bf16[8,128,256]{2,1,0:T(8,128)(2,1)S(1)} %copy-done.22), kind=kOutput, calls=%fused_computation.9 | convolution fusion | flops 537133056 | bytes 3145728 | tf_op jit(solution)/shard_map/dot_general | solution.py:38
  124.4 1.9 collective-permute-start.16
  126.3 2.3 %collective-permute-start.17 = (bf16[128,128]{1,0:T(8,128)(2,1)S(1)}, bf16[128,128]{1,0:T(8,128)(2,1)S(1)}, u32[]{:S(2)}, u32[]{:S(2)}) collective-permute-start(bf16[128,128]{1,0:T(8,128)(2,1)S(1)} %get-tuple-element.114), channel_id=1, source_target_pairs={{0,6},{1,7},{2,4},{3,5},{4,2},{5,3},{6,0},{7,1},{8,14},{9,15},{10,... | collective-permute-start | bytes 98312 | tf_op jit(solution)/shard_map/ppermute | solution.py:954
  129.8 1.8 collective-permute-done.16
  131.6 1.0 collective-permute-done.17
  132.7 1.7 collective-permute-start.18
  134.6 1.6 collective-permute-start.12
  136.2 1.9 collective-permute-start.13
  138.7 2.2 collective-permute-start.20
  140.8 4.3 %collective-permute-done.19 = bf16[128,128]{1,0:T(8,128)(2,1)S(1)} collective-permute-done((bf16[128,128]{1,0:T(8,128)(2,1)S(1)}, bf16[128,128]{1,0:T(8,128)(2,1)S(1)}, u32[]{:S(2)}, u32[]{:S(2)}) %collective-permute-start.19) | collective-permute-done | bytes 32800 | tf_op jit(solution)/shard_map/ppermute | solution.py:954
  145.4 1.3 collective-permute-done.21
  146.7 1.9 collective-permute-done.13
  148.5 10.3 %exit.1 = (bf16[1024,1024]{1,0:T(8,128)(2,1)}, bf16[1024,256]{1,0:T(8,128)(2,1)}, bf16[192,256]{1,0:T(8,128)(2,1)}, f32[1,1024]{1,0:T(1,128)}) custom-call(s32[1,4]{1,0:T(1,128)} %bitcast_subtract_fusion.1.starts_ref, bf16[1024,128]{1,0:T(8,128)(2,1)} %bitcast.180, f32[1024,256]{1,0:T(8,128)} %get-tuple-element.64.part_ref, ...), custom_call_target="tpu_custom_call" | custom-call | flops 11000000512 | bytes 1048576 | tf_op jit(solution)/shard_map/exit/pallas_call | solution.py:848
  161.0 1.4 collective-permute-start.23
  162.5 1.2 collective-permute-start.24
  164.0 3.0 %collective-permute-done.22 = bf16[320,256]{1,0:T(8,128)(2,1)S(1)} collective-permute-done((bf16[320,256]{1,0:T(8,128)(2,1)S(1)}, bf16[320,256]{1,0:T(8,128)(2,1)S(1)}, u32[]{:S(2)}, u32[]{:S(2)}) %collective-permute-start.22) | collective-permute-done | bytes 163872 | tf_op jit(solution)/shard_map/ppermute | solution.py:954
  167.0 2.9 %collective-permute-done.23 = bf16[320,256]{1,0:T(8,128)(2,1)S(1)} collective-permute-done((bf16[320,256]{1,0:T(8,128)(2,1)S(1)}, bf16[320,256]{1,0:T(8,128)(2,1)S(1)}, u32[]{:S(2)}, u32[]{:S(2)}) %collective-permute-start.23) | collective-permute-done | bytes 163872 | tf_op jit(solution)/shard_map/ppermute | solution.py:954
  170.8 3.4 %all-to-all-start.1 = ((bf16[8,80,256]{2,1,0:T(8,128)(2,1)}), bf16[8,80,256]{2,1,0:T(8,128)(2,1)S(1)}, u32[]{:S(2)}, u32[]{:S(2)}) async-start(bf16[8,80,256]{2,1,0:T(8,128)(2,1)} %fusion.2), calls=%async_computation.1 | async-start | bytes 655360 | tf_op jit(solution)/shard_map/all_to_all | solution.py:997
  174.2 1.1 collective-permute-start.25
  176.3 1.5 collective-permute-start.27
  177.8 2.8 %collective-permute-done.25.refs_5_ = bf16[64,1024]{1,0:T(8,128)(2,1)S(1)} collective-permute-done((bf16[64,1024]{1,0:T(8,128)(2,1)S(1)}, bf16[64,1024]{1,0:T(8,128)(2,1)S(1)}, u32[]{:S(2)}, u32[]{:S(2)}) %collective-permute-start.25) | collective-permute-done | bytes 131104 | tf_op jit(solution)/shard_map/ppermute | solution.py:954
  180.6 3.0 %collective-permute-done.26.refs_6_ = bf16[64,1024]{1,0:T(8,128)(2,1)S(1)} collective-permute-done((bf16[64,1024]{1,0:T(8,128)(2,1)S(1)}, bf16[64,1024]{1,0:T(8,128)(2,1)S(1)}, u32[]{:S(2)}, u32[]{:S(2)}) %collective-permute-start.26) | collective-permute-done | bytes 131104 | tf_op jit(solution)/shard_map/ppermute | solution.py:954
  183.6 6.8 %all-to-all-done.1.refs_8_ = bf16[8,80,256]{2,1,0:T(8,128)(2,1)S(1)} async-done(((bf16[8,80,256]{2,1,0:T(8,128)(2,1)}), bf16[8,80,256]{2,1,0:T(8,128)(2,1)S(1)}, u32[]{:S(2)}, u32[]{:S(2)}) %all-to-all-start.1) | async-done | bytes 327712 | tf_op jit(solution)/shard_map/all_to_all | solution.py:997
  190.4 1.2 collective-permute-start.28
  191.6 1.1 collective-permute-start.29
  192.6 1.3 collective-permute-start.30
  194.0 6.2 %collective-permute-done.28.refs_1_ = bf16[560,256]{1,0:T(8,128)(2,1)S(1)} collective-permute-done((bf16[560,256]{1,0:T(8,128)(2,1)S(1)}, bf16[560,256]{1,0:T(8,128)(2,1)S(1)}, u32[]{:S(2)}, u32[]{:S(2)}) %collective-permute-start.28) | collective-permute-done | bytes 286752 | tf_op jit(solution)/shard_map/ppermute | solution.py:954
  200.2 5.6 %collective-permute-done.29.refs_2_ = bf16[560,256]{1,0:T(8,128)(2,1)S(1)} collective-permute-done((bf16[560,256]{1,0:T(8,128)(2,1)S(1)}, bf16[560,256]{1,0:T(8,128)(2,1)S(1)}, u32[]{:S(2)}, u32[]{:S(2)}) %collective-permute-start.29) | collective-permute-done | bytes 286752 | tf_op jit(solution)/shard_map/ppermute | solution.py:954
  206.6 4.0 %finish.1 = (bf16[128,1024]{1,0:T(8,128)(2,1)}, bf16[128,1024]{1,0:T(8,128)(2,1)}, f32[1,128]{1,0:T(1,128)}, f32[128,4096]{1,0:T(8,128)}, f32[4,256]{1,0:T(4,128...) custom-call(s32[1]{0:T(128)} %bitcast.me_ref, ...), custom_call_target="tpu_custom_call" | custom-call | flops 4400000000 | bytes 1048576 | tf_op jit(solution)/shard_map/finish/pallas_call | solution.py:1056
  (154 shorter events, 21.7 us)
Async XLA Ops:
  7.2 9.3 %copy-start.21 = (s32[1,4]{1,0:T(1,128)S(1)}, s32[1,4]{1,0:T(1,128)}, u32[]{:S(2)}) copy-start(s32[1,4]{1,0:T(1,128)} %param.25) | copy-start | bytes 52
  7.2 38.0 %all-gather.3.cloned.1.call-start = ((), (), s32[]{:S(2)}) async-start(), calls=%async_computation.4 | async-start | bytes 2359296 | tf_op jit(solution)/shard_map/all_gather | solution.py:1108
  9.4 18.2 %all-to-all-start = ((bf16[8,32,2,256]{3,2,1,0:T(2,128)(2,1)}), bf16[8,32,2,256]{3,2,1,0:T(2,128)(2,1)S(1)}, u32[]{:S(2)}, u32[]{:S(2)}) async-start(bf16[8,32,2,256]{3,2,1,0:T(2,128)(2,1)} %copy.72), calls=%async_computation | async-start | bytes 524288 | tf_op jit(solution)/shard_map/all_to_all | solution.py:997
  15.7 65.7 %all-gather.5.cloned.1.call-start = ((), (), s32[]{:S(2)}) async-start(), calls=%async_computation.5 | async-start | bytes 2359296 | tf_op jit(solution)/shard_map/all_gather | solution.py:1115
  16.5 189.4 %reduce-scatter.3.cloned.1.call-start = ((), (), s32[]{:S(2)}) async-start(), calls=%async_computation.6 | async-start | bytes 2359296 | tf_op jit(solution)/shard_map/reduce_scatter | solution.py:1152
  28.5 7.2 %collective-permute-start = (bf16[8,32,512]{2,1,0:T(8,128)(2,1)}, bf16[8,32,512]{2,1,0:T(8,128)(2,1)S(1)}, u32[]{:S(2)}, u32[]{:S(2)}) collective-permute-start(bf16[8,32,512]{2,1,0:T(8,128)(2,1)} %reshape.149), channel_id=1, source_target_pairs={{0,8},{8,0},{16,24},{24,16},{1,9},{9,1},{17,25},{25,17},{2,10},{10... | collective-permute-start | bytes 786440 | tf_op jit(solution)/shard_map/ppermute | solution.py:954
  33.4 11.8 %collective-permute-start.1 = (bf16[8,32,512]{2,1,0:T(8,128)(2,1)}, bf16[8,32,512]{2,1,0:T(8,128)(2,1)S(1)}, u32[]{:S(2)}, u32[]{:S(2)}) collective-permute-start(bf16[8,32,512]{2,1,0:T(8,128)(2,1)} %reshape.149), channel_id=1, source_target_pairs={{0,16},{8,24},{16,0},{24,8},{1,17},{9,25},{17,1},{25,9},{2,18},{10... | collective-permute-start | bytes 786440 | tf_op jit(solution)/shard_map/ppermute | solution.py:954
  34.9 10.3 %collective-permute-start.2 = (bf16[8,32,512]{2,1,0:T(8,128)(2,1)}, bf16[8,32,512]{2,1,0:T(8,128)(2,1)S(1)}, u32[]{:S(2)}, u32[]{:S(2)}) collective-permute-start(bf16[8,32,512]{2,1,0:T(8,128)(2,1)} %reshape.149), channel_id=1, source_target_pairs={{0,24},{8,16},{16,8},{24,0},{1,25},{9,17},{17,9},{25,1},{2,26},{10... | collective-permute-start | bytes 786440 | tf_op jit(solution)/shard_map/ppermute | solution.py:954
  46.2 26.3 %copy-start.14 = (s32[1024]{0:T(1024)S(1)}, s32[1024]{0:T(1024)}, u32[]{:S(2)}) copy-start(s32[1024]{0:T(1024)} %param.26) | copy-start | bytes 12292
  46.2 26.5 %copy-start.12 = (bf16[64,256]{1,0:T(8,128)(2,1)S(1)}, bf16[64,256]{1,0:T(8,128)(2,1)}, u32[]{:S(2)}) copy-start(bf16[64,256]{1,0:T(8,128)(2,1)} %dtw_ref.1) | copy-start | bytes 98308
  55.5 1.4 collective-permute-start.3
  57.9 6.1 %collective-permute-start.4 = (bf16[128,128]{1,0:T(8,128)(2,1)S(1)}, bf16[128,128]{1,0:T(8,128)(2,1)S(1)}, u32[]{:S(2)}, u32[]{:S(2)}) collective-permute-start(bf16[128,128]{1,0:T(8,128)(2,1)S(1)} %get-tuple-element.116), channel_id=1, source_target_pairs={{0,2},{1,3},{2,0},{3,1},{4,6},{5,7},{6,4},{7,5},{8,10},{9,11},{10,... | collective-permute-start | bytes 98312 | tf_op jit(solution)/shard_map/ppermute | solution.py:954
  59.2 9.9 %collective-permute-start.5 = (bf16[128,128]{1,0:T(8,128)(2,1)S(1)}, bf16[128,128]{1,0:T(8,128)(2,1)S(1)}, u32[]{:S(2)}, u32[]{:S(2)}) collective-permute-start(bf16[128,128]{1,0:T(8,128)(2,1)S(1)} %get-tuple-element.118), channel_id=1, source_target_pairs={{0,4},{1,5},{2,6},{3,7},{4,0},{5,1},{6,2},{7,3},{8,12},{9,13},{10,... | collective-permute-start | bytes 98312 | tf_op jit(solution)/shard_map/ppermute | solution.py:954
  63.8 6.4 %collective-permute-start.6 = (bf16[128,128]{1,0:T(8,128)(2,1)S(1)}, bf16[128,128]{1,0:T(8,128)(2,1)S(1)}, u32[]{:S(2)}, u32[]{:S(2)}) collective-permute-start(bf16[128,128]{1,0:T(8,128)(2,1)S(1)} %get-tuple-element.117), channel_id=1, source_target_pairs={{0,6},{1,7},{2,4},{3,5},{4,2},{5,3},{6,0},{7,1},{8,14},{9,15},{10,... | collective-permute-start | bytes 98312 | tf_op jit(solution)/shard_map/ppermute | solution.py:954
  70.2 5.6 %collective-permute-start.7 = (bf16[128,128]{1,0:T(8,128)(2,1)S(1)}, bf16[128,128]{1,0:T(8,128)(2,1)S(1)}, u32[]{:S(2)}, u32[]{:S(2)}) collective-permute-start(bf16[128,128]{1,0:T(8,128)(2,1)S(1)} %get-tuple-element.103), channel_id=1, source_target_pairs={{0,2},{1,3},{2,0},{3,1},{4,6},{5,7},{6,4},{7,5},{8,10},{9,11},{10,... | collective-permute-start | bytes 98312 | tf_op jit(solution)/shard_map/ppermute | solution.py:954
  73.5 5.0 %collective-permute-start.8 = (bf16[128,128]{1,0:T(8,128)(2,1)S(1)}, bf16[128,128]{1,0:T(8,128)(2,1)S(1)}, u32[]{:S(2)}, u32[]{:S(2)}) collective-permute-start(bf16[128,128]{1,0:T(8,128)(2,1)S(1)} %get-tuple-element.103), channel_id=1, source_target_pairs={{0,4},{1,5},{2,6},{3,7},{4,0},{5,1},{6,2},{7,3},{8,12},{9,13},{10,... | collective-permute-start | bytes 98312 | tf_op jit(solution)/shard_map/ppermute | solution.py:954
  74.3 5.7 %collective-permute-start.9 = (bf16[128,128]{1,0:T(8,128)(2,1)S(1)}, bf16[128,128]{1,0:T(8,128)(2,1)S(1)}, u32[]{:S(2)}, u32[]{:S(2)}) collective-permute-start(bf16[128,128]{1,0:T(8,128)(2,1)S(1)} %get-tuple-element.103), channel_id=1, source_target_pairs={{0,6},{1,7},{2,4},{3,5},{4,2},{5,3},{6,0},{7,1},{8,14},{9,15},{10,... | collective-permute-start | bytes 98312 | tf_op jit(solution)/shard_map/ppermute | solution.py:954
  80.0 1.3 collective-permute-start.10
  120.4 85.5 %reduce-scatter.5.cloned.1.call-start = ((), (), s32[]{:S(2)}) async-start(), calls=%async_computation.7 | async-start | bytes 2359296 | tf_op jit(solution)/shard_map/reduce_scatter | solution.py:1174
  121.3 2.7 %collective-permute-start.14 = (bf16[4,128,128]{2,1,0:T(8,128)(2,1)S(1)}, bf16[4,128,128]{2,1,0:T(8,128)(2,1)S(1)}, u32[]{:S(2)}, u32[]{:S(2)}) collective-permute-start(bf16[4,128,128]{2,1,0:T(8,128)(2,1)S(1)} %dynamic-slice_bitcast_fusion.3), channel_id=1, source_target_pairs={{0,1},{1,0},{2,3},{3,2},{4,5},{5,4},{6,7},{7,6},{8,9},{9,8},{10,11... | collective-permute-start | bytes 393224 | tf_op jit(solution)/shard_map/ppermute | solution.py:954
  121.5 7.1 %copy-start.1 = (bf16[1024,1024]{1,0:T(8,128)(2,1)S(1)}, bf16[1024,1024]{1,0:T(8,128)(2,1)}, u32[]{:S(2)}) copy-start(bf16[1024,1024]{1,0:T(8,128)(2,1)} %all-gather.5.cloned.1.call-done) | copy-start | bytes 6291460
  121.5 7.1 %copy-start.5 = (bf16[8,128,256]{2,1,0:T(8,128)(2,1)S(1)}, bf16[8,128,256]{2,1,0:T(8,128)(2,1)}, u32[]{:S(2)}) copy-start(bf16[8,128,256]{2,1,0:T(8,128)(2,1)} %get-tuple-element.59) | copy-start | bytes 1572868
  124.1 5.7 %collective-permute-start.15 = (bf16[128,128]{1,0:T(8,128)(2,1)S(1)}, bf16[128,128]{1,0:T(8,128)(2,1)S(1)}, u32[]{:S(2)}, u32[]{:S(2)}) collective-permute-start(bf16[128,128]{1,0:T(8,128)(2,1)S(1)} %get-tuple-element.113), channel_id=1, source_target_pairs={{0,2},{1,3},{2,0},{3,1},{4,6},{5,7},{6,4},{7,5},{8,10},{9,11},{10,... | collective-permute-start | bytes 98312 | tf_op jit(solution)/shard_map/ppermute | solution.py:954
  124.4 7.2 %collective-permute-start.16 = (bf16[128,128]{1,0:T(8,128)(2,1)S(1)}, bf16[128,128]{1,0:T(8,128)(2,1)S(1)}, u32[]{:S(2)}, u32[]{:S(2)}) collective-permute-start(bf16[128,128]{1,0:T(8,128)(2,1)S(1)} %get-tuple-element.115), channel_id=1, source_target_pairs={{0,4},{1,5},{2,6},{3,7},{4,0},{5,1},{6,2},{7,3},{8,12},{9,13},{10,... | collective-permute-start | bytes 98312 | tf_op jit(solution)/shard_map/ppermute | solution.py:954
  126.3 6.4 %collective-permute-start.17 = (bf16[128,128]{1,0:T(8,128)(2,1)S(1)}, bf16[128,128]{1,0:T(8,128)(2,1)S(1)}, u32[]{:S(2)}, u32[]{:S(2)}) collective-permute-start(bf16[128,128]{1,0:T(8,128)(2,1)S(1)} %get-tuple-element.114), channel_id=1, source_target_pairs={{0,6},{1,7},{2,4},{3,5},{4,2},{5,3},{6,0},{7,1},{8,14},{9,15},{10,... | collective-permute-start | bytes 98312 | tf_op jit(solution)/shard_map/ppermute | solution.py:954
  132.7 5.9 %collective-permute-start.18 = (bf16[128,128]{1,0:T(8,128)(2,1)S(1)}, bf16[128,128]{1,0:T(8,128)(2,1)S(1)}, u32[]{:S(2)}, u32[]{:S(2)}) collective-permute-start(bf16[128,128]{1,0:T(8,128)(2,1)S(1)} %get-tuple-element.101), channel_id=1, source_target_pairs={{0,2},{1,3},{2,0},{3,1},{4,6},{5,7},{6,4},{7,5},{8,10},{9,11},{10,... | collective-permute-start | bytes 98312 | tf_op jit(solution)/shard_map/ppermute | solution.py:954
  134.5 12.1 %collective-permute-start.11 = (bf16[512,256]{1,0:T(8,128)(2,1)S(1)}, bf16[512,256]{1,0:T(8,128)(2,1)S(1)}, u32[]{:S(2)}, u32[]{:S(2)}) collective-permute-start(bf16[512,256]{1,0:T(8,128)(2,1)S(1)} %get-tuple-element.106), channel_id=1, source_target_pairs={{0,8},{8,0},{16,24},{24,16},{1,9},{9,1},{17,25},{25,17},{2,10},{10... | collective-permute-start | bytes 786440 | tf_op jit(solution)/shard_map/ppermute | solution.py:954
  134.6 12.1 %collective-permute-start.12 = (bf16[512,256]{1,0:T(8,128)(2,1)S(1)}, bf16[512,256]{1,0:T(8,128)(2,1)S(1)}, u32[]{:S(2)}, u32[]{:S(2)}) collective-permute-start(bf16[512,256]{1,0:T(8,128)(2,1)S(1)} %get-tuple-element.107), channel_id=1, source_target_pairs={{0,16},{8,24},{16,0},{24,8},{1,17},{9,25},{17,1},{25,9},{2,18},{10... | collective-permute-start | bytes 786440 | tf_op jit(solution)/shard_map/ppermute | solution.py:954
  136.2 12.4 %collective-permute-start.13 = (bf16[512,256]{1,0:T(8,128)(2,1)S(1)}, bf16[512,256]{1,0:T(8,128)(2,1)S(1)}, u32[]{:S(2)}, u32[]{:S(2)}) collective-permute-start(bf16[512,256]{1,0:T(8,128)(2,1)S(1)} %get-tuple-element.104), channel_id=1, source_target_pairs={{0,24},{8,16},{16,8},{24,0},{1,25},{9,17},{17,9},{25,1},{2,26},{10... | collective-permute-start | bytes 786440 | tf_op jit(solution)/shard_map/ppermute | solution.py:954
  138.1 7.1 %collective-permute-start.19 = (bf16[128,128]{1,0:T(8,128)(2,1)S(1)}, bf16[128,128]{1,0:T(8,128)(2,1)S(1)}, u32[]{:S(2)}, u32[]{:S(2)}) collective-permute-start(bf16[128,128]{1,0:T(8,128)(2,1)S(1)} %get-tuple-element.101), channel_id=1, source_target_pairs={{0,4},{1,5},{2,6},{3,7},{4,0},{5,1},{6,2},{7,3},{8,12},{9,13},{10,... | collective-permute-start | bytes 98312 | tf_op jit(solution)/shard_map/ppermute | solution.py:954
  138.7 6.6 %collective-permute-start.20 = (bf16[128,128]{1,0:T(8,128)(2,1)S(1)}, bf16[128,128]{1,0:T(8,128)(2,1)S(1)}, u32[]{:S(2)}, u32[]{:S(2)}) collective-permute-start(bf16[128,128]{1,0:T(8,128)(2,1)S(1)} %get-tuple-element.101), channel_id=1, source_target_pairs={{0,6},{1,7},{2,4},{3,5},{4,2},{5,3},{6,0},{7,1},{8,14},{9,15},{10,... | collective-permute-start | bytes 98312 | tf_op jit(solution)/shard_map/ppermute | solution.py:954
  145.3 1.4 collective-permute-start.21
  160.1 6.9 %collective-permute-start.22 = (bf16[320,256]{1,0:T(8,128)(2,1)S(1)}, bf16[320,256]{1,0:T(8,128)(2,1)S(1)}, u32[]{:S(2)}, u32[]{:S(2)}) collective-permute-start(bf16[320,256]{1,0:T(8,128)(2,1)S(1)} %get-tuple-element.108), channel_id=1, source_target_pairs={{0,8},{8,0},{16,24},{24,16},{1,9},{9,1},{17,25},{25,17},{2,10},{10... | collective-permute-start | bytes 491528 | tf_op jit(solution)/shard_map/ppermute | solution.py:954
  161.0 8.8 %collective-permute-start.23 = (bf16[320,256]{1,0:T(8,128)(2,1)S(1)}, bf16[320,256]{1,0:T(8,128)(2,1)S(1)}, u32[]{:S(2)}, u32[]{:S(2)}) collective-permute-start(bf16[320,256]{1,0:T(8,128)(2,1)S(1)} %get-tuple-element.110), channel_id=1, source_target_pairs={{0,16},{8,24},{16,0},{24,8},{1,17},{9,25},{17,1},{25,9},{2,18},{10... | collective-permute-start | bytes 491528 | tf_op jit(solution)/shard_map/ppermute | solution.py:954
  162.5 7.4 %collective-permute-start.24 = (bf16[320,256]{1,0:T(8,128)(2,1)S(1)}, bf16[320,256]{1,0:T(8,128)(2,1)S(1)}, u32[]{:S(2)}, u32[]{:S(2)}) collective-permute-start(bf16[320,256]{1,0:T(8,128)(2,1)S(1)} %get-tuple-element.109), channel_id=1, source_target_pairs={{0,24},{8,16},{16,8},{24,0},{1,25},{9,17},{17,9},{25,1},{2,26},{10... | collective-permute-start | bytes 491528 | tf_op jit(solution)/shard_map/ppermute | solution.py:954
  164.0 42.0 %copy-start.10 = (bf16[8,8,4,256]{3,1,2,0:T(8,128)(2,1)}, bf16[8,8,4,256]{3,1,2,0:T(8,128)(2,1)S(1)}, u32[]{:S(2)}) copy-start(bf16[8,8,4,256]{3,1,2,0:T(8,128)(2,1)S(1)} %copy.89) | copy-start | bytes 393220
  170.8 19.5 %all-to-all-start.1 = ((bf16[8,80,256]{2,1,0:T(8,128)(2,1)}), bf16[8,80,256]{2,1,0:T(8,128)(2,1)S(1)}, u32[]{:S(2)}, u32[]{:S(2)}) async-start(bf16[8,80,256]{2,1,0:T(8,128)(2,1)} %fusion.2), calls=%async_computation.1 | async-start | bytes 655360 | tf_op jit(solution)/shard_map/all_to_all | solution.py:997
  174.2 6.4 %collective-permute-start.25 = (bf16[64,1024]{1,0:T(8,128)(2,1)S(1)}, bf16[64,1024]{1,0:T(8,128)(2,1)S(1)}, u32[]{:S(2)}, u32[]{:S(2)}) collective-permute-start(bf16[64,1024]{1,0:T(8,128)(2,1)S(1)} %bitcast.183), channel_id=1, source_target_pairs={{0,8},{8,0},{16,24},{24,16},{1,9},{9,1},{17,25},{25,17},{2,10},{10... | collective-permute-start | bytes 393224 | tf_op jit(solution)/shard_map/ppermute | solution.py:954
  175.3 8.3 %collective-permute-start.26 = (bf16[64,1024]{1,0:T(8,128)(2,1)S(1)}, bf16[64,1024]{1,0:T(8,128)(2,1)S(1)}, u32[]{:S(2)}, u32[]{:S(2)}) collective-permute-start(bf16[64,1024]{1,0:T(8,128)(2,1)S(1)} %bitcast.184), channel_id=1, source_target_pairs={{0,16},{8,24},{16,0},{24,8},{1,17},{9,25},{17,1},{25,9},{2,18},{10... | collective-permute-start | bytes 393224 | tf_op jit(solution)/shard_map/ppermute | solution.py:954
  176.3 7.3 %collective-permute-start.27 = (bf16[64,1024]{1,0:T(8,128)(2,1)S(1)}, bf16[64,1024]{1,0:T(8,128)(2,1)S(1)}, u32[]{:S(2)}, u32[]{:S(2)}) collective-permute-start(bf16[64,1024]{1,0:T(8,128)(2,1)S(1)} %bitcast.185), channel_id=1, source_target_pairs={{0,24},{8,16},{16,8},{24,0},{1,25},{9,17},{17,9},{25,1},{2,26},{10... | collective-permute-start | bytes 393224 | tf_op jit(solution)/shard_map/ppermute | solution.py:954
  180.6 25.3 %copy-start.18 = (bf16[64,1024]{1,0:T(8,128)(2,1)}, bf16[64,1024]{1,0:T(8,128)(2,1)S(1)}, u32[]{:S(2)}) copy-start(bf16[64,1024]{1,0:T(8,128)(2,1)S(1)} %collective-permute-done.25.refs_5_) | copy-start | bytes 393220
  183.6 22.3 %copy-start.19 = (bf16[64,1024]{1,0:T(8,128)(2,1)}, bf16[64,1024]{1,0:T(8,128)(2,1)S(1)}, u32[]{:S(2)}) copy-start(bf16[64,1024]{1,0:T(8,128)(2,1)S(1)} %collective-permute-done.26.refs_6_) | copy-start | bytes 393220
  183.6 22.4 %copy-start.20 = (bf16[64,1024]{1,0:T(8,128)(2,1)}, bf16[64,1024]{1,0:T(8,128)(2,1)S(1)}, u32[]{:S(2)}) copy-start(bf16[64,1024]{1,0:T(8,128)(2,1)S(1)} %collective-permute-done.27.refs_7_) | copy-start | bytes 393220
  190.3 15.6 %copy-start.2 = (bf16[8,80,256]{2,1,0:T(8,128)(2,1)}, bf16[8,80,256]{2,1,0:T(8,128)(2,1)S(1)}, u32[]{:S(2)}) copy-start(bf16[8,80,256]{2,1,0:T(8,128)(2,1)S(1)} %all-to-all-done.1.refs_8_) | copy-start | bytes 983044
  190.4 15.6 %copy-start.6 = (bf16[560,256]{1,0:T(8,128)(2,1)}, bf16[560,256]{1,0:T(8,128)(2,1)S(1)}, u32[]{:S(2)}) copy-start(bf16[560,256]{1,0:T(8,128)(2,1)S(1)} %pad_maximum_fusion.1.refs_0_) | copy-start | bytes 860164
  190.4 9.8 %collective-permute-start.28 = (bf16[560,256]{1,0:T(8,128)(2,1)S(1)}, bf16[560,256]{1,0:T(8,128)(2,1)S(1)}, u32[]{:S(2)}, u32[]{:S(2)}) collective-permute-start(bf16[560,256]{1,0:T(8,128)(2,1)S(1)} %pad_maximum_fusion.1.refs_0_), channel_id=1, source_target_pairs={{0,8},{8,0},{16,24},{24,16},{1,9},{9,1},{17,25},{25,17},{2,10},{10... | collective-permute-start | bytes 860168 | tf_op jit(solution)/shard_map/ppermute | solution.py:954
  191.6 14.3 %collective-permute-start.29 = (bf16[560,256]{1,0:T(8,128)(2,1)S(1)}, bf16[560,256]{1,0:T(8,128)(2,1)S(1)}, u32[]{:S(2)}, u32[]{:S(2)}) collective-permute-start(bf16[560,256]{1,0:T(8,128)(2,1)S(1)} %pad_maximum_fusion.1.refs_0_), channel_id=1, source_target_pairs={{0,16},{8,24},{16,0},{24,8},{1,17},{9,25},{17,1},{25,9},{2,18},{10... | collective-permute-start | bytes 860168 | tf_op jit(solution)/shard_map/ppermute | solution.py:954
  192.6 13.2 %collective-permute-start.30 = (bf16[560,256]{1,0:T(8,128)(2,1)S(1)}, bf16[560,256]{1,0:T(8,128)(2,1)S(1)}, u32[]{:S(2)}, u32[]{:S(2)}) collective-permute-start(bf16[560,256]{1,0:T(8,128)(2,1)S(1)} %pad_maximum_fusion.1.refs_0_), channel_id=1, source_target_pairs={{0,24},{8,16},{16,8},{24,0},{1,25},{9,17},{17,9},{25,1},{2,26},{10... | collective-permute-start | bytes 860168 | tf_op jit(solution)/shard_map/ppermute | solution.py:954
  (12 other events, 17.7 us)
Sparse Core Ops, SparseCore 0:
  9.6 34.1 all-gather.2
  45.5 31.4 all-gather.4
  120.5 36.1 reduce-scatter.2
  159.4 38.3 reduce-scatter.4

commit v4 on v3

--- a/solution.py
+++ b/solution.py
@@ -86,60 +86,80 @@
     return jnp.concatenate([ref[g, rows, :] for g in range(groups)], axis=1) if groups > 1 else ref[0, rows, :]
 
 
+def piece_rows(me_ref, core, apart, chips, rows):
+    place = jnp.bitwise_xor(me_ref[0], core) * chips + jnp.bitwise_xor(me_ref[1], apart)
+    return pl.ds(pl.multiple_of(place * rows, rows), rows)
+
+
+def put_pieces(me_ref, refs, source_ref):
+    for core, ref in enumerate(refs):
+        for apart in range(ref.shape[0]):
+            ref[apart] = source_ref[piece_rows(me_ref, core, apart, ref.shape[0], ref.shape[1]), :]
+
+
+def take_pieces(me_ref, refs, target_ref):
+    for core, ref in enumerate(refs):
+        for apart in range(ref.shape[0]):
+            target_ref[piece_rows(me_ref, core, apart, ref.shape[0], ref.shape[1]), :] = ref[apart]
+
+
 def block_rows(t, size):
     return pl.ds(pl.multiple_of(t * size, size), size)
 
 
 def entry_kernel(
-    span, taps, rank_cols, starts_ref, hid_ref, w_ref, gain_ref, cw_ref, cb_ref, xw_ref,
-    normed_ref, scale_ref, x_ref, gate_ref, val_ref, pre_ref, proj_ref, s_x, s_mixing,
+    span, taps, me_ref, starts_ref, hid_ref, w_ref, gain_ref, cw_ref, cb_ref, xw_ref,
+    normed_ref, scale_ref, x_ref, gate_ref, val_ref, pre_ref, mine_ref, other_ref, s_x, s_mixing, s_proj,
 ):
     turn = pl.program_id(0)
-    turns = pl.num_programs(0)
+    turns = pl.num_programs(0) - 1
     chans = x_ref.shape[1]
     size = span * SEGS
     steps = span * turns
     halo = (taps - 1) * SEGS
+    groups, width = lane_groups(chans)
 
     @pl.when(turn == 0)
     def _():
         s_mixing[...] = mixing(span, False)
 
-    wide = hid_ref[...].astype(f32).reshape(size, hid_ref.shape[2])
-    scale = lax.rsqrt(jnp.mean(wide * wide, axis=1, keepdims=True) + eps)
-    normed = (wide * scale * gain_ref[...]).astype(bf16)
-    normed_ref[...] = normed.reshape(normed_ref.shape)
-    scale_ref[...] = jnp.broadcast_to(scale, (size, 128)).reshape(scale_ref.shape)
-    mixed = dot(normed, w_ref[...], (1, 0)).astype(bf16)
-    mixed = dot(s_mixing[...], mixed, (1, 0))
-    rows = block_rows(turn, size)
-    x_ref[rows, :] = mixed[:, :chans].astype(bf16)
-    gate_ref[rows, :] = mixed[:, chans:].astype(bf16)
-    s_x[pl.ds(pl.multiple_of(turn * size + halo, SEGS), size), :] = mixed[:, :chans]
-
-    @pl.when(turn == turns - 1)
+    @pl.when(turn < turns)
+    def _():
+        wide = hid_ref[...].astype(f32).reshape(size, hid_ref.shape[2])
+        scale = lax.rsqrt(jnp.mean(wide * wide, axis=1, keepdims=True) + eps)
+        normed = (wide * scale * gain_ref[...]).astype(bf16)
+        normed_ref[...] = normed.reshape(normed_ref.shape)
+        scale_ref[...] = jnp.broadcast_to(scale, (size, 128)).reshape(scale_ref.shape)
+        mixed = dot(normed, w_ref[...], (1, 0)).astype(bf16)
+        mixed = dot(s_mixing[...], mixed, (1, 0))
+        x_ref[...] = mixed[:, :chans].astype(bf16)
+        gate_ref[...] = mixed[:, chans:].astype(bf16)
+        s_x[pl.ds(pl.multiple_of(turn * size + halo, SEGS), size), :] = mixed[:, :chans]
+
+    @pl.when(turn == turns)
     def _():
         first = lax.broadcasted_iota(jnp.int32, (SEGS, chans), 0) == 0
         for j in range(taps - 1):
-            last = s_x[steps * SEGS + j * SEGS : steps * SEGS + (j + 1) * SEGS, :]
+            last = s_x[pl.ds(pl.multiple_of(steps * SEGS + j * SEGS, SEGS), SEGS), :]
             s_x[j * SEGS : (j + 1) * SEGS, :] = jnp.where(first, 0.0, pltpu.roll(last, 1, 0))
 
-        def step(t, carry):
-            groups, width = lane_groups(chans)
-            place = jnp.concatenate([context_positions(starts_ref, t * size, size, steps, width)] * groups, axis=1)
-            pre = cb_ref[...] + jnp.zeros((size, chans), f32)
-            for k in range(taps):
-                lag = taps - 1 - k
-                at = pl.ds(pl.multiple_of(t * size + halo - lag * SEGS, SEGS), size)
-                pre = pre + cw_ref[k : k + 1, :] * jnp.where(place >= lag, s_x[at, :], 0.0)
-            rows = block_rows(t, size)
-            pre_ref[rows, :] = pre
-            values = silu(pre).astype(bf16)
-            val_ref[rows, :] = values
-            proj_ref[rows, :] = dot(values, xw_ref[...], (1, 0)).astype(bf16)
-            return carry
-
-        lax.fori_loop(0, turns, step, 0)
+    @pl.when(turn > 0)
+    def _():
+        t = jnp.where(turn == turns, 0, turn)
+        place = jnp.concatenate([context_positions(starts_ref, t * size, size, steps, width)] * groups, axis=1)
+        pre = cb_ref[...] + jnp.zeros((size, chans), f32)
+        for k in range(taps):
+            lag = taps - 1 - k
+            at = pl.ds(pl.multiple_of(t * size + halo - lag * SEGS, SEGS), size)
+            pre = pre + cw_ref[k : k + 1, :] * jnp.where(place >= lag, s_x[at, :], 0.0)
+        pre_ref[...] = pre
+        values = silu(pre).astype(bf16)
+        val_ref[...] = values
+        s_proj[block_rows(t, size), :] = dot(values, xw_ref[...], (1, 0)).astype(bf16)
+
+    @pl.when(turn == turns)
+    def _():
+        put_pieces(me_ref, (mine_ref, other_ref), s_proj)
 
 
 def gate_kernel(
@@ -174,10 +194,11 @@
 
 
 def exit_kernel(
-    span, taps, low_cols, starts_ref, dproj_ref, part_ref, pre_ref, x_ref, val_ref, cw_ref, xw_ref, dgate_ref, w_ref,
+    span, taps, low_cols, packs, peers, me_ref, starts_ref, mine_ref, other_ref, part_ref, pre_ref, x_ref, val_ref, cw_ref, xw_ref, dgate_ref, w_ref,
     hid_ref, scale_ref, gain_ref, ddtw_ref, dalog_ref, ddtb_ref, dskip_ref,
-    dn_ref, din_ref, small_ref, dgain_ref, s_pre, s_dx, s_din, s_place,
+    dn_ref, *refs,
 ):
+    *out_refs, s_pre, s_dx, s_din, s_place, s_small, dgain_ref, dproj_ref = refs
     total, chans = x_ref.shape
     size = span * SEGS
     steps = total // SEGS
@@ -188,6 +209,7 @@
 
     @pl.when(turn == 0)
     def _():
+        take_pieces(me_ref, (mine_ref, other_ref), dproj_ref)
 
         def first(t, carry):
             rows = block_rows(t, size)
@@ -228,9 +250,9 @@
         s_din[...] = jnp.zeros_like(s_din)
         dgain_ref[...] = jnp.zeros_like(dgain_ref)
         rest = [*sums, d_bias, ddtb_ref[...], dskip_ref[...]]
-        pad = small_ref.shape[0] - low_cols - ddtw_ref.shape[0] - dalog_ref.shape[0] - len(rest)
-        small = [d_xw[:low_cols], ddtw_ref[...], dalog_ref[...], *rest, jnp.zeros((pad, chans), f32)]
-        small_ref[...] = jnp.concatenate(small, axis=0).astype(bf16)
+        small = [d_xw[:low_cols], ddtw_ref[...], dalog_ref[...], *rest]
+        pad = s_small.shape[0] - sum(a.shape[0] for a in small)
+        s_small[...] = jnp.concatenate([*small, jnp.zeros((pad, chans), f32)], axis=0)
 
     @pl.when(turn > 0)
     def _():
@@ -250,7 +272,28 @@
 
     @pl.when(turn == pl.num_programs(0) - 1)
     def _():
-        din_ref[...] = s_din[...].T.astype(bf16)
+        d_in = s_din[...].T
+        if len(out_refs) < packs:
+            out_refs[0][...] = d_in.astype(bf16)
+            out_refs[1][...] = s_small[...].astype(bf16)
+            out_refs[2][...] = dgain_ref[...]
+            return
+        each = s_small.shape[0] // packs
+        share = d_in.shape[0] // (peers * packs)
+        sides = d_in.shape[0] // chans
+        gain = [dgain_ref[:, i * chans : (i + 1) * chans] for i in range(sides)]
+        gain = jnp.concatenate([*gain, jnp.zeros((16 - sides, chans), f32)], axis=0).astype(bf16)
+        for d, ref in enumerate(out_refs):
+            who = jnp.bitwise_xor(me_ref[2], d)
+            ref[peers * share : peers * share + each, :] = s_small[block_rows(who, each), :].astype(bf16)
+            ref[peers * share + each :, :] = gain
+            for p in range(packs):
+
+                @pl.when(who == p)
+                def _():
+                    for q in range(peers):
+                        at = (q * packs + p) * share
+                        ref[q * share : (q + 1) * share, :] = d_in[at : at + share].astype(bf16)
 
 
 def prepare_spread(hot_ref, rank, states):
@@ -518,9 +561,9 @@
 
 
 def scan_kernel(
-    rank, states, span, proj_ref, val_ref, gate_ref, cut_ref, grad_ref, w_ref, dtw_ref, dtwt_ref, dtb_ref, alog_ref,
-    skip_ref, branch_ref, gated_ref, dgate_ref, part_ref, dval_ref, ddtw_ref, ddtb_ref, dalog_ref, dskip_ref,
-    s_cut, s_delta, s_val, s_dy, s_hist, s_b, s_c, s_y, s_rate, s_state, s_drate, s_mix, s_hot, s_in, s_out,
+    rank, states, span, me_ref, mine_ref, other_ref, val_ref, gate_ref, cut_ref, grad_ref, w_ref, dtw_ref, dtwt_ref, dtb_ref, alog_ref,
+    skip_ref, branch_ref, gated_ref, dgate_ref, pmine_ref, pother_ref, dval_ref, ddtw_ref, ddtb_ref, dalog_ref, dskip_ref,
+    s_cut, s_delta, s_val, s_dy, s_hist, s_b, s_c, s_y, s_rate, s_state, s_drate, s_mix, s_hot, s_in, s_out, s_even, proj_ref, part_ref,
 ):
     total, chans = val_ref.shape
     steps = total // SEGS
@@ -554,6 +597,8 @@
         s_in[...] = mixing(span, False)
         s_out[...] = mixing(span, True)
         prepare_spread(s_hot, rank, states)
+        take_pieces(me_ref, (mine_ref, other_ref), proj_ref)
+        s_even[...] = jnp.concatenate([s_hot[:, n * 128 : (n + 1) * 128] for n in range(0, 2 * states, 2)], axis=1)
 
         def fill(t, carry):
             rows = block_rows(t, size)
@@ -580,7 +625,7 @@
             return tuple(out), tuple(sums[g] + cuts[g] for g in every)
 
         begin = ((zero,) * len(pairs), (zero,) * groups)
-        chained(*lax.fori_loop(0, steps, sweep, begin, unroll=4), 0, 1)
+        chained(*lax.fori_loop(0, steps, sweep, begin, unroll=16), 0, 1)
 
     @pl.when(turn < turns)
     def _():
@@ -605,7 +650,7 @@
                 s_y[block_rows(k, SEGS), lane[g]] = ys[g]
             return tuple(out)
 
-        held = lax.fori_loop(0, span, sweep, tuple(s_state[j] for j in range(len(pairs))), unroll=4)
+        held = lax.fori_loop(0, span, sweep, tuple(s_state[j] for j in range(len(pairs))), unroll=16)
         for j in range(len(pairs)):
             s_state[j] = held[j]
 
@@ -615,19 +660,20 @@
 
         rows = block_rows(turn, size)
         vals = val_ref[rows, :].astype(f32)
-        gate = gate_ref[rows, :].astype(f32)
+        gate = gate_ref[...].astype(f32)
         sig = jax.nn.sigmoid(gate)
         act = gate * sig
         scanned = s_y[...] + skip_ref[...] * vals
-        gated = dot(s_out[...], (scanned * act).astype(bf16), (1, 0)).astype(bf16)
-        gated_ref[...] = gated.reshape(gated_ref.shape)
-        branch_ref[...] = dot(gated, w_ref[...], (1, 0)).astype(bf16).reshape(branch_ref.shape)
         grad = grad_ref[...].reshape(size, grad_ref.shape[2])
         d_gated = dot(s_in[...], dot(grad, w_ref[...], (1, 1)).astype(bf16), (1, 0))
         dy = d_gated * act
         put(s_dy, rows, dy, groups, width)
-        d_gate = (d_gated * scanned * (sig * (1.0 + gate * (1.0 - sig)))).astype(bf16)
-        dgate_ref[...] = dot(s_out[...], d_gate, (1, 0)).astype(bf16).reshape(dgate_ref.shape)
+        d_gate = d_gated * scanned * (sig * (1.0 + gate * (1.0 - sig)))
+        both = jnp.concatenate([(scanned * act).astype(bf16), d_gate.astype(bf16)], axis=1)
+        both = dot(s_out[...], both, (1, 0)).astype(bf16)
+        gated_ref[...] = both[:, :chans].reshape(gated_ref.shape)
+        dgate_ref[...] = both[:, chans:].reshape(dgate_ref.shape)
+        branch_ref[...] = dot(both[:, :chans], w_ref[...], (1, 0)).astype(bf16).reshape(branch_ref.shape)
         dskip_ref[...] += jnp.sum(dy * vals, axis=0, keepdims=True)
 
     @pl.when(turn == turns)
@@ -647,7 +693,7 @@
             return tuple(out), tuple(sums[g] + cuts[g] for g in every)
 
         begin = ((zero,) * len(pairs), (zero,) * groups)
-        chained(*lax.fori_loop(0, steps, sweep, begin, unroll=4), SEGS - 1, SEGS - 1)
+        chained(*lax.fori_loop(0, steps, sweep, begin, unroll=16), SEGS - 1, SEGS - 1)
 
     @pl.when(turn >= turns)
     def _():
@@ -689,10 +735,10 @@
                         s_mix[block_rows(k, 2 * SEGS), first * 64 : first * 64 + width] = two
             for g in every:
                 s_cut[g, at, :] = by_rate[g] * (1.0 / LOG2E) + by_b[g] * vals[g]
-                dval_ref[at, lane[g]] = by_b[g] * deltas[g] + dys[g] * skip_ref[:, lane[g]]
+                dval_ref[block_rows(k, SEGS), lane[g]] = by_b[g] * deltas[g] + dys[g] * skip_ref[:, lane[g]]
             return tuple(out)
 
-        held = lax.fori_loop(0, span, sweep, tuple(s_state[j] for j in range(len(pairs))), unroll=4)
+        held = lax.fori_loop(0, span, sweep, tuple(s_state[j] for j in range(len(pairs))), unroll=16)
         for j in range(len(pairs)):
             s_state[j] = held[j]
         rows = block_rows(place, size)
@@ -701,13 +747,13 @@
         ddtb_ref[...] += jnp.sum(d_pre, axis=0, keepdims=True)
         ddtw_ref[...] += split_dot(d_pre, proj_ref[rows, :rank], (0, 0), swapped=True)
         part = split_dot(d_pre, dtwt_ref[...], (1, 0))
-        even = jnp.concatenate([s_hot[:, n * 128 : (n + 1) * 128] for n in range(0, 2 * states, 2)], axis=1)
-        found = dot(s_mix[...], even, (1, 1)).reshape(span, 2, SEGS, part_ref.shape[1])
+        found = dot(s_mix[...], s_even[...], (1, 1)).reshape(span, 2, SEGS, part_ref.shape[1])
         odd = pltpu.roll(found[:, 1].reshape(size, part_ref.shape[1]), 1, 1)
         part_ref[rows, :] = (part + found[:, 0].reshape(size, part_ref.shape[1]) + odd).astype(bf16)
 
     @pl.when(turn == 2 * turns - 1)
     def _():
+        put_pieces(me_ref, (pmine_ref, pother_ref), part_ref)
         sums = [jnp.sum(s_drate[i], axis=0, keepdims=True) for i in range(states * groups)]
         rows = [jnp.concatenate(sums[n * groups : (n + 1) * groups], axis=1) for n in range(states)]
         dalog_ref[...] = jnp.concatenate(rows, axis=0) * s_rate[...] * (1.0 / LOG2E)
@@ -737,30 +783,42 @@
 SCALARS = pl.BlockSpec(memory_space=pltpu.SMEM)
 
 
-def run_entry(starts, hidden_all, weight, gain, conv_w, conv_b, x_w, span):
+def run_entry(me, starts, hidden_all, weight, gain, conv_w, conv_b, x_w, peers, span):
     total, width = hidden_all.shape
     taps, chans = conv_w.shape
     lanes = x_w.shape[1]
     steps = total // SEGS
-    segments = pl.BlockSpec((SEGS, span, width), lambda t: (0, t, 0))
+    turns = steps // span
+    size = span * SEGS
+    piece = (peers // 2, total // peers, lanes)
+
+    def segments(lanes):
+        return pl.BlockSpec((SEGS, span, lanes), lambda t: (0, jnp.minimum(t, turns - 1), 0))
+
+    mixed = pl.BlockSpec((size, chans), lambda t: (jnp.minimum(t, turns - 1), 0))
+
+    def late(lanes):
+        return pl.BlockSpec((size, lanes), lambda t: (jnp.where(t == turns, 0, jnp.maximum(t, 1)), 0))
+
     normed, scale, *rest = pl.pallas_call(
-        functools.partial(entry_kernel, span, taps, lanes),
-        grid=(steps // span,),
+        functools.partial(entry_kernel, span, taps),
+        grid=(turns + 1,),
         in_specs=[
-            SCALARS, segments, whole(width, 2 * chans), whole(1, width), whole(taps, chans), whole(1, chans),
+            SCALARS, SCALARS, segments(width), whole(width, 2 * chans), whole(1, width), whole(taps, chans), whole(1, chans),
             whole(chans, lanes),
         ],
-        out_specs=[segments, pl.BlockSpec((SEGS, span, 128), lambda t: (0, t, 0))]
-        + [whole(total, chans)] * 4 + [whole(total, lanes)],
+        out_specs=[segments(width), segments(128), mixed, mixed, late(chans), late(chans)]
+        + [whole(*piece)] * 2,
         out_shape=[like(SEGS, steps, width, dtype=bf16), like(SEGS, steps, 128)] + [like(total, chans, dtype=bf16)] * 3
-        + [like(total, chans), like(total, lanes, dtype=bf16)],
+        + [like(total, chans)] + [like(*piece, dtype=bf16)] * 2,
         scratch_shapes=[
-            pltpu.VMEM((total + (taps - 1) * SEGS, chans), f32), pltpu.VMEM((span * SEGS, span * SEGS), bf16),
+            pltpu.VMEM((total + (taps - 1) * SEGS, chans), f32), pltpu.VMEM((size, size), bf16),
+            pltpu.VMEM((total, lanes), bf16),
         ],
         compiler_params=pltpu.CompilerParams(vmem_limit_bytes=ROOM),
         cost_estimate=about(6 * total * chans / 262144),
         name="entry",
-    )(starts, hidden_all.reshape(SEGS, steps, width), weight, gain, conv_w, conv_b, x_w)
+    )(me, starts, hidden_all.reshape(SEGS, steps, width), weight, gain, conv_w, conv_b, x_w)
     return (normed, scale.reshape(total, 128), *rest)
 
 
@@ -786,14 +844,14 @@
     return branch.reshape(total, width), gated.reshape(total, chans), dy, d_gate.reshape(total, chans), d_skip
 
 
-def run_scan(proj, values, gate, cut, grad_all, out_w, dt_weight, dt_weight_t, dt_bias, a_log_t, skip, states, span):
+def run_scan(me, mine, other, values, gate, cut, grad_all, out_w, dt_weight, dt_weight_t, dt_bias, a_log_t, skip, states, span):
     total, chans = values.shape
     width_all = grad_all.shape[1]
     rank = dt_weight.shape[0]
     steps = total // SEGS
     groups, width = lane_groups(chans)
     count = states * groups
-    lanes = proj.shape[1]
+    lanes = mine.shape[2]
     turns = steps // span
     size = span * SEGS
     by_group = pltpu.VMEM((groups, total, width), f32)
@@ -802,38 +860,45 @@
     order = pltpu.VMEM((size, size), bf16)
     part = pl.BlockSpec((SEGS, span, chans), lambda t: (0, jnp.minimum(t, turns - 1), 0))
     full = pl.BlockSpec((SEGS, span, width_all), lambda t: (0, jnp.minimum(t, turns - 1), 0))
+    ahead = pl.BlockSpec((size, chans), lambda t: (jnp.minimum(t, turns - 1), 0))
+
+    def behind(lanes):
+        return pl.BlockSpec((size, lanes), lambda t: (jnp.minimum(turns, 2 * turns - t) - 1, 0))
+
     natural = like(SEGS, steps, chans, dtype=bf16)
     branch, gated, d_gate, *rest = pl.pallas_call(
         functools.partial(scan_kernel, rank, states, span),
         grid=(2 * turns,),
         in_specs=[
-            whole(total, lanes), whole(total, chans), whole(total, chans), whole(total, width), full,
+            SCALARS, whole(*mine.shape), whole(*mine.shape), whole(total, chans), ahead, whole(total, width), full,
             whole(chans, width_all), whole(rank, chans), whole(chans, lanes), whole(1, chans), whole(states, chans),
             whole(1, chans),
         ],
         out_specs=[
-            full, part, part, whole(total, lanes), whole(total, chans), whole(rank, chans), whole(1, chans),
+            full, part, part, whole(*mine.shape), whole(*mine.shape), behind(chans), whole(rank, chans), whole(1, chans),
             whole(states, chans), whole(1, chans),
         ],
         out_shape=[
-            like(SEGS, steps, width_all, dtype=bf16), natural, natural, like(total, lanes, dtype=bf16),
-            like(total, chans), like(rank, chans), like(1, chans), like(states, chans), like(1, chans),
+            like(SEGS, steps, width_all, dtype=bf16), natural, natural, like(*mine.shape, dtype=bf16),
+            like(*mine.shape, dtype=bf16), like(total, chans), like(rank, chans), like(1, chans), like(states, chans), like(1, chans),
         ],
         scratch_shapes=[
             by_group, by_group, by_group, by_group, pltpu.VMEM((steps + 1, count, SEGS, width), f32), spread, spread,
             pltpu.VMEM((size, chans), f32), pltpu.VMEM((states, chans), f32), held, held,
             pltpu.VMEM((2 * size, states * 128), bf16), pltpu.VMEM((lanes, 2 * states * 128), bf16), order, order,
+            pltpu.VMEM((lanes, states * 128), bf16), pltpu.VMEM((total, lanes), bf16), pltpu.VMEM((total, lanes), bf16),
         ],
         compiler_params=pltpu.CompilerParams(vmem_limit_bytes=ROOM),
         cost_estimate=about(38),
         name="scan",
-    )(proj, values, gate, cut, grad_all.reshape(SEGS, steps, width_all), out_w, dt_weight, dt_weight_t, dt_bias, a_log_t, skip)
+    )(me, mine, other, values, gate, cut, grad_all.reshape(SEGS, steps, width_all), out_w, dt_weight, dt_weight_t, dt_bias, a_log_t, skip)
     return (branch.reshape(total, width_all), gated.reshape(total, chans), d_gate.reshape(total, chans), *rest)
 
 
 def run_exit(
-    starts, d_proj, value_part, pre, x_in, values, conv_w, x_w, d_gate, weight, hidden_all, scale, gain,
-    d_dtw, d_alog_t, d_dtb, d_skip, low_cols, small_rows, span,
+    me, starts, mine, other, value_part, pre, x_in, values, conv_w, x_w, d_gate, weight, hidden_all, scale, gain,
+    d_dtw, d_alog_t, d_dtb, d_skip, low_cols, small_rows, packs, peers,
+    span,
 ):
     total, chans = x_in.shape
     taps = conv_w.shape[0]
@@ -845,29 +910,40 @@
     def rows(lanes):
         return pl.BlockSpec((size, lanes), lambda t: (jnp.maximum(t - 1, 0), 0))
 
-    return pl.pallas_call(
-        functools.partial(exit_kernel, span, taps, low_cols),
+    sides = width // chans
+    packed = width // (peers * packs) % 16 == 0 and sides <= 16
+    if packed:
+        shapes = [like((width + small_rows) // packs + 16, chans, dtype=bf16)] * packs
+    else:
+        shapes = [like(width, chans, dtype=bf16), like(small_rows, chans, dtype=bf16), like(1, width)]
+    d_normed, *out = pl.pallas_call(
+        functools.partial(exit_kernel, span, taps, low_cols, packs, peers),
         grid=(1 + total // size,),
-        in_specs=[SCALARS, whole(total, lanes)] + [whole(total, chans)] * 4 + [
+        in_specs=[SCALARS, SCALARS, whole(*mine.shape), whole(*mine.shape)] + [whole(total, chans)] * 4 + [
             whole(taps, chans), whole(chans, lanes), rows(chans), whole(width, 2 * chans), rows(width), rows(128),
             whole(1, width), whole(*d_dtw.shape), whole(*d_alog_t.shape), whole(1, chans), whole(1, chans),
         ],
-        out_specs=[rows(width), whole(width, chans), whole(small_rows, chans), whole(1, width)],
-        out_shape=[
-            like(total, width, dtype=bf16), like(width, chans, dtype=bf16), like(small_rows, chans, dtype=bf16),
-            like(1, width),
-        ],
+        out_specs=[rows(width)] + [whole(*a.shape) for a in shapes],
+        out_shape=[like(total, width, dtype=bf16), *shapes],
         scratch_shapes=[
             pltpu.VMEM((total + (taps - 1) * SEGS, chans), f32), pltpu.VMEM((SEGS, steps, chans), bf16),
             pltpu.VMEM((chans, width), f32), pltpu.VMEM((total + (taps - 1) * SEGS, lane_groups(chans)[1]), jnp.int32),
+            pltpu.VMEM((small_rows, chans), f32), pltpu.VMEM((1, width), f32), pltpu.VMEM((total, lanes), bf16),
         ],
         compiler_params=pltpu.CompilerParams(vmem_limit_bytes=ROOM),
         cost_estimate=about(10 * total * chans / 262144),
         name="exit",
     )(
-        starts, d_proj, value_part, pre, x_in, values, conv_w, x_w, d_gate, weight, hidden_all, scale, gain,
+        me, starts, mine, other, value_part, pre, x_in, values, conv_w, x_w, d_gate, weight, hidden_all, scale, gain,
         d_dtw, d_alog_t, d_dtb, d_skip,
     )
+    if packed:
+        return d_normed, out
+    late = jnp.moveaxis(out[0].reshape(peers, packs, -1, chans), 1, 0).reshape(packs, -1, chans)
+    gain = jnp.pad(out[2].astype(bf16).reshape(sides, chans), ((0, -sides % 16), (0, 0)))
+    late = [late, out[1].reshape(packs, -1, chans), jnp.broadcast_to(gain, (packs,) + gain.shape)]
+    late = jnp.concatenate(late, axis=1)
+    return d_normed, [pick(late, jnp.bitwise_xor(me[2], d)) for d in range(packs)]
 
 
 def run_forward(proj, values, cut, dt_weight, dt_bias, a_log_t, states, span):
@@ -966,9 +1042,12 @@
 
 
 def owned_parts(blocks, axis):
+    return [blocks[0]] + [swap(block, axis, d) for d, block in enumerate(blocks) if d]
+
+
+def by_distance(blocks, axis):
     me = lax.axis_index(axis)
-    size = lax.axis_size(axis)
-    return [pick(blocks, me)] + [swap(pick(blocks, me ^ d), axis, d) for d in range(1, size)]
+    return [pick(blocks, jnp.bitwise_xor(me, d)) for d in range(blocks.shape[0])]
 
 
 def collect(value, axis):
@@ -976,21 +1055,32 @@
     return collected([value] + [swap(value, axis, d) for d in range(1, lax.axis_size(axis))], me)
 
 
-def sum_over_peers(part):
+def sum_over_peers(mine, other, beside=()):
     peers = lax.axis_size("ch")
-    rows, lanes = part.shape
     if peers != 8:
-        got = lax.all_to_all(part.reshape(peers, rows // peers, lanes), "ch", split_axis=0, concat_axis=0, tiled=True)
-        return lax.all_gather(got.astype(f32).sum(axis=0).astype(bf16), "ch", axis=0, tiled=True)
-    core, chip = lax.axis_index("ch") % 2, lax.axis_index("ch") // 2
-    chips = peers // 2
-    halves = part.reshape(2, chips, rows // peers, lanes)
-    got = swap(pick(halves, 1 - core), "ch", 1)
-    half = tree_sum([pick(halves, core), got]).astype(bf16)
-    pieces = [pick(half, chip)] + [swap(pick(half, chip ^ d), "ch", 2 * d) for d in range(1, chips)]
+        part = jnp.concatenate([mine, other], axis=0).reshape(peers, -1, mine.shape[2])
+        got = lax.all_to_all(part, "ch", split_axis=0, concat_axis=0, tiled=True)
+        part = lax.all_gather(got.astype(f32).sum(axis=0).astype(bf16), "ch", axis=0, tiled=True).reshape(part.shape)
+        return part[: peers // 2], part[peers // 2 :], beside
+    half = tree_sum([mine, swap(other, "ch", 1)]).astype(bf16)
+    pieces = [half[0]] + [swap(half[d], "ch", 2 * d) for d in range(1, peers // 2)]
     own = tree_sum(pieces).astype(bf16)
-    half = collected([own] + [swap(own, "ch", 2 * d) for d in range(1, chips)], chip)
-    return collected([half, swap(half, "ch", 1)], core).reshape(rows, lanes)
+    pieces = [own] + [swap(own, "ch", 2 * d) for d in range(1, peers // 2)]
+    pieces, beside = lax.optimization_barrier((pieces, beside))
+    half = jnp.stack(pieces)
+    return half, swap(half, "ch", 1), beside
+
+
+def in_order(mine, other, place):
+    chips = jnp.bitwise_xor(jnp.arange(mine.shape[0]), place[1])
+    halves = jnp.stack([mine[chips], other[chips]])
+    return halves[jnp.bitwise_xor(jnp.arange(2), place[0])].reshape(-1, mine.shape[2])
+
+
+def by_place(part, peers, place):
+    halves = part.reshape(2, peers // 2, -1, part.shape[1])[jnp.bitwise_xor(jnp.arange(2), place[0])]
+    halves = halves[:, jnp.bitwise_xor(jnp.arange(peers // 2), place[1])]
+    return halves[0], halves[1]
 
 
 def to_peers(blocks):
@@ -1012,14 +1102,19 @@
     for d in range(n):
         who = jnp.bitwise_xor(me_ref[0], d)
         rows = block_rows(who, share)
+        sides = dout_ref.shape[1] // chans
+        out_share = dout_ref.shape[0] // n
         for p in range(peers):
-            block = late[d][p * 2 * share : (p + 1) * 2 * share, :].astype(f32)
-            din_ref[rows, p * chans : (p + 1) * chans] = block[:share]
-            din_ref[rows, inner + p * chans : inner + (p + 1) * chans] = block[share:]
-        small = late[d][2 * share * peers :, :].astype(f32)
+            here = slice(p * share, (p + 1) * share)
+            din_ref[rows, p * chans : (p + 1) * chans] = late[d][here, :].astype(f32)
+            here = slice(sides * out_share + p * share, sides * out_share + (p + 1) * share)
+            din_ref[rows, inner + p * chans : inner + (p + 1) * chans] = outs[d][here, :].astype(f32)
+        small = late[d][share * peers :, :].astype(f32)
         s_small[block_rows(who, small.shape[0]), :] = small
-        dout_ref[block_rows(who, outs[d].shape[0]), :] = outs[d][...].astype(f32)
-    gain = jnp.sum(cross_ref[:, 2 * share :, :].astype(f32), axis=0)
+        for i in range(sides):
+            part = outs[d][i * out_share : (i + 1) * out_share, :].astype(f32)
+            dout_ref[block_rows(who, out_share), i * chans : (i + 1) * chans] = part
+    gain = jnp.sum(cross_ref[:, share:, :].astype(f32), axis=0)
     dgain_ref[...] = gain[:1, : dgain_ref.shape[1]]
     at = low_cols + rank
     ddtw_ref[...] = s_small[low_cols:at, :]
@@ -1060,7 +1155,7 @@
         out_specs=[whole(*a.shape) for a in shapes],
         out_shape=shapes,
         scratch_shapes=[pltpu.VMEM((small_rows, chans), f32)],
-        compiler_params=pltpu.CompilerParams(vmem_limit_bytes=ROOM),
+        compiler_params=pltpu.CompilerParams(vmem_limit_bytes=20 * MIB),
         cost_estimate=about(4),
         name="finish",
     )(me[None], *wide)
@@ -1071,16 +1166,22 @@
     packs, peers, chans = len(late), cross.shape[0], late[0].shape[1]
     share = hidden.shape[1] // (peers * packs)
     late = collected(late, me).astype(f32)
-    halves = late[:, : 2 * share * peers].reshape(packs, peers, 2, share, chans)
-    d_in = jnp.transpose(halves, (0, 3, 2, 1, 4)).reshape(packs * share, 2 * peers * chans)
-    small = late[:, 2 * share * peers :].reshape(small_rows, chans)
+    outs = collected(outs, me).astype(f32)
+    sides = hidden.shape[1] // chans
+    out_share = chans // packs
+    halves = [late[:, : share * peers], outs[:, sides * out_share :]]
+    halves = jnp.stack(halves).reshape(2, packs, peers, share, chans)
+    d_in = jnp.transpose(halves, (1, 3, 0, 2, 4)).reshape(packs * share, 2 * peers * chans)
+    d_out = outs[:, : sides * out_share].reshape(packs, sides, out_share, chans)
+    d_out = jnp.moveaxis(d_out, 1, 2).reshape(chans, sides * chans)
+    small = late[:, share * peers :].reshape(small_rows, chans)
     parts = []
     at = 0
     for count in (low_cols, rank, states, taps, 1, 1, 1):
         parts.append(small[at : at + count])
         at += count
     d_xw, d_dtw, d_alog, d_cw, d_cb, d_dtb, d_skip = parts
-    d_gain = cross[:, 2 * share :].astype(f32).sum(axis=0).reshape(1, -1)[:, : share * packs]
+    d_gain = cross[:, share:].astype(f32).sum(axis=0).reshape(1, -1)[:, : share * packs]
     hidden = hidden.astype(f32)
     output = (hidden + branch.astype(f32)).astype(bf16)
     scale = lax.rsqrt(jnp.mean(hidden * hidden, axis=1, keepdims=True) + eps)
@@ -1088,7 +1189,6 @@
     d_unit = d_normed.astype(f32) * gain
     mean = jnp.mean(d_unit * unit, axis=1, keepdims=True)
     d_hidden = (grad.astype(f32) + scale * (d_unit - unit * mean)).astype(bf16)
-    d_out = collected(outs, me).astype(f32).reshape(chans, -1)
     return output, d_hidden, d_gain, d_in, d_cw, d_cb, d_xw, d_dtw, d_dtb, d_alog, d_skip, d_out
 
 
@@ -1110,8 +1210,6 @@
     share = in_rows // packs
     my_share = lax.dynamic_slice_in_dim(in_weight, lax.axis_index("ctx") * share, share, 0)
     got = to_peers(jnp.moveaxis(my_share.reshape(share, 2, peers, chans), 2, 0))
-    shares = collect(got.reshape(peers, share, 2 * chans), "ctx")
-    my_cols = jnp.moveaxis(shares, 0, 1).reshape(width, 2 * chans)
     grad_all = lax.all_gather(out_grad, "ch", axis=0, tiled=True)
 
     steps = total // SEGS
@@ -1129,26 +1227,37 @@
     x_w = lax.dynamic_slice_in_dim(x_weight, me * chans, chans, 0)
     x_w = jnp.pad(x_w, ((0, 0), (0, lanes - low_cols)))
 
-    normed, scale_all, x_in, gate, values, pre, proj_part = run_entry(
-        starts, hidden_all, my_cols, norm_gain[None, :], conv_w, conv_b, x_w, span
+    near = peers == 8
+    place = jnp.stack([me % 2 if near else 0 * me, me // 2 if near else 0 * me, lax.axis_index("ctx")])
+    dt_w_t = jnp.pad(dt_weight.T, ((0, 0), (0, lanes - rank)))
+    got, cut, dt_w_t, conv_w, conv_b, x_w, starts = lax.optimization_barrier(
+        (got, cut, dt_w_t, conv_w, conv_b, x_w, starts)
     )
-    proj = sum_over_peers(proj_part)
+    shares = collect(got.reshape(peers, share, 2 * chans), "ctx")
+    my_cols = jnp.moveaxis(shares, 0, 1).reshape(width, 2 * chans)
+
+    normed, scale_all, x_in, gate, values, pre, *proj_part = run_entry(
+        place, starts, hidden_all, my_cols, norm_gain[None, :], conv_w, conv_b, x_w, peers, span
+    )
+    mine, other, _ = sum_over_peers(*proj_part)
 
     a_log_t = a_log.T
     dt_b, skip_row = dt_bias[None, :], skip[None, :]
-    dt_w_t = jnp.pad(dt_weight.T, ((0, 0), (0, lanes - rank)))
     if total * chans * states <= 1 << 22 and chans % 128 == 0:
         (
-            branch_part, gated, d_gate, d_part, value_part, d_dt_weight, d_dt_bias, d_a_log_t, d_skip,
+            branch_part, gated, d_gate, d_mine, d_other, value_part, d_dt_weight, d_dt_bias, d_a_log_t, d_skip,
         ) = run_scan(
-            proj, values, gate, cut, grad_all, out_weight, dt_weight, dt_w_t, dt_b, a_log_t, skip_row, states, span
+            place, mine, other, values, gate, cut, grad_all, out_weight, dt_weight, dt_w_t, dt_b, a_log_t, skip_row,
+            states, span,
         )
     else:
+        proj = in_order(mine, other, place)
         y, hist, delta = run_forward(proj, values, cut, dt_weight, dt_b, a_log_t, states, span)
         branch_part, gated, dy, d_gate, d_skip = run_gate(grad_all, out_weight, gate, values, y, skip_row, span)
         d_part, value_part, d_dt_weight, d_dt_bias, d_a_log_t = run_backward(
             proj, values, cut, dy, delta, dt_weight, dt_w_t, dt_b, a_log_t, skip_row, hist, states, span
         )
+        d_mine, d_other = by_place(d_part, peers, place)
     branch = lax.psum_scatter(branch_part, "ch", scatter_dimension=0, tiled=True)
     sides = width // chans
     out_share = chans // packs
@@ -1159,36 +1268,31 @@
     def by_pack(d_in):
         return jnp.moveaxis(d_in.reshape(peers, packs, share, chans), 1, 0).reshape(packs, peers * share, chans)
 
-    early = owned_parts(jnp.concatenate([d_out, by_pack(d_in_gate)], axis=1), "ctx")
-
-    d_proj = sum_over_peers(d_part)
-    early, d_proj = lax.optimization_barrier((early, d_proj))
+    early = owned_parts(by_distance(jnp.concatenate([d_out, by_pack(d_in_gate)], axis=1), "ctx"), "ctx")
+
+    mine, other, early = sum_over_peers(d_mine, d_other, early)
     early = tree_sum(early).astype(bf16)
-    d_out = jnp.moveaxis(early[: out_share * sides].reshape(sides, out_share, chans), 0, 1).reshape(out_share, width)
     counts = (low_cols, rank, states, taps)
     small_rows = -(-(sum(counts) + 3) // (16 * packs)) * 16 * packs
-    d_normed_part, d_in_x, small, d_gain = run_exit(
-        starts, d_proj, value_part, pre, x_in, values, conv_w, x_w, d_gate, my_cols, hidden_all, scale_all,
-        norm_gain[None, :], d_dt_weight, d_a_log_t, d_dt_bias, d_skip, low_cols, small_rows, span,
+    d_normed_part, late = run_exit(
+        place, starts, mine, other, value_part, pre, x_in, values, conv_w, x_w, d_gate, my_cols, hidden_all, scale_all,
+        norm_gain[None, :], d_dt_weight, d_a_log_t, d_dt_bias, d_skip, low_cols, small_rows, packs, peers, span,
     )
     d_normed = lax.psum_scatter(d_normed_part, "ch", scatter_dimension=0, tiled=True)
 
-    gain_rows = d_gain.astype(bf16).reshape(sides, chans)
-    gain_rows = jnp.pad(gain_rows, ((0, -sides % 16), (0, 0)))
-    late = [by_pack(d_in_x), small.reshape(packs, small_rows // packs, chans)]
-    late.append(jnp.broadcast_to(gain_rows, (packs,) + gain_rows.shape))
-    late = tree_sum(owned_parts(jnp.concatenate(late, axis=1), "ctx")).astype(bf16)
+    late = tree_sum(owned_parts(late, "ctx")).astype(bf16)
     own_rows = peers * share
     gain_rows = late[own_rows + small_rows // packs :][:sides].reshape(peers, in_rows)
     pad_rows = -(-in_rows // chans)
     gain_rows = jnp.pad(gain_rows, ((0, 0), (0, pad_rows * chans - in_rows))).reshape(peers, pad_rows, chans)
     gain_rows = jnp.pad(gain_rows, ((0, 0), (0, -pad_rows % 16), (0, 0)))
-    cross = [late[:own_rows].reshape(peers, share, chans), early[out_share * sides :].reshape(peers, share, chans)]
-    cross, d_out = lax.optimization_barrier((jnp.concatenate([*cross, gain_rows], axis=1), d_out))
+    early_in = to_peers(early[out_share * sides :].reshape(peers, share, chans)).reshape(own_rows, chans)
+    early = jnp.concatenate([early[: out_share * sides], early_in], axis=0)
+    cross = jnp.concatenate([late[:own_rows].reshape(peers, share, chans), gain_rows], axis=1)
+    early, _ = lax.optimization_barrier((early, cross))
     cross = to_peers(cross)
-    outs = [d_out] + [swap(d_out, "ctx", d) for d in range(1, packs)]
-    outs, cross = lax.optimization_barrier((outs, cross))
-    own = [cross[:, : 2 * share].reshape(2 * own_rows, chans), late[own_rows : own_rows + small_rows // packs]]
+    outs = [early] + [swap(early, "ctx", d) for d in range(1, packs)]
+    own = [cross[:, :share].reshape(own_rows, chans), late[own_rows : own_rows + small_rows // packs]]
     own = jnp.concatenate(own, axis=0)
     late = [own] + [swap(own, "ctx", d) for d in range(1, packs)]
     finish = run_finish if share % 16 == 0 and chans % 128 == 0 else finish_plain

time: 218 us -> 210 us (0.963)
  Pallas kernels: 60.6 us -> 56.4 us
  waiting for transfers between devices: 74.3 us -> 70.1 us
    ppermute x31, waiting for transfers between devices: 56.4 us -> 50.2 us  [swap(): lax.ppermute(value, axis, [(i, i ^ mask) for i in range(lax.axis_size(axi...]
    ppermute x31, starting transfers between devices: 37.4 us -> 32.9 us  [swap(): lax.ppermute(value, axis, [(i, i ^ mask) for i in range(lax.axis_size(axi...]
    all_to_all x2 -> x3, starting transfers between devices: 9.76 us -> 13.1 us  [to_peers(): return lax.all_to_all(blocks, 'ch', split_axis=0, concat_axis=0, tiled=True)]
    unnamed x50 -> x49, local copies, waits for them, and re-layouts: 4.11 us -> 6.63 us
    all_to_all x2 -> x3, waiting for transfers between devices: 16.4 us -> 17 us  [to_peers(): return lax.all_to_all(blocks, 'ch', split_axis=0, concat_axis=0, tiled=True)]
  transfers between devices with their start and end apart: 37 -> 38, of which waited for: 22 -> 24; matrix products, arithmetic and copies ran while one was open for 7% -> 7% of each run, Pallas kernels for 9% -> 9%
where the time goes in v4:
time: 210 us; the launch traced here: 209 us
  waiting for transfers between devices  70.1 us (33%)
  Pallas kernels  56.4 us (27%)
  starting transfers between devices  46.3 us (22%)
  local copies, waits for them, and re-layouts  15.2 us (7%)
  between operations  14.4 us (7%)
  other arithmetic  3.47 us (2%)
  matrix products  3.22 us (2%)
    ppermute x31, waiting for transfers between devices, swap(): lax.ppermute(value, axis, [(i, i ^ mask) for i in range(lax.axis_size(axi...  50.2 us
    pallas_call x1, Pallas kernels, run_scan(): pl.pallas_call(functools.partial(scan_kernel, rank, states, span), grid=(...  36.1 us
    ppermute x31, starting transfers between devices, swap(): lax.ppermute(value, axis, [(i, i ^ mask) for i in range(lax.axis_size(axi...  32.9 us
    all_to_all x3, waiting for transfers between devices, to_peers(): return lax.all_to_all(blocks, 'ch', split_axis=0, concat_axis=0, tiled=True)  17 us
    all_to_all x3, starting transfers between devices, to_peers(): return lax.all_to_all(blocks, 'ch', split_axis=0, concat_axis=0, tiled=True)  13.1 us
    pallas_call x1, Pallas kernels, run_exit(): pl.pallas_call(functools.partial(exit_kernel, span, taps, low_cols, packs...  10.4 us
    pallas_call x1, Pallas kernels, run_entry(): pl.pallas_call(functools.partial(entry_kernel, span, taps), grid=(turns +...  7.76 us
    unnamed x49, local copies, waits for them, and re-layouts  6.63 us
  transfers between devices with their start and end apart: 38, of which 24 were waited for; matrix products, arithmetic and copies ran while one was open for 7% of the time, Pallas kernels for 9%

profile of v4, /device:TPU:0, one launch (start us, length us, event | category | flops | bytes accessed | tf_op | source)
XLA Modules:
  0.0 209.0 jit_solution(5645960663862770258)
XLA Ops:
  8.5 0.9 copy.66
  9.4 6.3 %all-to-all-start = ((bf16[8,32,2,256]{3,2,1,0:T(2,128)(2,1)}), bf16[8,32,2,256]{3,2,1,0:T(2,128)(2,1)S(1)}, u32[]{:S(2)}, u32[]{:S(2)}) async-start(bf16[8,32,2,256]{3,2,1,0:T(2,128)(2,1)} %copy.66), calls=%async_computation | async-start | bytes 524288 | tf_op jit(solution)/shard_map/all_to_all | solution.py:1087
  17.1 1.3 dynamic_slice.27
  20.7 1.3 dynamic-slice_bitcast_fusion.cw_ref
  22.5 5.1 %all-to-all-done = bf16[8,32,2,256]{3,2,1,0:T(2,128)(2,1)S(1)} async-done(((bf16[8,32,2,256]{3,2,1,0:T(2,128)(2,1)}), bf16[8,32,2,256]{3,2,1,0:T(2,128)(2,1)S(1)}, u32[]{:S(2)}, u32[]{:S(2)}) %all-to-all-start) | async-done | bytes 262176 | tf_op jit(solution)/shard_map/all_to_all | solution.py:1087
  27.7 0.9 broadcast_in_dim.61.cut_ref
  28.8 1.5 collective-permute-start
  31.0 1.6 collective-permute-start.2
  33.3 4.7 %collective-permute-done = bf16[8,32,512]{2,1,0:T(8,128)(2,1)S(1)} collective-permute-done((bf16[8,32,512]{2,1,0:T(8,128)(2,1)S(1)}, bf16[8,32,512]{2,1,0:T(8,128)(2,1)S(1)}, u32[]{:S(2)}, u32[]{:S(2)}) %collective-permute-start) | collective-permute-done | bytes 262176 | tf_op jit(solution)/shard_map/ppermute | solution.py:1030
  38.0 5.9 %collective-permute-done.1 = bf16[8,32,512]{2,1,0:T(8,128)(2,1)S(1)} collective-permute-done((bf16[8,32,512]{2,1,0:T(8,128)(2,1)S(1)}, bf16[8,32,512]{2,1,0:T(8,128)(2,1)S(1)}, u32[]{:S(2)}, u32[]{:S(2)}) %collective-permute-start.1) | collective-permute-done | bytes 262176 | tf_op jit(solution)/shard_map/ppermute | solution.py:1030
  44.0 0.9 copy-done.7
  44.9 7.8 %entry.1 = (bf16[8,128,1024]{2,1,0:T(8,128)(2,1)}, f32[8,128,128]{2,1,0:T(8,128)}, bf16[1024,256]{1,0:T(8,128)(2,1)}, bf16[1024,256]{1,0:T(8,128)(2,1)}, bf16[10...) custom-call(s32[3]{0:T(128)} %pad_add_fusion.me_ref, ...), custom_call_target="tpu_custom_call" | custom-call | flops 6600000000 | bytes 1048576 | tf_op jit(solution)/shard_map/entry/pallas_call | solution.py:803
  52.7 1.5 collective-permute-done.3
  54.3 0.9 add_convert_fusion.3
  55.3 1.3 collective-permute-start.4
  56.6 4.1 %collective-permute-start.6 = (bf16[128,128]{1,0:T(8,128)(2,1)S(1)}, bf16[128,128]{1,0:T(8,128)(2,1)S(1)}, u32[]{:S(2)}, u32[]{:S(2)}) collective-permute-start(bf16[128,128]{1,0:T(8,128)(2,1)S(1)} %get-tuple-element.132), channel_id=1, source_target_pairs={{0,6},{1,7},{2,4},{3,5},{4,2},{5,3},{6,0},{7,1},{8,14},{9,15},{10,... | collective-permute-start | bytes 98312 | tf_op jit(solution)/shard_map/ppermute | solution.py:1030
  61.2 3.7 %collective-permute-done.6 = bf16[128,128]{1,0:T(8,128)(2,1)S(1)} collective-permute-done((bf16[128,128]{1,0:T(8,128)(2,1)S(1)}, bf16[128,128]{1,0:T(8,128)(2,1)S(1)}, u32[]{:S(2)}, u32[]{:S(2)}) %collective-permute-start.6) | collective-permute-done | bytes 32800 | tf_op jit(solution)/shard_map/ppermute | solution.py:1030
  64.9 4.3 %collective-permute-done.5 = bf16[128,128]{1,0:T(8,128)(2,1)S(1)} collective-permute-done((bf16[128,128]{1,0:T(8,128)(2,1)S(1)}, bf16[128,128]{1,0:T(8,128)(2,1)S(1)}, u32[]{:S(2)}, u32[]{:S(2)}) %collective-permute-start.5) | collective-permute-done | bytes 32800 | tf_op jit(solution)/shard_map/ppermute | solution.py:1030
  69.2 3.4 %collective-permute-start.9 = (bf16[128,128]{1,0:T(8,128)(2,1)S(1)}, bf16[128,128]{1,0:T(8,128)(2,1)S(1)}, u32[]{:S(2)}, u32[]{:S(2)}) collective-permute-start(bf16[128,128]{1,0:T(8,128)(2,1)S(1)} %fusion.14), channel_id=1, source_target_pairs={{0,6},{1,7},{2,4},{3,5},{4,2},{5,3},{6,0},{7,1},{8,14},{9,15},{10,... | collective-permute-start | bytes 98312 | tf_op jit(solution)/shard_map/ppermute | solution.py:1030
  72.6 1.1 collective-permute-start.7
  73.7 2.0 collective-permute-done.9
  75.7 2.4 %collective-permute-done.8 = bf16[128,128]{1,0:T(8,128)(2,1)S(1)} collective-permute-done((bf16[128,128]{1,0:T(8,128)(2,1)S(1)}, bf16[128,128]{1,0:T(8,128)(2,1)S(1)}, u32[]{:S(2)}, u32[]{:S(2)}) %collective-permute-start.8) | collective-permute-done | bytes 32800 | tf_op jit(solution)/shard_map/ppermute | solution.py:1030
  78.4 1.4 all-gather.5.cloned.1.call-done
  80.4 36.1 %scan.1 = (bf16[8,128,1024]{2,1,0:T(8,128)(2,1)}, bf16[8,128,256]{2,1,0:T(8,128)(2,1)}, bf16[8,128,256]{2,1,0:T(8,128)(2,1)}, bf16[4,128,128]{2,1,0:T(8,128)(2,1...) custom-call(s32[3]{0:T(128)} %pad_add_fusion.me_ref, ...), custom_call_target="tpu_custom_call" | custom-call | flops 41799999488 | bytes 1048576 | tf_op jit(solution)/shard_map/scan/pallas_call | solution.py:869
  117.7 2.5 %fusion = bf16[1024,256]{1,0:T(8,128)(2,1)S(1)} fusion(bf16[8,128,1024]{2,1,0:T(8,128)(2,1)} %get-tuple-element.85, bf16[8,128,256]{2,1,0:T(8,128)(2,1)S(1)} %copy-done.22), kind=kOutput, calls=%fused_computation.9 | convolution fusion | flops 537133056 | bytes 3145728 | tf_op jit(solution)/shard_map/dot_general | solution.py:38
  122.0 2.5 %collective-permute-start.14 = (bf16[128,128]{1,0:T(8,128)(2,1)S(1)}, bf16[128,128]{1,0:T(8,128)(2,1)S(1)}, u32[]{:S(2)}, u32[]{:S(2)}) collective-permute-start(bf16[128,128]{1,0:T(8,128)(2,1)S(1)} %get-tuple-element.129), channel_id=1, source_target_pairs={{0,6},{1,7},{2,4},{3,5},{4,2},{5,3},{6,0},{7,1},{8,14},{9,15},{10,... | collective-permute-start | bytes 98312 | tf_op jit(solution)/shard_map/ppermute | solution.py:1030
  124.5 1.0 collective-permute-start.13
  125.5 2.4 %collective-permute-start.20 = (bf16[512,256]{1,0:T(8,128)(2,1)S(1)}, bf16[512,256]{1,0:T(8,128)(2,1)S(1)}, u32[]{:S(2)}, u32[]{:S(2)}) collective-permute-start(bf16[512,256]{1,0:T(8,128)(2,1)S(1)} %get-tuple-element.122), channel_id=1, source_target_pairs={{0,24},{8,16},{16,8},{24,0},{1,25},{9,17},{17,9},{25,1},{2,26},{10... | collective-permute-start | bytes 786440 | tf_op jit(solution)/shard_map/ppermute | solution.py:1030
  129.1 2.7 %collective-permute-done.13 = bf16[128,128]{1,0:T(8,128)(2,1)S(1)} collective-permute-done((bf16[128,128]{1,0:T(8,128)(2,1)S(1)}, bf16[128,128]{1,0:T(8,128)(2,1)S(1)}, u32[]{:S(2)}, u32[]{:S(2)}) %collective-permute-start.13) | collective-permute-done | bytes 32800 | tf_op jit(solution)/shard_map/ppermute | solution.py:1030
  132.3 6.2 %collective-permute-done.17 = bf16[128,128]{1,0:T(8,128)(2,1)S(1)} collective-permute-done((bf16[128,128]{1,0:T(8,128)(2,1)S(1)}, bf16[128,128]{1,0:T(8,128)(2,1)S(1)}, u32[]{:S(2)}, u32[]{:S(2)}) %collective-permute-start.17) | collective-permute-done | bytes 32800 | tf_op jit(solution)/shard_map/ppermute | solution.py:1030
  138.6 4.8 %collective-permute-done.15 = bf16[128,128]{1,0:T(8,128)(2,1)S(1)} collective-permute-done((bf16[128,128]{1,0:T(8,128)(2,1)S(1)}, bf16[128,128]{1,0:T(8,128)(2,1)S(1)}, u32[]{:S(2)}, u32[]{:S(2)}) %collective-permute-start.15) | collective-permute-done | bytes 32800 | tf_op jit(solution)/shard_map/ppermute | solution.py:1030
  143.5 1.3 collective-permute-done.21.other_ref
  145.5 10.4 %exit.1 = (bf16[1024,1024]{1,0:T(8,128)(2,1)}, bf16[320,256]{1,0:T(8,128)(2,1)}, bf16[320,256]{1,0:T(8,128)(2,1)}, bf16[320,256]{1,0:T(8,128)(2,1)}, bf16[320,256]{1,0:T(8,128)(2,1)}) custom-call(s32[3]{0:T(128)} %pad_add_fusion.me_ref, s32[1,4]{1,0:T(1,128)} %bitcast_subtract_fusion.starts_ref, bf16[4,128,128]{2,1,0:T(8,128)(2,1)} %copy-done.11, ...), custom_call_target="tpu_custom_call" | custom-call | flops 11000000512 | bytes 1048576 | tf_op jit(solution)/shard_map/exit/pallas_call | solution.py:919
  156.8 1.0 collective-permute-start.22
  157.8 1.8 collective-permute-start.23
  160.9 3.4 %all-to-all-start.2 = ((bf16[8,32,256]{2,1,0:T(8,128)(2,1)}), bf16[8,32,256]{2,1,0:T(8,128)(2,1)S(1)}, u32[]{:S(2)}, u32[]{:S(2)}) async-start(bf16[8,32,256]{2,1,0:T(8,128)(2,1)} %bitcast.60), calls=%async_computation.2 | async-start | bytes 262144 | tf_op jit(solution)/shard_map/all_to_all | solution.py:1087
  164.3 2.3 %collective-permute-done.23 = bf16[320,256]{1,0:T(8,128)(2,1)S(1)} collective-permute-done((bf16[320,256]{1,0:T(8,128)(2,1)S(1)}, bf16[320,256]{1,0:T(8,128)(2,1)S(1)}, u32[]{:S(2)}, u32[]{:S(2)}) %collective-permute-start.23) | collective-permute-done | bytes 163872 | tf_op jit(solution)/shard_map/ppermute | solution.py:1030
  168.2 4.6 %all-to-all-done.2 = bf16[8,32,256]{2,1,0:T(8,128)(2,1)S(1)} async-done(((bf16[8,32,256]{2,1,0:T(8,128)(2,1)}), bf16[8,32,256]{2,1,0:T(8,128)(2,1)S(1)}, u32[]{:S(2)}, u32[]{:S(2)}) %all-to-all-start.2) | async-done | bytes 131104 | tf_op jit(solution)/shard_map/all_to_all | solution.py:1087
  172.8 3.4 %all-to-all-start.1 = ((bf16[8,48,256]{2,1,0:T(8,128)(2,1)}), bf16[8,48,256]{2,1,0:T(8,128)(2,1)S(1)}, u32[]{:S(2)}, u32[]{:S(2)}) async-start(bf16[8,48,256]{2,1,0:T(8,128)(2,1)} %fusion.10), calls=%async_computation.1 | async-start | bytes 393216 | tf_op jit(solution)/shard_map/all_to_all | solution.py:1087
  176.2 2.6 %collective-permute-start.30 = (bf16[512,256]{1,0:T(8,128)(2,1)S(1)}, bf16[512,256]{1,0:T(8,128)(2,1)S(1)}, u32[]{:S(2)}, u32[]{:S(2)}) collective-permute-start(bf16[512,256]{1,0:T(8,128)(2,1)S(1)} %pad_maximum_fusion.refs_4_), channel_id=1, source_target_pairs={{0,24},{8,16},{16,8},{24,0},{1,25},{9,17},{17,9},{25,1},{2,26},{10... | collective-permute-start | bytes 786440 | tf_op jit(solution)/shard_map/ppermute | solution.py:1030
  179.8 7.3 %all-to-all-done.1.refs_8_ = bf16[8,48,256]{2,1,0:T(8,128)(2,1)S(1)} async-done(((bf16[8,48,256]{2,1,0:T(8,128)(2,1)}), bf16[8,48,256]{2,1,0:T(8,128)(2,1)S(1)}, u32[]{:S(2)}, u32[]{:S(2)}) %all-to-all-start.1) | async-done | bytes 196640 | tf_op jit(solution)/shard_map/all_to_all | solution.py:1087
  187.1 3.2 %collective-permute-start.27 = (bf16[304,256]{1,0:T(8,128)(2,1)S(1)}, bf16[304,256]{1,0:T(8,128)(2,1)S(1)}, u32[]{:S(2)}, u32[]{:S(2)}) collective-permute-start(bf16[304,256]{1,0:T(8,128)(2,1)S(1)} %pad_maximum_fusion.1.refs_0_), channel_id=1, source_target_pairs={{0,24},{8,16},{16,8},{24,0},{1,25},{9,17},{17,9},{25,1},{2,26},{10... | collective-permute-start | bytes 466952 | tf_op jit(solution)/shard_map/ppermute | solution.py:1030
  191.0 1.0 collective-permute-done.29.refs_6_
  192.1 3.2 %collective-permute-done.27.refs_3_ = bf16[304,256]{1,0:T(8,128)(2,1)S(1)} collective-permute-done((bf16[304,256]{1,0:T(8,128)(2,1)S(1)}, bf16[304,256]{1,0:T(8,128)(2,1)S(1)}, u32[]{:S(2)}, u32[]{:S(2)}) %collective-permute-start.27) | collective-permute-done | bytes 155680 | tf_op jit(solution)/shard_map/ppermute | solution.py:1030
  195.3 2.8 %collective-permute-done.26.refs_2_ = bf16[304,256]{1,0:T(8,128)(2,1)S(1)} collective-permute-done((bf16[304,256]{1,0:T(8,128)(2,1)S(1)}, bf16[304,256]{1,0:T(8,128)(2,1)S(1)}, u32[]{:S(2)}, u32[]{:S(2)}) %collective-permute-start.26) | collective-permute-done | bytes 155680 | tf_op jit(solution)/shard_map/ppermute | solution.py:1030
  198.4 0.9 copy-done.3
  199.3 0.9 copy-done.4
  200.3 2.2 %finish.1 = (bf16[128,1024]{1,0:T(8,128)(2,1)}, bf16[128,1024]{1,0:T(8,128)(2,1)}, f32[1,128]{1,0:T(1,128)}, f32[128,4096]{1,0:T(8,128)}, f32[4,256]{1,0:T(4,128...) custom-call(s32[1]{0:T(128)} %bitcast.me_ref, ...), custom_call_target="tpu_custom_call" | custom-call | flops 4400000000 | bytes 1048576 | tf_op jit(solution)/shard_map/finish/pallas_call | solution.py:1151
  (135 shorter events, 19.8 us)
Async XLA Ops:
  7.2 9.3 %copy-start.21 = (s32[1,4]{1,0:T(1,128)S(1)}, s32[1,4]{1,0:T(1,128)}, u32[]{:S(2)}) copy-start(s32[1,4]{1,0:T(1,128)} %param.25) | copy-start | bytes 52
  7.2 9.6 %copy-start.14 = (s32[1024]{0:T(1024)S(1)}, s32[1024]{0:T(1024)}, u32[]{:S(2)}) copy-start(s32[1024]{0:T(1024)} %param.26) | copy-start | bytes 12292
  7.2 12.1 %copy-start.13 = (bf16[64,256]{1,0:T(8,128)(2,1)S(1)}, bf16[64,256]{1,0:T(8,128)(2,1)}, u32[]{:S(2)}) copy-start(bf16[64,256]{1,0:T(8,128)(2,1)} %dtw_ref.1) | copy-start | bytes 98308
  7.2 36.7 %all-gather.3.cloned.1.call-start = ((), (), s32[]{:S(2)}) async-start(), calls=%async_computation.5 | async-start | bytes 2359296 | tf_op jit(solution)/shard_map/all_gather | solution.py:1208
  9.4 18.3 %all-to-all-start = ((bf16[8,32,2,256]{3,2,1,0:T(2,128)(2,1)}), bf16[8,32,2,256]{3,2,1,0:T(2,128)(2,1)S(1)}, u32[]{:S(2)}, u32[]{:S(2)}) async-start(bf16[8,32,2,256]{3,2,1,0:T(2,128)(2,1)} %copy.66), calls=%async_computation | async-start | bytes 524288 | tf_op jit(solution)/shard_map/all_to_all | solution.py:1087
  15.7 64.1 %all-gather.5.cloned.1.call-start = ((), (), s32[]{:S(2)}) async-start(), calls=%async_computation.6 | async-start | bytes 2359296 | tf_op jit(solution)/shard_map/all_gather | solution.py:1213
  16.5 181.9 %reduce-scatter.3.cloned.1.call-start = ((), (), s32[]{:S(2)}) async-start(), calls=%async_computation.7 | async-start | bytes 2359296 | tf_op jit(solution)/shard_map/reduce_scatter | solution.py:1261
  28.8 9.2 %collective-permute-start = (bf16[8,32,512]{2,1,0:T(8,128)(2,1)S(1)}, bf16[8,32,512]{2,1,0:T(8,128)(2,1)S(1)}, u32[]{:S(2)}, u32[]{:S(2)}) collective-permute-start(bf16[8,32,512]{2,1,0:T(8,128)(2,1)S(1)} %reshape.119), channel_id=1, source_target_pairs={{0,8},{8,0},{16,24},{24,16},{1,9},{9,1},{17,25},{25,17},{2,10},{10... | collective-permute-start | bytes 786440 | tf_op jit(solution)/shard_map/ppermute | solution.py:1030
  31.0 12.9 %collective-permute-start.2 = (bf16[8,32,512]{2,1,0:T(8,128)(2,1)S(1)}, bf16[8,32,512]{2,1,0:T(8,128)(2,1)S(1)}, u32[]{:S(2)}, u32[]{:S(2)}) collective-permute-start(bf16[8,32,512]{2,1,0:T(8,128)(2,1)S(1)} %reshape.119), channel_id=1, source_target_pairs={{0,24},{8,16},{16,8},{24,0},{1,25},{9,17},{17,9},{25,1},{2,26},{10... | collective-permute-start | bytes 786440 | tf_op jit(solution)/shard_map/ppermute | solution.py:1030
  32.6 11.3 %collective-permute-start.1 = (bf16[8,32,512]{2,1,0:T(8,128)(2,1)S(1)}, bf16[8,32,512]{2,1,0:T(8,128)(2,1)S(1)}, u32[]{:S(2)}, u32[]{:S(2)}) collective-permute-start(bf16[8,32,512]{2,1,0:T(8,128)(2,1)S(1)} %reshape.119), channel_id=1, source_target_pairs={{0,16},{8,24},{16,0},{24,8},{1,17},{9,25},{17,1},{25,9},{2,18},{10... | collective-permute-start | bytes 786440 | tf_op jit(solution)/shard_map/ppermute | solution.py:1030
  52.7 1.6 collective-permute-start.3
  55.3 6.0 %collective-permute-start.4 = (bf16[128,128]{1,0:T(8,128)(2,1)S(1)}, bf16[128,128]{1,0:T(8,128)(2,1)S(1)}, u32[]{:S(2)}, u32[]{:S(2)}) collective-permute-start(bf16[128,128]{1,0:T(8,128)(2,1)S(1)} %get-tuple-element.131), channel_id=1, source_target_pairs={{0,2},{1,3},{2,0},{3,1},{4,6},{5,7},{6,4},{7,5},{8,10},{9,11},{10,... | collective-permute-start | bytes 98312 | tf_op jit(solution)/shard_map/ppermute | solution.py:1030
  56.6 8.3 %collective-permute-start.6 = (bf16[128,128]{1,0:T(8,128)(2,1)S(1)}, bf16[128,128]{1,0:T(8,128)(2,1)S(1)}, u32[]{:S(2)}, u32[]{:S(2)}) collective-permute-start(bf16[128,128]{1,0:T(8,128)(2,1)S(1)} %get-tuple-element.132), channel_id=1, source_target_pairs={{0,6},{1,7},{2,4},{3,5},{4,2},{5,3},{6,0},{7,1},{8,14},{9,15},{10,... | collective-permute-start | bytes 98312 | tf_op jit(solution)/shard_map/ppermute | solution.py:1030
  60.7 8.5 %collective-permute-start.5 = (bf16[128,128]{1,0:T(8,128)(2,1)S(1)}, bf16[128,128]{1,0:T(8,128)(2,1)S(1)}, u32[]{:S(2)}, u32[]{:S(2)}) collective-permute-start(bf16[128,128]{1,0:T(8,128)(2,1)S(1)} %get-tuple-element.133), channel_id=1, source_target_pairs={{0,4},{1,5},{2,6},{3,7},{4,0},{5,1},{6,2},{7,3},{8,12},{9,13},{10,... | collective-permute-start | bytes 98312 | tf_op jit(solution)/shard_map/ppermute | solution.py:1030
  69.2 6.5 %collective-permute-start.9 = (bf16[128,128]{1,0:T(8,128)(2,1)S(1)}, bf16[128,128]{1,0:T(8,128)(2,1)S(1)}, u32[]{:S(2)}, u32[]{:S(2)}) collective-permute-start(bf16[128,128]{1,0:T(8,128)(2,1)S(1)} %fusion.14), channel_id=1, source_target_pairs={{0,6},{1,7},{2,4},{3,5},{4,2},{5,3},{6,0},{7,1},{8,14},{9,15},{10,... | collective-permute-start | bytes 98312 | tf_op jit(solution)/shard_map/ppermute | solution.py:1030
  72.6 5.5 %collective-permute-start.8 = (bf16[128,128]{1,0:T(8,128)(2,1)S(1)}, bf16[128,128]{1,0:T(8,128)(2,1)S(1)}, u32[]{:S(2)}, u32[]{:S(2)}) collective-permute-start(bf16[128,128]{1,0:T(8,128)(2,1)S(1)} %fusion.14), channel_id=1, source_target_pairs={{0,4},{1,5},{2,6},{3,7},{4,0},{5,1},{6,2},{7,3},{8,12},{9,13},{10,... | collective-permute-start | bytes 98312 | tf_op jit(solution)/shard_map/ppermute | solution.py:1030
  72.6 5.7 %collective-permute-start.7 = (bf16[128,128]{1,0:T(8,128)(2,1)S(1)}, bf16[128,128]{1,0:T(8,128)(2,1)S(1)}, u32[]{:S(2)}, u32[]{:S(2)}) collective-permute-start(bf16[128,128]{1,0:T(8,128)(2,1)S(1)} %fusion.14), channel_id=1, source_target_pairs={{0,2},{1,3},{2,0},{3,1},{4,6},{5,7},{6,4},{7,5},{8,10},{9,11},{10,... | collective-permute-start | bytes 98312 | tf_op jit(solution)/shard_map/ppermute | solution.py:1030
  78.3 1.5 collective-permute-start.10
  116.6 81.8 %reduce-scatter.5.cloned.1.call-start = ((), (), s32[]{:S(2)}) async-start(), calls=%async_computation.8 | async-start | bytes 2359296 | tf_op jit(solution)/shard_map/reduce_scatter | solution.py:1281
  117.4 4.0 %collective-permute-start.11 = (bf16[4,128,128]{2,1,0:T(8,128)(2,1)S(1)}, bf16[4,128,128]{2,1,0:T(8,128)(2,1)S(1)}, u32[]{:S(2)}, u32[]{:S(2)}) collective-permute-start(bf16[4,128,128]{2,1,0:T(8,128)(2,1)S(1)} %copy-done.18), channel_id=1, source_target_pairs={{0,1},{1,0},{2,3},{3,2},{4,5},{5,4},{6,7},{7,6},{8,9},{9,8},{10,11... | collective-permute-start | bytes 393224 | tf_op jit(solution)/shard_map/ppermute | solution.py:1030
  117.7 2.5 %copy-start.6 = (bf16[1024,1024]{1,0:T(8,128)(2,1)S(1)}, bf16[1024,1024]{1,0:T(8,128)(2,1)}, u32[]{:S(2)}) copy-start(bf16[1024,1024]{1,0:T(8,128)(2,1)} %all-gather.5.cloned.1.call-done) | copy-start | bytes 6291460
  117.7 2.5 %copy-start.8 = (bf16[8,128,256]{2,1,0:T(8,128)(2,1)S(1)}, bf16[8,128,256]{2,1,0:T(8,128)(2,1)}, u32[]{:S(2)}) copy-start(bf16[8,128,256]{2,1,0:T(8,128)(2,1)} %get-tuple-element.84) | copy-start | bytes 1572868
  121.9 6.6 %collective-permute-start.12 = (bf16[128,128]{1,0:T(8,128)(2,1)S(1)}, bf16[128,128]{1,0:T(8,128)(2,1)S(1)}, u32[]{:S(2)}, u32[]{:S(2)}) collective-permute-start(bf16[128,128]{1,0:T(8,128)(2,1)S(1)} %get-tuple-element.128), channel_id=1, source_target_pairs={{0,2},{1,3},{2,0},{3,1},{4,6},{5,7},{6,4},{7,5},{8,10},{9,11},{10,... | collective-permute-start | bytes 98312 | tf_op jit(solution)/shard_map/ppermute | solution.py:1030
  122.0 7.1 %collective-permute-start.14 = (bf16[128,128]{1,0:T(8,128)(2,1)S(1)}, bf16[128,128]{1,0:T(8,128)(2,1)S(1)}, u32[]{:S(2)}, u32[]{:S(2)}) collective-permute-start(bf16[128,128]{1,0:T(8,128)(2,1)S(1)} %get-tuple-element.129), channel_id=1, source_target_pairs={{0,6},{1,7},{2,4},{3,5},{4,2},{5,3},{6,0},{7,1},{8,14},{9,15},{10,... | collective-permute-start | bytes 98312 | tf_op jit(solution)/shard_map/ppermute | solution.py:1030
  124.5 7.3 %collective-permute-start.13 = (bf16[128,128]{1,0:T(8,128)(2,1)S(1)}, bf16[128,128]{1,0:T(8,128)(2,1)S(1)}, u32[]{:S(2)}, u32[]{:S(2)}) collective-permute-start(bf16[128,128]{1,0:T(8,128)(2,1)S(1)} %get-tuple-element.130), channel_id=1, source_target_pairs={{0,4},{1,5},{2,6},{3,7},{4,0},{5,1},{6,2},{7,3},{8,12},{9,13},{10,... | collective-permute-start | bytes 98312 | tf_op jit(solution)/shard_map/ppermute | solution.py:1030
  125.5 17.8 %collective-permute-start.20 = (bf16[512,256]{1,0:T(8,128)(2,1)S(1)}, bf16[512,256]{1,0:T(8,128)(2,1)S(1)}, u32[]{:S(2)}, u32[]{:S(2)}) collective-permute-start(bf16[512,256]{1,0:T(8,128)(2,1)S(1)} %get-tuple-element.122), channel_id=1, source_target_pairs={{0,24},{8,16},{16,8},{24,0},{1,25},{9,17},{17,9},{25,1},{2,26},{10... | collective-permute-start | bytes 786440 | tf_op jit(solution)/shard_map/ppermute | solution.py:1030
  127.9 15.4 %collective-permute-start.18 = (bf16[512,256]{1,0:T(8,128)(2,1)S(1)}, bf16[512,256]{1,0:T(8,128)(2,1)S(1)}, u32[]{:S(2)}, u32[]{:S(2)}) collective-permute-start(bf16[512,256]{1,0:T(8,128)(2,1)S(1)} %get-tuple-element.124), channel_id=1, source_target_pairs={{0,8},{8,0},{16,24},{24,16},{1,9},{9,1},{17,25},{25,17},{2,10},{10... | collective-permute-start | bytes 786440 | tf_op jit(solution)/shard_map/ppermute | solution.py:1030
  128.5 14.9 %collective-permute-start.19 = (bf16[512,256]{1,0:T(8,128)(2,1)S(1)}, bf16[512,256]{1,0:T(8,128)(2,1)S(1)}, u32[]{:S(2)}, u32[]{:S(2)}) collective-permute-start(bf16[512,256]{1,0:T(8,128)(2,1)S(1)} %get-tuple-element.125), channel_id=1, source_target_pairs={{0,16},{8,24},{16,0},{24,8},{1,17},{9,25},{17,1},{25,9},{2,18},{10... | collective-permute-start | bytes 786440 | tf_op jit(solution)/shard_map/ppermute | solution.py:1030
  131.8 6.7 %collective-permute-start.17 = (bf16[128,128]{1,0:T(8,128)(2,1)S(1)}, bf16[128,128]{1,0:T(8,128)(2,1)S(1)}, u32[]{:S(2)}, u32[]{:S(2)}) collective-permute-start(bf16[128,128]{1,0:T(8,128)(2,1)S(1)} %fusion.12), channel_id=1, source_target_pairs={{0,6},{1,7},{2,4},{3,5},{4,2},{5,3},{6,0},{7,1},{8,14},{9,15},{10,... | collective-permute-start | bytes 98312 | tf_op jit(solution)/shard_map/ppermute | solution.py:1030
  131.9 6.6 %collective-permute-start.16 = (bf16[128,128]{1,0:T(8,128)(2,1)S(1)}, bf16[128,128]{1,0:T(8,128)(2,1)S(1)}, u32[]{:S(2)}, u32[]{:S(2)}) collective-permute-start(bf16[128,128]{1,0:T(8,128)(2,1)S(1)} %fusion.12), channel_id=1, source_target_pairs={{0,4},{1,5},{2,6},{3,7},{4,0},{5,1},{6,2},{7,3},{8,12},{9,13},{10,... | collective-permute-start | bytes 98312 | tf_op jit(solution)/shard_map/ppermute | solution.py:1030
  138.6 4.8 %collective-permute-start.15 = (bf16[128,128]{1,0:T(8,128)(2,1)S(1)}, bf16[128,128]{1,0:T(8,128)(2,1)S(1)}, u32[]{:S(2)}, u32[]{:S(2)}) collective-permute-start(bf16[128,128]{1,0:T(8,128)(2,1)S(1)} %fusion.12), channel_id=1, source_target_pairs={{0,2},{1,3},{2,0},{3,1},{4,6},{5,7},{6,4},{7,5},{8,10},{9,11},{10,... | collective-permute-start | bytes 98312 | tf_op jit(solution)/shard_map/ppermute | solution.py:1030
  143.4 1.4 collective-permute-start.21
  155.9 3.8 %copy-start.15 = (bf16[320,256]{1,0:T(8,128)(2,1)S(1)}, bf16[320,256]{1,0:T(8,128)(2,1)}, u32[]{:S(2)}) copy-start(bf16[320,256]{1,0:T(8,128)(2,1)} %get-tuple-element.102) | copy-start | bytes 491524
  155.9 11.5 %copy-start.9 = (bf16[320,256]{1,0:T(8,128)(2,1)S(1)}, bf16[320,256]{1,0:T(8,128)(2,1)}, u32[]{:S(2)}) copy-start(bf16[320,256]{1,0:T(8,128)(2,1)} %get-tuple-element.99) | copy-start | bytes 491524
  156.0 42.3 %copy-start.1 = (bf16[128,1024]{1,0:T(8,128)(2,1)S(1)}, bf16[128,1024]{1,0:T(8,128)(2,1)}, u32[]{:S(2)}) copy-start(bf16[128,1024]{1,0:T(8,128)(2,1)} %refs_11_.1) | copy-start | bytes 786436
  156.1 42.3 %copy-start.2 = (bf16[128,1024]{1,0:T(8,128)(2,1)S(1)}, bf16[128,1024]{1,0:T(8,128)(2,1)}, u32[]{:S(2)}) copy-start(bf16[128,1024]{1,0:T(8,128)(2,1)} %refs_12_.1) | copy-start | bytes 786436
  156.1 42.3 %copy-start.5 = (f32[1024]{0:T(1024)S(1)}, f32[1024]{0:T(1024)}, u32[]{:S(2)}) copy-start(f32[1024]{0:T(1024)} %param.15) | copy-start | bytes 12292
  156.8 7.5 %collective-permute-start.22 = (bf16[320,256]{1,0:T(8,128)(2,1)S(1)}, bf16[320,256]{1,0:T(8,128)(2,1)S(1)}, u32[]{:S(2)}, u32[]{:S(2)}) collective-permute-start(bf16[320,256]{1,0:T(8,128)(2,1)S(1)} %copy-done.17), channel_id=1, source_target_pairs={{0,8},{8,0},{16,24},{24,16},{1,9},{9,1},{17,25},{25,17},{2,10},{10... | collective-permute-start | bytes 491528 | tf_op jit(solution)/shard_map/ppermute | solution.py:1030
  157.8 8.8 %collective-permute-start.23 = (bf16[320,256]{1,0:T(8,128)(2,1)S(1)}, bf16[320,256]{1,0:T(8,128)(2,1)S(1)}, u32[]{:S(2)}, u32[]{:S(2)}) collective-permute-start(bf16[320,256]{1,0:T(8,128)(2,1)S(1)} %copy-done.16), channel_id=1, source_target_pairs={{0,16},{8,24},{16,0},{24,8},{1,17},{9,25},{17,1},{25,9},{2,18},{10... | collective-permute-start | bytes 491528 | tf_op jit(solution)/shard_map/ppermute | solution.py:1030
  159.6 7.7 %collective-permute-start.24 = (bf16[320,256]{1,0:T(8,128)(2,1)S(1)}, bf16[320,256]{1,0:T(8,128)(2,1)S(1)}, u32[]{:S(2)}, u32[]{:S(2)}) collective-permute-start(bf16[320,256]{1,0:T(8,128)(2,1)S(1)} %copy-done.15), channel_id=1, source_target_pairs={{0,24},{8,16},{16,8},{24,0},{1,25},{9,17},{17,9},{25,1},{2,26},{10... | collective-permute-start | bytes 491528 | tf_op jit(solution)/shard_map/ppermute | solution.py:1030
  160.9 11.9 %all-to-all-start.2 = ((bf16[8,32,256]{2,1,0:T(8,128)(2,1)}), bf16[8,32,256]{2,1,0:T(8,128)(2,1)S(1)}, u32[]{:S(2)}, u32[]{:S(2)}) async-start(bf16[8,32,256]{2,1,0:T(8,128)(2,1)} %bitcast.60), calls=%async_computation.2 | async-start | bytes 262144 | tf_op jit(solution)/shard_map/all_to_all | solution.py:1087
  172.8 14.3 %all-to-all-start.1 = ((bf16[8,48,256]{2,1,0:T(8,128)(2,1)}), bf16[8,48,256]{2,1,0:T(8,128)(2,1)S(1)}, u32[]{:S(2)}, u32[]{:S(2)}) async-start(bf16[8,48,256]{2,1,0:T(8,128)(2,1)} %fusion.10), calls=%async_computation.1 | async-start | bytes 393216 | tf_op jit(solution)/shard_map/all_to_all | solution.py:1087
  176.2 14.1 %collective-permute-start.30 = (bf16[512,256]{1,0:T(8,128)(2,1)S(1)}, bf16[512,256]{1,0:T(8,128)(2,1)S(1)}, u32[]{:S(2)}, u32[]{:S(2)}) collective-permute-start(bf16[512,256]{1,0:T(8,128)(2,1)S(1)} %pad_maximum_fusion.refs_4_), channel_id=1, source_target_pairs={{0,24},{8,16},{16,8},{24,0},{1,25},{9,17},{17,9},{25,1},{2,26},{10... | collective-permute-start | bytes 786440 | tf_op jit(solution)/shard_map/ppermute | solution.py:1030
  178.9 13.1 %collective-permute-start.29 = (bf16[512,256]{1,0:T(8,128)(2,1)S(1)}, bf16[512,256]{1,0:T(8,128)(2,1)S(1)}, u32[]{:S(2)}, u32[]{:S(2)}) collective-permute-start(bf16[512,256]{1,0:T(8,128)(2,1)S(1)} %pad_maximum_fusion.refs_4_), channel_id=1, source_target_pairs={{0,16},{8,24},{16,0},{24,8},{1,17},{9,25},{17,1},{25,9},{2,18},{10... | collective-permute-start | bytes 786440 | tf_op jit(solution)/shard_map/ppermute | solution.py:1030
  179.2 12.9 %collective-permute-start.28 = (bf16[512,256]{1,0:T(8,128)(2,1)S(1)}, bf16[512,256]{1,0:T(8,128)(2,1)S(1)}, u32[]{:S(2)}, u32[]{:S(2)}) collective-permute-start(bf16[512,256]{1,0:T(8,128)(2,1)S(1)} %pad_maximum_fusion.refs_4_), channel_id=1, source_target_pairs={{0,8},{8,0},{16,24},{24,16},{1,9},{9,1},{17,25},{25,17},{2,10},{10... | collective-permute-start | bytes 786440 | tf_op jit(solution)/shard_map/ppermute | solution.py:1030
  187.1 8.2 %collective-permute-start.27 = (bf16[304,256]{1,0:T(8,128)(2,1)S(1)}, bf16[304,256]{1,0:T(8,128)(2,1)S(1)}, u32[]{:S(2)}, u32[]{:S(2)}) collective-permute-start(bf16[304,256]{1,0:T(8,128)(2,1)S(1)} %pad_maximum_fusion.1.refs_0_), channel_id=1, source_target_pairs={{0,24},{8,16},{16,8},{24,0},{1,25},{9,17},{17,9},{25,1},{2,26},{10... | collective-permute-start | bytes 466952 | tf_op jit(solution)/shard_map/ppermute | solution.py:1030
  190.3 7.8 %collective-permute-start.26 = (bf16[304,256]{1,0:T(8,128)(2,1)S(1)}, bf16[304,256]{1,0:T(8,128)(2,1)S(1)}, u32[]{:S(2)}, u32[]{:S(2)}) collective-permute-start(bf16[304,256]{1,0:T(8,128)(2,1)S(1)} %pad_maximum_fusion.1.refs_0_), channel_id=1, source_target_pairs={{0,16},{8,24},{16,0},{24,8},{1,17},{9,25},{17,1},{25,9},{2,18},{10... | collective-permute-start | bytes 466952 | tf_op jit(solution)/shard_map/ppermute | solution.py:1030
  190.3 8.1 %collective-permute-start.25 = (bf16[304,256]{1,0:T(8,128)(2,1)S(1)}, bf16[304,256]{1,0:T(8,128)(2,1)S(1)}, u32[]{:S(2)}, u32[]{:S(2)}) collective-permute-start(bf16[304,256]{1,0:T(8,128)(2,1)S(1)} %pad_maximum_fusion.1.refs_0_), channel_id=1, source_target_pairs={{0,8},{8,0},{16,24},{24,16},{1,9},{9,1},{17,25},{25,17},{2,10},{10... | collective-permute-start | bytes 466952 | tf_op jit(solution)/shard_map/ppermute | solution.py:1030
  (13 other events, 14.2 us)
Sparse Core Ops, SparseCore 0:
  9.7 34.1 all-gather.2
  45.5 34.2 all-gather.4
  116.7 37.4 reduce-scatter.2
  156.9 37.3 reduce-scatter.4

commit v5 on v4

--- a/solution.py
+++ b/solution.py
@@ -798,7 +798,7 @@
     mixed = pl.BlockSpec((size, chans), lambda t: (jnp.minimum(t, turns - 1), 0))
 
     def late(lanes):
-        return pl.BlockSpec((size, lanes), lambda t: (jnp.where(t == turns, 0, jnp.maximum(t, 1)), 0))
+        return pl.BlockSpec((size, lanes), lambda t: (jnp.where(t == turns, 0, jnp.maximum(t, min(1, turns - 1))), 0))
 
     normed, scale, *rest = pl.pallas_call(
         functools.partial(entry_kernel, span, taps),
@@ -905,7 +905,7 @@
     lanes = x_w.shape[1]
     width = hidden_all.shape[1]
     steps = total // SEGS
-    size = math.gcd(total, 256)
+    size = math.gcd(total, 512)
 
     def rows(lanes):
         return pl.BlockSpec((size, lanes), lambda t: (jnp.maximum(t - 1, 0), 0))

time: 210 us -> 209 us (level)
  transfers between devices with their start and end apart: 38 -> 38, of which waited for: 24 -> 22; matrix products, arithmetic and copies ran while one was open for 7% -> 7% of each run, Pallas kernels for 9% -> 8%
where the time goes in v5:
time: 209 us
  waiting for transfers between devices  70.8 us (34%)
  Pallas kernels  55.5 us (27%)
  starting transfers between devices  46 us (22%)
  local copies, waits for them, and re-layouts  15.2 us (7%)
  between operations  14.4 us (7%)
  other arithmetic  3.47 us (2%)
  matrix products  3.22 us (2%)
    ppermute x31, waiting for transfers between devices, swap(): lax.ppermute(value, axis, [(i, i ^ mask) for i in range(lax.axis_size(axi...  49.5 us
    pallas_call x1, Pallas kernels, run_scan(): pl.pallas_call(functools.partial(scan_kernel, rank, states, span), grid=(...  36.1 us
    ppermute x31, starting transfers between devices, swap(): lax.ppermute(value, axis, [(i, i ^ mask) for i in range(lax.axis_size(axi...  32.6 us
    all_to_all x3, waiting for transfers between devices, to_peers(): return lax.all_to_all(blocks, 'ch', split_axis=0, concat_axis=0, tiled=True)  18.4 us
    all_to_all x3, starting transfers between devices, to_peers(): return lax.all_to_all(blocks, 'ch', split_axis=0, concat_axis=0, tiled=True)  13.1 us
    pallas_call x1, Pallas kernels, run_exit(): pl.pallas_call(functools.partial(exit_kernel, span, taps, low_cols, packs...  9.52 us
    pallas_call x1, Pallas kernels, run_entry(): pl.pallas_call(functools.partial(entry_kernel, span, taps), grid=(turns +...  7.76 us
    unnamed x49, local copies, waits for them, and re-layouts  6.63 us
  transfers between devices with their start and end apart: 38, of which 22 were waited for; matrix products, arithmetic and copies ran while one was open for 7% of the time, Pallas kernels for 8%

profile of v5, /device:TPU:0, one launch (start us, length us, event | category | flops | bytes accessed | tf_op | source)
XLA Modules:
  0.0 208.5 jit_solution(8106022403326575758)
XLA Ops:
  8.5 0.9 copy.66
  9.4 6.3 %all-to-all-start = ((bf16[8,32,2,256]{3,2,1,0:T(2,128)(2,1)}), bf16[8,32,2,256]{3,2,1,0:T(2,128)(2,1)S(1)}, u32[]{:S(2)}, u32[]{:S(2)}) async-start(bf16[8,32,2,256]{3,2,1,0:T(2,128)(2,1)} %copy.66), calls=%async_computation | async-start | bytes 524288 | tf_op jit(solution)/shard_map/all_to_all | solution.py:1087
  17.1 1.3 dynamic_slice.27
  20.7 1.3 dynamic-slice_bitcast_fusion.cw_ref
  22.5 5.1 %all-to-all-done = bf16[8,32,2,256]{3,2,1,0:T(2,128)(2,1)S(1)} async-done(((bf16[8,32,2,256]{3,2,1,0:T(2,128)(2,1)}), bf16[8,32,2,256]{3,2,1,0:T(2,128)(2,1)S(1)}, u32[]{:S(2)}, u32[]{:S(2)}) %all-to-all-start) | async-done | bytes 262176 | tf_op jit(solution)/shard_map/all_to_all | solution.py:1087
  28.8 1.5 collective-permute-start
  31.0 1.6 collective-permute-start.2
  33.3 4.7 %collective-permute-done = bf16[8,32,512]{2,1,0:T(8,128)(2,1)S(1)} collective-permute-done((bf16[8,32,512]{2,1,0:T(8,128)(2,1)S(1)}, bf16[8,32,512]{2,1,0:T(8,128)(2,1)S(1)}, u32[]{:S(2)}, u32[]{:S(2)}) %collective-permute-start) | collective-permute-done | bytes 262176 | tf_op jit(solution)/shard_map/ppermute | solution.py:1030
  38.0 5.9 %collective-permute-done.1 = bf16[8,32,512]{2,1,0:T(8,128)(2,1)S(1)} collective-permute-done((bf16[8,32,512]{2,1,0:T(8,128)(2,1)S(1)}, bf16[8,32,512]{2,1,0:T(8,128)(2,1)S(1)}, u32[]{:S(2)}, u32[]{:S(2)}) %collective-permute-start.1) | collective-permute-done | bytes 262176 | tf_op jit(solution)/shard_map/ppermute | solution.py:1030
  44.0 0.9 copy-done.7
  44.9 7.8 %entry.1 = (bf16[8,128,1024]{2,1,0:T(8,128)(2,1)}, f32[8,128,128]{2,1,0:T(8,128)}, bf16[1024,256]{1,0:T(8,128)(2,1)}, bf16[1024,256]{1,0:T(8,128)(2,1)}, bf16[10...) custom-call(s32[3]{0:T(128)} %pad_add_fusion.me_ref, ...), custom_call_target="tpu_custom_call" | custom-call | flops 6600000000 | bytes 1048576 | tf_op jit(solution)/shard_map/entry/pallas_call | solution.py:803
  52.7 1.5 collective-permute-done.3
  54.3 0.9 add_convert_fusion.3
  55.3 1.3 collective-permute-start.4
  56.6 4.1 %collective-permute-start.6 = (bf16[128,128]{1,0:T(8,128)(2,1)S(1)}, bf16[128,128]{1,0:T(8,128)(2,1)S(1)}, u32[]{:S(2)}, u32[]{:S(2)}) collective-permute-start(bf16[128,128]{1,0:T(8,128)(2,1)S(1)} %get-tuple-element.132), channel_id=1, source_target_pairs={{0,6},{1,7},{2,4},{3,5},{4,2},{5,3},{6,0},{7,1},{8,14},{9,15},{10,... | collective-permute-start | bytes 98312 | tf_op jit(solution)/shard_map/ppermute | solution.py:1030
  61.2 3.7 %collective-permute-done.6 = bf16[128,128]{1,0:T(8,128)(2,1)S(1)} collective-permute-done((bf16[128,128]{1,0:T(8,128)(2,1)S(1)}, bf16[128,128]{1,0:T(8,128)(2,1)S(1)}, u32[]{:S(2)}, u32[]{:S(2)}) %collective-permute-start.6) | collective-permute-done | bytes 32800 | tf_op jit(solution)/shard_map/ppermute | solution.py:1030
  64.9 4.3 %collective-permute-done.5 = bf16[128,128]{1,0:T(8,128)(2,1)S(1)} collective-permute-done((bf16[128,128]{1,0:T(8,128)(2,1)S(1)}, bf16[128,128]{1,0:T(8,128)(2,1)S(1)}, u32[]{:S(2)}, u32[]{:S(2)}) %collective-permute-start.5) | collective-permute-done | bytes 32800 | tf_op jit(solution)/shard_map/ppermute | solution.py:1030
  69.2 3.4 %collective-permute-start.9 = (bf16[128,128]{1,0:T(8,128)(2,1)S(1)}, bf16[128,128]{1,0:T(8,128)(2,1)S(1)}, u32[]{:S(2)}, u32[]{:S(2)}) collective-permute-start(bf16[128,128]{1,0:T(8,128)(2,1)S(1)} %fusion.14), channel_id=1, source_target_pairs={{0,6},{1,7},{2,4},{3,5},{4,2},{5,3},{6,0},{7,1},{8,14},{9,15},{10,... | collective-permute-start | bytes 98312 | tf_op jit(solution)/shard_map/ppermute | solution.py:1030
  72.6 1.1 collective-permute-start.7
  73.7 2.0 collective-permute-done.9
  75.7 2.4 %collective-permute-done.8 = bf16[128,128]{1,0:T(8,128)(2,1)S(1)} collective-permute-done((bf16[128,128]{1,0:T(8,128)(2,1)S(1)}, bf16[128,128]{1,0:T(8,128)(2,1)S(1)}, u32[]{:S(2)}, u32[]{:S(2)}) %collective-permute-start.8) | collective-permute-done | bytes 32800 | tf_op jit(solution)/shard_map/ppermute | solution.py:1030
  78.4 1.4 all-gather.5.cloned.1.call-done
  80.4 36.1 %scan.1 = (bf16[8,128,1024]{2,1,0:T(8,128)(2,1)}, bf16[8,128,256]{2,1,0:T(8,128)(2,1)}, bf16[8,128,256]{2,1,0:T(8,128)(2,1)}, bf16[4,128,128]{2,1,0:T(8,128)(2,1...) custom-call(s32[3]{0:T(128)} %pad_add_fusion.me_ref, ...), custom_call_target="tpu_custom_call" | custom-call | flops 41799999488 | bytes 1048576 | tf_op jit(solution)/shard_map/scan/pallas_call | solution.py:869
  117.7 2.5 %fusion = bf16[1024,256]{1,0:T(8,128)(2,1)S(1)} fusion(bf16[8,128,1024]{2,1,0:T(8,128)(2,1)} %get-tuple-element.85, bf16[8,128,256]{2,1,0:T(8,128)(2,1)S(1)} %copy-done.22), kind=kOutput, calls=%fused_computation.9 | convolution fusion | flops 537133056 | bytes 3145728 | tf_op jit(solution)/shard_map/dot_general | solution.py:38
  122.0 2.5 %collective-permute-start.14 = (bf16[128,128]{1,0:T(8,128)(2,1)S(1)}, bf16[128,128]{1,0:T(8,128)(2,1)S(1)}, u32[]{:S(2)}, u32[]{:S(2)}) collective-permute-start(bf16[128,128]{1,0:T(8,128)(2,1)S(1)} %get-tuple-element.129), channel_id=1, source_target_pairs={{0,6},{1,7},{2,4},{3,5},{4,2},{5,3},{6,0},{7,1},{8,14},{9,15},{10,... | collective-permute-start | bytes 98312 | tf_op jit(solution)/shard_map/ppermute | solution.py:1030
  124.5 1.0 collective-permute-start.13
  125.5 2.4 %collective-permute-start.20 = (bf16[512,256]{1,0:T(8,128)(2,1)S(1)}, bf16[512,256]{1,0:T(8,128)(2,1)S(1)}, u32[]{:S(2)}, u32[]{:S(2)}) collective-permute-start(bf16[512,256]{1,0:T(8,128)(2,1)S(1)} %get-tuple-element.122), channel_id=1, source_target_pairs={{0,24},{8,16},{16,8},{24,0},{1,25},{9,17},{17,9},{25,1},{2,26},{10... | collective-permute-start | bytes 786440 | tf_op jit(solution)/shard_map/ppermute | solution.py:1030
  129.1 2.7 %collective-permute-done.13 = bf16[128,128]{1,0:T(8,128)(2,1)S(1)} collective-permute-done((bf16[128,128]{1,0:T(8,128)(2,1)S(1)}, bf16[128,128]{1,0:T(8,128)(2,1)S(1)}, u32[]{:S(2)}, u32[]{:S(2)}) %collective-permute-start.13) | collective-permute-done | bytes 32800 | tf_op jit(solution)/shard_map/ppermute | solution.py:1030
  132.3 6.2 %collective-permute-done.17 = bf16[128,128]{1,0:T(8,128)(2,1)S(1)} collective-permute-done((bf16[128,128]{1,0:T(8,128)(2,1)S(1)}, bf16[128,128]{1,0:T(8,128)(2,1)S(1)}, u32[]{:S(2)}, u32[]{:S(2)}) %collective-permute-start.17) | collective-permute-done | bytes 32800 | tf_op jit(solution)/shard_map/ppermute | solution.py:1030
  138.6 4.8 %collective-permute-done.15 = bf16[128,128]{1,0:T(8,128)(2,1)S(1)} collective-permute-done((bf16[128,128]{1,0:T(8,128)(2,1)S(1)}, bf16[128,128]{1,0:T(8,128)(2,1)S(1)}, u32[]{:S(2)}, u32[]{:S(2)}) %collective-permute-start.15) | collective-permute-done | bytes 32800 | tf_op jit(solution)/shard_map/ppermute | solution.py:1030
  143.5 1.3 collective-permute-done.21.other_ref
  145.5 9.5 %exit.1 = (bf16[1024,1024]{1,0:T(8,128)(2,1)}, bf16[320,256]{1,0:T(8,128)(2,1)}, bf16[320,256]{1,0:T(8,128)(2,1)}, bf16[320,256]{1,0:T(8,128)(2,1)}, bf16[320,256]{1,0:T(8,128)(2,1)}) custom-call(s32[3]{0:T(128)} %pad_add_fusion.me_ref, s32[1,4]{1,0:T(1,128)} %bitcast_subtract_fusion.starts_ref, bf16[4,128,128]{2,1,0:T(8,128)(2,1)} %copy-done.11, ...), custom_call_target="tpu_custom_call" | custom-call | flops 11000000512 | bytes 1048576 | tf_op jit(solution)/shard_map/exit/pallas_call | solution.py:919
  155.9 1.0 collective-permute-start.22
  156.9 1.8 collective-permute-start.23
  160.1 3.4 %all-to-all-start.2 = ((bf16[8,32,256]{2,1,0:T(8,128)(2,1)}), bf16[8,32,256]{2,1,0:T(8,128)(2,1)S(1)}, u32[]{:S(2)}, u32[]{:S(2)}) async-start(bf16[8,32,256]{2,1,0:T(8,128)(2,1)} %bitcast.60), calls=%async_computation.2 | async-start | bytes 262144 | tf_op jit(solution)/shard_map/all_to_all | solution.py:1087
  163.5 2.3 %collective-permute-done.23 = bf16[320,256]{1,0:T(8,128)(2,1)S(1)} collective-permute-done((bf16[320,256]{1,0:T(8,128)(2,1)S(1)}, bf16[320,256]{1,0:T(8,128)(2,1)S(1)}, u32[]{:S(2)}, u32[]{:S(2)}) %collective-permute-start.23) | collective-permute-done | bytes 163872 | tf_op jit(solution)/shard_map/ppermute | solution.py:1030
  167.3 5.2 %all-to-all-done.2 = bf16[8,32,256]{2,1,0:T(8,128)(2,1)S(1)} async-done(((bf16[8,32,256]{2,1,0:T(8,128)(2,1)}), bf16[8,32,256]{2,1,0:T(8,128)(2,1)S(1)}, u32[]{:S(2)}, u32[]{:S(2)}) %all-to-all-start.2) | async-done | bytes 131104 | tf_op jit(solution)/shard_map/all_to_all | solution.py:1087
  172.5 3.4 %all-to-all-start.1 = ((bf16[8,48,256]{2,1,0:T(8,128)(2,1)}), bf16[8,48,256]{2,1,0:T(8,128)(2,1)S(1)}, u32[]{:S(2)}, u32[]{:S(2)}) async-start(bf16[8,48,256]{2,1,0:T(8,128)(2,1)} %fusion.10), calls=%async_computation.1 | async-start | bytes 393216 | tf_op jit(solution)/shard_map/all_to_all | solution.py:1087
  176.0 2.4 %collective-permute-start.30 = (bf16[512,256]{1,0:T(8,128)(2,1)S(1)}, bf16[512,256]{1,0:T(8,128)(2,1)S(1)}, u32[]{:S(2)}, u32[]{:S(2)}) collective-permute-start(bf16[512,256]{1,0:T(8,128)(2,1)S(1)} %pad_maximum_fusion.refs_4_), channel_id=1, source_target_pairs={{0,24},{8,16},{16,8},{24,0},{1,25},{9,17},{17,9},{25,1},{2,26},{10... | collective-permute-start | bytes 786440 | tf_op jit(solution)/shard_map/ppermute | solution.py:1030
  178.5 1.0 collective-permute-start.28
  179.5 8.1 %all-to-all-done.1.refs_8_ = bf16[8,48,256]{2,1,0:T(8,128)(2,1)S(1)} async-done(((bf16[8,48,256]{2,1,0:T(8,128)(2,1)}), bf16[8,48,256]{2,1,0:T(8,128)(2,1)S(1)}, u32[]{:S(2)}, u32[]{:S(2)}) %all-to-all-start.1) | async-done | bytes 196640 | tf_op jit(solution)/shard_map/all_to_all | solution.py:1087
  187.7 2.3 %collective-permute-start.27 = (bf16[304,256]{1,0:T(8,128)(2,1)S(1)}, bf16[304,256]{1,0:T(8,128)(2,1)S(1)}, u32[]{:S(2)}, u32[]{:S(2)}) collective-permute-start(bf16[304,256]{1,0:T(8,128)(2,1)S(1)} %pad_maximum_fusion.1.refs_0_), channel_id=1, source_target_pairs={{0,24},{8,16},{16,8},{24,0},{1,25},{9,17},{17,9},{25,1},{2,26},{10... | collective-permute-start | bytes 466952 | tf_op jit(solution)/shard_map/ppermute | solution.py:1030
  190.0 1.2 collective-permute-start.25
  191.8 3.9 %collective-permute-done.27.refs_3_ = bf16[304,256]{1,0:T(8,128)(2,1)S(1)} collective-permute-done((bf16[304,256]{1,0:T(8,128)(2,1)S(1)}, bf16[304,256]{1,0:T(8,128)(2,1)S(1)}, u32[]{:S(2)}, u32[]{:S(2)}) %collective-permute-start.27) | collective-permute-done | bytes 155680 | tf_op jit(solution)/shard_map/ppermute | solution.py:1030
  195.6 2.2 %collective-permute-done.26.refs_2_ = bf16[304,256]{1,0:T(8,128)(2,1)S(1)} collective-permute-done((bf16[304,256]{1,0:T(8,128)(2,1)S(1)}, bf16[304,256]{1,0:T(8,128)(2,1)S(1)}, u32[]{:S(2)}, u32[]{:S(2)}) %collective-permute-start.26) | collective-permute-done | bytes 155680 | tf_op jit(solution)/shard_map/ppermute | solution.py:1030
  197.9 0.9 copy-done.3
  198.9 0.9 copy-done.4
  199.8 2.2 %finish.1 = (bf16[128,1024]{1,0:T(8,128)(2,1)}, bf16[128,1024]{1,0:T(8,128)(2,1)}, f32[1,128]{1,0:T(1,128)}, f32[128,4096]{1,0:T(8,128)}, f32[4,256]{1,0:T(4,128...) custom-call(s32[1]{0:T(128)} %bitcast.me_ref, ...), custom_call_target="tpu_custom_call" | custom-call | flops 4400000000 | bytes 1048576 | tf_op jit(solution)/shard_map/finish/pallas_call | solution.py:1151
  (135 shorter events, 19.4 us)
Async XLA Ops:
  7.2 9.3 %copy-start.21 = (s32[1,4]{1,0:T(1,128)S(1)}, s32[1,4]{1,0:T(1,128)}, u32[]{:S(2)}) copy-start(s32[1,4]{1,0:T(1,128)} %param.25) | copy-start | bytes 52
  7.2 9.6 %copy-start.14 = (s32[1024]{0:T(1024)S(1)}, s32[1024]{0:T(1024)}, u32[]{:S(2)}) copy-start(s32[1024]{0:T(1024)} %param.26) | copy-start | bytes 12292
  7.2 12.1 %copy-start.13 = (bf16[64,256]{1,0:T(8,128)(2,1)S(1)}, bf16[64,256]{1,0:T(8,128)(2,1)}, u32[]{:S(2)}) copy-start(bf16[64,256]{1,0:T(8,128)(2,1)} %dtw_ref.1) | copy-start | bytes 98308
  7.2 36.7 %all-gather.3.cloned.1.call-start = ((), (), s32[]{:S(2)}) async-start(), calls=%async_computation.5 | async-start | bytes 2359296 | tf_op jit(solution)/shard_map/all_gather | solution.py:1208
  9.4 18.3 %all-to-all-start = ((bf16[8,32,2,256]{3,2,1,0:T(2,128)(2,1)}), bf16[8,32,2,256]{3,2,1,0:T(2,128)(2,1)S(1)}, u32[]{:S(2)}, u32[]{:S(2)}) async-start(bf16[8,32,2,256]{3,2,1,0:T(2,128)(2,1)} %copy.66), calls=%async_computation | async-start | bytes 524288 | tf_op jit(solution)/shard_map/all_to_all | solution.py:1087
  15.7 64.1 %all-gather.5.cloned.1.call-start = ((), (), s32[]{:S(2)}) async-start(), calls=%async_computation.6 | async-start | bytes 2359296 | tf_op jit(solution)/shard_map/all_gather | solution.py:1213
  16.5 181.4 %reduce-scatter.3.cloned.1.call-start = ((), (), s32[]{:S(2)}) async-start(), calls=%async_computation.7 | async-start | bytes 2359296 | tf_op jit(solution)/shard_map/reduce_scatter | solution.py:1261
  28.8 9.2 %collective-permute-start = (bf16[8,32,512]{2,1,0:T(8,128)(2,1)S(1)}, bf16[8,32,512]{2,1,0:T(8,128)(2,1)S(1)}, u32[]{:S(2)}, u32[]{:S(2)}) collective-permute-start(bf16[8,32,512]{2,1,0:T(8,128)(2,1)S(1)} %reshape.119), channel_id=1, source_target_pairs={{0,8},{8,0},{16,24},{24,16},{1,9},{9,1},{17,25},{25,17},{2,10},{10... | collective-permute-start | bytes 786440 | tf_op jit(solution)/shard_map/ppermute | solution.py:1030
  31.0 12.9 %collective-permute-start.2 = (bf16[8,32,512]{2,1,0:T(8,128)(2,1)S(1)}, bf16[8,32,512]{2,1,0:T(8,128)(2,1)S(1)}, u32[]{:S(2)}, u32[]{:S(2)}) collective-permute-start(bf16[8,32,512]{2,1,0:T(8,128)(2,1)S(1)} %reshape.119), channel_id=1, source_target_pairs={{0,24},{8,16},{16,8},{24,0},{1,25},{9,17},{17,9},{25,1},{2,26},{10... | collective-permute-start | bytes 786440 | tf_op jit(solution)/shard_map/ppermute | solution.py:1030
  32.6 11.3 %collective-permute-start.1 = (bf16[8,32,512]{2,1,0:T(8,128)(2,1)S(1)}, bf16[8,32,512]{2,1,0:T(8,128)(2,1)S(1)}, u32[]{:S(2)}, u32[]{:S(2)}) collective-permute-start(bf16[8,32,512]{2,1,0:T(8,128)(2,1)S(1)} %reshape.119), channel_id=1, source_target_pairs={{0,16},{8,24},{16,0},{24,8},{1,17},{9,25},{17,1},{25,9},{2,18},{10... | collective-permute-start | bytes 786440 | tf_op jit(solution)/shard_map/ppermute | solution.py:1030
  52.7 1.6 collective-permute-start.3
  55.3 6.0 %collective-permute-start.4 = (bf16[128,128]{1,0:T(8,128)(2,1)S(1)}, bf16[128,128]{1,0:T(8,128)(2,1)S(1)}, u32[]{:S(2)}, u32[]{:S(2)}) collective-permute-start(bf16[128,128]{1,0:T(8,128)(2,1)S(1)} %get-tuple-element.131), channel_id=1, source_target_pairs={{0,2},{1,3},{2,0},{3,1},{4,6},{5,7},{6,4},{7,5},{8,10},{9,11},{10,... | collective-permute-start | bytes 98312 | tf_op jit(solution)/shard_map/ppermute | solution.py:1030
  56.6 8.3 %collective-permute-start.6 = (bf16[128,128]{1,0:T(8,128)(2,1)S(1)}, bf16[128,128]{1,0:T(8,128)(2,1)S(1)}, u32[]{:S(2)}, u32[]{:S(2)}) collective-permute-start(bf16[128,128]{1,0:T(8,128)(2,1)S(1)} %get-tuple-element.132), channel_id=1, source_target_pairs={{0,6},{1,7},{2,4},{3,5},{4,2},{5,3},{6,0},{7,1},{8,14},{9,15},{10,... | collective-permute-start | bytes 98312 | tf_op jit(solution)/shard_map/ppermute | solution.py:1030
  60.7 8.5 %collective-permute-start.5 = (bf16[128,128]{1,0:T(8,128)(2,1)S(1)}, bf16[128,128]{1,0:T(8,128)(2,1)S(1)}, u32[]{:S(2)}, u32[]{:S(2)}) collective-permute-start(bf16[128,128]{1,0:T(8,128)(2,1)S(1)} %get-tuple-element.133), channel_id=1, source_target_pairs={{0,4},{1,5},{2,6},{3,7},{4,0},{5,1},{6,2},{7,3},{8,12},{9,13},{10,... | collective-permute-start | bytes 98312 | tf_op jit(solution)/shard_map/ppermute | solution.py:1030
  69.2 6.5 %collective-permute-start.9 = (bf16[128,128]{1,0:T(8,128)(2,1)S(1)}, bf16[128,128]{1,0:T(8,128)(2,1)S(1)}, u32[]{:S(2)}, u32[]{:S(2)}) collective-permute-start(bf16[128,128]{1,0:T(8,128)(2,1)S(1)} %fusion.14), channel_id=1, source_target_pairs={{0,6},{1,7},{2,4},{3,5},{4,2},{5,3},{6,0},{7,1},{8,14},{9,15},{10,... | collective-permute-start | bytes 98312 | tf_op jit(solution)/shard_map/ppermute | solution.py:1030
  72.6 5.5 %collective-permute-start.8 = (bf16[128,128]{1,0:T(8,128)(2,1)S(1)}, bf16[128,128]{1,0:T(8,128)(2,1)S(1)}, u32[]{:S(2)}, u32[]{:S(2)}) collective-permute-start(bf16[128,128]{1,0:T(8,128)(2,1)S(1)} %fusion.14), channel_id=1, source_target_pairs={{0,4},{1,5},{2,6},{3,7},{4,0},{5,1},{6,2},{7,3},{8,12},{9,13},{10,... | collective-permute-start | bytes 98312 | tf_op jit(solution)/shard_map/ppermute | solution.py:1030
  72.6 5.7 %collective-permute-start.7 = (bf16[128,128]{1,0:T(8,128)(2,1)S(1)}, bf16[128,128]{1,0:T(8,128)(2,1)S(1)}, u32[]{:S(2)}, u32[]{:S(2)}) collective-permute-start(bf16[128,128]{1,0:T(8,128)(2,1)S(1)} %fusion.14), channel_id=1, source_target_pairs={{0,2},{1,3},{2,0},{3,1},{4,6},{5,7},{6,4},{7,5},{8,10},{9,11},{10,... | collective-permute-start | bytes 98312 | tf_op jit(solution)/shard_map/ppermute | solution.py:1030
  78.3 1.5 collective-permute-start.10
  116.6 81.4 %reduce-scatter.5.cloned.1.call-start = ((), (), s32[]{:S(2)}) async-start(), calls=%async_computation.8 | async-start | bytes 2359296 | tf_op jit(solution)/shard_map/reduce_scatter | solution.py:1281
  117.4 4.0 %collective-permute-start.11 = (bf16[4,128,128]{2,1,0:T(8,128)(2,1)S(1)}, bf16[4,128,128]{2,1,0:T(8,128)(2,1)S(1)}, u32[]{:S(2)}, u32[]{:S(2)}) collective-permute-start(bf16[4,128,128]{2,1,0:T(8,128)(2,1)S(1)} %copy-done.18), channel_id=1, source_target_pairs={{0,1},{1,0},{2,3},{3,2},{4,5},{5,4},{6,7},{7,6},{8,9},{9,8},{10,11... | collective-permute-start | bytes 393224 | tf_op jit(solution)/shard_map/ppermute | solution.py:1030
  117.7 2.5 %copy-start.6 = (bf16[1024,1024]{1,0:T(8,128)(2,1)S(1)}, bf16[1024,1024]{1,0:T(8,128)(2,1)}, u32[]{:S(2)}) copy-start(bf16[1024,1024]{1,0:T(8,128)(2,1)} %all-gather.5.cloned.1.call-done) | copy-start | bytes 6291460
  117.7 2.5 %copy-start.8 = (bf16[8,128,256]{2,1,0:T(8,128)(2,1)S(1)}, bf16[8,128,256]{2,1,0:T(8,128)(2,1)}, u32[]{:S(2)}) copy-start(bf16[8,128,256]{2,1,0:T(8,128)(2,1)} %get-tuple-element.84) | copy-start | bytes 1572868
  121.9 6.6 %collective-permute-start.12 = (bf16[128,128]{1,0:T(8,128)(2,1)S(1)}, bf16[128,128]{1,0:T(8,128)(2,1)S(1)}, u32[]{:S(2)}, u32[]{:S(2)}) collective-permute-start(bf16[128,128]{1,0:T(8,128)(2,1)S(1)} %get-tuple-element.128), channel_id=1, source_target_pairs={{0,2},{1,3},{2,0},{3,1},{4,6},{5,7},{6,4},{7,5},{8,10},{9,11},{10,... | collective-permute-start | bytes 98312 | tf_op jit(solution)/shard_map/ppermute | solution.py:1030
  122.0 7.1 %collective-permute-start.14 = (bf16[128,128]{1,0:T(8,128)(2,1)S(1)}, bf16[128,128]{1,0:T(8,128)(2,1)S(1)}, u32[]{:S(2)}, u32[]{:S(2)}) collective-permute-start(bf16[128,128]{1,0:T(8,128)(2,1)S(1)} %get-tuple-element.129), channel_id=1, source_target_pairs={{0,6},{1,7},{2,4},{3,5},{4,2},{5,3},{6,0},{7,1},{8,14},{9,15},{10,... | collective-permute-start | bytes 98312 | tf_op jit(solution)/shard_map/ppermute | solution.py:1030
  124.5 7.3 %collective-permute-start.13 = (bf16[128,128]{1,0:T(8,128)(2,1)S(1)}, bf16[128,128]{1,0:T(8,128)(2,1)S(1)}, u32[]{:S(2)}, u32[]{:S(2)}) collective-permute-start(bf16[128,128]{1,0:T(8,128)(2,1)S(1)} %get-tuple-element.130), channel_id=1, source_target_pairs={{0,4},{1,5},{2,6},{3,7},{4,0},{5,1},{6,2},{7,3},{8,12},{9,13},{10,... | collective-permute-start | bytes 98312 | tf_op jit(solution)/shard_map/ppermute | solution.py:1030
  125.5 17.8 %collective-permute-start.20 = (bf16[512,256]{1,0:T(8,128)(2,1)S(1)}, bf16[512,256]{1,0:T(8,128)(2,1)S(1)}, u32[]{:S(2)}, u32[]{:S(2)}) collective-permute-start(bf16[512,256]{1,0:T(8,128)(2,1)S(1)} %get-tuple-element.122), channel_id=1, source_target_pairs={{0,24},{8,16},{16,8},{24,0},{1,25},{9,17},{17,9},{25,1},{2,26},{10... | collective-permute-start | bytes 786440 | tf_op jit(solution)/shard_map/ppermute | solution.py:1030
  127.9 15.4 %collective-permute-start.18 = (bf16[512,256]{1,0:T(8,128)(2,1)S(1)}, bf16[512,256]{1,0:T(8,128)(2,1)S(1)}, u32[]{:S(2)}, u32[]{:S(2)}) collective-permute-start(bf16[512,256]{1,0:T(8,128)(2,1)S(1)} %get-tuple-element.124), channel_id=1, source_target_pairs={{0,8},{8,0},{16,24},{24,16},{1,9},{9,1},{17,25},{25,17},{2,10},{10... | collective-permute-start | bytes 786440 | tf_op jit(solution)/shard_map/ppermute | solution.py:1030
  128.5 14.9 %collective-permute-start.19 = (bf16[512,256]{1,0:T(8,128)(2,1)S(1)}, bf16[512,256]{1,0:T(8,128)(2,1)S(1)}, u32[]{:S(2)}, u32[]{:S(2)}) collective-permute-start(bf16[512,256]{1,0:T(8,128)(2,1)S(1)} %get-tuple-element.125), channel_id=1, source_target_pairs={{0,16},{8,24},{16,0},{24,8},{1,17},{9,25},{17,1},{25,9},{2,18},{10... | collective-permute-start | bytes 786440 | tf_op jit(solution)/shard_map/ppermute | solution.py:1030
  131.8 6.7 %collective-permute-start.17 = (bf16[128,128]{1,0:T(8,128)(2,1)S(1)}, bf16[128,128]{1,0:T(8,128)(2,1)S(1)}, u32[]{:S(2)}, u32[]{:S(2)}) collective-permute-start(bf16[128,128]{1,0:T(8,128)(2,1)S(1)} %fusion.12), channel_id=1, source_target_pairs={{0,6},{1,7},{2,4},{3,5},{4,2},{5,3},{6,0},{7,1},{8,14},{9,15},{10,... | collective-permute-start | bytes 98312 | tf_op jit(solution)/shard_map/ppermute | solution.py:1030
  131.9 6.6 %collective-permute-start.16 = (bf16[128,128]{1,0:T(8,128)(2,1)S(1)}, bf16[128,128]{1,0:T(8,128)(2,1)S(1)}, u32[]{:S(2)}, u32[]{:S(2)}) collective-permute-start(bf16[128,128]{1,0:T(8,128)(2,1)S(1)} %fusion.12), channel_id=1, source_target_pairs={{0,4},{1,5},{2,6},{3,7},{4,0},{5,1},{6,2},{7,3},{8,12},{9,13},{10,... | collective-permute-start | bytes 98312 | tf_op jit(solution)/shard_map/ppermute | solution.py:1030
  138.6 4.8 %collective-permute-start.15 = (bf16[128,128]{1,0:T(8,128)(2,1)S(1)}, bf16[128,128]{1,0:T(8,128)(2,1)S(1)}, u32[]{:S(2)}, u32[]{:S(2)}) collective-permute-start(bf16[128,128]{1,0:T(8,128)(2,1)S(1)} %fusion.12), channel_id=1, source_target_pairs={{0,2},{1,3},{2,0},{3,1},{4,6},{5,7},{6,4},{7,5},{8,10},{9,11},{10,... | collective-permute-start | bytes 98312 | tf_op jit(solution)/shard_map/ppermute | solution.py:1030
  143.4 1.4 collective-permute-start.21
  155.0 3.8 %copy-start.15 = (bf16[320,256]{1,0:T(8,128)(2,1)S(1)}, bf16[320,256]{1,0:T(8,128)(2,1)}, u32[]{:S(2)}) copy-start(bf16[320,256]{1,0:T(8,128)(2,1)} %get-tuple-element.102) | copy-start | bytes 491524
  155.0 11.5 %copy-start.9 = (bf16[320,256]{1,0:T(8,128)(2,1)S(1)}, bf16[320,256]{1,0:T(8,128)(2,1)}, u32[]{:S(2)}) copy-start(bf16[320,256]{1,0:T(8,128)(2,1)} %get-tuple-element.99) | copy-start | bytes 491524
  155.2 42.7 %copy-start.1 = (bf16[128,1024]{1,0:T(8,128)(2,1)S(1)}, bf16[128,1024]{1,0:T(8,128)(2,1)}, u32[]{:S(2)}) copy-start(bf16[128,1024]{1,0:T(8,128)(2,1)} %refs_11_.1) | copy-start | bytes 786436
  155.2 42.7 %copy-start.2 = (bf16[128,1024]{1,0:T(8,128)(2,1)S(1)}, bf16[128,1024]{1,0:T(8,128)(2,1)}, u32[]{:S(2)}) copy-start(bf16[128,1024]{1,0:T(8,128)(2,1)} %refs_12_.1) | copy-start | bytes 786436
  155.2 42.7 %copy-start.5 = (f32[1024]{0:T(1024)S(1)}, f32[1024]{0:T(1024)}, u32[]{:S(2)}) copy-start(f32[1024]{0:T(1024)} %param.15) | copy-start | bytes 12292
  155.9 7.6 %collective-permute-start.22 = (bf16[320,256]{1,0:T(8,128)(2,1)S(1)}, bf16[320,256]{1,0:T(8,128)(2,1)S(1)}, u32[]{:S(2)}, u32[]{:S(2)}) collective-permute-start(bf16[320,256]{1,0:T(8,128)(2,1)S(1)} %copy-done.17), channel_id=1, source_target_pairs={{0,8},{8,0},{16,24},{24,16},{1,9},{9,1},{17,25},{25,17},{2,10},{10... | collective-permute-start | bytes 491528 | tf_op jit(solution)/shard_map/ppermute | solution.py:1030
  156.9 8.8 %collective-permute-start.23 = (bf16[320,256]{1,0:T(8,128)(2,1)S(1)}, bf16[320,256]{1,0:T(8,128)(2,1)S(1)}, u32[]{:S(2)}, u32[]{:S(2)}) collective-permute-start(bf16[320,256]{1,0:T(8,128)(2,1)S(1)} %copy-done.16), channel_id=1, source_target_pairs={{0,16},{8,24},{16,0},{24,8},{1,17},{9,25},{17,1},{25,9},{2,18},{10... | collective-permute-start | bytes 491528 | tf_op jit(solution)/shard_map/ppermute | solution.py:1030
  158.8 7.7 %collective-permute-start.24 = (bf16[320,256]{1,0:T(8,128)(2,1)S(1)}, bf16[320,256]{1,0:T(8,128)(2,1)S(1)}, u32[]{:S(2)}, u32[]{:S(2)}) collective-permute-start(bf16[320,256]{1,0:T(8,128)(2,1)S(1)} %copy-done.15), channel_id=1, source_target_pairs={{0,24},{8,16},{16,8},{24,0},{1,25},{9,17},{17,9},{25,1},{2,26},{10... | collective-permute-start | bytes 491528 | tf_op jit(solution)/shard_map/ppermute | solution.py:1030
  160.1 12.5 %all-to-all-start.2 = ((bf16[8,32,256]{2,1,0:T(8,128)(2,1)}), bf16[8,32,256]{2,1,0:T(8,128)(2,1)S(1)}, u32[]{:S(2)}, u32[]{:S(2)}) async-start(bf16[8,32,256]{2,1,0:T(8,128)(2,1)} %bitcast.60), calls=%async_computation.2 | async-start | bytes 262144 | tf_op jit(solution)/shard_map/all_to_all | solution.py:1087
  172.5 15.1 %all-to-all-start.1 = ((bf16[8,48,256]{2,1,0:T(8,128)(2,1)}), bf16[8,48,256]{2,1,0:T(8,128)(2,1)S(1)}, u32[]{:S(2)}, u32[]{:S(2)}) async-start(bf16[8,48,256]{2,1,0:T(8,128)(2,1)} %fusion.10), calls=%async_computation.1 | async-start | bytes 393216 | tf_op jit(solution)/shard_map/all_to_all | solution.py:1087
  176.0 14.0 %collective-permute-start.30 = (bf16[512,256]{1,0:T(8,128)(2,1)S(1)}, bf16[512,256]{1,0:T(8,128)(2,1)S(1)}, u32[]{:S(2)}, u32[]{:S(2)}) collective-permute-start(bf16[512,256]{1,0:T(8,128)(2,1)S(1)} %pad_maximum_fusion.refs_4_), channel_id=1, source_target_pairs={{0,24},{8,16},{16,8},{24,0},{1,25},{9,17},{17,9},{25,1},{2,26},{10... | collective-permute-start | bytes 786440 | tf_op jit(solution)/shard_map/ppermute | solution.py:1030
  178.4 13.4 %collective-permute-start.29 = (bf16[512,256]{1,0:T(8,128)(2,1)S(1)}, bf16[512,256]{1,0:T(8,128)(2,1)S(1)}, u32[]{:S(2)}, u32[]{:S(2)}) collective-permute-start(bf16[512,256]{1,0:T(8,128)(2,1)S(1)} %pad_maximum_fusion.refs_4_), channel_id=1, source_target_pairs={{0,16},{8,24},{16,0},{24,8},{1,17},{9,25},{17,1},{25,9},{2,18},{10... | collective-permute-start | bytes 786440 | tf_op jit(solution)/shard_map/ppermute | solution.py:1030
  178.5 13.3 %collective-permute-start.28 = (bf16[512,256]{1,0:T(8,128)(2,1)S(1)}, bf16[512,256]{1,0:T(8,128)(2,1)S(1)}, u32[]{:S(2)}, u32[]{:S(2)}) collective-permute-start(bf16[512,256]{1,0:T(8,128)(2,1)S(1)} %pad_maximum_fusion.refs_4_), channel_id=1, source_target_pairs={{0,8},{8,0},{16,24},{24,16},{1,9},{9,1},{17,25},{25,17},{2,10},{10... | collective-permute-start | bytes 786440 | tf_op jit(solution)/shard_map/ppermute | solution.py:1030
  187.7 8.0 %collective-permute-start.27 = (bf16[304,256]{1,0:T(8,128)(2,1)S(1)}, bf16[304,256]{1,0:T(8,128)(2,1)S(1)}, u32[]{:S(2)}, u32[]{:S(2)}) collective-permute-start(bf16[304,256]{1,0:T(8,128)(2,1)S(1)} %pad_maximum_fusion.1.refs_0_), channel_id=1, source_target_pairs={{0,24},{8,16},{16,8},{24,0},{1,25},{9,17},{17,9},{25,1},{2,26},{10... | collective-permute-start | bytes 466952 | tf_op jit(solution)/shard_map/ppermute | solution.py:1030
  190.0 7.9 %collective-permute-start.26 = (bf16[304,256]{1,0:T(8,128)(2,1)S(1)}, bf16[304,256]{1,0:T(8,128)(2,1)S(1)}, u32[]{:S(2)}, u32[]{:S(2)}) collective-permute-start(bf16[304,256]{1,0:T(8,128)(2,1)S(1)} %pad_maximum_fusion.1.refs_0_), channel_id=1, source_target_pairs={{0,16},{8,24},{16,0},{24,8},{1,17},{9,25},{17,1},{25,9},{2,18},{10... | collective-permute-start | bytes 466952 | tf_op jit(solution)/shard_map/ppermute | solution.py:1030
  190.0 7.9 %collective-permute-start.25 = (bf16[304,256]{1,0:T(8,128)(2,1)S(1)}, bf16[304,256]{1,0:T(8,128)(2,1)S(1)}, u32[]{:S(2)}, u32[]{:S(2)}) collective-permute-start(bf16[304,256]{1,0:T(8,128)(2,1)S(1)} %pad_maximum_fusion.1.refs_0_), channel_id=1, source_target_pairs={{0,8},{8,0},{16,24},{24,16},{1,9},{9,1},{17,25},{25,17},{2,10},{10... | collective-permute-start | bytes 466952 | tf_op jit(solution)/shard_map/ppermute | solution.py:1030
  (13 other events, 14.2 us)
Sparse Core Ops, SparseCore 0:
  9.7 34.1 all-gather.2
  45.5 34.2 all-gather.4
  116.7 37.4 reduce-scatter.2
  156.9 36.9 reduce-scatter.4

commit v6 on v5

--- a/solution.py
+++ b/solution.py
@@ -1042,7 +1042,8 @@
 
 
 def owned_parts(blocks, axis):
-    return [blocks[0]] + [swap(block, axis, d) for d, block in enumerate(blocks) if d]
+    got = {d: swap(blocks[d], axis, d) for d in reversed(range(1, len(blocks)))}
+    return [blocks[0]] + [got[d] for d in range(1, len(blocks))]
 
 
 def by_distance(blocks, axis):

time: 209 us -> 209 us (level)
  no operation moved by 1% of the time
where the time goes in v6:
time: 209 us
  waiting for transfers between devices  70.8 us (34%)
  Pallas kernels  55.5 us (27%)
  starting transfers between devices  46 us (22%)
  local copies, waits for them, and re-layouts  15.2 us (7%)
  between operations  14.4 us (7%)
  other arithmetic  3.47 us (2%)
  matrix products  3.22 us (2%)
    ppermute x31, waiting for transfers between devices, swap(): lax.ppermute(value, axis, [(i, i ^ mask) for i in range(lax.axis_size(axi...  49.5 us
    pallas_call x1, Pallas kernels, run_scan(): pl.pallas_call(functools.partial(scan_kernel, rank, states, span), grid=(...  36.1 us
    ppermute x31, starting transfers between devices, swap(): lax.ppermute(value, axis, [(i, i ^ mask) for i in range(lax.axis_size(axi...  32.6 us
    all_to_all x3, waiting for transfers between devices, to_peers(): return lax.all_to_all(blocks, 'ch', split_axis=0, concat_axis=0, tiled=True)  18.4 us
    all_to_all x3, starting transfers between devices, to_peers(): return lax.all_to_all(blocks, 'ch', split_axis=0, concat_axis=0, tiled=True)  13.1 us
    pallas_call x1, Pallas kernels, run_exit(): pl.pallas_call(functools.partial(exit_kernel, span, taps, low_cols, packs...  9.52 us
    pallas_call x1, Pallas kernels, run_entry(): pl.pallas_call(functools.partial(entry_kernel, span, taps), grid=(turns +...  7.76 us
    unnamed x49, local copies, waits for them, and re-layouts  6.63 us
  transfers between devices with their start and end apart: 38, of which 22 were waited for; matrix products, arithmetic and copies ran while one was open for 7% of the time, Pallas kernels for 8%

profile of v6, /device:TPU:0, one launch (start us, length us, event | category | flops | bytes accessed | tf_op | source)
XLA Modules:
  0.0 208.5 jit_solution(8106022403326575758)
XLA Ops:
  8.5 0.9 copy.66
  9.4 6.3 %all-to-all-start = ((bf16[8,32,2,256]{3,2,1,0:T(2,128)(2,1)}), bf16[8,32,2,256]{3,2,1,0:T(2,128)(2,1)S(1)}, u32[]{:S(2)}, u32[]{:S(2)}) async-start(bf16[8,32,2,256]{3,2,1,0:T(2,128)(2,1)} %copy.66), calls=%async_computation | async-start | bytes 524288 | tf_op jit(solution)/shard_map/all_to_all | solution.py:1088
  17.1 1.3 dynamic_slice.27
  20.7 1.3 dynamic-slice_bitcast_fusion.cw_ref
  22.5 5.1 %all-to-all-done = bf16[8,32,2,256]{3,2,1,0:T(2,128)(2,1)S(1)} async-done(((bf16[8,32,2,256]{3,2,1,0:T(2,128)(2,1)}), bf16[8,32,2,256]{3,2,1,0:T(2,128)(2,1)S(1)}, u32[]{:S(2)}, u32[]{:S(2)}) %all-to-all-start) | async-done | bytes 262176 | tf_op jit(solution)/shard_map/all_to_all | solution.py:1088
  28.8 1.5 collective-permute-start
  31.0 1.6 collective-permute-start.2
  33.3 4.7 %collective-permute-done = bf16[8,32,512]{2,1,0:T(8,128)(2,1)S(1)} collective-permute-done((bf16[8,32,512]{2,1,0:T(8,128)(2,1)S(1)}, bf16[8,32,512]{2,1,0:T(8,128)(2,1)S(1)}, u32[]{:S(2)}, u32[]{:S(2)}) %collective-permute-start) | collective-permute-done | bytes 262176 | tf_op jit(solution)/shard_map/ppermute | solution.py:1030
  38.0 5.9 %collective-permute-done.1 = bf16[8,32,512]{2,1,0:T(8,128)(2,1)S(1)} collective-permute-done((bf16[8,32,512]{2,1,0:T(8,128)(2,1)S(1)}, bf16[8,32,512]{2,1,0:T(8,128)(2,1)S(1)}, u32[]{:S(2)}, u32[]{:S(2)}) %collective-permute-start.1) | collective-permute-done | bytes 262176 | tf_op jit(solution)/shard_map/ppermute | solution.py:1030
  44.0 0.9 copy-done.7
  44.9 7.8 %entry.1 = (bf16[8,128,1024]{2,1,0:T(8,128)(2,1)}, f32[8,128,128]{2,1,0:T(8,128)}, bf16[1024,256]{1,0:T(8,128)(2,1)}, bf16[1024,256]{1,0:T(8,128)(2,1)}, bf16[10...) custom-call(s32[3]{0:T(128)} %pad_add_fusion.me_ref, ...), custom_call_target="tpu_custom_call" | custom-call | flops 6600000000 | bytes 1048576 | tf_op jit(solution)/shard_map/entry/pallas_call | solution.py:803
  52.7 1.5 collective-permute-done.3
  54.3 0.9 add_convert_fusion.3
  55.3 1.3 collective-permute-start.4
  56.6 4.1 %collective-permute-start.6 = (bf16[128,128]{1,0:T(8,128)(2,1)S(1)}, bf16[128,128]{1,0:T(8,128)(2,1)S(1)}, u32[]{:S(2)}, u32[]{:S(2)}) collective-permute-start(bf16[128,128]{1,0:T(8,128)(2,1)S(1)} %get-tuple-element.132), channel_id=1, source_target_pairs={{0,6},{1,7},{2,4},{3,5},{4,2},{5,3},{6,0},{7,1},{8,14},{9,15},{10,... | collective-permute-start | bytes 98312 | tf_op jit(solution)/shard_map/ppermute | solution.py:1030
  61.2 3.7 %collective-permute-done.6 = bf16[128,128]{1,0:T(8,128)(2,1)S(1)} collective-permute-done((bf16[128,128]{1,0:T(8,128)(2,1)S(1)}, bf16[128,128]{1,0:T(8,128)(2,1)S(1)}, u32[]{:S(2)}, u32[]{:S(2)}) %collective-permute-start.6) | collective-permute-done | bytes 32800 | tf_op jit(solution)/shard_map/ppermute | solution.py:1030
  64.9 4.3 %collective-permute-done.5 = bf16[128,128]{1,0:T(8,128)(2,1)S(1)} collective-permute-done((bf16[128,128]{1,0:T(8,128)(2,1)S(1)}, bf16[128,128]{1,0:T(8,128)(2,1)S(1)}, u32[]{:S(2)}, u32[]{:S(2)}) %collective-permute-start.5) | collective-permute-done | bytes 32800 | tf_op jit(solution)/shard_map/ppermute | solution.py:1030
  69.2 3.4 %collective-permute-start.9 = (bf16[128,128]{1,0:T(8,128)(2,1)S(1)}, bf16[128,128]{1,0:T(8,128)(2,1)S(1)}, u32[]{:S(2)}, u32[]{:S(2)}) collective-permute-start(bf16[128,128]{1,0:T(8,128)(2,1)S(1)} %fusion.14), channel_id=1, source_target_pairs={{0,6},{1,7},{2,4},{3,5},{4,2},{5,3},{6,0},{7,1},{8,14},{9,15},{10,... | collective-permute-start | bytes 98312 | tf_op jit(solution)/shard_map/ppermute | solution.py:1030
  72.6 1.1 collective-permute-start.7
  73.7 2.0 collective-permute-done.9
  75.7 2.4 %collective-permute-done.8 = bf16[128,128]{1,0:T(8,128)(2,1)S(1)} collective-permute-done((bf16[128,128]{1,0:T(8,128)(2,1)S(1)}, bf16[128,128]{1,0:T(8,128)(2,1)S(1)}, u32[]{:S(2)}, u32[]{:S(2)}) %collective-permute-start.8) | collective-permute-done | bytes 32800 | tf_op jit(solution)/shard_map/ppermute | solution.py:1030
  78.4 1.4 all-gather.5.cloned.1.call-done
  80.4 36.1 %scan.1 = (bf16[8,128,1024]{2,1,0:T(8,128)(2,1)}, bf16[8,128,256]{2,1,0:T(8,128)(2,1)}, bf16[8,128,256]{2,1,0:T(8,128)(2,1)}, bf16[4,128,128]{2,1,0:T(8,128)(2,1...) custom-call(s32[3]{0:T(128)} %pad_add_fusion.me_ref, ...), custom_call_target="tpu_custom_call" | custom-call | flops 41799999488 | bytes 1048576 | tf_op jit(solution)/shard_map/scan/pallas_call | solution.py:869
  117.7 2.5 %fusion = bf16[1024,256]{1,0:T(8,128)(2,1)S(1)} fusion(bf16[8,128,1024]{2,1,0:T(8,128)(2,1)} %get-tuple-element.85, bf16[8,128,256]{2,1,0:T(8,128)(2,1)S(1)} %copy-done.22), kind=kOutput, calls=%fused_computation.9 | convolution fusion | flops 537133056 | bytes 3145728 | tf_op jit(solution)/shard_map/dot_general | solution.py:38
  122.0 2.5 %collective-permute-start.14 = (bf16[128,128]{1,0:T(8,128)(2,1)S(1)}, bf16[128,128]{1,0:T(8,128)(2,1)S(1)}, u32[]{:S(2)}, u32[]{:S(2)}) collective-permute-start(bf16[128,128]{1,0:T(8,128)(2,1)S(1)} %get-tuple-element.129), channel_id=1, source_target_pairs={{0,6},{1,7},{2,4},{3,5},{4,2},{5,3},{6,0},{7,1},{8,14},{9,15},{10,... | collective-permute-start | bytes 98312 | tf_op jit(solution)/shard_map/ppermute | solution.py:1030
  124.5 1.0 collective-permute-start.13
  125.5 2.4 %collective-permute-start.20 = (bf16[512,256]{1,0:T(8,128)(2,1)S(1)}, bf16[512,256]{1,0:T(8,128)(2,1)S(1)}, u32[]{:S(2)}, u32[]{:S(2)}) collective-permute-start(bf16[512,256]{1,0:T(8,128)(2,1)S(1)} %get-tuple-element.122), channel_id=1, source_target_pairs={{0,24},{8,16},{16,8},{24,0},{1,25},{9,17},{17,9},{25,1},{2,26},{10... | collective-permute-start | bytes 786440 | tf_op jit(solution)/shard_map/ppermute | solution.py:1030
  129.1 2.7 %collective-permute-done.13 = bf16[128,128]{1,0:T(8,128)(2,1)S(1)} collective-permute-done((bf16[128,128]{1,0:T(8,128)(2,1)S(1)}, bf16[128,128]{1,0:T(8,128)(2,1)S(1)}, u32[]{:S(2)}, u32[]{:S(2)}) %collective-permute-start.13) | collective-permute-done | bytes 32800 | tf_op jit(solution)/shard_map/ppermute | solution.py:1030
  132.3 6.2 %collective-permute-done.17 = bf16[128,128]{1,0:T(8,128)(2,1)S(1)} collective-permute-done((bf16[128,128]{1,0:T(8,128)(2,1)S(1)}, bf16[128,128]{1,0:T(8,128)(2,1)S(1)}, u32[]{:S(2)}, u32[]{:S(2)}) %collective-permute-start.17) | collective-permute-done | bytes 32800 | tf_op jit(solution)/shard_map/ppermute | solution.py:1030
  138.6 4.8 %collective-permute-done.15 = bf16[128,128]{1,0:T(8,128)(2,1)S(1)} collective-permute-done((bf16[128,128]{1,0:T(8,128)(2,1)S(1)}, bf16[128,128]{1,0:T(8,128)(2,1)S(1)}, u32[]{:S(2)}, u32[]{:S(2)}) %collective-permute-start.15) | collective-permute-done | bytes 32800 | tf_op jit(solution)/shard_map/ppermute | solution.py:1030
  143.5 1.3 collective-permute-done.21.other_ref
  145.5 9.5 %exit.1 = (bf16[1024,1024]{1,0:T(8,128)(2,1)}, bf16[320,256]{1,0:T(8,128)(2,1)}, bf16[320,256]{1,0:T(8,128)(2,1)}, bf16[320,256]{1,0:T(8,128)(2,1)}, bf16[320,256]{1,0:T(8,128)(2,1)}) custom-call(s32[3]{0:T(128)} %pad_add_fusion.me_ref, s32[1,4]{1,0:T(1,128)} %bitcast_subtract_fusion.starts_ref, bf16[4,128,128]{2,1,0:T(8,128)(2,1)} %copy-done.11, ...), custom_call_target="tpu_custom_call" | custom-call | flops 11000000512 | bytes 1048576 | tf_op jit(solution)/shard_map/exit/pallas_call | solution.py:919
  155.9 1.0 collective-permute-start.22
  156.9 1.8 collective-permute-start.23
  160.1 3.4 %all-to-all-start.2 = ((bf16[8,32,256]{2,1,0:T(8,128)(2,1)}), bf16[8,32,256]{2,1,0:T(8,128)(2,1)S(1)}, u32[]{:S(2)}, u32[]{:S(2)}) async-start(bf16[8,32,256]{2,1,0:T(8,128)(2,1)} %bitcast.60), calls=%async_computation.2 | async-start | bytes 262144 | tf_op jit(solution)/shard_map/all_to_all | solution.py:1088
  163.5 2.3 %collective-permute-done.23 = bf16[320,256]{1,0:T(8,128)(2,1)S(1)} collective-permute-done((bf16[320,256]{1,0:T(8,128)(2,1)S(1)}, bf16[320,256]{1,0:T(8,128)(2,1)S(1)}, u32[]{:S(2)}, u32[]{:S(2)}) %collective-permute-start.23) | collective-permute-done | bytes 163872 | tf_op jit(solution)/shard_map/ppermute | solution.py:1030
  167.3 5.2 %all-to-all-done.2 = bf16[8,32,256]{2,1,0:T(8,128)(2,1)S(1)} async-done(((bf16[8,32,256]{2,1,0:T(8,128)(2,1)}), bf16[8,32,256]{2,1,0:T(8,128)(2,1)S(1)}, u32[]{:S(2)}, u32[]{:S(2)}) %all-to-all-start.2) | async-done | bytes 131104 | tf_op jit(solution)/shard_map/all_to_all | solution.py:1088
  172.5 3.4 %all-to-all-start.1 = ((bf16[8,48,256]{2,1,0:T(8,128)(2,1)}), bf16[8,48,256]{2,1,0:T(8,128)(2,1)S(1)}, u32[]{:S(2)}, u32[]{:S(2)}) async-start(bf16[8,48,256]{2,1,0:T(8,128)(2,1)} %fusion.10), calls=%async_computation.1 | async-start | bytes 393216 | tf_op jit(solution)/shard_map/all_to_all | solution.py:1088
  176.0 2.4 %collective-permute-start.30 = (bf16[512,256]{1,0:T(8,128)(2,1)S(1)}, bf16[512,256]{1,0:T(8,128)(2,1)S(1)}, u32[]{:S(2)}, u32[]{:S(2)}) collective-permute-start(bf16[512,256]{1,0:T(8,128)(2,1)S(1)} %pad_maximum_fusion.refs_4_), channel_id=1, source_target_pairs={{0,24},{8,16},{16,8},{24,0},{1,25},{9,17},{17,9},{25,1},{2,26},{10... | collective-permute-start | bytes 786440 | tf_op jit(solution)/shard_map/ppermute | solution.py:1030
  178.5 1.0 collective-permute-start.28
  179.5 8.1 %all-to-all-done.1.refs_8_ = bf16[8,48,256]{2,1,0:T(8,128)(2,1)S(1)} async-done(((bf16[8,48,256]{2,1,0:T(8,128)(2,1)}), bf16[8,48,256]{2,1,0:T(8,128)(2,1)S(1)}, u32[]{:S(2)}, u32[]{:S(2)}) %all-to-all-start.1) | async-done | bytes 196640 | tf_op jit(solution)/shard_map/all_to_all | solution.py:1088
  187.7 2.3 %collective-permute-start.27 = (bf16[304,256]{1,0:T(8,128)(2,1)S(1)}, bf16[304,256]{1,0:T(8,128)(2,1)S(1)}, u32[]{:S(2)}, u32[]{:S(2)}) collective-permute-start(bf16[304,256]{1,0:T(8,128)(2,1)S(1)} %pad_maximum_fusion.1.refs_0_), channel_id=1, source_target_pairs={{0,24},{8,16},{16,8},{24,0},{1,25},{9,17},{17,9},{25,1},{2,26},{10... | collective-permute-start | bytes 466952 | tf_op jit(solution)/shard_map/ppermute | solution.py:1030
  190.0 1.2 collective-permute-start.25
  191.8 3.9 %collective-permute-done.27.refs_3_ = bf16[304,256]{1,0:T(8,128)(2,1)S(1)} collective-permute-done((bf16[304,256]{1,0:T(8,128)(2,1)S(1)}, bf16[304,256]{1,0:T(8,128)(2,1)S(1)}, u32[]{:S(2)}, u32[]{:S(2)}) %collective-permute-start.27) | collective-permute-done | bytes 155680 | tf_op jit(solution)/shard_map/ppermute | solution.py:1030
  195.6 2.2 %collective-permute-done.26.refs_2_ = bf16[304,256]{1,0:T(8,128)(2,1)S(1)} collective-permute-done((bf16[304,256]{1,0:T(8,128)(2,1)S(1)}, bf16[304,256]{1,0:T(8,128)(2,1)S(1)}, u32[]{:S(2)}, u32[]{:S(2)}) %collective-permute-start.26) | collective-permute-done | bytes 155680 | tf_op jit(solution)/shard_map/ppermute | solution.py:1030
  197.9 0.9 copy-done.3
  198.9 0.9 copy-done.4
  199.8 2.2 %finish.1 = (bf16[128,1024]{1,0:T(8,128)(2,1)}, bf16[128,1024]{1,0:T(8,128)(2,1)}, f32[1,128]{1,0:T(1,128)}, f32[128,4096]{1,0:T(8,128)}, f32[4,256]{1,0:T(4,128...) custom-call(s32[1]{0:T(128)} %bitcast.me_ref, ...), custom_call_target="tpu_custom_call" | custom-call | flops 4400000000 | bytes 1048576 | tf_op jit(solution)/shard_map/finish/pallas_call | solution.py:1152
  (135 shorter events, 19.4 us)
Async XLA Ops:
  7.2 9.3 %copy-start.21 = (s32[1,4]{1,0:T(1,128)S(1)}, s32[1,4]{1,0:T(1,128)}, u32[]{:S(2)}) copy-start(s32[1,4]{1,0:T(1,128)} %param.25) | copy-start | bytes 52
  7.2 9.6 %copy-start.14 = (s32[1024]{0:T(1024)S(1)}, s32[1024]{0:T(1024)}, u32[]{:S(2)}) copy-start(s32[1024]{0:T(1024)} %param.26) | copy-start | bytes 12292
  7.2 12.1 %copy-start.13 = (bf16[64,256]{1,0:T(8,128)(2,1)S(1)}, bf16[64,256]{1,0:T(8,128)(2,1)}, u32[]{:S(2)}) copy-start(bf16[64,256]{1,0:T(8,128)(2,1)} %dtw_ref.1) | copy-start | bytes 98308
  7.2 36.7 %all-gather.3.cloned.1.call-start = ((), (), s32[]{:S(2)}) async-start(), calls=%async_computation.5 | async-start | bytes 2359296 | tf_op jit(solution)/shard_map/all_gather | solution.py:1209
  9.4 18.3 %all-to-all-start = ((bf16[8,32,2,256]{3,2,1,0:T(2,128)(2,1)}), bf16[8,32,2,256]{3,2,1,0:T(2,128)(2,1)S(1)}, u32[]{:S(2)}, u32[]{:S(2)}) async-start(bf16[8,32,2,256]{3,2,1,0:T(2,128)(2,1)} %copy.66), calls=%async_computation | async-start | bytes 524288 | tf_op jit(solution)/shard_map/all_to_all | solution.py:1088
  15.7 64.1 %all-gather.5.cloned.1.call-start = ((), (), s32[]{:S(2)}) async-start(), calls=%async_computation.6 | async-start | bytes 2359296 | tf_op jit(solution)/shard_map/all_gather | solution.py:1214
  16.5 181.4 %reduce-scatter.3.cloned.1.call-start = ((), (), s32[]{:S(2)}) async-start(), calls=%async_computation.7 | async-start | bytes 2359296 | tf_op jit(solution)/shard_map/reduce_scatter | solution.py:1262
  28.8 9.2 %collective-permute-start = (bf16[8,32,512]{2,1,0:T(8,128)(2,1)S(1)}, bf16[8,32,512]{2,1,0:T(8,128)(2,1)S(1)}, u32[]{:S(2)}, u32[]{:S(2)}) collective-permute-start(bf16[8,32,512]{2,1,0:T(8,128)(2,1)S(1)} %reshape.119), channel_id=1, source_target_pairs={{0,8},{8,0},{16,24},{24,16},{1,9},{9,1},{17,25},{25,17},{2,10},{10... | collective-permute-start | bytes 786440 | tf_op jit(solution)/shard_map/ppermute | solution.py:1030
  31.0 12.9 %collective-permute-start.2 = (bf16[8,32,512]{2,1,0:T(8,128)(2,1)S(1)}, bf16[8,32,512]{2,1,0:T(8,128)(2,1)S(1)}, u32[]{:S(2)}, u32[]{:S(2)}) collective-permute-start(bf16[8,32,512]{2,1,0:T(8,128)(2,1)S(1)} %reshape.119), channel_id=1, source_target_pairs={{0,24},{8,16},{16,8},{24,0},{1,25},{9,17},{17,9},{25,1},{2,26},{10... | collective-permute-start | bytes 786440 | tf_op jit(solution)/shard_map/ppermute | solution.py:1030
  32.6 11.3 %collective-permute-start.1 = (bf16[8,32,512]{2,1,0:T(8,128)(2,1)S(1)}, bf16[8,32,512]{2,1,0:T(8,128)(2,1)S(1)}, u32[]{:S(2)}, u32[]{:S(2)}) collective-permute-start(bf16[8,32,512]{2,1,0:T(8,128)(2,1)S(1)} %reshape.119), channel_id=1, source_target_pairs={{0,16},{8,24},{16,0},{24,8},{1,17},{9,25},{17,1},{25,9},{2,18},{10... | collective-permute-start | bytes 786440 | tf_op jit(solution)/shard_map/ppermute | solution.py:1030
  52.7 1.6 collective-permute-start.3
  55.3 6.0 %collective-permute-start.4 = (bf16[128,128]{1,0:T(8,128)(2,1)S(1)}, bf16[128,128]{1,0:T(8,128)(2,1)S(1)}, u32[]{:S(2)}, u32[]{:S(2)}) collective-permute-start(bf16[128,128]{1,0:T(8,128)(2,1)S(1)} %get-tuple-element.131), channel_id=1, source_target_pairs={{0,2},{1,3},{2,0},{3,1},{4,6},{5,7},{6,4},{7,5},{8,10},{9,11},{10,... | collective-permute-start | bytes 98312 | tf_op jit(solution)/shard_map/ppermute | solution.py:1030
  56.6 8.3 %collective-permute-start.6 = (bf16[128,128]{1,0:T(8,128)(2,1)S(1)}, bf16[128,128]{1,0:T(8,128)(2,1)S(1)}, u32[]{:S(2)}, u32[]{:S(2)}) collective-permute-start(bf16[128,128]{1,0:T(8,128)(2,1)S(1)} %get-tuple-element.132), channel_id=1, source_target_pairs={{0,6},{1,7},{2,4},{3,5},{4,2},{5,3},{6,0},{7,1},{8,14},{9,15},{10,... | collective-permute-start | bytes 98312 | tf_op jit(solution)/shard_map/ppermute | solution.py:1030
  60.7 8.5 %collective-permute-start.5 = (bf16[128,128]{1,0:T(8,128)(2,1)S(1)}, bf16[128,128]{1,0:T(8,128)(2,1)S(1)}, u32[]{:S(2)}, u32[]{:S(2)}) collective-permute-start(bf16[128,128]{1,0:T(8,128)(2,1)S(1)} %get-tuple-element.133), channel_id=1, source_target_pairs={{0,4},{1,5},{2,6},{3,7},{4,0},{5,1},{6,2},{7,3},{8,12},{9,13},{10,... | collective-permute-start | bytes 98312 | tf_op jit(solution)/shard_map/ppermute | solution.py:1030
  69.2 6.5 %collective-permute-start.9 = (bf16[128,128]{1,0:T(8,128)(2,1)S(1)}, bf16[128,128]{1,0:T(8,128)(2,1)S(1)}, u32[]{:S(2)}, u32[]{:S(2)}) collective-permute-start(bf16[128,128]{1,0:T(8,128)(2,1)S(1)} %fusion.14), channel_id=1, source_target_pairs={{0,6},{1,7},{2,4},{3,5},{4,2},{5,3},{6,0},{7,1},{8,14},{9,15},{10,... | collective-permute-start | bytes 98312 | tf_op jit(solution)/shard_map/ppermute | solution.py:1030
  72.6 5.5 %collective-permute-start.8 = (bf16[128,128]{1,0:T(8,128)(2,1)S(1)}, bf16[128,128]{1,0:T(8,128)(2,1)S(1)}, u32[]{:S(2)}, u32[]{:S(2)}) collective-permute-start(bf16[128,128]{1,0:T(8,128)(2,1)S(1)} %fusion.14), channel_id=1, source_target_pairs={{0,4},{1,5},{2,6},{3,7},{4,0},{5,1},{6,2},{7,3},{8,12},{9,13},{10,... | collective-permute-start | bytes 98312 | tf_op jit(solution)/shard_map/ppermute | solution.py:1030
  72.6 5.7 %collective-permute-start.7 = (bf16[128,128]{1,0:T(8,128)(2,1)S(1)}, bf16[128,128]{1,0:T(8,128)(2,1)S(1)}, u32[]{:S(2)}, u32[]{:S(2)}) collective-permute-start(bf16[128,128]{1,0:T(8,128)(2,1)S(1)} %fusion.14), channel_id=1, source_target_pairs={{0,2},{1,3},{2,0},{3,1},{4,6},{5,7},{6,4},{7,5},{8,10},{9,11},{10,... | collective-permute-start | bytes 98312 | tf_op jit(solution)/shard_map/ppermute | solution.py:1030
  78.3 1.5 collective-permute-start.10
  116.6 81.4 %reduce-scatter.5.cloned.1.call-start = ((), (), s32[]{:S(2)}) async-start(), calls=%async_computation.8 | async-start | bytes 2359296 | tf_op jit(solution)/shard_map/reduce_scatter | solution.py:1282
  117.4 4.0 %collective-permute-start.11 = (bf16[4,128,128]{2,1,0:T(8,128)(2,1)S(1)}, bf16[4,128,128]{2,1,0:T(8,128)(2,1)S(1)}, u32[]{:S(2)}, u32[]{:S(2)}) collective-permute-start(bf16[4,128,128]{2,1,0:T(8,128)(2,1)S(1)} %copy-done.18), channel_id=1, source_target_pairs={{0,1},{1,0},{2,3},{3,2},{4,5},{5,4},{6,7},{7,6},{8,9},{9,8},{10,11... | collective-permute-start | bytes 393224 | tf_op jit(solution)/shard_map/ppermute | solution.py:1030
  117.7 2.5 %copy-start.6 = (bf16[1024,1024]{1,0:T(8,128)(2,1)S(1)}, bf16[1024,1024]{1,0:T(8,128)(2,1)}, u32[]{:S(2)}) copy-start(bf16[1024,1024]{1,0:T(8,128)(2,1)} %all-gather.5.cloned.1.call-done) | copy-start | bytes 6291460
  117.7 2.5 %copy-start.8 = (bf16[8,128,256]{2,1,0:T(8,128)(2,1)S(1)}, bf16[8,128,256]{2,1,0:T(8,128)(2,1)}, u32[]{:S(2)}) copy-start(bf16[8,128,256]{2,1,0:T(8,128)(2,1)} %get-tuple-element.84) | copy-start | bytes 1572868
  121.9 6.6 %collective-permute-start.12 = (bf16[128,128]{1,0:T(8,128)(2,1)S(1)}, bf16[128,128]{1,0:T(8,128)(2,1)S(1)}, u32[]{:S(2)}, u32[]{:S(2)}) collective-permute-start(bf16[128,128]{1,0:T(8,128)(2,1)S(1)} %get-tuple-element.128), channel_id=1, source_target_pairs={{0,2},{1,3},{2,0},{3,1},{4,6},{5,7},{6,4},{7,5},{8,10},{9,11},{10,... | collective-permute-start | bytes 98312 | tf_op jit(solution)/shard_map/ppermute | solution.py:1030
  122.0 7.1 %collective-permute-start.14 = (bf16[128,128]{1,0:T(8,128)(2,1)S(1)}, bf16[128,128]{1,0:T(8,128)(2,1)S(1)}, u32[]{:S(2)}, u32[]{:S(2)}) collective-permute-start(bf16[128,128]{1,0:T(8,128)(2,1)S(1)} %get-tuple-element.129), channel_id=1, source_target_pairs={{0,6},{1,7},{2,4},{3,5},{4,2},{5,3},{6,0},{7,1},{8,14},{9,15},{10,... | collective-permute-start | bytes 98312 | tf_op jit(solution)/shard_map/ppermute | solution.py:1030
  124.5 7.3 %collective-permute-start.13 = (bf16[128,128]{1,0:T(8,128)(2,1)S(1)}, bf16[128,128]{1,0:T(8,128)(2,1)S(1)}, u32[]{:S(2)}, u32[]{:S(2)}) collective-permute-start(bf16[128,128]{1,0:T(8,128)(2,1)S(1)} %get-tuple-element.130), channel_id=1, source_target_pairs={{0,4},{1,5},{2,6},{3,7},{4,0},{5,1},{6,2},{7,3},{8,12},{9,13},{10,... | collective-permute-start | bytes 98312 | tf_op jit(solution)/shard_map/ppermute | solution.py:1030
  125.5 17.8 %collective-permute-start.20 = (bf16[512,256]{1,0:T(8,128)(2,1)S(1)}, bf16[512,256]{1,0:T(8,128)(2,1)S(1)}, u32[]{:S(2)}, u32[]{:S(2)}) collective-permute-start(bf16[512,256]{1,0:T(8,128)(2,1)S(1)} %get-tuple-element.122), channel_id=1, source_target_pairs={{0,24},{8,16},{16,8},{24,0},{1,25},{9,17},{17,9},{25,1},{2,26},{10... | collective-permute-start | bytes 786440 | tf_op jit(solution)/shard_map/ppermute | solution.py:1030
  127.9 15.4 %collective-permute-start.18 = (bf16[512,256]{1,0:T(8,128)(2,1)S(1)}, bf16[512,256]{1,0:T(8,128)(2,1)S(1)}, u32[]{:S(2)}, u32[]{:S(2)}) collective-permute-start(bf16[512,256]{1,0:T(8,128)(2,1)S(1)} %get-tuple-element.124), channel_id=1, source_target_pairs={{0,8},{8,0},{16,24},{24,16},{1,9},{9,1},{17,25},{25,17},{2,10},{10... | collective-permute-start | bytes 786440 | tf_op jit(solution)/shard_map/ppermute | solution.py:1030
  128.5 14.9 %collective-permute-start.19 = (bf16[512,256]{1,0:T(8,128)(2,1)S(1)}, bf16[512,256]{1,0:T(8,128)(2,1)S(1)}, u32[]{:S(2)}, u32[]{:S(2)}) collective-permute-start(bf16[512,256]{1,0:T(8,128)(2,1)S(1)} %get-tuple-element.125), channel_id=1, source_target_pairs={{0,16},{8,24},{16,0},{24,8},{1,17},{9,25},{17,1},{25,9},{2,18},{10... | collective-permute-start | bytes 786440 | tf_op jit(solution)/shard_map/ppermute | solution.py:1030
  131.8 6.7 %collective-permute-start.17 = (bf16[128,128]{1,0:T(8,128)(2,1)S(1)}, bf16[128,128]{1,0:T(8,128)(2,1)S(1)}, u32[]{:S(2)}, u32[]{:S(2)}) collective-permute-start(bf16[128,128]{1,0:T(8,128)(2,1)S(1)} %fusion.12), channel_id=1, source_target_pairs={{0,6},{1,7},{2,4},{3,5},{4,2},{5,3},{6,0},{7,1},{8,14},{9,15},{10,... | collective-permute-start | bytes 98312 | tf_op jit(solution)/shard_map/ppermute | solution.py:1030
  131.9 6.6 %collective-permute-start.16 = (bf16[128,128]{1,0:T(8,128)(2,1)S(1)}, bf16[128,128]{1,0:T(8,128)(2,1)S(1)}, u32[]{:S(2)}, u32[]{:S(2)}) collective-permute-start(bf16[128,128]{1,0:T(8,128)(2,1)S(1)} %fusion.12), channel_id=1, source_target_pairs={{0,4},{1,5},{2,6},{3,7},{4,0},{5,1},{6,2},{7,3},{8,12},{9,13},{10,... | collective-permute-start | bytes 98312 | tf_op jit(solution)/shard_map/ppermute | solution.py:1030
  138.6 4.8 %collective-permute-start.15 = (bf16[128,128]{1,0:T(8,128)(2,1)S(1)}, bf16[128,128]{1,0:T(8,128)(2,1)S(1)}, u32[]{:S(2)}, u32[]{:S(2)}) collective-permute-start(bf16[128,128]{1,0:T(8,128)(2,1)S(1)} %fusion.12), channel_id=1, source_target_pairs={{0,2},{1,3},{2,0},{3,1},{4,6},{5,7},{6,4},{7,5},{8,10},{9,11},{10,... | collective-permute-start | bytes 98312 | tf_op jit(solution)/shard_map/ppermute | solution.py:1030
  143.4 1.4 collective-permute-start.21
  155.0 3.8 %copy-start.15 = (bf16[320,256]{1,0:T(8,128)(2,1)S(1)}, bf16[320,256]{1,0:T(8,128)(2,1)}, u32[]{:S(2)}) copy-start(bf16[320,256]{1,0:T(8,128)(2,1)} %get-tuple-element.102) | copy-start | bytes 491524
  155.0 11.5 %copy-start.9 = (bf16[320,256]{1,0:T(8,128)(2,1)S(1)}, bf16[320,256]{1,0:T(8,128)(2,1)}, u32[]{:S(2)}) copy-start(bf16[320,256]{1,0:T(8,128)(2,1)} %get-tuple-element.99) | copy-start | bytes 491524
  155.2 42.7 %copy-start.1 = (bf16[128,1024]{1,0:T(8,128)(2,1)S(1)}, bf16[128,1024]{1,0:T(8,128)(2,1)}, u32[]{:S(2)}) copy-start(bf16[128,1024]{1,0:T(8,128)(2,1)} %refs_11_.1) | copy-start | bytes 786436
  155.2 42.7 %copy-start.2 = (bf16[128,1024]{1,0:T(8,128)(2,1)S(1)}, bf16[128,1024]{1,0:T(8,128)(2,1)}, u32[]{:S(2)}) copy-start(bf16[128,1024]{1,0:T(8,128)(2,1)} %refs_12_.1) | copy-start | bytes 786436
  155.2 42.7 %copy-start.5 = (f32[1024]{0:T(1024)S(1)}, f32[1024]{0:T(1024)}, u32[]{:S(2)}) copy-start(f32[1024]{0:T(1024)} %param.15) | copy-start | bytes 12292
  155.9 7.6 %collective-permute-start.22 = (bf16[320,256]{1,0:T(8,128)(2,1)S(1)}, bf16[320,256]{1,0:T(8,128)(2,1)S(1)}, u32[]{:S(2)}, u32[]{:S(2)}) collective-permute-start(bf16[320,256]{1,0:T(8,128)(2,1)S(1)} %copy-done.17), channel_id=1, source_target_pairs={{0,8},{8,0},{16,24},{24,16},{1,9},{9,1},{17,25},{25,17},{2,10},{10... | collective-permute-start | bytes 491528 | tf_op jit(solution)/shard_map/ppermute | solution.py:1030
  156.9 8.8 %collective-permute-start.23 = (bf16[320,256]{1,0:T(8,128)(2,1)S(1)}, bf16[320,256]{1,0:T(8,128)(2,1)S(1)}, u32[]{:S(2)}, u32[]{:S(2)}) collective-permute-start(bf16[320,256]{1,0:T(8,128)(2,1)S(1)} %copy-done.16), channel_id=1, source_target_pairs={{0,16},{8,24},{16,0},{24,8},{1,17},{9,25},{17,1},{25,9},{2,18},{10... | collective-permute-start | bytes 491528 | tf_op jit(solution)/shard_map/ppermute | solution.py:1030
  158.8 7.7 %collective-permute-start.24 = (bf16[320,256]{1,0:T(8,128)(2,1)S(1)}, bf16[320,256]{1,0:T(8,128)(2,1)S(1)}, u32[]{:S(2)}, u32[]{:S(2)}) collective-permute-start(bf16[320,256]{1,0:T(8,128)(2,1)S(1)} %copy-done.15), channel_id=1, source_target_pairs={{0,24},{8,16},{16,8},{24,0},{1,25},{9,17},{17,9},{25,1},{2,26},{10... | collective-permute-start | bytes 491528 | tf_op jit(solution)/shard_map/ppermute | solution.py:1030
  160.1 12.5 %all-to-all-start.2 = ((bf16[8,32,256]{2,1,0:T(8,128)(2,1)}), bf16[8,32,256]{2,1,0:T(8,128)(2,1)S(1)}, u32[]{:S(2)}, u32[]{:S(2)}) async-start(bf16[8,32,256]{2,1,0:T(8,128)(2,1)} %bitcast.60), calls=%async_computation.2 | async-start | bytes 262144 | tf_op jit(solution)/shard_map/all_to_all | solution.py:1088
  172.5 15.1 %all-to-all-start.1 = ((bf16[8,48,256]{2,1,0:T(8,128)(2,1)}), bf16[8,48,256]{2,1,0:T(8,128)(2,1)S(1)}, u32[]{:S(2)}, u32[]{:S(2)}) async-start(bf16[8,48,256]{2,1,0:T(8,128)(2,1)} %fusion.10), calls=%async_computation.1 | async-start | bytes 393216 | tf_op jit(solution)/shard_map/all_to_all | solution.py:1088
  176.0 14.0 %collective-permute-start.30 = (bf16[512,256]{1,0:T(8,128)(2,1)S(1)}, bf16[512,256]{1,0:T(8,128)(2,1)S(1)}, u32[]{:S(2)}, u32[]{:S(2)}) collective-permute-start(bf16[512,256]{1,0:T(8,128)(2,1)S(1)} %pad_maximum_fusion.refs_4_), channel_id=1, source_target_pairs={{0,24},{8,16},{16,8},{24,0},{1,25},{9,17},{17,9},{25,1},{2,26},{10... | collective-permute-start | bytes 786440 | tf_op jit(solution)/shard_map/ppermute | solution.py:1030
  178.4 13.4 %collective-permute-start.29 = (bf16[512,256]{1,0:T(8,128)(2,1)S(1)}, bf16[512,256]{1,0:T(8,128)(2,1)S(1)}, u32[]{:S(2)}, u32[]{:S(2)}) collective-permute-start(bf16[512,256]{1,0:T(8,128)(2,1)S(1)} %pad_maximum_fusion.refs_4_), channel_id=1, source_target_pairs={{0,16},{8,24},{16,0},{24,8},{1,17},{9,25},{17,1},{25,9},{2,18},{10... | collective-permute-start | bytes 786440 | tf_op jit(solution)/shard_map/ppermute | solution.py:1030
  178.5 13.3 %collective-permute-start.28 = (bf16[512,256]{1,0:T(8,128)(2,1)S(1)}, bf16[512,256]{1,0:T(8,128)(2,1)S(1)}, u32[]{:S(2)}, u32[]{:S(2)}) collective-permute-start(bf16[512,256]{1,0:T(8,128)(2,1)S(1)} %pad_maximum_fusion.refs_4_), channel_id=1, source_target_pairs={{0,8},{8,0},{16,24},{24,16},{1,9},{9,1},{17,25},{25,17},{2,10},{10... | collective-permute-start | bytes 786440 | tf_op jit(solution)/shard_map/ppermute | solution.py:1030
  187.7 8.0 %collective-permute-start.27 = (bf16[304,256]{1,0:T(8,128)(2,1)S(1)}, bf16[304,256]{1,0:T(8,128)(2,1)S(1)}, u32[]{:S(2)}, u32[]{:S(2)}) collective-permute-start(bf16[304,256]{1,0:T(8,128)(2,1)S(1)} %pad_maximum_fusion.1.refs_0_), channel_id=1, source_target_pairs={{0,24},{8,16},{16,8},{24,0},{1,25},{9,17},{17,9},{25,1},{2,26},{10... | collective-permute-start | bytes 466952 | tf_op jit(solution)/shard_map/ppermute | solution.py:1030
  190.0 7.9 %collective-permute-start.26 = (bf16[304,256]{1,0:T(8,128)(2,1)S(1)}, bf16[304,256]{1,0:T(8,128)(2,1)S(1)}, u32[]{:S(2)}, u32[]{:S(2)}) collective-permute-start(bf16[304,256]{1,0:T(8,128)(2,1)S(1)} %pad_maximum_fusion.1.refs_0_), channel_id=1, source_target_pairs={{0,16},{8,24},{16,0},{24,8},{1,17},{9,25},{17,1},{25,9},{2,18},{10... | collective-permute-start | bytes 466952 | tf_op jit(solution)/shard_map/ppermute | solution.py:1030
  190.0 7.9 %collective-permute-start.25 = (bf16[304,256]{1,0:T(8,128)(2,1)S(1)}, bf16[304,256]{1,0:T(8,128)(2,1)S(1)}, u32[]{:S(2)}, u32[]{:S(2)}) collective-permute-start(bf16[304,256]{1,0:T(8,128)(2,1)S(1)} %pad_maximum_fusion.1.refs_0_), channel_id=1, source_target_pairs={{0,8},{8,0},{16,24},{24,16},{1,9},{9,1},{17,25},{25,17},{2,10},{10... | collective-permute-start | bytes 466952 | tf_op jit(solution)/shard_map/ppermute | solution.py:1030
  (13 other events, 14.2 us)
Sparse Core Ops, SparseCore 0:
  9.7 34.1 all-gather.2
  45.5 34.2 all-gather.4
  116.7 37.4 reduce-scatter.2
  156.9 36.9 reduce-scatter.4
